TPU v7x, 32 devices: a whole 2x2x4 slice. The times are simulated.
32 devices in a mesh: row: 4 (over y, x), col: 8 (over z, core).
Axes of the slice: x: 2, y: 2, z: 4, core: 2. Of those that a mesh axis runs over, the one named last changes fastest.
Arguments:
- grad_out: bfloat16 [1536, 8192], P('row', 'col'), may hold values from -6 to 6
- gate_act: bfloat16 [1536, 28672], P('row', 'col'), may hold values from -6 to 6
- up_act: bfloat16 [1536, 28672], P('row', 'col'), may hold values from -6 to 6
- down_weight: bfloat16 [28672, 8192], P('col', 'row'), may hold values from -0.0625 to 0.0625
Outputs:
- grad_gate: bfloat16 [1536, 28672], P('row', 'col')
- grad_up: bfloat16 [1536, 28672], P('row', 'col')
- grad_weight: float32 [28672, 8192], P('col', 'row')
All inputs are finite; a program needn't handle non-finite values.
Results may differ from a plain program's by a relative error of at most 0.0028.
Values may be sent and summed in bfloat16 or wider, within the bound.
No kernel may reach another device: no remote copies, remote signals or barrier semaphores. Data moves between devices by JAX's collectives and lax.ppermute only.
A program may use at most 192 MiB of HBM per device.

v0:
```python
import jax
import jax.numpy as jnp
from jax import lax
from jax.sharding import PartitionSpec as P

CHUNKS = 2
BOTH = ("row", "col")


def exchange_pairs(rows, cols, step):
    bits = rows.bit_length() - 1
    return [
        (r * cols + c, (r ^ (1 << ((step + c) % bits))) * cols + c)
        for r in range(rows)
        for c in range(cols)
    ]


def row_offset(rows, place, turn):
    bits = rows.bit_length() - 1
    return sum(1 << ((step + turn) % bits) for step in range(bits) if place >> step & 1)


def collect_tokens(grad_out, front, front_came, rows, cols):
    share = cols // rows
    part = grad_out.shape[0] // cols
    row, col = lax.axis_index("row"), lax.axis_index("col")
    plane, lane = col // share, col % share

    pieces = grad_out.reshape(rows, share, part, grad_out.shape[1])
    arrived = []
    for shift in range(share):
        piece = lax.dynamic_index_in_dim(pieces, (lane + shift) % share, 1, keepdims=False)
        if shift:
            pairs = [
                (p * share + k, p * share + (k + shift) % share)
                for p in range(rows)
                for k in range(share)
            ]
            piece = lax.ppermute(piece, "col", pairs)
        arrived.append(piece)
    arrived = jnp.stack(arrived)
    mine = jnp.concatenate(
        [
            lax.dynamic_index_in_dim(arrived, (lane - k) % share, 0, keepdims=False)
            for k in range(share)
        ],
        axis=2,
    )

    mine, _ = lax.optimization_barrier((mine, front))

    held = []
    for flip in range(rows):
        piece = lax.dynamic_index_in_dim(mine, plane ^ flip, 0, keepdims=False)
        if flip:
            pairs = [(c, (c // share ^ flip) * share + c % share) for c in range(cols)]
            piece = lax.ppermute(piece, "col", pairs)
        held.append(piece)
    held, _ = lax.optimization_barrier((jnp.stack(held), front_came))

    blocks = [None] * rows
    for flip in reversed(range(rows)):
        piece = lax.dynamic_index_in_dim(held, row ^ flip ^ plane, 0, keepdims=False)
        if flip < rows - 1:
            piece, _ = lax.optimization_barrier((piece, blocks[-1]))
        if flip:
            piece = lax.ppermute(piece, "row", [(r, r ^ flip) for r in range(rows)])
        blocks[flip] = piece
    first = lax.all_gather(blocks[-1], "col", axis=0, tiled=True)
    rest = lax.all_gather(jnp.stack(blocks[:-1]), "col", axis=1, tiled=True)
    return [rest[flip] for flip in range(rows - 1)] + [first]


def on_device(grad_out, gate_act, up_act, down_weight):
    rows, cols = lax.axis_size("row"), lax.axis_size("col")
    steps = rows.bit_length() - 1
    pairs = [exchange_pairs(rows, cols, step) for step in range(steps)]

    def activation(gate, up):
        gate = gate.astype(jnp.float32)
        return (gate * jax.nn.sigmoid(gate) * up.astype(jnp.float32)).astype(jnp.bfloat16)

    gate_halves, up_halves = jnp.split(gate_act, 2), jnp.split(up_act, 2)
    front = activation(gate_halves[0], up_halves[0])
    front_came = lax.ppermute(front, BOTH, pairs[0])
    front, *late = lax.optimization_barrier((front, gate_halves[1], up_halves[1]))
    back = activation(*late)
    gathered = [
        jnp.concatenate([front, back]),
        jnp.concatenate([front_came, lax.ppermute(back, BOTH, pairs[0])]),
    ]
    gathered[0], _ = lax.optimization_barrier((gathered[0], front_came))
    for step in range(1, steps):
        gathered = gathered + [lax.ppermute(part, BOTH, pairs[step]) for part in gathered]

    blocks = collect_tokens(grad_out, front, front_came, rows, cols)
    gate_act, up_act, _ = lax.optimization_barrier((gate_act, up_act, front_came))
    turn = lax.axis_index("col") % steps
    grads = [
        lax.select_n(turn, *(blocks[row_offset(rows, place, t)] for t in range(steps)))
        if 0 < place < rows - 1
        else blocks[place]
        for place in range(rows)
    ]
    width = down_weight.shape[0] // CHUNKS
    weights = [
        lax.slice_in_dim(down_weight, chunk * width, (chunk + 1) * width, axis=0)
        for chunk in range(CHUNKS)
    ]
    came = [[[] for _ in range(rows)] for _ in range(CHUNKS)]

    def partial(chunk, place):
        return lax.dot_general(
            grads[place],
            weights[chunk],
            (((1,), (1,)), ((), ())),
            preferred_element_type=jnp.float32,
        )

    for step in range(steps):
        for place in reversed(range(rows)):
            if place & ((1 << step) - 1) or not place >> step & 1:
                continue
            for chunk in range(CHUNKS):
                arrived = came[chunk][place]
                if step == steps - 1:
                    if chunk == 0:
                        every_token, _ = lax.optimization_barrier(
                            (jnp.concatenate(grads, axis=0), total)
                        )
                        grad_weight = lax.dot_general(
                            jnp.concatenate(gathered, axis=0),
                            every_token,
                            (((0,), (0,)), ((), ())),
                            preferred_element_type=jnp.float32,
                        )
                    arrived[0], came[chunk][0][-1] = lax.optimization_barrier(
                        (arrived[0], came[chunk][0][-1])
                    )
                    if chunk == CHUNKS - 1:
                        arrived[0], grad_weight = lax.optimization_barrier(
                            (arrived[0], grad_weight)
                        )
                total = partial(chunk, place)
                for block in arrived:
                    total = total + block.astype(jnp.float32)
                total = total.astype(jnp.bfloat16)
                if place == rows - 1:
                    total, _ = lax.optimization_barrier((total, gathered[rows // 2]))
                elif step == 0:
                    total, _ = lax.optimization_barrier((total, gathered[rows - 1]))
                sent = lax.ppermute(total, BOTH, pairs[step])
                came[chunk][place ^ (1 << step)].append(sent)
    sums = []
    for chunk in range(CHUNKS):
        total, *arrived = lax.optimization_barrier((partial(chunk, 0), *came[chunk][0]))
        for block in arrived:
            total = total + block.astype(jnp.float32)
        sums.append(total)
    grad_hidden = jnp.concatenate(sums, axis=1)

    gate_value = gate_act.astype(jnp.float32)
    up_value = up_act.astype(jnp.float32)
    sigmoid_gate = jax.nn.sigmoid(gate_value)
    grad_gate = (
        grad_hidden * up_value * sigmoid_gate * (1.0 + gate_value * (1.0 - sigmoid_gate))
    ).astype(jnp.bfloat16)
    grad_up = (grad_hidden * (gate_value * sigmoid_gate)).astype(jnp.bfloat16)
    return (grad_gate, grad_up, grad_weight)


def solution(mesh):
    placed = (P("row", "col"), P("row", "col"), P("row", "col"), P("col", "row"))
    return jax.shard_map(
        on_device,
        mesh=mesh,
        in_specs=placed,
        out_specs=(P("row", "col"), P("row", "col"), P("col", "row")),
        check_vma=False,
    )
```

profile of v0, /device:TPU:0, one launch (start us, length us, event | category | flops | bytes accessed | tf_op | source)
XLA Modules:
  0.0 258.9 jit_solution(6957292317969305073)
XLA Ops:
  7.3 1.2 dynamic-slice_bitcast_fusion
  9.0 3.7 %fusion.51 = bf16[192,3584]{1,0:T(8,128)(2,1)} fusion(bf16[384,3584]{1,0:T(8,128)(2,1)} %param.6, bf16[384,3584]{1,0:T(8,128)(2,1)} %param.5), kind=kLoop, calls=%fused_computation.53 | loop fusion | flops 5505024 | bytes 4128768 | tf_op jit(solution)/shard_map/convert_element_type | solution.py:82
  12.6 2.5 collective-permute-start.4
  15.5 0.8 constant_dynamic-slice_fusion
  16.3 3.6 %collective-permute-start.3 = (bf16[48,2048]{1,0:T(8,128)(2,1)}, bf16[48,2048]{1,0:T(8,128)(2,1)S(1)}, u32[]{:S(2)}, u32[]{:S(2)}) collective-permute-start(bf16[48,2048]{1,0:T(8,128)(2,1)} %get-tuple-element.69), channel_id=1, source_target_pairs={{0,6},{1,7},{2,4},{3,5},{4,2},{5,3},{6,0},{7,1},{8,14},{9,15},{10,... | collective-permute-start | bytes 589832 | tf_op jit(solution)/shard_map/ppermute | solution.py:58
  19.9 0.8 collective-permute-start.1
  20.7 5.5 %collective-permute-done.3 = bf16[48,2048]{1,0:T(8,128)(2,1)S(1)} collective-permute-done((bf16[48,2048]{1,0:T(8,128)(2,1)}, bf16[48,2048]{1,0:T(8,128)(2,1)S(1)}, u32[]{:S(2)}, u32[]{:S(2)}) %collective-permute-start.3) | collective-permute-done | bytes 196640 | tf_op jit(solution)/shard_map/ppermute | solution.py:58
  26.2 11.1 %collective-permute-done.2 = bf16[48,2048]{1,0:T(8,128)(2,1)} collective-permute-done((bf16[48,2048]{1,0:T(8,128)(2,1)S(1)}, bf16[48,2048]{1,0:T(8,128)(2,1)}, u32[]{:S(2)}, u32[]{:S(2)}) %collective-permute-start.2) | collective-permute-done | bytes 196640 | tf_op jit(solution)/shard_map/ppermute | solution.py:58
  37.3 1.1 pad_maximum_fusion.5
  38.5 1.5 collective-permute-start.5
  40.0 5.7 %collective-permute-done.5 = bf16[48,2048]{1,0:T(8,128)(2,1)S(1)} collective-permute-done((bf16[48,2048]{1,0:T(8,128)(2,1)S(1)}, bf16[48,2048]{1,0:T(8,128)(2,1)S(1)}, u32[]{:S(2)}, u32[]{:S(2)}) %collective-permute-start.5) | collective-permute-done | bytes 196640 | tf_op jit(solution)/shard_map/ppermute | solution.py:68
  45.7 0.7 copy-done.5
  46.5 1.8 collective-permute-start.6
  48.5 4.1 %collective-permute-done.6 = bf16[48,2048]{1,0:T(8,128)(2,1)S(1)} collective-permute-done((bf16[48,2048]{1,0:T(8,128)(2,1)S(1)}, bf16[48,2048]{1,0:T(8,128)(2,1)S(1)}, u32[]{:S(2)}, u32[]{:S(2)}) %collective-permute-start.6) | collective-permute-done | bytes 196640 | tf_op jit(solution)/shard_map/ppermute | solution.py:68
  52.6 1.5 collective-permute-done.7
  54.1 0.9 pad_maximum_fusion.6
  55.0 0.8 fusion.50
  56.3 1.5 pad_maximum_fusion.2
  58.2 30.8 %collective-permute-done.10 = bf16[192,3584]{1,0:T(8,128)(2,1)S(1)} collective-permute-done((bf16[192,3584]{1,0:T(8,128)(2,1)S(1)}, bf16[192,3584]{1,0:T(8,128)(2,1)S(1)}, u32[]{:S(2)}, u32[]{:S(2)}) %collective-permute-start.10) | collective-permute-done | bytes 1376288 | tf_op jit(solution)/shard_map/ppermute | solution.py:91
  89.0 1.1 copy-done.2
  90.1 3.1 %pad_maximum_fusion.3 = bf16[384,3584]{1,0:T(8,128)(2,1)} fusion(bf16[192,3584]{1,0:T(8,128)(2,1)S(1)} %collective-permute-done.10, bf16[192,3584]{1,0:T(8,128)(2,1)} %collective-permute-done.4), kind=kLoop, calls=%fused_computation.48 | loop fusion | flops 5505024 | bytes 5505024 | tf_op jit(solution)/shard_map/concatenate | solution.py:91
  93.3 1.7 constant_dynamic-update-slice_fusion.4
  94.9 2.5 constant_dynamic-update-slice_fusion.3
  97.5 1.2 constant_dynamic-update-slice_fusion.2
  98.7 2.3 collective-permute-done.8
  100.9 3.6 %constant_dynamic-update-slice_fusion.1 = bf16[1536,3584]{1,0:T(8,128)(2,1)} fusion(bf16[1536,3584]{1,0:T(8,128)(2,1)} %constant_dynamic-update-slice_fusion.2, bf16[384,3584]{1,0:T(8,128)(2,1)} %collective-permute-done.8), kind=kLoop, calls=%fused_computation.78 | loop fusion | bytes 5505024
  104.5 25.9 %collective-permute-done.11 = bf16[384,3584]{1,0:T(8,128)(2,1)} collective-permute-done((bf16[384,3584]{1,0:T(8,128)(2,1)}, bf16[384,3584]{1,0:T(8,128)(2,1)}, u32[]{:S(2)}, u32[]{:S(2)}) %collective-permute-start.11) | collective-permute-done | bytes 2752544 | tf_op jit(solution)/shard_map/ppermute | solution.py:95
  130.4 3.5 %constant_dynamic-update-slice_fusion = bf16[1536,3584]{1,0:T(8,128)(2,1)} fusion(bf16[1536,3584]{1,0:T(8,128)(2,1)} %constant_dynamic-update-slice_fusion.1, bf16[384,3584]{1,0:T(8,128)(2,1)} %collective-permute-done.11), kind=kLoop, calls=%fused_computation.77 | loop fusion | bytes 5505024 | tf_op jit(solution)/shard_map/concatenate | solution.py:133
  133.9 7.8 %fusion.36 = bf16[384,1792]{1,0:T(8,128)(2,1)} fusion(bf16[384,2048]{1,0:T(8,128)(2,1)} %all-gather.5.cloned.1.call-done, bf16[3584,2048]{1,0:T(8,128)(2,1)} %param.7), kind=kOutput, calls=%fused_computation.37 | convolution fusion | flops 2819260416 | bytes 10289152 | tf_op jit(solution)/shard_map/dot_general | solution.py:114
  141.7 9.1 %fusion.30 = bf16[384,1792]{1,0:T(8,128)(2,1)} fusion(bf16[384,2048]{1,0:T(8,128)(2,1)S(1)} %copy-done.4, bf16[3584,2048]{1,0:T(8,128)(2,1)} %param.7), kind=kOutput, calls=%fused_computation.35 | convolution fusion | flops 2819260416 | bytes 10289152 | tf_op jit(solution)/shard_map/dot_general | solution.py:114
  150.8 0.6 collective-permute-start.9
  151.4 1.5 collective-permute-start.14
  152.8 2.8 %slice_bitcast_fusion = (bf16[384,2048]{1,0:T(8,128)(2,1)S(1)}, bf16[384,2048]{1,0:T(8,128)(2,1)S(1)}, bf16[384,2048]{1,0:T(8,128)(2,1)S(1)}) fusion(bf16[3,384,2048]{2,1,0:T(8,128)(2,1)} %all-gather.3.cloned.1.call-done, pred[]{:T(512)S(6)} %select_n.100), kind=kLoop, calls=%fused_computation.54 | loop fusion | flops 1572864 | bytes 9437185 | tf_op jit(solution)/shard_map/squeeze | solution.py:72
  155.7 6.9 %fusion.39 = bf16[384,1792]{1,0:T(8,128)(2,1)S(1)} fusion(bf16[384,2048]{1,0:T(8,128)(2,1)S(1)} %get-tuple-element.62, bf16[3584,2048]{1,0:T(8,128)(2,1)} %param.7), kind=kOutput, calls=%fused_computation.38 | convolution fusion | flops 2819260416 | bytes 10289152 | tf_op jit(solution)/shard_map/dot_general | solution.py:114
  162.6 6.0 %fusion.33 = bf16[384,1792]{1,0:T(8,128)(2,1)} fusion(bf16[384,2048]{1,0:T(8,128)(2,1)S(1)} %get-tuple-element.62, bf16[3584,2048]{1,0:T(8,128)(2,1)S(1)} %bitcast.55), kind=kOutput, calls=%fused_computation.36 | convolution fusion | flops 2819260416 | bytes 10289152 | tf_op jit(solution)/shard_map/dot_general | solution.py:114
  168.6 0.6 collective-permute-start.15
  169.1 1.1 pad_maximum_fusion
  170.5 1.5 collective-permute-start.12
  171.9 28.6 %fusion.56 = f32[3584,2048]{1,0:T(8,128)} fusion(bf16[1536,3584]{1,0:T(8,128)(2,1)} %constant_dynamic-update-slice_fusion, bf16[1536,2048]{1,0:T(8,128)(2,1)S(1)} %pad_maximum_fusion), kind=kOutput, calls=%fused_computation.83 | convolution fusion | flops 22548578304 | bytes 46661632 | tf_op jit(solution)/shard_map/dot_general | solution.py:132
  200.5 5.7 %fusion.16 = f32[384,1792]{1,0:T(8,128)S(1)} fusion(bf16[384,2048]{1,0:T(8,128)(2,1)S(1)} %get-tuple-element.63, bf16[3584,2048]{1,0:T(8,128)(2,1)} %param.7), kind=kOutput, calls=%fused_computation.21 | convolution fusion | flops 2818572288 | bytes 11665408 | tf_op jit(solution)/shard_map/dot_general | solution.py:114
  206.2 7.3 %collective-permute-done.12 = bf16[384,1792]{1,0:T(8,128)(2,1)S(1)} collective-permute-done((bf16[384,1792]{1,0:T(8,128)(2,1)S(1)}, bf16[384,1792]{1,0:T(8,128)(2,1)S(1)}, u32[]{:S(2)}, u32[]{:S(2)}) %collective-permute-start.12) | collective-permute-done | bytes 1376288 | tf_op jit(solution)/shard_map/ppermute | solution.py:153
  214.3 6.8 %fusion.27 = bf16[384,1792]{1,0:T(8,128)(2,1)S(1)} fusion(bf16[384,2048]{1,0:T(8,128)(2,1)S(1)} %get-tuple-element.63, bf16[3584,2048]{1,0:T(8,128)(2,1)} %param.7, bf16[384,1792]{1,0:T(8,128)(2,1)} %collective-permute-done.14), kind=kOutput, calls=%fused_computation.34 | convolution fusion | flops 2820636672 | bytes 11665408 | tf_op jit(solution)/shard_map/dot_general | solution.py:114
  221.1 1.4 collective-permute-start.16
  222.5 5.7 %fusion.22 = f32[384,1792]{1,0:T(8,128)S(1)} fusion(bf16[3584,2048]{1,0:T(8,128)(2,1)} %param.7, bf16[3,384,2048]{2,1,0:T(8,128)(2,1)S(1)} %bitcast.47), kind=kOutput, calls=%fused_computation.27 | convolution fusion | flops 2818572288 | bytes 11665408 | tf_op jit(solution)/shard_map/dot_general | solution.py:114
  228.2 6.0 %fusion.14 = f32[384,1792]{1,0:T(8,128)S(1)} fusion(bf16[3584,2048]{1,0:T(8,128)(2,1)} %param.7, bf16[3,384,2048]{2,1,0:T(8,128)(2,1)S(1)} %bitcast.47), kind=kOutput, calls=%fused_computation.19 | convolution fusion | flops 2818572288 | bytes 11665408 | tf_op jit(solution)/shard_map/dot_general | solution.py:114
  234.3 12.7 %collective-permute-done.16 = bf16[384,1792]{1,0:T(8,128)(2,1)S(1)} collective-permute-done((bf16[384,1792]{1,0:T(8,128)(2,1)S(1)}, bf16[384,1792]{1,0:T(8,128)(2,1)S(1)}, u32[]{:S(2)}, u32[]{:S(2)}) %collective-permute-start.16) | collective-permute-done | bytes 1376288 | tf_op jit(solution)/shard_map/ppermute | solution.py:153
  247.0 0.7 convert_add_fusion
  247.7 4.3 %fusion.7 = (bf16[384,3584]{1,0:T(8,128)(2,1)}, bf16[384,3584]{1,0:T(8,128)(2,1)}) fusion(bf16[384,3584]{1,0:T(8,128)(2,1)S(1)} %copy-done, f32[384,1792]{1,0:T(8,128)S(1)} %get-tuple-element.76, f32[384,1792]{1,0:T(8,128)S(1)} %get-tuple-element.77, bf16[384,3584]{1,0:T(8,128)(2,1)S(1)} %copy-done.1), kind=kLoop, calls=%fused_computation.11 | loop fusion | flops 22020096 | bytes 16515072 | tf_op jit(solution)/shard_map/convert_element_type | solution.py:169
  (54 shorter events, 3.3 us)
Async XLA Ops:
  7.2 126.7 %all-gather.5.cloned.1.call-start = ((), (), s32[]{:S(2)}) async-start(), calls=%async_computation.1 | async-start | bytes 1769472 | tf_op jit(solution)/shard_map/all_gather | solution.py:70
  8.5 6.7 %collective-permute-start = (bf16[4,48,1024]{2,1,0:T(8,128)(2,1)S(1)}, bf16[4,48,1024]{2,1,0:T(8,128)(2,1)S(1)}, u32[]{:S(2)}, u32[]{:S(2)}) collective-permute-start(bf16[4,48,1024]{2,1,0:T(8,128)(2,1)S(1)} %get-tuple-element.74), channel_id=1, source_target_pairs={{0,1},{1,0},{2,3},{3,2},{4,5},{5,4},{6,7},{7,6},{8,9},{9,8},{10,11... | collective-permute-start | bytes 1179656 | tf_op jit(solution)/shard_map/ppermute | solution.py:40
  12.6 25.8 %collective-permute-start.4 = (bf16[192,3584]{1,0:T(8,128)(2,1)}, bf16[192,3584]{1,0:T(8,128)(2,1)}, u32[]{:S(2)}, u32[]{:S(2)}) collective-permute-start(bf16[192,3584]{1,0:T(8,128)(2,1)} %fusion.51), channel_id=1, source_target_pairs={{0,8},{1,17},{2,10},{3,19},{4,12},{5,21},{6,14},{7,23},{8,0},{9,25... | collective-permute-start | bytes 4128776 | tf_op jit(solution)/shard_map/ppermute | solution.py:86
  16.3 38.7 %slice-start = ((bf16[384,3584]{1,0:T(8,128)(2,1)}), bf16[192,3584]{1,0:T(8,128)(2,1)S(1)}, s32[]{:S(2)}) async-start(bf16[384,3584]{1,0:T(8,128)(2,1)} %param.5), calls=%async_computation.2 | async-start | bytes 2752512 | tf_op jit(solution)/shard_map/split | solution.py:84
  16.3 38.7 %slice-start.1 = ((bf16[384,3584]{1,0:T(8,128)(2,1)}), bf16[192,3584]{1,0:T(8,128)(2,1)S(1)}, s32[]{:S(2)}) async-start(bf16[384,3584]{1,0:T(8,128)(2,1)} %param.6), calls=%async_computation.3 | async-start | bytes 2752512 | tf_op jit(solution)/shard_map/split | solution.py:84
  16.3 9.9 %collective-permute-start.3 = (bf16[48,2048]{1,0:T(8,128)(2,1)}, bf16[48,2048]{1,0:T(8,128)(2,1)S(1)}, u32[]{:S(2)}, u32[]{:S(2)}) collective-permute-start(bf16[48,2048]{1,0:T(8,128)(2,1)} %get-tuple-element.69), channel_id=1, source_target_pairs={{0,6},{1,7},{2,4},{3,5},{4,2},{5,3},{6,0},{7,1},{8,14},{9,15},{10,... | collective-permute-start | bytes 589832 | tf_op jit(solution)/shard_map/ppermute | solution.py:58
  19.9 17.4 %collective-permute-start.2 = (bf16[48,2048]{1,0:T(8,128)(2,1)S(1)}, bf16[48,2048]{1,0:T(8,128)(2,1)}, u32[]{:S(2)}, u32[]{:S(2)}) collective-permute-start(bf16[48,2048]{1,0:T(8,128)(2,1)S(1)} %get-tuple-element.70), channel_id=1, source_target_pairs={{0,4},{1,5},{2,6},{3,7},{4,0},{5,1},{6,2},{7,3},{8,12},{9,13},{10,... | collective-permute-start | bytes 589832 | tf_op jit(solution)/shard_map/ppermute | solution.py:58
  19.9 17.4 %collective-permute-start.1 = (bf16[48,2048]{1,0:T(8,128)(2,1)S(1)}, bf16[48,2048]{1,0:T(8,128)(2,1)}, u32[]{:S(2)}, u32[]{:S(2)}) collective-permute-start(bf16[48,2048]{1,0:T(8,128)(2,1)S(1)} %get-tuple-element.71), channel_id=1, source_target_pairs={{0,2},{1,3},{2,0},{3,1},{4,6},{5,7},{6,4},{7,5},{8,10},{9,11},{10,... | collective-permute-start | bytes 589832 | tf_op jit(solution)/shard_map/ppermute | solution.py:58
  38.5 7.2 %collective-permute-start.5 = (bf16[48,2048]{1,0:T(8,128)(2,1)S(1)}, bf16[48,2048]{1,0:T(8,128)(2,1)S(1)}, u32[]{:S(2)}, u32[]{:S(2)}) collective-permute-start(bf16[48,2048]{1,0:T(8,128)(2,1)S(1)} %get-tuple-element.67), channel_id=1, source_target_pairs={{0,24},{8,16},{16,8},{24,0},{1,25},{9,17},{17,9},{25,1},{2,26},{10... | collective-permute-start | bytes 589832 | tf_op jit(solution)/shard_map/ppermute | solution.py:68
  45.7 0.7 copy-start.5
  46.4 106.4 %all-gather.3.cloned.1.call-start = ((), (), s32[]{:S(2)}) async-start(), calls=%async_computation | async-start | bytes 5308416 | tf_op jit(solution)/shard_map/all_gather | solution.py:71
  46.5 6.1 %collective-permute-start.6 = (bf16[48,2048]{1,0:T(8,128)(2,1)S(1)}, bf16[48,2048]{1,0:T(8,128)(2,1)S(1)}, u32[]{:S(2)}, u32[]{:S(2)}) collective-permute-start(bf16[48,2048]{1,0:T(8,128)(2,1)S(1)} %get-tuple-element.35), channel_id=1, source_target_pairs={{0,8},{8,0},{16,24},{24,16},{1,9},{9,1},{17,25},{25,17},{2,10},{10... | collective-permute-start | bytes 589832 | tf_op jit(solution)/shard_map/ppermute | solution.py:68
  48.3 5.8 %collective-permute-start.7 = (bf16[48,2048]{1,0:T(8,128)(2,1)S(1)}, bf16[48,2048]{1,0:T(8,128)(2,1)S(1)}, u32[]{:S(2)}, u32[]{:S(2)}) collective-permute-start(bf16[48,2048]{1,0:T(8,128)(2,1)S(1)} %get-tuple-element.36), channel_id=1, source_target_pairs={{0,16},{8,24},{16,0},{24,8},{1,17},{9,25},{17,1},{25,9},{2,18},{10... | collective-permute-start | bytes 589832 | tf_op jit(solution)/shard_map/ppermute | solution.py:68
  55.9 33.1 %collective-permute-start.10 = (bf16[192,3584]{1,0:T(8,128)(2,1)S(1)}, bf16[192,3584]{1,0:T(8,128)(2,1)S(1)}, u32[]{:S(2)}, u32[]{:S(2)}) collective-permute-start(bf16[192,3584]{1,0:T(8,128)(2,1)S(1)} %fusion.50), channel_id=1, source_target_pairs={{0,8},{1,17},{2,10},{3,19},{4,12},{5,21},{6,14},{7,23},{8,0},{9,25... | collective-permute-start | bytes 4128776 | tf_op jit(solution)/shard_map/ppermute | solution.py:91
  57.8 43.1 %collective-permute-start.8 = (bf16[384,3584]{1,0:T(8,128)(2,1)S(1)}, bf16[384,3584]{1,0:T(8,128)(2,1)}, u32[]{:S(2)}, u32[]{:S(2)}) collective-permute-start(bf16[384,3584]{1,0:T(8,128)(2,1)S(1)} %pad_maximum_fusion.2), channel_id=1, source_target_pairs={{0,16},{1,9},{2,18},{3,11},{4,20},{5,13},{6,22},{7,15},{8,24},{9,1... | collective-permute-start | bytes 8257544 | tf_op jit(solution)/shard_map/ppermute | solution.py:95
  89.0 1.1 copy-start.2
  93.1 37.3 %collective-permute-start.11 = (bf16[384,3584]{1,0:T(8,128)(2,1)}, bf16[384,3584]{1,0:T(8,128)(2,1)}, u32[]{:S(2)}, u32[]{:S(2)}) collective-permute-start(bf16[384,3584]{1,0:T(8,128)(2,1)} %pad_maximum_fusion.3), channel_id=1, source_target_pairs={{0,16},{1,9},{2,18},{3,11},{4,20},{5,13},{6,22},{7,15},{8,24},{9,1... | collective-permute-start | bytes 8257544 | tf_op jit(solution)/shard_map/ppermute | solution.py:95
  93.2 4.2 %copy-start.3 = (bf16[192,3584]{1,0:T(8,128)(2,1)S(1)}, bf16[192,3584]{1,0:T(8,128)(2,1)}, u32[]{:S(2)}) copy-start(bf16[192,3584]{1,0:T(8,128)(2,1)} %copy-done.2) | copy-start | bytes 4128772
  133.9 7.8 %copy-start.4 = (bf16[384,2048]{1,0:T(8,128)(2,1)S(1)}, bf16[384,2048]{1,0:T(8,128)(2,1)}, u32[]{:S(2)}) copy-start(bf16[384,2048]{1,0:T(8,128)(2,1)} %all-gather.5.cloned.1.call-done) | copy-start | bytes 4718596
  150.8 55.4 %collective-permute-start.9 = (bf16[384,1792]{1,0:T(8,128)(2,1)}, bf16[384,1792]{1,0:T(8,128)(2,1)S(1)}, u32[]{:S(2)}, u32[]{:S(2)}) collective-permute-start(bf16[384,1792]{1,0:T(8,128)(2,1)} %fusion.30), channel_id=1, source_target_pairs={{0,8},{1,17},{2,10},{3,19},{4,12},{5,21},{6,14},{7,23},{8,0},{9,25... | collective-permute-start | bytes 4128776 | tf_op jit(solution)/shard_map/ppermute | solution.py:153
  151.4 63.0 %collective-permute-start.14 = (bf16[384,1792]{1,0:T(8,128)(2,1)}, bf16[384,1792]{1,0:T(8,128)(2,1)}, u32[]{:S(2)}, u32[]{:S(2)}) collective-permute-start(bf16[384,1792]{1,0:T(8,128)(2,1)} %fusion.36), channel_id=1, source_target_pairs={{0,8},{1,17},{2,10},{3,19},{4,12},{5,21},{6,14},{7,23},{8,0},{9,25... | collective-permute-start | bytes 4128776 | tf_op jit(solution)/shard_map/ppermute | solution.py:153
  152.8 9.7 %slice-start.4 = ((s8[14680064]{0:T(1024)(128)(4,1)}), s8[4194304]{0:T(1024)(128)(4,1)S(1)}, s32[]{:S(2)}) async-start(s8[14680064]{0:T(1024)(128)(4,1)} %bitcast.54), calls=%async_computation.6 | async-start | bytes 8388608
  152.8 9.8 %slice-start.5 = ((s8[14680064]{0:T(1024)(128)(4,1)}), s8[4194304]{0:T(1024)(128)(4,1)S(1)}, s32[]{:S(2)}) async-start(s8[14680064]{0:T(1024)(128)(4,1)} %bitcast.54), calls=%async_computation.7 | async-start | bytes 8388608
  155.6 7.0 %slice-start.6 = ((s8[14680064]{0:T(1024)(128)(4,1)}), s8[4194304]{0:T(1024)(128)(4,1)S(1)}, s32[]{:S(2)}) async-start(s8[14680064]{0:T(1024)(128)(4,1)} %bitcast.54), calls=%async_computation.8 | async-start | bytes 8388608
  155.6 6.9 %slice-start.7 = ((s8[14680064]{0:T(1024)(128)(4,1)}), s8[2097152]{0:T(1024)(128)(4,1)S(1)}, s32[]{:S(2)}) async-start(s8[14680064]{0:T(1024)(128)(4,1)} %bitcast.54), calls=%async_computation.9 | async-start | bytes 4194304
  168.6 45.7 %collective-permute-start.15 = (bf16[384,1792]{1,0:T(8,128)(2,1)S(1)}, bf16[384,1792]{1,0:T(8,128)(2,1)S(1)}, u32[]{:S(2)}, u32[]{:S(2)}) collective-permute-start(bf16[384,1792]{1,0:T(8,128)(2,1)S(1)} %fusion.39), channel_id=1, source_target_pairs={{0,8},{1,17},{2,10},{3,19},{4,12},{5,21},{6,14},{7,23},{8,0},{9,25... | collective-permute-start | bytes 4128776 | tf_op jit(solution)/shard_map/ppermute | solution.py:153
  169.1 1.3 copy-start.6
  170.5 43.1 %collective-permute-start.12 = (bf16[384,1792]{1,0:T(8,128)(2,1)S(1)}, bf16[384,1792]{1,0:T(8,128)(2,1)S(1)}, u32[]{:S(2)}, u32[]{:S(2)}) collective-permute-start(bf16[384,1792]{1,0:T(8,128)(2,1)S(1)} %copy-done.6), channel_id=1, source_target_pairs={{0,8},{1,17},{2,10},{3,19},{4,12},{5,21},{6,14},{7,23},{8,0},{9,25... | collective-permute-start | bytes 4128776 | tf_op jit(solution)/shard_map/ppermute | solution.py:153
  213.5 9.0 %slice-start.2 = ((s8[4718592]{0:T(1024)(128)(4,1)}), s8[4194304]{0:T(1024)(128)(4,1)S(1)}, s32[]{:S(2)}) async-start(s8[4718592]{0:T(1024)(128)(4,1)} %bitcast.46), calls=%async_computation.4 | async-start | bytes 8388608
  213.9 8.7 %slice-start.3 = ((s8[4718592]{0:T(1024)(128)(4,1)}), s8[524288]{0:T(1024)(128)(4,1)S(1)}, s32[]{:S(2)}) async-start(s8[4718592]{0:T(1024)(128)(4,1)} %bitcast.46), calls=%async_computation.5 | async-start | bytes 1048576
  213.9 20.4 %collective-permute-start.13 = (bf16[384,1792]{1,0:T(8,128)(2,1)S(1)}, bf16[384,1792]{1,0:T(8,128)(2,1)S(1)}, u32[]{:S(2)}, u32[]{:S(2)}) collective-permute-start(bf16[384,1792]{1,0:T(8,128)(2,1)S(1)} %add_convert_fusion), channel_id=1, source_target_pairs={{0,16},{1,9},{2,18},{3,11},{4,20},{5,13},{6,22},{7,15},{8,24},{9,1... | collective-permute-start | bytes 4128776 | tf_op jit(solution)/shard_map/ppermute | solution.py:153
  221.1 25.9 %collective-permute-start.16 = (bf16[384,1792]{1,0:T(8,128)(2,1)S(1)}, bf16[384,1792]{1,0:T(8,128)(2,1)S(1)}, u32[]{:S(2)}, u32[]{:S(2)}) collective-permute-start(bf16[384,1792]{1,0:T(8,128)(2,1)S(1)} %fusion.27), channel_id=1, source_target_pairs={{0,16},{1,9},{2,18},{3,11},{4,20},{5,13},{6,22},{7,15},{8,24},{9,1... | collective-permute-start | bytes 4128776 | tf_op jit(solution)/shard_map/ppermute | solution.py:153
  234.2 13.5 %copy-start = (bf16[384,3584]{1,0:T(8,128)(2,1)S(1)}, bf16[384,3584]{1,0:T(8,128)(2,1)}, u32[]{:S(2)}) copy-start(bf16[384,3584]{1,0:T(8,128)(2,1)} %param.5) | copy-start | bytes 8257540
  234.2 13.5 %copy-start.1 = (bf16[384,3584]{1,0:T(8,128)(2,1)S(1)}, bf16[384,3584]{1,0:T(8,128)(2,1)}, u32[]{:S(2)}) copy-start(bf16[384,3584]{1,0:T(8,128)(2,1)} %param.6) | copy-start | bytes 8257540
Sparse Core Ops, SparseCore 0:
  46.6 24.4 all-gather.4
  73.2 51.1 all-gather.2
where the time goes:
time: 259 us
  waiting for transfers between devices  107 us (41%)
  matrix products  82.5 us (32%)
  other arithmetic  20.7 us (8%)
  starting transfers between devices  17.8 us (7%)
  local copies, waits for them, and re-layouts  16.6 us (6%)
  between operations  14.3 us (6%)
    dot_general x8, matrix products, partial(): lax.dot_general(grads[place], weights[chunk], (((1,), (1,)), ((), ())), p...  54 us
    ppermute x1, waiting for transfers between devices, on_device(): lax.ppermute(back, BOTH, pairs[0])  30.8 us
    dot_general x1, matrix products, on_device(): lax.dot_general(jnp.concatenate(gathered, axis=0), every_token, (((0,), (...  28.6 us
    ppermute x2, waiting for transfers between devices, on_device(): lax.ppermute(part, BOTH, pairs[step])  28.2 us
    ppermute x6, waiting for transfers between devices, on_device(): sent = lax.ppermute(total, BOTH, pairs[step])  20.1 us
    ppermute x4, waiting for transfers between devices, collect_tokens(): piece = lax.ppermute(piece, 'col', pairs)  16.6 us
    ppermute x3, waiting for transfers between devices, collect_tokens(): piece = lax.ppermute(piece, 'row', [(r, r ^ flip) for r in range(rows)])  11.3 us
    unnamed x30, local copies, waits for them, and re-layouts  11.1 us
  transfers between devices with their start and end apart: 19, of which 10 were waited for; matrix products, arithmetic and copies ran while one was open for 43% of the time, Pallas kernels for 0%

commit v1 on v0

--- a/solution.py
+++ b/solution.py
@@ -91,8 +91,9 @@
         jnp.concatenate([front_came, lax.ppermute(back, BOTH, pairs[0])]),
     ]
     gathered[0], _ = lax.optimization_barrier((gathered[0], front_came))
-    for step in range(1, steps):
+    for step in range(1, steps - 1):
         gathered = gathered + [lax.ppermute(part, BOTH, pairs[step]) for part in gathered]
+    gathered.append(lax.ppermute(gathered[0], BOTH, pairs[-1]))
 
     blocks = collect_tokens(grad_out, front, front_came, rows, cols)
     gate_act, up_act, _ = lax.optimization_barrier((gate_act, up_act, front_came))
@@ -126,6 +127,8 @@
                 arrived = came[chunk][place]
                 if step == steps - 1:
                     if chunk == 0:
+                        arrived[0], _ = lax.optimization_barrier((arrived[0], total))
+                    if chunk == CHUNKS - 1:
                         every_token, _ = lax.optimization_barrier(
                             (jnp.concatenate(grads, axis=0), total)
                         )
@@ -135,10 +138,6 @@
                             (((0,), (0,)), ((), ())),
                             preferred_element_type=jnp.float32,
                         )
-                    arrived[0], came[chunk][0][-1] = lax.optimization_barrier(
-                        (arrived[0], came[chunk][0][-1])
-                    )
-                    if chunk == CHUNKS - 1:
                         arrived[0], grad_weight = lax.optimization_barrier(
                             (arrived[0], grad_weight)
                         )
@@ -148,8 +147,10 @@
                 total = total.astype(jnp.bfloat16)
                 if place == rows - 1:
                     total, _ = lax.optimization_barrier((total, gathered[rows // 2]))
-                elif step == 0:
-                    total, _ = lax.optimization_barrier((total, gathered[rows - 1]))
+                    if chunk == CHUNKS - 1:
+                        for part in gathered[1 : rows // 2]:
+                            part, _ = lax.optimization_barrier((part, total))
+                            gathered.append(lax.ppermute(part, BOTH, pairs[-1]))
                 sent = lax.ppermute(total, BOTH, pairs[step])
                 came[chunk][place ^ (1 << step)].append(sent)
     sums = []

time: 259 us -> 262 us (1.012)
  other arithmetic: 20.7 us -> 25.6 us
  matrix products: 82.5 us -> 79.5 us
    ppermute x6, waiting for transfers between devices: 20.1 us -> 12.6 us  [on_device(): sent = lax.ppermute(total, BOTH, pairs[step])]
    ppermute x2, waiting for transfers between devices: 28.2 us -> 32.9 us  [the longest x1 32.5 us: on_device(): gathered.append(lax.ppermute(part, BOTH, pairs[-1]))]
    dot_general x8, matrix products: 54 us -> 50.7 us  [partial(): lax.dot_general(grads[place], weights[chunk], (((1,), (1,)), ((), ())), p...]
    unnamed x30 -> x36, local copies, waits for them, and re-layouts: 11.1 us -> 12.5 us
where the time goes in v1:
time: 262 us
  waiting for transfers between devices  106 us (40%)
  matrix products  79.5 us (30%)
  other arithmetic  25.6 us (10%)
  starting transfers between devices  19.8 us (8%)
  local copies, waits for them, and re-layouts  16.2 us (6%)
  between operations  14.4 us (5%)
    dot_general x8, matrix products, partial(): lax.dot_general(grads[place], weights[chunk], (((1,), (1,)), ((), ())), p...  50.7 us
    ppermute x1, waiting for transfers between devices, on_device(): lax.ppermute(back, BOTH, pairs[0])  33 us
    ppermute x1, waiting for transfers between devices, on_device(): gathered.append(lax.ppermute(part, BOTH, pairs[-1]))  32.5 us
    dot_general x1, matrix products, on_device(): lax.dot_general(jnp.concatenate(gathered, axis=0), every_token, (((0,), (...  28.8 us
    ppermute x4, waiting for transfers between devices, collect_tokens(): piece = lax.ppermute(piece, 'col', pairs)  16.6 us
    ppermute x6, waiting for transfers between devices, on_device(): sent = lax.ppermute(total, BOTH, pairs[step])  12.6 us
    unnamed x36, local copies, waits for them, and re-layouts  12.5 us
    ppermute x3, waiting for transfers between devices, collect_tokens(): piece = lax.ppermute(piece, 'row', [(r, r ^ flip) for r in range(rows)])  11.3 us
  transfers between devices with their start and end apart: 19, of which 10 were waited for; matrix products, arithmetic and copies ran while one was open for 43% of the time, Pallas kernels for 0%

profile of v1, /device:TPU:0, one launch (start us, length us, event | category | flops | bytes accessed | tf_op | source)
XLA Modules:
  0.0 261.9 jit_solution(4353741948664464081)
XLA Ops:
  7.3 1.2 dynamic-slice_bitcast_fusion
  9.0 3.7 %fusion.45 = bf16[192,3584]{1,0:T(8,128)(2,1)} fusion(bf16[384,3584]{1,0:T(8,128)(2,1)} %param.6, bf16[384,3584]{1,0:T(8,128)(2,1)} %param.5), kind=kLoop, calls=%fused_computation.52 | loop fusion | flops 5505024 | bytes 4128768 | tf_op jit(solution)/shard_map/convert_element_type | solution.py:82
  12.6 2.5 collective-permute-start.4
  15.5 0.8 constant_dynamic-slice_fusion
  16.3 3.6 %collective-permute-start.3 = (bf16[48,2048]{1,0:T(8,128)(2,1)}, bf16[48,2048]{1,0:T(8,128)(2,1)S(1)}, u32[]{:S(2)}, u32[]{:S(2)}) collective-permute-start(bf16[48,2048]{1,0:T(8,128)(2,1)} %get-tuple-element.61), channel_id=1, source_target_pairs={{0,6},{1,7},{2,4},{3,5},{4,2},{5,3},{6,0},{7,1},{8,14},{9,15},{10,... | collective-permute-start | bytes 589832 | tf_op jit(solution)/shard_map/ppermute | solution.py:58
  19.9 0.8 collective-permute-start.2
  20.7 5.4 %collective-permute-done.3 = bf16[48,2048]{1,0:T(8,128)(2,1)S(1)} collective-permute-done((bf16[48,2048]{1,0:T(8,128)(2,1)}, bf16[48,2048]{1,0:T(8,128)(2,1)S(1)}, u32[]{:S(2)}, u32[]{:S(2)}) %collective-permute-start.3) | collective-permute-done | bytes 196640 | tf_op jit(solution)/shard_map/ppermute | solution.py:58
  26.1 4.8 %collective-permute-done.1 = bf16[48,2048]{1,0:T(8,128)(2,1)} collective-permute-done((bf16[48,2048]{1,0:T(8,128)(2,1)S(1)}, bf16[48,2048]{1,0:T(8,128)(2,1)}, u32[]{:S(2)}, u32[]{:S(2)}) %collective-permute-start.1) | collective-permute-done | bytes 196640 | tf_op jit(solution)/shard_map/ppermute | solution.py:58
  30.8 6.5 %collective-permute-done.2 = bf16[48,2048]{1,0:T(8,128)(2,1)} collective-permute-done((bf16[48,2048]{1,0:T(8,128)(2,1)S(1)}, bf16[48,2048]{1,0:T(8,128)(2,1)}, u32[]{:S(2)}, u32[]{:S(2)}) %collective-permute-start.2) | collective-permute-done | bytes 196640 | tf_op jit(solution)/shard_map/ppermute | solution.py:58
  37.3 1.1 pad_maximum_fusion.5
  38.5 1.5 collective-permute-start.5
  40.0 5.7 %collective-permute-done.5 = bf16[48,2048]{1,0:T(8,128)(2,1)S(1)} collective-permute-done((bf16[48,2048]{1,0:T(8,128)(2,1)S(1)}, bf16[48,2048]{1,0:T(8,128)(2,1)S(1)}, u32[]{:S(2)}, u32[]{:S(2)}) %collective-permute-start.5) | collective-permute-done | bytes 196640 | tf_op jit(solution)/shard_map/ppermute | solution.py:68
  46.4 1.8 collective-permute-start.6
  48.4 4.1 %collective-permute-done.6 = bf16[48,2048]{1,0:T(8,128)(2,1)S(1)} collective-permute-done((bf16[48,2048]{1,0:T(8,128)(2,1)S(1)}, bf16[48,2048]{1,0:T(8,128)(2,1)S(1)}, u32[]{:S(2)}, u32[]{:S(2)}) %collective-permute-start.6) | collective-permute-done | bytes 196640 | tf_op jit(solution)/shard_map/ppermute | solution.py:68
  52.6 1.5 collective-permute-done.7
  54.0 0.9 pad_maximum_fusion.6
  55.0 1.9 fusion.44
  56.9 1.9 pad_maximum_fusion.2
  59.6 33.0 %collective-permute-done.14 = bf16[192,3584]{1,0:T(8,128)(2,1)} collective-permute-done((bf16[192,3584]{1,0:T(8,128)(2,1)}, bf16[192,3584]{1,0:T(8,128)(2,1)}, u32[]{:S(2)}, u32[]{:S(2)}) %collective-permute-start.14) | collective-permute-done | bytes 1376288 | tf_op jit(solution)/shard_map/ppermute | solution.py:91
  92.6 3.5 %pad_maximum_fusion.3 = bf16[384,3584]{1,0:T(8,128)(2,1)} fusion(bf16[192,3584]{1,0:T(8,128)(2,1)} %collective-permute-done.14, bf16[192,3584]{1,0:T(8,128)(2,1)} %collective-permute-done.4), kind=kLoop, calls=%fused_computation.46 | loop fusion | flops 5505024 | bytes 5505024 | tf_op jit(solution)/shard_map/concatenate | solution.py:91
  96.1 7.9 %fusion.33 = bf16[384,1792]{1,0:T(8,128)(2,1)} fusion(bf16[384,2048]{1,0:T(8,128)(2,1)} %all-gather.5.cloned.1.call-done, bf16[3584,2048]{1,0:T(8,128)(2,1)} %param.7), kind=kOutput, calls=%fused_computation.36 | convolution fusion | flops 2819260416 | bytes 10289152 | tf_op jit(solution)/shard_map/dot_general | solution.py:115
  104.4 1.4 collective-permute-start.15
  105.8 1.7 constant_dynamic-update-slice_fusion.4
  107.5 2.7 %constant_dynamic-update-slice_fusion.3 = bf16[1536,3584]{1,0:T(8,128)(2,1)} fusion(bf16[1536,3584]{1,0:T(8,128)(2,1)} %constant_dynamic-update-slice_fusion.4, bf16[192,3584]{1,0:T(8,128)(2,1)} %collective-permute-done.4), kind=kLoop, calls=%fused_computation.79 | loop fusion | bytes 2752512
  110.2 2.6 constant_dynamic-update-slice_fusion.2
  112.8 3.7 %constant_dynamic-update-slice_fusion.1 = bf16[1536,3584]{1,0:T(8,128)(2,1)} fusion(bf16[1536,3584]{1,0:T(8,128)(2,1)} %constant_dynamic-update-slice_fusion.2, bf16[384,3584]{1,0:T(8,128)(2,1)} %collective-permute-done.9), kind=kLoop, calls=%fused_computation.77 | loop fusion | bytes 5505024
  117.0 6.2 %fusion.27 = bf16[384,1792]{1,0:T(8,128)(2,1)} fusion(bf16[384,2048]{1,0:T(8,128)(2,1)S(1)} %copy-done.3, bf16[3584,2048]{1,0:T(8,128)(2,1)S(1)} %bitcast.55), kind=kOutput, calls=%fused_computation.34 | convolution fusion | flops 2819260416 | bytes 10289152 | tf_op jit(solution)/shard_map/dot_general | solution.py:115
  123.1 1.5 collective-permute-start.10
  124.7 32.5 %collective-permute-done.15 = bf16[384,3584]{1,0:T(8,128)(2,1)S(1)} collective-permute-done((bf16[384,3584]{1,0:T(8,128)(2,1)S(1)}, bf16[384,3584]{1,0:T(8,128)(2,1)S(1)}, u32[]{:S(2)}, u32[]{:S(2)}) %collective-permute-start.15) | collective-permute-done | bytes 2752544 | tf_op jit(solution)/shard_map/ppermute | solution.py:153
  157.2 1.7 constant_dynamic-update-slice_fusion
  158.9 2.8 %slice_bitcast_fusion = (bf16[384,2048]{1,0:T(8,128)(2,1)S(1)}, bf16[384,2048]{1,0:T(8,128)(2,1)S(1)}, bf16[384,2048]{1,0:T(8,128)(2,1)S(1)}) fusion(bf16[3,384,2048]{2,1,0:T(8,128)(2,1)} %all-gather.3.cloned.1.call-done, pred[]{:T(512)S(6)} %select_n.100), kind=kLoop, calls=%fused_computation.53 | loop fusion | flops 1572864 | bytes 9437185 | tf_op jit(solution)/shard_map/squeeze | solution.py:72
  161.7 9.9 %fusion.30 = bf16[384,1792]{1,0:T(8,128)(2,1)} fusion(bf16[384,2048]{1,0:T(8,128)(2,1)S(1)} %get-tuple-element.54, bf16[3584,2048]{1,0:T(8,128)(2,1)} %param.7), kind=kOutput, calls=%fused_computation.35 | convolution fusion | flops 2819260416 | bytes 10289152 | tf_op jit(solution)/shard_map/dot_general | solution.py:115
  171.6 1.5 collective-permute-start.12
  173.1 3.0 %fusion.18 = f32[384,1792]{1,0:T(8,128)S(1)} fusion(bf16[384,2048]{1,0:T(8,128)(2,1)S(1)} %get-tuple-element.55, bf16[3584,2048]{1,0:T(8,128)(2,1)S(1)} %bitcast.57), kind=kOutput, calls=%fused_computation.23 | convolution fusion | flops 2818572288 | bytes 11665408 | tf_op jit(solution)/shard_map/dot_general | solution.py:115
  176.1 1.6 add_convert_fusion.1
  177.7 1.1 collective-permute-start.11
  178.8 1.1 pad_maximum_fusion
  179.9 28.8 %fusion.50 = f32[3584,2048]{1,0:T(8,128)} fusion(bf16[1536,3584]{1,0:T(8,128)(2,1)} %constant_dynamic-update-slice_fusion, bf16[1536,2048]{1,0:T(8,128)(2,1)S(1)} %pad_maximum_fusion), kind=kOutput, calls=%fused_computation.82 | convolution fusion | flops 22548578304 | bytes 46661632 | tf_op jit(solution)/shard_map/dot_general | solution.py:135
  208.7 5.8 %fusion.10 = f32[384,1792]{1,0:T(8,128)S(1)} fusion(bf16[384,2048]{1,0:T(8,128)(2,1)S(1)} %get-tuple-element.55, bf16[3584,2048]{1,0:T(8,128)(2,1)} %param.7), kind=kOutput, calls=%fused_computation.15 | convolution fusion | flops 2818572288 | bytes 11665408 | tf_op jit(solution)/shard_map/dot_general | solution.py:115
  214.5 6.3 %fusion.24 = bf16[384,1792]{1,0:T(8,128)(2,1)S(1)} fusion(bf16[384,2048]{1,0:T(8,128)(2,1)S(1)} %get-tuple-element.54, bf16[3584,2048]{1,0:T(8,128)(2,1)} %param.7), kind=kOutput, calls=%fused_computation.33 | convolution fusion | flops 2819260416 | bytes 10289152 | tf_op jit(solution)/shard_map/dot_general | solution.py:115
  221.0 1.1 collective-permute-start.16
  222.1 1.1 collective-permute-start.8
  223.2 5.7 %fusion.12 = f32[384,1792]{1,0:T(8,128)S(1)} fusion(bf16[3584,2048]{1,0:T(8,128)(2,1)} %param.7, bf16[3,384,2048]{2,1,0:T(8,128)(2,1)S(1)} %bitcast.47), kind=kOutput, calls=%fused_computation.17 | convolution fusion | flops 2818572288 | bytes 11665408 | tf_op jit(solution)/shard_map/dot_general | solution.py:115
  228.9 6.0 %fusion.22 = f32[384,1792]{1,0:T(8,128)S(1)} fusion(bf16[3584,2048]{1,0:T(8,128)(2,1)} %param.7, bf16[3,384,2048]{2,1,0:T(8,128)(2,1)S(1)} %bitcast.47), kind=kOutput, calls=%fused_computation.27 | convolution fusion | flops 2818572288 | bytes 11665408 | tf_op jit(solution)/shard_map/dot_general | solution.py:115
  234.9 12.6 %collective-permute-done.16 = bf16[384,1792]{1,0:T(8,128)(2,1)S(1)} collective-permute-done((bf16[384,1792]{1,0:T(8,128)(2,1)S(1)}, bf16[384,1792]{1,0:T(8,128)(2,1)S(1)}, u32[]{:S(2)}, u32[]{:S(2)}) %collective-permute-start.16) | collective-permute-done | bytes 1376288 | tf_op jit(solution)/shard_map/ppermute | solution.py:154
  247.5 1.1 copy-done.4
  248.6 2.2 convert_add_fusion
  250.8 4.3 %fusion.7 = (bf16[384,3584]{1,0:T(8,128)(2,1)}, bf16[384,3584]{1,0:T(8,128)(2,1)}) fusion(bf16[384,3584]{1,0:T(8,128)(2,1)S(1)} %copy-done, f32[384,1792]{1,0:T(8,128)S(1)} %get-tuple-element.68, f32[384,1792]{1,0:T(8,128)S(1)} %get-tuple-element.69, bf16[384,3584]{1,0:T(8,128)(2,1)S(1)} %copy-done.1), kind=kLoop, calls=%fused_computation.11 | loop fusion | flops 22020096 | bytes 16515072 | tf_op jit(solution)/shard_map/convert_element_type | solution.py:170
  (62 shorter events, 3.9 us)
Async XLA Ops:
  7.2 88.9 %all-gather.5.cloned.1.call-start = ((), (), s32[]{:S(2)}) async-start(), calls=%async_computation.1 | async-start | bytes 1769472 | tf_op jit(solution)/shard_map/all_gather | solution.py:70
  8.5 6.7 %collective-permute-start = (bf16[4,48,1024]{2,1,0:T(8,128)(2,1)S(1)}, bf16[4,48,1024]{2,1,0:T(8,128)(2,1)S(1)}, u32[]{:S(2)}, u32[]{:S(2)}) collective-permute-start(bf16[4,48,1024]{2,1,0:T(8,128)(2,1)S(1)} %get-tuple-element.66), channel_id=1, source_target_pairs={{0,1},{1,0},{2,3},{3,2},{4,5},{5,4},{6,7},{7,6},{8,9},{9,8},{10,11... | collective-permute-start | bytes 1179656 | tf_op jit(solution)/shard_map/ppermute | solution.py:40
  12.6 25.8 %collective-permute-start.4 = (bf16[192,3584]{1,0:T(8,128)(2,1)}, bf16[192,3584]{1,0:T(8,128)(2,1)}, u32[]{:S(2)}, u32[]{:S(2)}) collective-permute-start(bf16[192,3584]{1,0:T(8,128)(2,1)} %fusion.45), channel_id=1, source_target_pairs={{0,8},{1,17},{2,10},{3,19},{4,12},{5,21},{6,14},{7,23},{8,0},{9,25... | collective-permute-start | bytes 4128776 | tf_op jit(solution)/shard_map/ppermute | solution.py:86
  16.3 38.7 %slice-start = ((bf16[384,3584]{1,0:T(8,128)(2,1)}), bf16[192,3584]{1,0:T(8,128)(2,1)S(1)}, s32[]{:S(2)}) async-start(bf16[384,3584]{1,0:T(8,128)(2,1)} %param.5), calls=%async_computation.2 | async-start | bytes 2752512 | tf_op jit(solution)/shard_map/split | solution.py:84
  16.3 38.7 %slice-start.1 = ((bf16[384,3584]{1,0:T(8,128)(2,1)}), bf16[192,3584]{1,0:T(8,128)(2,1)S(1)}, s32[]{:S(2)}) async-start(bf16[384,3584]{1,0:T(8,128)(2,1)} %param.6), calls=%async_computation.3 | async-start | bytes 2752512 | tf_op jit(solution)/shard_map/split | solution.py:84
  16.3 9.8 %collective-permute-start.3 = (bf16[48,2048]{1,0:T(8,128)(2,1)}, bf16[48,2048]{1,0:T(8,128)(2,1)S(1)}, u32[]{:S(2)}, u32[]{:S(2)}) collective-permute-start(bf16[48,2048]{1,0:T(8,128)(2,1)} %get-tuple-element.61), channel_id=1, source_target_pairs={{0,6},{1,7},{2,4},{3,5},{4,2},{5,3},{6,0},{7,1},{8,14},{9,15},{10,... | collective-permute-start | bytes 589832 | tf_op jit(solution)/shard_map/ppermute | solution.py:58
  19.9 10.9 %collective-permute-start.1 = (bf16[48,2048]{1,0:T(8,128)(2,1)S(1)}, bf16[48,2048]{1,0:T(8,128)(2,1)}, u32[]{:S(2)}, u32[]{:S(2)}) collective-permute-start(bf16[48,2048]{1,0:T(8,128)(2,1)S(1)} %get-tuple-element.63), channel_id=1, source_target_pairs={{0,2},{1,3},{2,0},{3,1},{4,6},{5,7},{6,4},{7,5},{8,10},{9,11},{10,... | collective-permute-start | bytes 589832 | tf_op jit(solution)/shard_map/ppermute | solution.py:58
  19.9 17.4 %collective-permute-start.2 = (bf16[48,2048]{1,0:T(8,128)(2,1)S(1)}, bf16[48,2048]{1,0:T(8,128)(2,1)}, u32[]{:S(2)}, u32[]{:S(2)}) collective-permute-start(bf16[48,2048]{1,0:T(8,128)(2,1)S(1)} %get-tuple-element.62), channel_id=1, source_target_pairs={{0,4},{1,5},{2,6},{3,7},{4,0},{5,1},{6,2},{7,3},{8,12},{9,13},{10,... | collective-permute-start | bytes 589832 | tf_op jit(solution)/shard_map/ppermute | solution.py:58
  38.5 7.2 %collective-permute-start.5 = (bf16[48,2048]{1,0:T(8,128)(2,1)S(1)}, bf16[48,2048]{1,0:T(8,128)(2,1)S(1)}, u32[]{:S(2)}, u32[]{:S(2)}) collective-permute-start(bf16[48,2048]{1,0:T(8,128)(2,1)S(1)} %get-tuple-element.59), channel_id=1, source_target_pairs={{0,24},{8,16},{16,8},{24,0},{1,25},{9,17},{17,9},{25,1},{2,26},{10... | collective-permute-start | bytes 589832 | tf_op jit(solution)/shard_map/ppermute | solution.py:68
  45.7 0.7 copy-start.5
  46.4 112.5 %all-gather.3.cloned.1.call-start = ((), (), s32[]{:S(2)}) async-start(), calls=%async_computation | async-start | bytes 5308416 | tf_op jit(solution)/shard_map/all_gather | solution.py:71
  46.4 6.1 %collective-permute-start.6 = (bf16[48,2048]{1,0:T(8,128)(2,1)S(1)}, bf16[48,2048]{1,0:T(8,128)(2,1)S(1)}, u32[]{:S(2)}, u32[]{:S(2)}) collective-permute-start(bf16[48,2048]{1,0:T(8,128)(2,1)S(1)} %get-tuple-element.31), channel_id=1, source_target_pairs={{0,8},{8,0},{16,24},{24,16},{1,9},{9,1},{17,25},{25,17},{2,10},{10... | collective-permute-start | bytes 589832 | tf_op jit(solution)/shard_map/ppermute | solution.py:68
  48.2 5.8 %collective-permute-start.7 = (bf16[48,2048]{1,0:T(8,128)(2,1)S(1)}, bf16[48,2048]{1,0:T(8,128)(2,1)S(1)}, u32[]{:S(2)}, u32[]{:S(2)}) collective-permute-start(bf16[48,2048]{1,0:T(8,128)(2,1)S(1)} %get-tuple-element.32), channel_id=1, source_target_pairs={{0,16},{8,24},{16,0},{24,8},{1,17},{9,25},{17,1},{25,9},{2,18},{10... | collective-permute-start | bytes 589832 | tf_op jit(solution)/shard_map/ppermute | solution.py:68
  58.8 45.6 %collective-permute-start.9 = (bf16[384,3584]{1,0:T(8,128)(2,1)S(1)}, bf16[384,3584]{1,0:T(8,128)(2,1)}, u32[]{:S(2)}, u32[]{:S(2)}) collective-permute-start(bf16[384,3584]{1,0:T(8,128)(2,1)S(1)} %pad_maximum_fusion.2), channel_id=1, source_target_pairs={{0,16},{1,9},{2,18},{3,11},{4,20},{5,13},{6,22},{7,15},{8,24},{9,1... | collective-permute-start | bytes 8257544 | tf_op jit(solution)/shard_map/ppermute | solution.py:96
  59.2 33.4 %collective-permute-start.14 = (bf16[192,3584]{1,0:T(8,128)(2,1)}, bf16[192,3584]{1,0:T(8,128)(2,1)}, u32[]{:S(2)}, u32[]{:S(2)}) collective-permute-start(bf16[192,3584]{1,0:T(8,128)(2,1)} %fusion.44), channel_id=1, source_target_pairs={{0,8},{1,17},{2,10},{3,19},{4,12},{5,21},{6,14},{7,23},{8,0},{9,25... | collective-permute-start | bytes 4128776 | tf_op jit(solution)/shard_map/ppermute | solution.py:91
  96.1 8.4 %copy-start.2 = (bf16[384,3584]{1,0:T(8,128)(2,1)S(1)}, bf16[384,3584]{1,0:T(8,128)(2,1)}, u32[]{:S(2)}) copy-start(bf16[384,3584]{1,0:T(8,128)(2,1)} %pad_maximum_fusion.3) | copy-start | bytes 8257540
  96.1 20.9 %slice-start.4 = ((s8[14680064]{0:T(1024)(128)(4,1)}), s8[4194304]{0:T(1024)(128)(4,1)S(1)}, s32[]{:S(2)}) async-start(s8[14680064]{0:T(1024)(128)(4,1)} %bitcast.54), calls=%async_computation.6 | async-start | bytes 8388608
  96.1 20.9 %slice-start.5 = ((s8[14680064]{0:T(1024)(128)(4,1)}), s8[4194304]{0:T(1024)(128)(4,1)S(1)}, s32[]{:S(2)}) async-start(s8[14680064]{0:T(1024)(128)(4,1)} %bitcast.54), calls=%async_computation.7 | async-start | bytes 8388608
  96.1 20.9 %slice-start.6 = ((s8[14680064]{0:T(1024)(128)(4,1)}), s8[4194304]{0:T(1024)(128)(4,1)S(1)}, s32[]{:S(2)}) async-start(s8[14680064]{0:T(1024)(128)(4,1)} %bitcast.54), calls=%async_computation.8 | async-start | bytes 8388608
  104.4 52.8 %collective-permute-start.15 = (bf16[384,3584]{1,0:T(8,128)(2,1)S(1)}, bf16[384,3584]{1,0:T(8,128)(2,1)S(1)}, u32[]{:S(2)}, u32[]{:S(2)}) collective-permute-start(bf16[384,3584]{1,0:T(8,128)(2,1)S(1)} %copy-done.2), channel_id=1, source_target_pairs={{0,16},{1,9},{2,18},{3,11},{4,20},{5,13},{6,22},{7,15},{8,24},{9,1... | collective-permute-start | bytes 8257544 | tf_op jit(solution)/shard_map/ppermute | solution.py:153
  107.5 9.5 %slice-start.7 = ((s8[14680064]{0:T(1024)(128)(4,1)}), s8[2097152]{0:T(1024)(128)(4,1)S(1)}, s32[]{:S(2)}) async-start(s8[14680064]{0:T(1024)(128)(4,1)} %bitcast.54), calls=%async_computation.9 | async-start | bytes 4194304
  112.8 4.2 %copy-start.3 = (bf16[384,2048]{1,0:T(8,128)(2,1)S(1)}, bf16[384,2048]{1,0:T(8,128)(2,1)}, u32[]{:S(2)}) copy-start(bf16[384,2048]{1,0:T(8,128)(2,1)} %all-gather.5.cloned.1.call-done) | copy-start | bytes 4718596
  116.4 104.3 %collective-permute-start.13 = (bf16[384,1792]{1,0:T(8,128)(2,1)}, bf16[384,1792]{1,0:T(8,128)(2,1)S(1)}, u32[]{:S(2)}, u32[]{:S(2)}) collective-permute-start(bf16[384,1792]{1,0:T(8,128)(2,1)} %fusion.33), channel_id=1, source_target_pairs={{0,8},{1,17},{2,10},{3,19},{4,12},{5,21},{6,14},{7,23},{8,0},{9,25... | collective-permute-start | bytes 4128776 | tf_op jit(solution)/shard_map/ppermute | solution.py:154
  123.1 49.9 %collective-permute-start.10 = (bf16[384,1792]{1,0:T(8,128)(2,1)}, bf16[384,1792]{1,0:T(8,128)(2,1)}, u32[]{:S(2)}, u32[]{:S(2)}) collective-permute-start(bf16[384,1792]{1,0:T(8,128)(2,1)} %fusion.27), channel_id=1, source_target_pairs={{0,8},{1,17},{2,10},{3,19},{4,12},{5,21},{6,14},{7,23},{8,0},{9,25... | collective-permute-start | bytes 4128776 | tf_op jit(solution)/shard_map/ppermute | solution.py:154
  158.9 14.2 %slice-start.8 = ((s8[14680064]{0:T(1024)(128)(4,1)}), s8[4194304]{0:T(1024)(128)(4,1)S(1)}, s32[]{:S(2)}) async-start(s8[14680064]{0:T(1024)(128)(4,1)} %bitcast.56), calls=%async_computation.10 | async-start | bytes 8388608
  158.9 14.2 %slice-start.9 = ((s8[14680064]{0:T(1024)(128)(4,1)}), s8[4194304]{0:T(1024)(128)(4,1)S(1)}, s32[]{:S(2)}) async-start(s8[14680064]{0:T(1024)(128)(4,1)} %bitcast.56), calls=%async_computation.11 | async-start | bytes 8388608
  161.7 11.4 %slice-start.10 = ((s8[14680064]{0:T(1024)(128)(4,1)}), s8[4194304]{0:T(1024)(128)(4,1)S(1)}, s32[]{:S(2)}) async-start(s8[14680064]{0:T(1024)(128)(4,1)} %bitcast.56), calls=%async_computation.12 | async-start | bytes 8388608
  161.7 11.4 %slice-start.11 = ((s8[14680064]{0:T(1024)(128)(4,1)}), s8[2097152]{0:T(1024)(128)(4,1)S(1)}, s32[]{:S(2)}) async-start(s8[14680064]{0:T(1024)(128)(4,1)} %bitcast.56), calls=%async_computation.13 | async-start | bytes 4194304
  171.6 75.9 %collective-permute-start.12 = (bf16[384,1792]{1,0:T(8,128)(2,1)}, bf16[384,1792]{1,0:T(8,128)(2,1)S(1)}, u32[]{:S(2)}, u32[]{:S(2)}) collective-permute-start(bf16[384,1792]{1,0:T(8,128)(2,1)} %fusion.30), channel_id=1, source_target_pairs={{0,8},{1,17},{2,10},{3,19},{4,12},{5,21},{6,14},{7,23},{8,0},{9,25... | collective-permute-start | bytes 4128776 | tf_op jit(solution)/shard_map/ppermute | solution.py:154
  177.7 69.8 %collective-permute-start.11 = (bf16[384,1792]{1,0:T(8,128)(2,1)S(1)}, bf16[384,1792]{1,0:T(8,128)(2,1)S(1)}, u32[]{:S(2)}, u32[]{:S(2)}) collective-permute-start(bf16[384,1792]{1,0:T(8,128)(2,1)S(1)} %add_convert_fusion.1), channel_id=1, source_target_pairs={{0,16},{1,9},{2,18},{3,11},{4,20},{5,13},{6,22},{7,15},{8,24},{9,1... | collective-permute-start | bytes 4128776 | tf_op jit(solution)/shard_map/ppermute | solution.py:154
  208.7 14.5 %slice-start.2 = ((s8[4718592]{0:T(1024)(128)(4,1)}), s8[524288]{0:T(1024)(128)(4,1)S(1)}, s32[]{:S(2)}) async-start(s8[4718592]{0:T(1024)(128)(4,1)} %bitcast.46), calls=%async_computation.4 | async-start | bytes 1048576
  214.5 8.7 %slice-start.3 = ((s8[4718592]{0:T(1024)(128)(4,1)}), s8[4194304]{0:T(1024)(128)(4,1)S(1)}, s32[]{:S(2)}) async-start(s8[4718592]{0:T(1024)(128)(4,1)} %bitcast.46), calls=%async_computation.5 | async-start | bytes 8388608
  221.0 26.5 %collective-permute-start.16 = (bf16[384,1792]{1,0:T(8,128)(2,1)S(1)}, bf16[384,1792]{1,0:T(8,128)(2,1)S(1)}, u32[]{:S(2)}, u32[]{:S(2)}) collective-permute-start(bf16[384,1792]{1,0:T(8,128)(2,1)S(1)} %add_convert_fusion), channel_id=1, source_target_pairs={{0,16},{1,9},{2,18},{3,11},{4,20},{5,13},{6,22},{7,15},{8,24},{9,1... | collective-permute-start | bytes 4128776 | tf_op jit(solution)/shard_map/ppermute | solution.py:154
  222.1 26.5 %collective-permute-start.8 = (bf16[384,1792]{1,0:T(8,128)(2,1)S(1)}, bf16[384,1792]{1,0:T(8,128)(2,1)S(1)}, u32[]{:S(2)}, u32[]{:S(2)}) collective-permute-start(bf16[384,1792]{1,0:T(8,128)(2,1)S(1)} %fusion.24), channel_id=1, source_target_pairs={{0,8},{1,17},{2,10},{3,19},{4,12},{5,21},{6,14},{7,23},{8,0},{9,25... | collective-permute-start | bytes 4128776 | tf_op jit(solution)/shard_map/ppermute | solution.py:154
  234.9 15.9 %copy-start = (bf16[384,3584]{1,0:T(8,128)(2,1)S(1)}, bf16[384,3584]{1,0:T(8,128)(2,1)}, u32[]{:S(2)}) copy-start(bf16[384,3584]{1,0:T(8,128)(2,1)} %param.5) | copy-start | bytes 8257540
  234.9 15.9 %copy-start.1 = (bf16[384,3584]{1,0:T(8,128)(2,1)S(1)}, bf16[384,3584]{1,0:T(8,128)(2,1)}, u32[]{:S(2)}) copy-start(bf16[384,3584]{1,0:T(8,128)(2,1)} %param.6) | copy-start | bytes 8257540
  247.5 1.1 copy-start.4
Sparse Core Ops, SparseCore 0:
  46.5 24.4 all-gather.4
  72.6 51.1 all-gather.2

commit v2 on v1

v2 whole, which is shorter than its diff:
```python
import jax
import jax.numpy as jnp
from jax import lax
from jax.sharding import PartitionSpec as P

BOTH = ("row", "col")


def exchange_pairs(rows, cols, step):
    bits = rows.bit_length() - 1
    return [
        (r * cols + c, (r ^ (1 << ((step + c) % bits))) * cols + c)
        for r in range(rows)
        for c in range(cols)
    ]


def row_offset(rows, place, turn):
    bits = rows.bit_length() - 1
    return sum(1 << ((step + turn) % bits) for step in range(bits) if place >> step & 1)


def collect_tokens(grad_out, front, front_came, later, rows, cols):
    share = cols // rows
    part = grad_out.shape[0] // cols
    row, col = lax.axis_index("row"), lax.axis_index("col")
    plane, lane = col // share, col % share

    pieces = grad_out.reshape(rows, share, part, grad_out.shape[1])
    arrived = []
    for shift in range(share):
        piece = lax.dynamic_index_in_dim(pieces, (lane + shift) % share, 1, keepdims=False)
        if shift:
            pairs = [
                (p * share + k, p * share + (k + shift) % share)
                for p in range(rows)
                for k in range(share)
            ]
            piece = lax.ppermute(piece, "col", pairs)
        arrived.append(piece)
    arrived = jnp.stack(arrived)
    mine = jnp.concatenate(
        [
            lax.dynamic_index_in_dim(arrived, (lane - k) % share, 0, keepdims=False)
            for k in range(share)
        ],
        axis=2,
    )

    mine, _ = lax.optimization_barrier((mine, front))

    held = []
    for flip in range(rows):
        piece = lax.dynamic_index_in_dim(mine, plane ^ flip, 0, keepdims=False)
        if flip:
            pairs = [(c, (c // share ^ flip) * share + c % share) for c in range(cols)]
            piece = lax.ppermute(piece, "col", pairs)
        held.append(piece)
    held, _ = lax.optimization_barrier((jnp.stack(held), front_came))

    blocks = [None] * rows
    for flip in reversed(range(rows)):
        piece = lax.dynamic_index_in_dim(held, row ^ flip ^ plane, 0, keepdims=False)
        if flip < rows - 1:
            piece, _ = lax.optimization_barrier((piece, blocks[-1]))
        if flip:
            piece = lax.ppermute(piece, "row", [(r, r ^ flip) for r in range(rows)])
        blocks[flip] = piece
    first = lax.all_gather(blocks[-1], "col", axis=0, tiled=True)
    rest, *_ = lax.optimization_barrier((jnp.stack(blocks[:-1]), *later))
    rest = lax.all_gather(rest, "col", axis=1, tiled=True)
    return [rest[flip] for flip in range(rows - 1)] + [first]


def on_device(grad_out, gate_act, up_act, down_weight):
    rows, cols = lax.axis_size("row"), lax.axis_size("col")
    steps = rows.bit_length() - 1
    tokens = grad_out.shape[0]
    pairs = [exchange_pairs(rows, cols, step) for step in range(steps)]

    def after(value, *others):
        return lax.optimization_barrier((value, *others))[0]

    def activation(gate, up):
        gate = gate.astype(jnp.float32)
        return (gate * jax.nn.sigmoid(gate) * up.astype(jnp.float32)).astype(jnp.bfloat16)

    size = tokens * 3 // 4
    front = activation(gate_act[:size], up_act[:size])
    front_came = lax.ppermute(front, BOTH, pairs[0])
    back = activation(after(gate_act[size:], front), after(up_act[size:], front))
    back_came = lax.ppermute(after(back, front_came), BOTH, pairs[0])
    halves = jnp.split(after(jnp.concatenate([front, back]), front_came), 2)
    halves_came = [lax.ppermute(half, BOTH, pairs[-1]) for half in halves]
    gathered = [jnp.concatenate([front, back]), jnp.concatenate([front_came, back_came])]
    for step in range(1, steps - 1):
        gathered = gathered + [lax.ppermute(part, BOTH, pairs[step]) for part in gathered]
    gathered += [jnp.concatenate(halves_came)] + [
        lax.ppermute(part, BOTH, pairs[-1]) for part in gathered[1:]
    ]

    blocks = collect_tokens(grad_out, front, front_came, [back_came, halves_came[0]], rows, cols)
    turn = lax.axis_index("col") % steps
    grads = [
        lax.select_n(turn, *(blocks[row_offset(rows, place, t)] for t in range(steps)))
        if 0 < place < rows - 1
        else blocks[place]
        for place in range(rows)
    ]

    width = down_weight.shape[0]
    weights = jnp.split(down_weight, [width // 7, width // 7 + width // 2])
    chunks = range(len(weights))
    came = [[[] for _ in range(rows)] for _ in chunks]
    total = front

    def partial(chunk, place, before):
        return lax.dot_general(
            after(grads[place], before),
            weights[chunk],
            (((1,), (1,)), ((), ())),
            preferred_element_type=jnp.float32,
        )

    for step in range(steps):
        for place in reversed(range(rows)):
            if place & ((1 << step) - 1) or not place >> step & 1:
                continue
            for chunk in chunks:
                total = partial(chunk, place, total)
                for block in came[chunk][place]:
                    total = total + block.astype(jnp.float32)
                total = total.astype(jnp.bfloat16)
                if place == rows - 1 and chunk == 0:
                    total = after(total, halves_came[1], *gathered[rows // 2 + 1 :])
                sent = lax.ppermute(total, BOTH, pairs[step])
                came[chunk][place ^ (1 << step)].append(sent)

    own = []
    for chunk in chunks:
        total = partial(chunk, 0, total)
        own.append(total)

    gathered, grads, own = lax.optimization_barrier((gathered, grads, own))
    grad_weight = lax.dot_general(
        jnp.concatenate(gathered, axis=0),
        jnp.concatenate(grads, axis=0),
        (((0,), (0,)), ((), ())),
        preferred_element_type=jnp.float32,
    )
    own, grad_weight = lax.optimization_barrier((own, grad_weight))

    sums = []
    for chunk in chunks:
        total = own[chunk]
        for block in came[chunk][0]:
            total = total + block.astype(jnp.float32)
        sums.append(total)
    grad_hidden = jnp.concatenate(sums, axis=1)
    gate_value = after(gate_act, front_came).astype(jnp.float32)
    up_value = after(up_act, front_came).astype(jnp.float32)
    sigmoid_gate = jax.nn.sigmoid(gate_value)
    grad_gate = (
        grad_hidden * up_value * sigmoid_gate * (1.0 + gate_value * (1.0 - sigmoid_gate))
    ).astype(jnp.bfloat16)
    grad_up = (grad_hidden * (gate_value * sigmoid_gate)).astype(jnp.bfloat16)
    return (grad_gate, grad_up, grad_weight)


def solution(mesh):
    placed = (P("row", "col"), P("row", "col"), P("row", "col"), P("col", "row"))
    return jax.shard_map(
        on_device,
        mesh=mesh,
        in_specs=placed,
        out_specs=(P("row", "col"), P("row", "col"), P("col", "row")),
        check_vma=False,
    )
```

time: 262 us -> 257 us (0.981)
  waiting for transfers between devices: 106 us -> 93.3 us
  matrix products: 79.5 us -> 87.6 us
  local copies, waits for them, and re-layouts: 16.2 us -> 11.5 us
  starting transfers between devices: 19.8 us -> 23.9 us
    ppermute x3 -> x4, waiting for transfers between devices: 65.9 us -> 46.1 us  [the longest x2 46.1 us: on_device(): halves_came = [lax.ppermute(half, BOTH, pairs[-1]) for half in halves]]
    ppermute x3, waiting for transfers between devices: 11.3 us -> 28.7 us  [collect_tokens(): piece = lax.ppermute(piece, 'row', [(r, r ^ flip) for r in range(rows)])]
    ppermute x6 -> x9, waiting for transfers between devices: 12.6 us -> 0.02 us  [on_device(): sent = lax.ppermute(total, BOTH, pairs[step])]
    dot_general x9 -> x13, matrix products: 79.5 us -> 87.6 us  [the longest x12 57.2 us: partial(): lax.dot_general(after(grads[place], before), weights[chunk], (((1,), (1,)...]
    unnamed x36 -> x39, local copies, waits for them, and re-layouts: 12.5 us -> 5.22 us
    add x1 -> x3, other arithmetic: 2.18 us -> 5.7 us  [on_device(): total = total + block.astype(jnp.float32)]
    ppermute x6 -> x9, starting transfers between devices: 6.7 us -> 8.85 us  [on_device(): sent = lax.ppermute(total, BOTH, pairs[step])]
  transfers between devices with their start and end apart: 19 -> 23, of which waited for: 10 -> 7; matrix products, arithmetic and copies ran while one was open for 43% -> 44% of each run, Pallas kernels for 0% -> 0%
where the time goes in v2:
time: 257 us
  waiting for transfers between devices  93.3 us (36%)
  matrix products  87.6 us (34%)
  other arithmetic  26.2 us (10%)
  starting transfers between devices  23.9 us (9%)
  between operations  14.4 us (6%)
  local copies, waits for them, and re-layouts  11.5 us (4%)
    dot_general x12, matrix products, partial(): lax.dot_general(after(grads[place], before), weights[chunk], (((1,), (1,)...  57.2 us
    ppermute x2, waiting for transfers between devices, on_device(): halves_came = [lax.ppermute(half, BOTH, pairs[-1]) for half in halves]  46.1 us
    dot_general x1, matrix products, on_device(): lax.dot_general(jnp.concatenate(gathered, axis=0), jnp.concatenate(grads,...  30.4 us
    ppermute x3, waiting for transfers between devices, collect_tokens(): piece = lax.ppermute(piece, 'row', [(r, r ^ flip) for r in range(rows)])  28.7 us
    ppermute x4, waiting for transfers between devices, collect_tokens(): piece = lax.ppermute(piece, 'col', pairs)  18.5 us
    ppermute x9, starting transfers between devices, on_device(): sent = lax.ppermute(total, BOTH, pairs[step])  8.85 us
    add x3, other arithmetic, on_device(): total = total + block.astype(jnp.float32)  5.7 us
    unnamed x39, local copies, waits for them, and re-layouts  5.22 us
  transfers between devices with their start and end apart: 23, of which 7 were waited for; matrix products, arithmetic and copies ran while one was open for 44% of the time, Pallas kernels for 0%

profile of v2, /device:TPU:0, one launch (start us, length us, event | category | flops | bytes accessed | tf_op | source)
XLA Modules:
  0.0 256.9 jit_solution(2136555322240446015)
XLA Ops:
  7.2 3.5 %fusion.35 = bf16[288,3584]{1,0:T(8,128)(2,1)S(1)} fusion(bf16[384,3584]{1,0:T(8,128)(2,1)} %param.6, bf16[384,3584]{1,0:T(8,128)(2,1)} %param.5), kind=kLoop, calls=%fused_computation.41 | loop fusion | flops 8257536 | bytes 6193152 | tf_op jit(solution)/shard_map/convert_element_type | solution.py:86
  10.7 3.0 %collective-permute-start = (bf16[288,3584]{1,0:T(8,128)(2,1)S(1)}, bf16[288,3584]{1,0:T(8,128)(2,1)}, u32[]{:S(2)}, u32[]{:S(2)}) collective-permute-start(bf16[288,3584]{1,0:T(8,128)(2,1)S(1)} %fusion.35), channel_id=1, source_target_pairs={{0,8},{1,17},{2,10},{3,19},{4,12},{5,21},{6,14},{7,23},{8,0},{9,25... | collective-permute-start | bytes 6193160 | tf_op jit(solution)/shard_map/ppermute | solution.py:90
  13.8 0.8 dynamic-slice_bitcast_fusion
  14.6 1.9 collective-permute-done.5
  16.9 0.9 constant_dynamic-slice_fusion
  17.8 3.6 %collective-permute-start.8 = (bf16[48,2048]{1,0:T(8,128)(2,1)}, bf16[48,2048]{1,0:T(8,128)(2,1)}, u32[]{:S(2)}, u32[]{:S(2)}) collective-permute-start(bf16[48,2048]{1,0:T(8,128)(2,1)} %get-tuple-element.95), channel_id=1, source_target_pairs={{0,6},{1,7},{2,4},{3,5},{4,2},{5,3},{6,0},{7,1},{8,14},{9,15},{10,... | collective-permute-start | bytes 589832 | tf_op jit(solution)/shard_map/ppermute | solution.py:57
  22.2 5.6 %collective-permute-done.8 = bf16[48,2048]{1,0:T(8,128)(2,1)} collective-permute-done((bf16[48,2048]{1,0:T(8,128)(2,1)}, bf16[48,2048]{1,0:T(8,128)(2,1)}, u32[]{:S(2)}, u32[]{:S(2)}) %collective-permute-start.8) | collective-permute-done | bytes 196640 | tf_op jit(solution)/shard_map/ppermute | solution.py:57
  27.8 10.9 %collective-permute-done.7 = bf16[48,2048]{1,0:T(8,128)(2,1)} collective-permute-done((bf16[48,2048]{1,0:T(8,128)(2,1)}, bf16[48,2048]{1,0:T(8,128)(2,1)}, u32[]{:S(2)}, u32[]{:S(2)}) %collective-permute-start.7) | collective-permute-done | bytes 196640 | tf_op jit(solution)/shard_map/ppermute | solution.py:57
  38.7 1.3 pad_maximum_fusion.4
  40.0 0.9 dynamic-slice_bitcast_fusion.5
  40.9 1.5 collective-permute-start.9
  42.4 1.3 fusion.60
  43.6 4.3 %collective-permute-done.9 = bf16[48,2048]{1,0:T(8,128)(2,1)S(1)} collective-permute-done((bf16[48,2048]{1,0:T(8,128)(2,1)S(1)}, bf16[48,2048]{1,0:T(8,128)(2,1)S(1)}, u32[]{:S(2)}, u32[]{:S(2)}) %collective-permute-start.9) | collective-permute-done | bytes 196640 | tf_op jit(solution)/shard_map/ppermute | solution.py:67
  48.6 2.0 pad_maximum_fusion.1
  50.7 1.7 fusion.80
  52.4 1.5 collective-permute-start.2
  54.4 1.5 collective-permute-start.10
  56.4 20.1 %collective-permute-done.10 = bf16[48,2048]{1,0:T(8,128)(2,1)S(1)} collective-permute-done((bf16[48,2048]{1,0:T(8,128)(2,1)S(1)}, bf16[48,2048]{1,0:T(8,128)(2,1)S(1)}, u32[]{:S(2)}, u32[]{:S(2)}) %collective-permute-start.10) | collective-permute-done | bytes 196640 | tf_op jit(solution)/shard_map/ppermute | solution.py:67
  76.5 4.4 %collective-permute-done.11 = bf16[48,2048]{1,0:T(8,128)(2,1)S(1)} collective-permute-done((bf16[48,2048]{1,0:T(8,128)(2,1)S(1)}, bf16[48,2048]{1,0:T(8,128)(2,1)S(1)}, u32[]{:S(2)}, u32[]{:S(2)}) %collective-permute-start.11) | collective-permute-done | bytes 196640 | tf_op jit(solution)/shard_map/ppermute | solution.py:67
  80.8 0.9 pad_maximum_fusion.5
  81.8 3.0 %constant_dynamic-update-slice_fusion.1 = bf16[384,3584]{1,0:T(8,128)(2,1)} fusion(bf16[288,3584]{1,0:T(8,128)(2,1)} %collective-permute-done), kind=kLoop, calls=%fused_computation.103 | loop fusion | bytes 4128768
  84.8 2.0 constant_dynamic-update-slice_fusion
  87.4 1.4 collective-permute-start.3
  88.8 46.1 %collective-permute-done.3 = bf16[192,3584]{1,0:T(8,128)(2,1)} collective-permute-done((bf16[192,3584]{1,0:T(8,128)(2,1)}, bf16[192,3584]{1,0:T(8,128)(2,1)}, u32[]{:S(2)}, u32[]{:S(2)}) %collective-permute-start.3) | collective-permute-done | bytes 1376288 | tf_op jit(solution)/shard_map/ppermute | solution.py:94
  134.9 3.5 %pad_maximum_fusion.2 = bf16[384,3584]{1,0:T(8,128)(2,1)} fusion(bf16[192,3584]{1,0:T(8,128)(2,1)} %collective-permute-done.3, bf16[192,3584]{1,0:T(8,128)(2,1)} %collective-permute-done.2), kind=kLoop, calls=%fused_computation.55 | loop fusion | flops 5505024 | bytes 5505024 | tf_op jit(solution)/shard_map/concatenate | solution.py:98
  138.4 3.2 %fusion.69 = bf16[384,512]{1,0:T(8,128)(2,1)S(1)} fusion(bf16[384,2048]{1,0:T(8,128)(2,1)} %all-gather.5.cloned.1.call-done, bf16[3584,2048]{1,0:T(8,128)(2,1)} %param.7), kind=kOutput, calls=%fused_computation.78 | convolution fusion | flops 805502976 | bytes 4063232 | tf_op jit(solution)/shard_map/dot_general | solution.py:118
  142.2 9.2 %fusion.50 = bf16[384,1792]{1,0:T(8,128)(2,1)} fusion(bf16[384,2048]{1,0:T(8,128)(2,1)S(1)} %copy-done.14, bf16[3584,2048]{1,0:T(8,128)(2,1)} %param.7), kind=kOutput, calls=%fused_computation.52 | convolution fusion | flops 2819260416 | bytes 10289152 | tf_op jit(solution)/shard_map/dot_general | solution.py:118
  151.4 1.5 collective-permute-start.13
  152.8 5.8 %fusion.44 = bf16[384,1280]{1,0:T(8,128)(2,1)} fusion(bf16[384,2048]{1,0:T(8,128)(2,1)S(1)} %copy-done.14, bf16[3584,2048]{1,0:T(8,128)(2,1)} %param.7), kind=kOutput, calls=%fused_computation.50 | convolution fusion | flops 2013757440 | bytes 7798784 | tf_op jit(solution)/shard_map/dot_general | solution.py:118
  159.2 2.7 %slice_bitcast_fusion = (bf16[384,2048]{1,0:T(8,128)(2,1)S(1)}, bf16[384,2048]{1,0:T(8,128)(2,1)S(1)}, bf16[384,2048]{1,0:T(8,128)(2,1)S(1)}) fusion(bf16[3,384,2048]{2,1,0:T(8,128)(2,1)} %all-gather.3.cloned.1.call-done, pred[]{:T(512)S(6)} %select_n.100), kind=kLoop, calls=%fused_computation.62 | loop fusion | flops 1572864 | bytes 9437185 | tf_op jit(solution)/shard_map/squeeze | solution.py:72
  161.9 4.4 %fusion.72 = bf16[384,512]{1,0:T(8,128)(2,1)S(1)} fusion(bf16[384,2048]{1,0:T(8,128)(2,1)S(1)} %get-tuple-element.74, bf16[3584,2048]{1,0:T(8,128)(2,1)} %param.7), kind=kOutput, calls=%fused_computation.79 | convolution fusion | flops 805502976 | bytes 4063232 | tf_op jit(solution)/shard_map/dot_general | solution.py:118
  166.3 1.5 collective-permute-start.15
  167.8 9.8 %fusion.53 = bf16[384,1792]{1,0:T(8,128)(2,1)} fusion(bf16[384,2048]{1,0:T(8,128)(2,1)S(1)} %get-tuple-element.74, bf16[3584,2048]{1,0:T(8,128)(2,1)} %param.7), kind=kOutput, calls=%fused_computation.53 | convolution fusion | flops 2819260416 | bytes 10289152 | tf_op jit(solution)/shard_map/dot_general | solution.py:118
  177.7 3.3 %fusion.47 = bf16[384,1280]{1,0:T(8,128)(2,1)} fusion(bf16[384,2048]{1,0:T(8,128)(2,1)S(1)} %get-tuple-element.74, bf16[3584,2048]{1,0:T(8,128)(2,1)S(1)} %bitcast.54), kind=kOutput, calls=%fused_computation.51 | convolution fusion | flops 2013757440 | bytes 7798784 | tf_op jit(solution)/shard_map/dot_general | solution.py:118
  181.0 1.0 fusion.63
  182.0 0.9 add_convert_fusion.2
  183.5 1.5 collective-permute-start.19
  185.5 7.1 %add_convert_fusion = bf16[384,1792]{1,0:T(8,128)(2,1)} fusion(bf16[384,1792]{1,0:T(8,128)(2,1)} %collective-permute-done.13, bf16[384,2048]{1,0:T(8,128)(2,1)S(1)} %get-tuple-element.75, bf16[3584,2048]{1,0:T(8,128)(2,1)S(1)} %bitcast.54), kind=kOutput, calls=%fused_computation.57 | convolution fusion | flops 2820636672 | bytes 11665408 | tf_op jit(solution)/shard_map/dot_general | solution.py:118
  192.6 4.4 %add_convert_fusion.1 = bf16[384,1280]{1,0:T(8,128)(2,1)} fusion(bf16[384,1280]{1,0:T(8,128)(2,1)} %collective-permute-done.14, bf16[384,2048]{1,0:T(8,128)(2,1)S(1)} %get-tuple-element.75, bf16[3584,2048]{1,0:T(8,128)(2,1)S(1)} %bitcast.54), kind=kOutput, calls=%fused_computation.59 | convolution fusion | flops 2014740480 | bytes 8781824 | tf_op jit(solution)/shard_map/dot_general | solution.py:118
  197.0 1.4 collective-permute-start.20
  198.4 1.0 fusion.61
  199.4 4.6 %fusion.23 = f32[384,1792]{1,0:T(8,128)} fusion(bf16[384,2048]{1,0:T(8,128)(2,1)S(1)} %get-tuple-element.73, bf16[3584,2048]{1,0:T(8,128)(2,1)S(1)} %bitcast.54), kind=kOutput, calls=%fused_computation.29 | convolution fusion | flops 2818572288 | bytes 11665408 | tf_op jit(solution)/shard_map/dot_general | solution.py:118
  204.0 3.5 %fusion.36 = f32[384,1280]{1,0:T(8,128)} fusion(bf16[384,2048]{1,0:T(8,128)(2,1)S(1)} %get-tuple-element.73, bf16[3584,2048]{1,0:T(8,128)(2,1)S(1)} %bitcast.54), kind=kOutput, calls=%fused_computation.42 | convolution fusion | flops 2013265920 | bytes 8781824 | tf_op jit(solution)/shard_map/dot_general | solution.py:118
  208.2 30.4 %fusion = f32[3584,2048]{1,0:T(8,128)} fusion(bf16[384,3584]{1,0:T(8,128)(2,1)} %collective-permute-done.4, bf16[384,3584]{1,0:T(8,128)(2,1)} %pad_maximum_fusion.2, bf16[384,3584]{1,0:T(8,128)(2,1)} %constant_dynamic-update-slice_fusion, bf16[384,3584]{1,0:T(8,128)(2,1)S(1)} %pad_maximum_fusion.1, bf16[384,2048]{1,0:T(8,128)(2,1)} %all-gather.5.cloned.1.call-done, ...), kind=kOutput, calls=%fused_computation | convolution fusion | flops 22617784320 | bytes 46661632 | tf_op jit(solution)/shard_map/dot_general | solution.py:145
  238.6 1.4 convert_add_fusion.2
  240.3 2.0 convert_add_fusion.1
  242.4 2.3 convert_add_fusion
  245.8 4.2 %fusion.22 = (bf16[384,3584]{1,0:T(8,128)(2,1)}, bf16[384,3584]{1,0:T(8,128)(2,1)}) fusion(bf16[384,3584]{1,0:T(8,128)(2,1)S(1)} %copy-done, f32[384,1280]{1,0:T(8,128)S(1)} %convert_add_fusion.1, f32[384,1792]{1,0:T(8,128)S(1)} %convert_add_fusion, f32[384,512]{1,0:T(8,128)S(1)} %convert_add_fusion.2, bf16[384,3584]{1,0:T(8,128)(2,1)S(1)} %copy-done.1), kind=kLoop, calls=%fused_computation.25 | loop fusion | flops 23396352 | bytes 16515072 | tf_op jit(solution)/shard_map/convert_element_type | solution.py:166
  (76 shorter events, 8.1 us)
Async XLA Ops:
  7.2 6.6 %copy-start.10 = (bf16[384,1024]{1,0:T(8,128)(2,1)S(1)}, bf16[384,1024]{1,0:T(8,128)(2,1)}, u32[]{:S(2)}) copy-start(bf16[384,1024]{1,0:T(8,128)(2,1)} %param.4) | copy-start | bytes 2359300
  7.2 131.2 %all-gather.5.cloned.1.call-start = ((), (), s32[]{:S(2)}) async-start(), calls=%async_computation.1 | async-start | bytes 1769472 | tf_op jit(solution)/shard_map/all_gather | solution.py:69
  10.7 7.0 %copy-start.2 = (bf16[288,3584]{1,0:T(8,128)(2,1)}, bf16[288,3584]{1,0:T(8,128)(2,1)S(1)}, u32[]{:S(2)}) copy-start(bf16[288,3584]{1,0:T(8,128)(2,1)S(1)} %fusion.35) | copy-start | bytes 6193156
  10.7 29.3 %collective-permute-start = (bf16[288,3584]{1,0:T(8,128)(2,1)S(1)}, bf16[288,3584]{1,0:T(8,128)(2,1)}, u32[]{:S(2)}, u32[]{:S(2)}) collective-permute-start(bf16[288,3584]{1,0:T(8,128)(2,1)S(1)} %fusion.35), channel_id=1, source_target_pairs={{0,8},{1,17},{2,10},{3,19},{4,12},{5,21},{6,14},{7,23},{8,0},{9,25... | collective-permute-start | bytes 6193160 | tf_op jit(solution)/shard_map/ppermute | solution.py:90
  14.6 1.9 collective-permute-start.5
  17.8 10.0 %collective-permute-start.8 = (bf16[48,2048]{1,0:T(8,128)(2,1)}, bf16[48,2048]{1,0:T(8,128)(2,1)}, u32[]{:S(2)}, u32[]{:S(2)}) collective-permute-start(bf16[48,2048]{1,0:T(8,128)(2,1)} %get-tuple-element.95), channel_id=1, source_target_pairs={{0,6},{1,7},{2,4},{3,5},{4,2},{5,3},{6,0},{7,1},{8,14},{9,15},{10,... | collective-permute-start | bytes 589832 | tf_op jit(solution)/shard_map/ppermute | solution.py:57
  21.4 17.3 %collective-permute-start.7 = (bf16[48,2048]{1,0:T(8,128)(2,1)}, bf16[48,2048]{1,0:T(8,128)(2,1)}, u32[]{:S(2)}, u32[]{:S(2)}) collective-permute-start(bf16[48,2048]{1,0:T(8,128)(2,1)} %get-tuple-element.96), channel_id=1, source_target_pairs={{0,4},{1,5},{2,6},{3,7},{4,0},{5,1},{6,2},{7,3},{8,12},{9,13},{10,... | collective-permute-start | bytes 589832 | tf_op jit(solution)/shard_map/ppermute | solution.py:57
  21.4 17.3 %collective-permute-start.6 = (bf16[48,2048]{1,0:T(8,128)(2,1)}, bf16[48,2048]{1,0:T(8,128)(2,1)}, u32[]{:S(2)}, u32[]{:S(2)}) collective-permute-start(bf16[48,2048]{1,0:T(8,128)(2,1)} %get-tuple-element.97), channel_id=1, source_target_pairs={{0,2},{1,3},{2,0},{3,1},{4,6},{5,7},{6,4},{7,5},{8,10},{9,11},{10,... | collective-permute-start | bytes 589832 | tf_op jit(solution)/shard_map/ppermute | solution.py:57
  22.2 20.2 %slice-start = ((bf16[384,3584]{1,0:T(8,128)(2,1)}), bf16[96,3584]{1,0:T(8,128)(2,1)S(1)}, s32[]{:S(2)}) async-start(bf16[384,3584]{1,0:T(8,128)(2,1)} %param.5), calls=%async_computation.2 | async-start | bytes 1376256 | tf_op jit(solution)/shard_map/slice | solution.py:91
  22.2 20.2 %slice-start.1 = ((bf16[384,3584]{1,0:T(8,128)(2,1)}), bf16[96,3584]{1,0:T(8,128)(2,1)S(1)}, s32[]{:S(2)}) async-start(bf16[384,3584]{1,0:T(8,128)(2,1)} %param.6), calls=%async_computation.3 | async-start | bytes 1376256 | tf_op jit(solution)/shard_map/slice | solution.py:91
  40.9 7.0 %collective-permute-start.9 = (bf16[48,2048]{1,0:T(8,128)(2,1)S(1)}, bf16[48,2048]{1,0:T(8,128)(2,1)S(1)}, u32[]{:S(2)}, u32[]{:S(2)}) collective-permute-start(bf16[48,2048]{1,0:T(8,128)(2,1)S(1)} %get-tuple-element.93), channel_id=1, source_target_pairs={{0,24},{8,16},{16,8},{24,0},{1,25},{9,17},{17,9},{25,1},{2,26},{10... | collective-permute-start | bytes 589832 | tf_op jit(solution)/shard_map/ppermute | solution.py:67
  47.9 0.7 copy-start.13
  48.6 110.6 %all-gather.3.cloned.1.call-start = ((), (), s32[]{:S(2)}) async-start(), calls=%async_computation | async-start | bytes 5308416 | tf_op jit(solution)/shard_map/all_gather | solution.py:71
  50.6 3.3 %copy-start.4 = (bf16[96,3584]{1,0:T(8,128)(2,1)S(1)}, bf16[96,3584]{1,0:T(8,128)(2,1)}, u32[]{:S(2)}) copy-start(bf16[96,3584]{1,0:T(8,128)(2,1)} %fusion.60) | copy-start | bytes 2064388
  50.6 3.8 %copy-start.12 = (bf16[48,2048]{1,0:T(8,128)(2,1)S(1)}, bf16[48,2048]{1,0:T(8,128)(2,1)}, u32[]{:S(2)}) copy-start(bf16[48,2048]{1,0:T(8,128)(2,1)} %get-tuple-element.50) | copy-start | bytes 589828
  50.6 5.3 %copy-start.11 = (bf16[48,2048]{1,0:T(8,128)(2,1)S(1)}, bf16[48,2048]{1,0:T(8,128)(2,1)}, u32[]{:S(2)}) copy-start(bf16[48,2048]{1,0:T(8,128)(2,1)} %get-tuple-element.51) | copy-start | bytes 589828
  50.6 30.2 %copy-start.9 = (bf16[48,2048]{1,0:T(8,128)(2,1)S(1)}, bf16[48,2048]{1,0:T(8,128)(2,1)}, u32[]{:S(2)}) copy-start(bf16[48,2048]{1,0:T(8,128)(2,1)} %get-tuple-element.49) | copy-start | bytes 589828
  52.4 29.4 %collective-permute-start.2 = (bf16[192,3584]{1,0:T(8,128)(2,1)}, bf16[192,3584]{1,0:T(8,128)(2,1)}, u32[]{:S(2)}, u32[]{:S(2)}) collective-permute-start(bf16[192,3584]{1,0:T(8,128)(2,1)} %get-tuple-element.89), channel_id=1, source_target_pairs={{0,16},{1,9},{2,18},{3,11},{4,20},{5,13},{6,22},{7,15},{8,24},{9,1... | collective-permute-start | bytes 4128776 | tf_op jit(solution)/shard_map/ppermute | solution.py:94
  53.9 27.9 %collective-permute-start.1 = (bf16[96,3584]{1,0:T(8,128)(2,1)S(1)}, bf16[96,3584]{1,0:T(8,128)(2,1)}, u32[]{:S(2)}, u32[]{:S(2)}) collective-permute-start(bf16[96,3584]{1,0:T(8,128)(2,1)S(1)} %copy-done.4), channel_id=1, source_target_pairs={{0,8},{1,17},{2,10},{3,19},{4,12},{5,21},{6,14},{7,23},{8,0},{9,25... | collective-permute-start | bytes 2064392 | tf_op jit(solution)/shard_map/ppermute | solution.py:92
  54.4 22.1 %collective-permute-start.10 = (bf16[48,2048]{1,0:T(8,128)(2,1)S(1)}, bf16[48,2048]{1,0:T(8,128)(2,1)S(1)}, u32[]{:S(2)}, u32[]{:S(2)}) collective-permute-start(bf16[48,2048]{1,0:T(8,128)(2,1)S(1)} %copy-done.12), channel_id=1, source_target_pairs={{0,8},{8,0},{16,24},{24,16},{1,9},{9,1},{17,25},{25,17},{2,10},{10... | collective-permute-start | bytes 589832 | tf_op jit(solution)/shard_map/ppermute | solution.py:67
  55.9 24.9 %collective-permute-start.11 = (bf16[48,2048]{1,0:T(8,128)(2,1)S(1)}, bf16[48,2048]{1,0:T(8,128)(2,1)S(1)}, u32[]{:S(2)}, u32[]{:S(2)}) collective-permute-start(bf16[48,2048]{1,0:T(8,128)(2,1)S(1)} %copy-done.11), channel_id=1, source_target_pairs={{0,16},{8,24},{16,0},{24,8},{1,17},{9,25},{17,1},{25,9},{2,18},{10... | collective-permute-start | bytes 589832 | tf_op jit(solution)/shard_map/ppermute | solution.py:67
  86.8 54.8 %collective-permute-start.4 = (bf16[384,3584]{1,0:T(8,128)(2,1)}, bf16[384,3584]{1,0:T(8,128)(2,1)}, u32[]{:S(2)}, u32[]{:S(2)}) collective-permute-start(bf16[384,3584]{1,0:T(8,128)(2,1)} %constant_dynamic-update-slice_fusion), channel_id=1, source_target_pairs={{0,16},{1,9},{2,18},{3,11},{4,20},{5,13},{6,22},{7,15},{8,24},{9,1... | collective-permute-start | bytes 8257544 | tf_op jit(solution)/shard_map/ppermute | solution.py:99
  87.4 47.5 %collective-permute-start.3 = (bf16[192,3584]{1,0:T(8,128)(2,1)}, bf16[192,3584]{1,0:T(8,128)(2,1)}, u32[]{:S(2)}, u32[]{:S(2)}) collective-permute-start(bf16[192,3584]{1,0:T(8,128)(2,1)} %get-tuple-element.88), channel_id=1, source_target_pairs={{0,16},{1,9},{2,18},{3,11},{4,20},{5,13},{6,22},{7,15},{8,24},{9,1... | collective-permute-start | bytes 4128776 | tf_op jit(solution)/shard_map/ppermute | solution.py:94
  138.4 3.9 %copy-start.14 = (bf16[384,2048]{1,0:T(8,128)(2,1)S(1)}, bf16[384,2048]{1,0:T(8,128)(2,1)}, u32[]{:S(2)}) copy-start(bf16[384,2048]{1,0:T(8,128)(2,1)} %all-gather.5.cloned.1.call-done) | copy-start | bytes 4718596
  141.6 40.4 %collective-permute-start.12 = (bf16[384,512]{1,0:T(8,128)(2,1)S(1)}, bf16[384,512]{1,0:T(8,128)(2,1)S(1)}, u32[]{:S(2)}, u32[]{:S(2)}) collective-permute-start(bf16[384,512]{1,0:T(8,128)(2,1)S(1)} %fusion.69), channel_id=1, source_target_pairs={{0,8},{1,17},{2,10},{3,19},{4,12},{5,21},{6,14},{7,23},{8,0},{9,25... | collective-permute-start | bytes 1179656 | tf_op jit(solution)/shard_map/ppermute | solution.py:136
  151.4 33.6 %collective-permute-start.13 = (bf16[384,1792]{1,0:T(8,128)(2,1)}, bf16[384,1792]{1,0:T(8,128)(2,1)}, u32[]{:S(2)}, u32[]{:S(2)}) collective-permute-start(bf16[384,1792]{1,0:T(8,128)(2,1)} %fusion.50), channel_id=1, source_target_pairs={{0,8},{1,17},{2,10},{3,19},{4,12},{5,21},{6,14},{7,23},{8,0},{9,25... | collective-permute-start | bytes 4128776 | tf_op jit(solution)/shard_map/ppermute | solution.py:136
  158.6 34.0 %collective-permute-start.14 = (bf16[384,1280]{1,0:T(8,128)(2,1)}, bf16[384,1280]{1,0:T(8,128)(2,1)}, u32[]{:S(2)}, u32[]{:S(2)}) collective-permute-start(bf16[384,1280]{1,0:T(8,128)(2,1)} %fusion.44), channel_id=1, source_target_pairs={{0,8},{1,17},{2,10},{3,19},{4,12},{5,21},{6,14},{7,23},{8,0},{9,25... | collective-permute-start | bytes 2949128 | tf_op jit(solution)/shard_map/ppermute | solution.py:136
  161.8 15.8 %copy-start.7 = (bf16[384,2048]{1,0:T(8,128)(2,1)}, bf16[384,2048]{1,0:T(8,128)(2,1)S(1)}, u32[]{:S(2)}) copy-start(bf16[384,2048]{1,0:T(8,128)(2,1)S(1)} %get-tuple-element.74) | copy-start | bytes 4718596
  161.8 30.8 %copy-start.8 = (bf16[384,2048]{1,0:T(8,128)(2,1)}, bf16[384,2048]{1,0:T(8,128)(2,1)S(1)}, u32[]{:S(2)}) copy-start(bf16[384,2048]{1,0:T(8,128)(2,1)S(1)} %get-tuple-element.75) | copy-start | bytes 4718596
  161.8 42.2 %copy-start.6 = (bf16[384,2048]{1,0:T(8,128)(2,1)}, bf16[384,2048]{1,0:T(8,128)(2,1)S(1)}, u32[]{:S(2)}) copy-start(bf16[384,2048]{1,0:T(8,128)(2,1)S(1)} %get-tuple-element.73) | copy-start | bytes 4718596
  161.9 15.8 %slice-start.2 = ((s8[14680064]{0:T(1024)(128)(4,1)}), s8[4194304]{0:T(1024)(128)(4,1)S(1)}, s32[]{:S(2)}) async-start(s8[14680064]{0:T(1024)(128)(4,1)} %bitcast.53), calls=%async_computation.4 | async-start | bytes 8388608
  161.9 15.8 %slice-start.3 = ((s8[14680064]{0:T(1024)(128)(4,1)}), s8[4194304]{0:T(1024)(128)(4,1)S(1)}, s32[]{:S(2)}) async-start(s8[14680064]{0:T(1024)(128)(4,1)} %bitcast.53), calls=%async_computation.5 | async-start | bytes 8388608
  166.3 11.4 %slice-start.4 = ((s8[14680064]{0:T(1024)(128)(4,1)}), s8[4194304]{0:T(1024)(128)(4,1)S(1)}, s32[]{:S(2)}) async-start(s8[14680064]{0:T(1024)(128)(4,1)} %bitcast.53), calls=%async_computation.6 | async-start | bytes 8388608
  166.3 11.4 %slice-start.5 = ((s8[14680064]{0:T(1024)(128)(4,1)}), s8[2097152]{0:T(1024)(128)(4,1)S(1)}, s32[]{:S(2)}) async-start(s8[14680064]{0:T(1024)(128)(4,1)} %bitcast.53), calls=%async_computation.7 | async-start | bytes 4194304
  166.3 41.2 %collective-permute-start.15 = (bf16[384,512]{1,0:T(8,128)(2,1)S(1)}, bf16[384,512]{1,0:T(8,128)(2,1)}, u32[]{:S(2)}, u32[]{:S(2)}) collective-permute-start(bf16[384,512]{1,0:T(8,128)(2,1)S(1)} %fusion.72), channel_id=1, source_target_pairs={{0,8},{1,17},{2,10},{3,19},{4,12},{5,21},{6,14},{7,23},{8,0},{9,25... | collective-permute-start | bytes 1179656 | tf_op jit(solution)/shard_map/ppermute | solution.py:136
  182.9 55.7 %collective-permute-start.16 = (bf16[384,512]{1,0:T(8,128)(2,1)}, bf16[384,512]{1,0:T(8,128)(2,1)}, u32[]{:S(2)}, u32[]{:S(2)}) collective-permute-start(bf16[384,512]{1,0:T(8,128)(2,1)} %add_convert_fusion.2), channel_id=1, source_target_pairs={{0,16},{1,9},{2,18},{3,11},{4,20},{5,13},{6,22},{7,15},{8,24},{9,1... | collective-permute-start | bytes 1179656 | tf_op jit(solution)/shard_map/ppermute | solution.py:136
  183.5 56.5 %collective-permute-start.19 = (bf16[384,1280]{1,0:T(8,128)(2,1)}, bf16[384,1280]{1,0:T(8,128)(2,1)}, u32[]{:S(2)}, u32[]{:S(2)}) collective-permute-start(bf16[384,1280]{1,0:T(8,128)(2,1)} %fusion.47), channel_id=1, source_target_pairs={{0,8},{1,17},{2,10},{3,19},{4,12},{5,21},{6,14},{7,23},{8,0},{9,25... | collective-permute-start | bytes 2949128 | tf_op jit(solution)/shard_map/ppermute | solution.py:136
  185.0 57.4 %collective-permute-start.17 = (bf16[384,1792]{1,0:T(8,128)(2,1)}, bf16[384,1792]{1,0:T(8,128)(2,1)}, u32[]{:S(2)}, u32[]{:S(2)}) collective-permute-start(bf16[384,1792]{1,0:T(8,128)(2,1)} %fusion.53), channel_id=1, source_target_pairs={{0,8},{1,17},{2,10},{3,19},{4,12},{5,21},{6,14},{7,23},{8,0},{9,25... | collective-permute-start | bytes 4128776 | tf_op jit(solution)/shard_map/ppermute | solution.py:136
  197.0 43.0 %collective-permute-start.20 = (bf16[384,1280]{1,0:T(8,128)(2,1)}, bf16[384,1280]{1,0:T(8,128)(2,1)}, u32[]{:S(2)}, u32[]{:S(2)}) collective-permute-start(bf16[384,1280]{1,0:T(8,128)(2,1)} %add_convert_fusion.1), channel_id=1, source_target_pairs={{0,16},{1,9},{2,18},{3,11},{4,20},{5,13},{6,22},{7,15},{8,24},{9,1... | collective-permute-start | bytes 2949128 | tf_op jit(solution)/shard_map/ppermute | solution.py:136
  207.6 34.9 %collective-permute-start.18 = (bf16[384,1792]{1,0:T(8,128)(2,1)}, bf16[384,1792]{1,0:T(8,128)(2,1)}, u32[]{:S(2)}, u32[]{:S(2)}) collective-permute-start(bf16[384,1792]{1,0:T(8,128)(2,1)} %add_convert_fusion), channel_id=1, source_target_pairs={{0,16},{1,9},{2,18},{3,11},{4,20},{5,13},{6,22},{7,15},{8,24},{9,1... | collective-permute-start | bytes 4128776 | tf_op jit(solution)/shard_map/ppermute | solution.py:136
  238.6 1.8 copy-start.5
  240.0 2.5 copy-start.3
  242.4 2.6 %copy-start = (bf16[384,3584]{1,0:T(8,128)(2,1)S(1)}, bf16[384,3584]{1,0:T(8,128)(2,1)}, u32[]{:S(2)}) copy-start(bf16[384,3584]{1,0:T(8,128)(2,1)} %param.5) | copy-start | bytes 8257540
  242.4 3.4 %copy-start.1 = (bf16[384,3584]{1,0:T(8,128)(2,1)S(1)}, bf16[384,3584]{1,0:T(8,128)(2,1)}, u32[]{:S(2)}) copy-start(bf16[384,3584]{1,0:T(8,128)(2,1)} %param.6) | copy-start | bytes 8257540
Sparse Core Ops, SparseCore 0:
  48.7 24.2 all-gather.4
  81.9 50.8 all-gather.2

commit v3 on v2

v3 whole, which is shorter than its diff:
```python
import math

import jax
import jax.numpy as jnp
from jax import lax
from jax.experimental import pallas as pl
from jax.experimental.pallas import tpu as pltpu
from jax.sharding import PartitionSpec as P

BOTH = ("row", "col")


def exchange_pairs(rows, cols, step):
    bits = rows.bit_length() - 1
    return [
        (r * cols + c, (r ^ (1 << ((step + c) % bits))) * cols + c)
        for r in range(rows)
        for c in range(cols)
    ]


def row_offset(rows, place, turn):
    bits = rows.bit_length() - 1
    return sum(1 << ((step + turn) % bits) for step in range(bits) if place >> step & 1)


def spread_tokens(grad_out, hidden, hidden_came, rows, cols):
    share = cols // rows
    part = grad_out.shape[0] // cols
    row, col = lax.axis_index("row"), lax.axis_index("col")
    plane, lane = col // share, col % share

    pieces = grad_out.reshape(rows, share, part, grad_out.shape[1])
    arrived = []
    for shift in range(share):
        piece = lax.dynamic_index_in_dim(pieces, (lane + shift) % share, 1, keepdims=False)
        if shift:
            pairs = [
                (p * share + k, p * share + (k + shift) % share)
                for p in range(rows)
                for k in range(share)
            ]
            piece = lax.ppermute(piece, "col", pairs)
        arrived.append(piece)
    arrived = jnp.stack(arrived)
    mine = jnp.concatenate(
        [
            lax.dynamic_index_in_dim(arrived, (lane - k) % share, 0, keepdims=False)
            for k in range(share)
        ],
        axis=2,
    )

    mine, _ = lax.optimization_barrier((mine, hidden))

    held = []
    for flip in range(rows):
        piece = lax.dynamic_index_in_dim(mine, plane ^ flip, 0, keepdims=False)
        if flip:
            pairs = [(c, (c // share ^ flip) * share + c % share) for c in range(cols)]
            piece = lax.ppermute(piece, "col", pairs)
        held.append(piece)
    held, _ = lax.optimization_barrier((jnp.stack(held), hidden_came))

    blocks = [None] * rows
    for flip in reversed(range(rows)):
        piece = lax.dynamic_index_in_dim(held, row ^ flip ^ plane, 0, keepdims=False)
        if flip < rows - 1:
            piece, _ = lax.optimization_barrier((piece, blocks[-1]))
        if flip:
            piece = lax.ppermute(piece, "row", [(r, r ^ flip) for r in range(rows)])
        blocks[flip] = piece
    return blocks


def gather_tokens(blocks):
    first = lax.all_gather(blocks[-1], "col", axis=0, tiled=True)
    rest = lax.all_gather(jnp.stack(blocks[:-1]), "col", axis=1, tiled=True)
    return [rest[flip] for flip in range(len(blocks) - 1)] + [first]


def finish_kernel(own_ref, *refs):
    *came_refs, gate_ref, up_ref = refs[: len(refs) - 2]
    gate_out_ref, up_out_ref = refs[-2:]
    grad_hidden = own_ref[...]
    for came_ref in came_refs:
        grad_hidden = grad_hidden + came_ref[...].astype(jnp.float32)
    gate_value = gate_ref[...].astype(jnp.float32)
    up_value = up_ref[...].astype(jnp.float32)
    sigmoid_gate = 1.0 / (1.0 + jnp.exp(-gate_value))
    gate_out_ref[...] = (
        grad_hidden * up_value * sigmoid_gate * (1.0 + gate_value * (1.0 - sigmoid_gate))
    ).astype(jnp.bfloat16)
    up_out_ref[...] = (grad_hidden * (gate_value * sigmoid_gate)).astype(jnp.bfloat16)


def finish(own, last, whole, gate_act, up_act, outs, start, block):
    tokens, width = own.shape
    inner = pl.BlockSpec((tokens, block), lambda i: (0, i))
    outer = pl.BlockSpec((tokens, block), lambda i: (0, start // block + i))
    operands = [own, last, *whole, gate_act, up_act]
    specs = [inner] * 2 + [outer] * (len(whole) + 2)
    kernel, aliases = finish_kernel, {}
    if outs:
        aliases = {len(operands): 0, len(operands) + 1: 1}
        operands += outs
        specs += [pl.BlockSpec(memory_space=pl.ANY)] * 2
        read = len(operands) - 2

        def kernel(*refs):
            finish_kernel(*refs[:read], *refs[read + 2 :])

    shape = jax.ShapeDtypeStruct(gate_act.shape, jnp.bfloat16)
    return pl.pallas_call(
        kernel,
        grid=(width // block,),
        in_specs=specs,
        out_specs=[outer, outer],
        out_shape=[shape, shape],
        input_output_aliases=aliases,
        compiler_params=pltpu.CompilerParams(vmem_limit_bytes=32 * 1024 * 1024),
    )(*operands)


def on_device(grad_out, gate_act, up_act, down_weight):
    rows, cols = lax.axis_size("row"), lax.axis_size("col")
    steps = rows.bit_length() - 1
    tokens = grad_out.shape[0]
    pairs = [exchange_pairs(rows, cols, step) for step in range(steps)]

    def after(value, *others):
        return lax.optimization_barrier((value, *others))[0]

    def activation(gate, up):
        gate = gate.astype(jnp.float32)
        return (gate * jax.nn.sigmoid(gate) * up.astype(jnp.float32)).astype(jnp.bfloat16)

    hidden = activation(gate_act, up_act)
    hidden_came = lax.ppermute(hidden, BOTH, pairs[0])
    pieces = spread_tokens(grad_out, hidden, hidden_came, rows, cols)
    gathered = [hidden, hidden_came]
    for step in range(1, steps - 1):
        gathered = gathered + [lax.ppermute(part, BOTH, pairs[step]) for part in gathered]

    front, back = jnp.split(after(hidden, *pieces), [tokens * 3 // 4])
    front_came = lax.ppermute(front, BOTH, pairs[-1])
    back_came = lax.ppermute(back, BOTH, pairs[-1])
    gathered.append(jnp.concatenate([front_came, back_came]))

    blocks = gather_tokens(pieces)
    width = down_weight.shape[0]

    def product(block, start, stop, *before):
        return lax.dot_general(
            after(block, *before),
            down_weight[start:stop],
            (((1,), (1,)), ((), ())),
            preferred_element_type=jnp.float32,
        )

    def send(total, step):
        return lax.ppermute(total, BOTH, pairs[step])

    unit = width // 7
    total = [
        product(blocks[-1], 0, 3 * unit, front_came).astype(jnp.bfloat16),
        product(blocks[-1], 3 * unit, width, front_came).astype(jnp.bfloat16),
    ]
    tails = []
    for part in gathered[1 : rows // 2]:
        fore, rear = jnp.split(part, 2)
        fore = send(after(fore, total[0], back_came), steps - 1)
        rear = send(after(rear, total[1], back_came), steps - 1)
        gathered.append(jnp.concatenate([fore, rear]))
        tails += [fore, rear]
    total = after(jnp.concatenate(total, axis=1), *tails)

    blocks[:-1] = lax.optimization_barrier((*blocks[:-1], total))[:-1]
    turn = lax.axis_index("col") % steps
    grads = [
        lax.select_n(turn, *(blocks[row_offset(rows, place, t)] for t in range(steps)))
        if 0 < place < rows - 1
        else blocks[place]
        for place in range(rows)
    ]

    came = [[] for _ in range(rows)]
    came[rows - 2].append(send(total, 0))
    for step in range(steps - 1):
        for place in reversed(range(rows - 1)):
            if place & ((1 << step) - 1) or not place >> step & 1:
                continue
            total = product(grads[place], 0, width, total)
            for block in came[place]:
                total = total + block.astype(jnp.float32)
            total = total.astype(jnp.bfloat16)
            came[place ^ (1 << step)].append(send(total, step))

    starts, stops = [0, 3 * unit, 6 * unit], [3 * unit, 6 * unit, width]
    last = []
    for start, stop in zip(starts, stops):
        total = product(grads[rows // 2], start, stop, total)
        for block in came[rows // 2]:
            total = total + block[:, start:stop].astype(jnp.float32)
        total = total.astype(jnp.bfloat16)
        last.append(send(total, steps - 1))
    own = []
    for start, stop in zip(starts, stops):
        total = product(grads[0], start, stop, total)
        own.append(total)

    gathered, grads, own = lax.optimization_barrier((gathered, grads, own))
    grad_weight = lax.dot_general(
        jnp.concatenate(gathered, axis=0),
        jnp.concatenate(grads, axis=0),
        (((0,), (0,)), ((), ())),
        preferred_element_type=jnp.float32,
    )
    own, grad_weight = lax.optimization_barrier((own, grad_weight))

    gate_act, up_act = after(gate_act, hidden_came), after(up_act, hidden_came)
    outs = []
    for chunk, start in enumerate(starts):
        outs = finish(
            own[chunk], last[chunk], came[0], gate_act, up_act, outs, start, math.gcd(unit, 256)
        )
    return (*outs, grad_weight)


def solution(mesh):
    placed = (P("row", "col"), P("row", "col"), P("row", "col"), P("col", "row"))
    return jax.shard_map(
        on_device,
        mesh=mesh,
        in_specs=placed,
        out_specs=(P("row", "col"), P("row", "col"), P("col", "row")),
        check_vma=False,
    )
```

time: 257 us -> 260 us (1.012)
  Pallas kernels: 0 us -> 14.2 us
  other arithmetic: 26.2 us -> 14.1 us
    pallas_call x0 -> x3, Pallas kernels: none -> 14.2 us  [finish(): pl.pallas_call(kernel, grid=(width // block,), in_specs=specs, out_specs=...]
    add x3 -> x0, other arithmetic: 5.7 us -> none  [on_device(): total = total + block.astype(jnp.float32)]
    convert_element_type x2 -> x0, other arithmetic: 5.11 us -> none  [the longest x1 4.23 us: on_device(): grad_up = (grad_hidden * (gate_value * sigmoid_gate)).astype(jnp.bfloat16)]
    squeeze x2 -> x3, local copies, waits for them, and re-layouts: 1.67 us -> 4.83 us  [the longest x1 2.85 us: gather_tokens(): return [rest[flip] for flip in range(len(blocks) - 1)] + [first]]
    squeeze x2 -> x1, other arithmetic: 2.95 us -> 0.29 us  [spread_tokens(): lax.dynamic_index_in_dim(arrived, (lane - k) % share, 0, keepdims=False)]
    dot_general x12 -> x9, matrix products: 57.2 us -> 54.9 us  [product(): lax.dot_general(after(block, *before), down_weight[start:stop], (((1,), (...]
    concatenate x3 -> x4, other arithmetic: 5.49 us -> 7.27 us  [the longest x1 3.55 us: on_device(): gathered.append(jnp.concatenate([front_came, back_came]))]
    unnamed x39 -> x34, local copies, waits for them, and re-layouts: 5.22 us -> 4.17 us
  transfers between devices with their start and end apart: 23 -> 19, of which waited for: 7 -> 11; matrix products, arithmetic and copies ran while one was open for 44% -> 40% of each run, Pallas kernels for 0% -> 5%
where the time goes in v3:
time: 260 us; the launch traced here: 259 us
  waiting for transfers between devices  93.7 us (36%)
  matrix products  85.8 us (33%)
  starting transfers between devices  24 us (9%)
  Pallas kernels  14.2 us (5%)
  between operations  14.2 us (5%)
  other arithmetic  14.1 us (5%)
  local copies, waits for them, and re-layouts  13.4 us (5%)
    dot_general x9, matrix products, product(): lax.dot_general(after(block, *before), down_weight[start:stop], (((1,), (...  54.9 us
    ppermute x7, waiting for transfers between devices, send(): return lax.ppermute(total, BOTH, pairs[step])  42.8 us
    dot_general x1, matrix products, on_device(): lax.dot_general(jnp.concatenate(gathered, axis=0), jnp.concatenate(grads,...  30.9 us
    ppermute x1, waiting for transfers between devices, on_device(): front_came = lax.ppermute(front, BOTH, pairs[-1])  20.1 us
    ppermute x4, waiting for transfers between devices, spread_tokens(): piece = lax.ppermute(piece, 'col', pairs)  18.5 us
    pallas_call x3, Pallas kernels, finish(): pl.pallas_call(kernel, grid=(width // block,), in_specs=specs, out_specs=...  14.2 us
    ppermute x3, waiting for transfers between devices, spread_tokens(): piece = lax.ppermute(piece, 'row', [(r, r ^ flip) for r in range(rows)])  8.2 us
    ppermute x7, starting transfers between devices, send(): return lax.ppermute(total, BOTH, pairs[step])  7.73 us
  transfers between devices with their start and end apart: 19, of which 11 were waited for; matrix products, arithmetic and copies ran while one was open for 40% of the time, Pallas kernels for 5%

profile of v3, /device:TPU:0, one launch (start us, length us, event | category | flops | bytes accessed | tf_op | source)
XLA Modules:
  0.0 259.3 jit_solution(4572072831030398405)
XLA Ops:
  7.2 4.3 %fusion.25 = bf16[384,3584]{1,0:T(8,128)(2,1)S(1)} fusion(bf16[384,3584]{1,0:T(8,128)(2,1)} %refs_4_.1, bf16[384,3584]{1,0:T(8,128)(2,1)} %refs_3_.2), kind=kLoop, calls=%fused_computation.28 | loop fusion | flops 11010048 | bytes 8257536 | tf_op jit(solution)/shard_map/convert_element_type | solution.py:136
  11.5 3.0 %collective-permute-start = (bf16[384,3584]{1,0:T(8,128)(2,1)S(1)}, bf16[384,3584]{1,0:T(8,128)(2,1)}, u32[]{:S(2)}, u32[]{:S(2)}) collective-permute-start(bf16[384,3584]{1,0:T(8,128)(2,1)S(1)} %fusion.25), channel_id=1, source_target_pairs={{0,8},{1,17},{2,10},{3,19},{4,12},{5,21},{6,14},{7,23},{8,0},{9,25... | collective-permute-start | bytes 8257544 | tf_op jit(solution)/shard_map/ppermute | solution.py:139
  14.5 1.9 dynamic-slice_bitcast_fusion
  16.4 1.9 collective-permute-done.1
  18.7 0.8 constant_dynamic-slice_fusion
  19.5 3.6 %collective-permute-start.4 = (bf16[48,2048]{1,0:T(8,128)(2,1)}, bf16[48,2048]{1,0:T(8,128)(2,1)S(1)}, u32[]{:S(2)}, u32[]{:S(2)}) collective-permute-start(bf16[48,2048]{1,0:T(8,128)(2,1)} %get-tuple-element.101), channel_id=1, source_target_pairs={{0,6},{1,7},{2,4},{3,5},{4,2},{5,3},{6,0},{7,1},{8,14},{9,15},{10,... | collective-permute-start | bytes 589832 | tf_op jit(solution)/shard_map/ppermute | solution.py:61
  23.1 0.8 collective-permute-start.2
  23.9 5.5 %collective-permute-done.4 = bf16[48,2048]{1,0:T(8,128)(2,1)S(1)} collective-permute-done((bf16[48,2048]{1,0:T(8,128)(2,1)}, bf16[48,2048]{1,0:T(8,128)(2,1)S(1)}, u32[]{:S(2)}, u32[]{:S(2)}) %collective-permute-start.4) | collective-permute-done | bytes 196640 | tf_op jit(solution)/shard_map/ppermute | solution.py:61
  29.4 11.0 %collective-permute-done.3 = bf16[48,2048]{1,0:T(8,128)(2,1)} collective-permute-done((bf16[48,2048]{1,0:T(8,128)(2,1)S(1)}, bf16[48,2048]{1,0:T(8,128)(2,1)}, u32[]{:S(2)}, u32[]{:S(2)}) %collective-permute-start.3) | collective-permute-done | bytes 196640 | tf_op jit(solution)/shard_map/ppermute | solution.py:61
  40.4 1.1 pad_maximum_fusion.4
  41.5 4.1 %collective-permute-done = bf16[384,3584]{1,0:T(8,128)(2,1)} collective-permute-done((bf16[384,3584]{1,0:T(8,128)(2,1)S(1)}, bf16[384,3584]{1,0:T(8,128)(2,1)}, u32[]{:S(2)}, u32[]{:S(2)}) %collective-permute-start) | collective-permute-done | bytes 2752544 | tf_op jit(solution)/shard_map/ppermute | solution.py:139
  45.7 3.0 %collective-permute-start.5 = (bf16[48,2048]{1,0:T(8,128)(2,1)S(1)}, bf16[48,2048]{1,0:T(8,128)(2,1)S(1)}, u32[]{:S(2)}, u32[]{:S(2)}) collective-permute-start(bf16[48,2048]{1,0:T(8,128)(2,1)S(1)} %get-tuple-element.98), channel_id=1, source_target_pairs={{0,24},{8,16},{16,8},{24,0},{1,25},{9,17},{17,9},{25,1},{2,26},{10... | collective-permute-start | bytes 589832 | tf_op jit(solution)/shard_map/ppermute | solution.py:71
  48.7 4.0 %collective-permute-done.5 = bf16[48,2048]{1,0:T(8,128)(2,1)S(1)} collective-permute-done((bf16[48,2048]{1,0:T(8,128)(2,1)S(1)}, bf16[48,2048]{1,0:T(8,128)(2,1)S(1)}, u32[]{:S(2)}, u32[]{:S(2)}) %collective-permute-start.5) | collective-permute-done | bytes 196640 | tf_op jit(solution)/shard_map/ppermute | solution.py:71
  52.8 0.7 copy-done.11
  53.7 1.7 collective-permute-start.6
  55.5 1.5 collective-permute-start.7
  57.0 2.5 collective-permute-done.6
  59.5 1.7 collective-permute-done.7
  61.1 0.9 pad_maximum_fusion.5
  62.2 1.6 collective-permute-start.8
  63.8 3.5 %fusion.47 = (bf16[192,3584]{1,0:T(8,128)(2,1)}, bf16[192,3584]{1,0:T(8,128)(2,1)}) fusion(bf16[384,3584]{1,0:T(8,128)(2,1)} %collective-permute-done), kind=kLoop, calls=%fused_computation.74 | loop fusion | bytes 5505024 | tf_op jit(solution)/shard_map/split | solution.py:171
  67.3 0.7 collective-permute-start.9
  68.0 20.1 %collective-permute-done.8 = bf16[288,3584]{1,0:T(8,128)(2,1)} collective-permute-done((bf16[288,3584]{1,0:T(8,128)(2,1)S(1)}, bf16[288,3584]{1,0:T(8,128)(2,1)}, u32[]{:S(2)}, u32[]{:S(2)}) %collective-permute-start.8) | collective-permute-done | bytes 2064416 | tf_op jit(solution)/shard_map/ppermute | solution.py:146
  88.1 7.6 %fusion.35 = bf16[384,1536]{1,0:T(8,128)(2,1)} fusion(bf16[384,2048]{1,0:T(8,128)(2,1)} %all-gather.3.cloned.1.call-done, bf16[3584,2048]{1,0:T(8,128)(2,1)} %param.7), kind=kOutput, calls=%fused_computation.36 | convolution fusion | flops 2416508928 | bytes 9043968 | tf_op jit(solution)/shard_map/dot_general | solution.py:154
  95.7 8.1 %fusion.32 = bf16[384,2048]{1,0:T(8,128)(2,1)} fusion(bf16[384,2048]{1,0:T(8,128)(2,1)S(1)} %copy-done.12, bf16[3584,2048]{1,0:T(8,128)(2,1)} %param.7), kind=kOutput, calls=%fused_computation.35 | convolution fusion | flops 3222011904 | bytes 11534336 | tf_op jit(solution)/shard_map/dot_general | solution.py:154
  103.7 1.6 collective-permute-start.11
  105.8 3.6 %pad_maximum_fusion = bf16[384,3584]{1,0:T(8,128)(2,1)} fusion(bf16[96,3584]{1,0:T(8,128)(2,1)S(1)} %collective-permute-done.9, bf16[288,3584]{1,0:T(8,128)(2,1)} %collective-permute-done.8), kind=kLoop, calls=%fused_computation.37 | loop fusion | flops 5505024 | bytes 5505024 | tf_op jit(solution)/shard_map/concatenate | solution.py:148
  109.5 12.8 %collective-permute-done.11 = bf16[192,3584]{1,0:T(8,128)(2,1)} collective-permute-done((bf16[192,3584]{1,0:T(8,128)(2,1)}, bf16[192,3584]{1,0:T(8,128)(2,1)}, u32[]{:S(2)}, u32[]{:S(2)}) %collective-permute-start.11) | collective-permute-done | bytes 1376288 | tf_op jit(solution)/shard_map/ppermute | solution.py:162
  122.4 17.2 %collective-permute-done.10 = bf16[192,3584]{1,0:T(8,128)(2,1)} collective-permute-done((bf16[192,3584]{1,0:T(8,128)(2,1)}, bf16[192,3584]{1,0:T(8,128)(2,1)}, u32[]{:S(2)}, u32[]{:S(2)}) %collective-permute-start.10) | collective-permute-done | bytes 1376288 | tf_op jit(solution)/shard_map/ppermute | solution.py:162
  139.9 3.5 %pad_maximum_fusion.1 = bf16[384,3584]{1,0:T(8,128)(2,1)} fusion(bf16[192,3584]{1,0:T(8,128)(2,1)} %collective-permute-done.11, bf16[192,3584]{1,0:T(8,128)(2,1)} %collective-permute-done.10), kind=kLoop, calls=%fused_computation.38 | loop fusion | flops 5505024 | bytes 5505024 | tf_op jit(solution)/shard_map/concatenate | solution.py:174
  143.4 2.8 %slice_bitcast_fusion = (bf16[384,2048]{1,0:T(8,128)(2,1)S(1)}, bf16[384,2048]{1,0:T(8,128)(2,1)S(1)}, bf16[384,2048]{1,0:T(8,128)(2,1)S(1)}) fusion(bf16[3,384,2048]{2,1,0:T(8,128)(2,1)} %all-gather.5.cloned.1.call-done), kind=kLoop, calls=%fused_computation.46 | loop fusion | bytes 9437184 | tf_op jit(solution)/shard_map/squeeze | solution.py:79
  146.5 11.8 %convolution_convert_fusion = bf16[384,3584]{1,0:T(8,128)(2,1)} fusion(bf16[384,2048]{1,0:T(8,128)(2,1)S(1)} %get-tuple-element.74, bf16[3584,2048]{1,0:T(8,128)(2,1)} %param.7), kind=kOutput, calls=%fused_computation.19 | convolution fusion | flops 5638520832 | bytes 19005440 | tf_op jit(solution)/shard_map/dot_general | solution.py:154
  158.3 1.6 collective-permute-start.14
  159.9 12.8 %collective-permute-done.12 = bf16[384,3584]{1,0:T(8,128)(2,1)} collective-permute-done((bf16[384,3584]{1,0:T(8,128)(2,1)S(1)}, bf16[384,3584]{1,0:T(8,128)(2,1)}, u32[]{:S(2)}, u32[]{:S(2)}) %collective-permute-start.12) | collective-permute-done | bytes 2752544 | tf_op jit(solution)/shard_map/ppermute | solution.py:162
  172.7 7.0 %add_convert_fusion.1 = bf16[384,1536]{1,0:T(8,128)(2,1)} fusion(bf16[384,3584]{1,0:T(8,128)(2,1)} %collective-permute-done.12, bf16[384,2048]{1,0:T(8,128)(2,1)S(1)} %get-tuple-element.75, bf16[3584,2048]{1,0:T(8,128)(2,1)} %param.7), kind=kOutput, calls=%fused_computation.41 | convolution fusion | flops 2417688576 | bytes 10223616 | tf_op jit(solution)/shard_map/dot_general | solution.py:154
  179.7 7.0 %add_convert_fusion = bf16[384,1536]{1,0:T(8,128)(2,1)} fusion(bf16[384,3584]{1,0:T(8,128)(2,1)} %collective-permute-done.12, bf16[384,2048]{1,0:T(8,128)(2,1)S(1)} %get-tuple-element.75, bf16[3584,2048]{1,0:T(8,128)(2,1)} %param.7), kind=kOutput, calls=%fused_computation.40 | convolution fusion | flops 2417688576 | bytes 10223616 | tf_op jit(solution)/shard_map/dot_general | solution.py:154
  186.7 1.7 collective-permute-start.15
  188.7 2.7 %add_convert_fusion.2 = bf16[384,512]{1,0:T(8,128)(2,1)} fusion(bf16[384,3584]{1,0:T(8,128)(2,1)} %collective-permute-done.12, bf16[384,2048]{1,0:T(8,128)(2,1)S(1)} %get-tuple-element.75, bf16[3584,2048]{1,0:T(8,128)(2,1)S(1)} %bitcast.53), kind=kOutput, calls=%fused_computation.57 | convolution fusion | flops 805896192 | bytes 4456448 | tf_op jit(solution)/shard_map/dot_general | solution.py:154
  191.5 1.7 collective-permute-start.13
  193.1 4.1 %fusion.26.own_ref = f32[384,1536]{1,0:T(8,128)} fusion(bf16[384,2048]{1,0:T(8,128)(2,1)S(1)} %get-tuple-element.73, bf16[3584,2048]{1,0:T(8,128)(2,1)S(1)} %bitcast.53), kind=kOutput, calls=%fused_computation.29 | convolution fusion | flops 2415919104 | bytes 10223616 | tf_op jit(solution)/shard_map/dot_general | solution.py:154
  197.2 4.1 %fusion.17.refs_0_ = f32[384,1536]{1,0:T(8,128)} fusion(bf16[384,2048]{1,0:T(8,128)(2,1)S(1)} %get-tuple-element.73, bf16[3584,2048]{1,0:T(8,128)(2,1)S(1)} %bitcast.53), kind=kOutput, calls=%fused_computation.20 | convolution fusion | flops 2415919104 | bytes 10223616 | tf_op jit(solution)/shard_map/dot_general | solution.py:154
  201.2 2.6 %fusion.38.refs_0_ = f32[384,512]{1,0:T(8,128)S(1)} fusion(bf16[384,2048]{1,0:T(8,128)(2,1)S(1)} %get-tuple-element.73, bf16[3584,2048]{1,0:T(8,128)(2,1)} %param.7), kind=kOutput, calls=%fused_computation.42 | convolution fusion | flops 805306368 | bytes 4456448 | tf_op jit(solution)/shard_map/dot_general | solution.py:154
  203.9 30.9 %fusion = f32[3584,2048]{1,0:T(8,128)} fusion(bf16[384,3584]{1,0:T(8,128)(2,1)} %pad_maximum_fusion.1, bf16[384,3584]{1,0:T(8,128)(2,1)} %pad_maximum_fusion, bf16[384,3584]{1,0:T(8,128)(2,1)} %collective-permute-done, bf16[384,3584]{1,0:T(8,128)(2,1)} %copy-done.5, bf16[384,2048]{1,0:T(8,128)(2,1)} %all-gather.3.cloned.1.call-done, ...), kind=kOutput, calls=%fused_computation | convolution fusion | flops 22617784320 | bytes 46661632 | tf_op jit(solution)/shard_map/dot_general | solution.py:213
  234.9 1.8 copy-done.1
  236.6 1.7 copy-done.4
  238.3 6.2 %shard_map.67 = (bf16[384,3584]{1,0:T(8,128)(2,1)}, bf16[384,3584]{1,0:T(8,128)(2,1)}) custom-call(f32[384,1536]{1,0:T(8,128)S(1)} %copy-done.4, bf16[384,1536]{1,0:T(8,128)(2,1)} %collective-permute-done.16.refs_0_, bf16[384,3584]{1,0:T(8,128)(2,1)} %collective-permute-done.14.refs_1_.refs_2_, bf16[384,3584]{1,0:T(8,128)(2,1)S(1)} %copy-done, ...), custom_call_target="tpu_custom_call" | custom-call | tf_op jit(solution)/shard_map/pallas_call | solution.py:114
  244.5 5.6 %shard_map.68 = (bf16[384,3584]{1,0:T(8,128)(2,1)}, bf16[384,3584]{1,0:T(8,128)(2,1)}) custom-call(f32[384,1536]{1,0:T(8,128)S(1)} %copy-done.3, bf16[384,1536]{1,0:T(8,128)(2,1)} %collective-permute-done.15.refs_1_, bf16[384,3584]{1,0:T(8,128)(2,1)} %collective-permute-done.14.refs_1_.refs_2_, ...), custom_call_target="tpu_custom_call", output_to_operand_aliasing={{0}: (5, {}), {1}: (6, {})} | custom-call | tf_op jit(solution)/shard_map/pallas_call | solution.py:114
  250.1 2.3 shard_map.69
  (56 shorter events, 2.6 us)
Async XLA Ops:
  7.2 80.9 %all-gather.3.cloned.1.call-start = ((), (), s32[]{:S(2)}) async-start(), calls=%async_computation | async-start | bytes 1769472 | tf_op jit(solution)/shard_map/all_gather | solution.py:77
  11.5 55.8 %copy-start.5 = (bf16[384,3584]{1,0:T(8,128)(2,1)}, bf16[384,3584]{1,0:T(8,128)(2,1)S(1)}, u32[]{:S(2)}) copy-start(bf16[384,3584]{1,0:T(8,128)(2,1)S(1)} %fusion.25) | copy-start | bytes 8257540
  11.5 34.1 %collective-permute-start = (bf16[384,3584]{1,0:T(8,128)(2,1)S(1)}, bf16[384,3584]{1,0:T(8,128)(2,1)}, u32[]{:S(2)}, u32[]{:S(2)}) collective-permute-start(bf16[384,3584]{1,0:T(8,128)(2,1)S(1)} %fusion.25), channel_id=1, source_target_pairs={{0,8},{1,17},{2,10},{3,19},{4,12},{5,21},{6,14},{7,23},{8,0},{9,25... | collective-permute-start | bytes 8257544 | tf_op jit(solution)/shard_map/ppermute | solution.py:139
  16.4 1.9 collective-permute-start.1
  19.5 9.9 %collective-permute-start.4 = (bf16[48,2048]{1,0:T(8,128)(2,1)}, bf16[48,2048]{1,0:T(8,128)(2,1)S(1)}, u32[]{:S(2)}, u32[]{:S(2)}) collective-permute-start(bf16[48,2048]{1,0:T(8,128)(2,1)} %get-tuple-element.101), channel_id=1, source_target_pairs={{0,6},{1,7},{2,4},{3,5},{4,2},{5,3},{6,0},{7,1},{8,14},{9,15},{10,... | collective-permute-start | bytes 589832 | tf_op jit(solution)/shard_map/ppermute | solution.py:61
  23.1 17.3 %collective-permute-start.3 = (bf16[48,2048]{1,0:T(8,128)(2,1)S(1)}, bf16[48,2048]{1,0:T(8,128)(2,1)}, u32[]{:S(2)}, u32[]{:S(2)}) collective-permute-start(bf16[48,2048]{1,0:T(8,128)(2,1)S(1)} %get-tuple-element.102), channel_id=1, source_target_pairs={{0,4},{1,5},{2,6},{3,7},{4,0},{5,1},{6,2},{7,3},{8,12},{9,13},{10,... | collective-permute-start | bytes 589832 | tf_op jit(solution)/shard_map/ppermute | solution.py:61
  23.1 17.3 %collective-permute-start.2 = (bf16[48,2048]{1,0:T(8,128)(2,1)S(1)}, bf16[48,2048]{1,0:T(8,128)(2,1)}, u32[]{:S(2)}, u32[]{:S(2)}) collective-permute-start(bf16[48,2048]{1,0:T(8,128)(2,1)S(1)} %get-tuple-element.103), channel_id=1, source_target_pairs={{0,2},{1,3},{2,0},{3,1},{4,6},{5,7},{6,4},{7,5},{8,10},{9,11},{10,... | collective-permute-start | bytes 589832 | tf_op jit(solution)/shard_map/ppermute | solution.py:61
  45.7 7.1 %collective-permute-start.5 = (bf16[48,2048]{1,0:T(8,128)(2,1)S(1)}, bf16[48,2048]{1,0:T(8,128)(2,1)S(1)}, u32[]{:S(2)}, u32[]{:S(2)}) collective-permute-start(bf16[48,2048]{1,0:T(8,128)(2,1)S(1)} %get-tuple-element.98), channel_id=1, source_target_pairs={{0,24},{8,16},{16,8},{24,0},{1,25},{9,17},{17,9},{25,1},{2,26},{10... | collective-permute-start | bytes 589832 | tf_op jit(solution)/shard_map/ppermute | solution.py:71
  52.8 0.7 copy-start.11
  53.5 89.9 %all-gather.5.cloned.1.call-start = ((), (), s32[]{:S(2)}) async-start(), calls=%async_computation.1 | async-start | bytes 5308416 | tf_op jit(solution)/shard_map/all_gather | solution.py:78
  53.7 5.7 %collective-permute-start.6 = (bf16[48,2048]{1,0:T(8,128)(2,1)S(1)}, bf16[48,2048]{1,0:T(8,128)(2,1)S(1)}, u32[]{:S(2)}, u32[]{:S(2)}) collective-permute-start(bf16[48,2048]{1,0:T(8,128)(2,1)S(1)} %get-tuple-element.49), channel_id=1, source_target_pairs={{0,8},{8,0},{16,24},{24,16},{1,9},{9,1},{17,25},{25,17},{2,10},{10... | collective-permute-start | bytes 589832 | tf_op jit(solution)/shard_map/ppermute | solution.py:71
  55.5 5.7 %collective-permute-start.7 = (bf16[48,2048]{1,0:T(8,128)(2,1)S(1)}, bf16[48,2048]{1,0:T(8,128)(2,1)S(1)}, u32[]{:S(2)}, u32[]{:S(2)}) collective-permute-start(bf16[48,2048]{1,0:T(8,128)(2,1)S(1)} %get-tuple-element.50), channel_id=1, source_target_pairs={{0,16},{8,24},{16,0},{24,8},{1,17},{9,25},{17,1},{25,9},{2,18},{10... | collective-permute-start | bytes 589832 | tf_op jit(solution)/shard_map/ppermute | solution.py:71
  62.2 25.9 %collective-permute-start.8 = (bf16[288,3584]{1,0:T(8,128)(2,1)S(1)}, bf16[288,3584]{1,0:T(8,128)(2,1)}, u32[]{:S(2)}, u32[]{:S(2)}) collective-permute-start(bf16[288,3584]{1,0:T(8,128)(2,1)S(1)} %split.12), channel_id=1, source_target_pairs={{0,16},{1,9},{2,18},{3,11},{4,20},{5,13},{6,22},{7,15},{8,24},{9,1... | collective-permute-start | bytes 6193160 | tf_op jit(solution)/shard_map/ppermute | solution.py:146
  67.3 28.4 %collective-permute-start.9 = (bf16[96,3584]{1,0:T(8,128)(2,1)S(1)}, bf16[96,3584]{1,0:T(8,128)(2,1)S(1)}, u32[]{:S(2)}, u32[]{:S(2)}) collective-permute-start(bf16[96,3584]{1,0:T(8,128)(2,1)S(1)} %split.13), channel_id=1, source_target_pairs={{0,16},{1,9},{2,18},{3,11},{4,20},{5,13},{6,22},{7,15},{8,24},{9,1... | collective-permute-start | bytes 2064392 | tf_op jit(solution)/shard_map/ppermute | solution.py:147
  88.1 7.6 %copy-start.12 = (bf16[384,2048]{1,0:T(8,128)(2,1)S(1)}, bf16[384,2048]{1,0:T(8,128)(2,1)}, u32[]{:S(2)}) copy-start(bf16[384,2048]{1,0:T(8,128)(2,1)} %all-gather.3.cloned.1.call-done) | copy-start | bytes 4718596
  103.7 18.6 %collective-permute-start.11 = (bf16[192,3584]{1,0:T(8,128)(2,1)}, bf16[192,3584]{1,0:T(8,128)(2,1)}, u32[]{:S(2)}, u32[]{:S(2)}) collective-permute-start(bf16[192,3584]{1,0:T(8,128)(2,1)} %get-tuple-element.54), channel_id=1, source_target_pairs={{0,16},{1,9},{2,18},{3,11},{4,20},{5,13},{6,22},{7,15},{8,24},{9,1... | collective-permute-start | bytes 4128776 | tf_op jit(solution)/shard_map/ppermute | solution.py:162
  105.3 34.2 %collective-permute-start.10 = (bf16[192,3584]{1,0:T(8,128)(2,1)}, bf16[192,3584]{1,0:T(8,128)(2,1)}, u32[]{:S(2)}, u32[]{:S(2)}) collective-permute-start(bf16[192,3584]{1,0:T(8,128)(2,1)} %get-tuple-element.53), channel_id=1, source_target_pairs={{0,16},{1,9},{2,18},{3,11},{4,20},{5,13},{6,22},{7,15},{8,24},{9,1... | collective-permute-start | bytes 4128776 | tf_op jit(solution)/shard_map/ppermute | solution.py:162
  105.8 3.6 %copy-start.9 = (bf16[384,2048]{1,0:T(8,128)(2,1)S(1)}, bf16[384,2048]{1,0:T(8,128)(2,1)}, u32[]{:S(2)}) copy-start(bf16[384,2048]{1,0:T(8,128)(2,1)} %fusion.32) | copy-start | bytes 4718596
  105.8 3.6 %copy-start.10 = (bf16[384,1536]{1,0:T(8,128)(2,1)S(1)}, bf16[384,1536]{1,0:T(8,128)(2,1)}, u32[]{:S(2)}) copy-start(bf16[384,1536]{1,0:T(8,128)(2,1)} %fusion.35) | copy-start | bytes 3538948
  139.5 33.2 %collective-permute-start.12 = (bf16[384,3584]{1,0:T(8,128)(2,1)S(1)}, bf16[384,3584]{1,0:T(8,128)(2,1)}, u32[]{:S(2)}, u32[]{:S(2)}) collective-permute-start(bf16[384,3584]{1,0:T(8,128)(2,1)S(1)} %pad_maximum_fusion.2), channel_id=1, source_target_pairs={{0,8},{1,17},{2,10},{3,19},{4,12},{5,21},{6,14},{7,23},{8,0},{9,25... | collective-permute-start | bytes 8257544 | tf_op jit(solution)/shard_map/ppermute | solution.py:162
  146.3 55.0 %copy-start.6 = (bf16[384,2048]{1,0:T(8,128)(2,1)}, bf16[384,2048]{1,0:T(8,128)(2,1)S(1)}, u32[]{:S(2)}) copy-start(bf16[384,2048]{1,0:T(8,128)(2,1)S(1)} %get-tuple-element.73) | copy-start | bytes 4718596
  146.5 11.8 %copy-start.8 = (bf16[384,2048]{1,0:T(8,128)(2,1)}, bf16[384,2048]{1,0:T(8,128)(2,1)S(1)}, u32[]{:S(2)}) copy-start(bf16[384,2048]{1,0:T(8,128)(2,1)S(1)} %get-tuple-element.74) | copy-start | bytes 4718596
  146.5 42.2 %copy-start.7 = (bf16[384,2048]{1,0:T(8,128)(2,1)}, bf16[384,2048]{1,0:T(8,128)(2,1)S(1)}, u32[]{:S(2)}) copy-start(bf16[384,2048]{1,0:T(8,128)(2,1)S(1)} %get-tuple-element.75) | copy-start | bytes 4718596
  158.3 76.6 %collective-permute-start.14 = (bf16[384,3584]{1,0:T(8,128)(2,1)}, bf16[384,3584]{1,0:T(8,128)(2,1)}, u32[]{:S(2)}, u32[]{:S(2)}) collective-permute-start(bf16[384,3584]{1,0:T(8,128)(2,1)} %convolution_convert_fusion), channel_id=1, source_target_pairs={{0,8},{1,17},{2,10},{3,19},{4,12},{5,21},{6,14},{7,23},{8,0},{9,25... | collective-permute-start | bytes 8257544 | tf_op jit(solution)/shard_map/ppermute | solution.py:162
  172.7 16.0 %slice-start = ((s8[14680064]{0:T(1024)(128)(4,1)}), s8[4194304]{0:T(1024)(128)(4,1)S(1)}, s32[]{:S(2)}) async-start(s8[14680064]{0:T(1024)(128)(4,1)} %bitcast.52), calls=%async_computation.2 | async-start | bytes 8388608
  172.7 16.0 %slice-start.1 = ((s8[14680064]{0:T(1024)(128)(4,1)}), s8[4194304]{0:T(1024)(128)(4,1)S(1)}, s32[]{:S(2)}) async-start(s8[14680064]{0:T(1024)(128)(4,1)} %bitcast.52), calls=%async_computation.3 | async-start | bytes 8388608
  172.7 16.0 %slice-start.2 = ((s8[14680064]{0:T(1024)(128)(4,1)}), s8[4194304]{0:T(1024)(128)(4,1)S(1)}, s32[]{:S(2)}) async-start(s8[14680064]{0:T(1024)(128)(4,1)} %bitcast.52), calls=%async_computation.4 | async-start | bytes 8388608
  179.7 9.0 %slice-start.3 = ((s8[14680064]{0:T(1024)(128)(4,1)}), s8[2097152]{0:T(1024)(128)(4,1)S(1)}, s32[]{:S(2)}) async-start(s8[14680064]{0:T(1024)(128)(4,1)} %bitcast.52), calls=%async_computation.5 | async-start | bytes 4194304
  186.7 57.9 %collective-permute-start.15 = (bf16[384,1536]{1,0:T(8,128)(2,1)}, bf16[384,1536]{1,0:T(8,128)(2,1)}, u32[]{:S(2)}, u32[]{:S(2)}) collective-permute-start(bf16[384,1536]{1,0:T(8,128)(2,1)} %add_convert_fusion), channel_id=1, source_target_pairs={{0,16},{1,9},{2,18},{3,11},{4,20},{5,13},{6,22},{7,15},{8,24},{9,1... | collective-permute-start | bytes 3538952 | tf_op jit(solution)/shard_map/ppermute | solution.py:162
  188.3 46.5 %collective-permute-start.16 = (bf16[384,1536]{1,0:T(8,128)(2,1)}, bf16[384,1536]{1,0:T(8,128)(2,1)}, u32[]{:S(2)}, u32[]{:S(2)}) collective-permute-start(bf16[384,1536]{1,0:T(8,128)(2,1)} %add_convert_fusion.1), channel_id=1, source_target_pairs={{0,16},{1,9},{2,18},{3,11},{4,20},{5,13},{6,22},{7,15},{8,24},{9,1... | collective-permute-start | bytes 3538952 | tf_op jit(solution)/shard_map/ppermute | solution.py:162
  191.5 58.7 %collective-permute-start.13 = (bf16[384,512]{1,0:T(8,128)(2,1)}, bf16[384,512]{1,0:T(8,128)(2,1)}, u32[]{:S(2)}, u32[]{:S(2)}) collective-permute-start(bf16[384,512]{1,0:T(8,128)(2,1)} %add_convert_fusion.2), channel_id=1, source_target_pairs={{0,16},{1,9},{2,18},{3,11},{4,20},{5,13},{6,22},{7,15},{8,24},{9,1... | collective-permute-start | bytes 1179656 | tf_op jit(solution)/shard_map/ppermute | solution.py:162
  203.9 31.0 %copy-start = (bf16[384,3584]{1,0:T(8,128)(2,1)S(1)}, bf16[384,3584]{1,0:T(8,128)(2,1)}, u32[]{:S(2)}) copy-start(bf16[384,3584]{1,0:T(8,128)(2,1)} %refs_3_.2) | copy-start | bytes 8257540
  234.8 1.8 copy-start.1
  236.6 1.7 copy-start.4
  238.3 6.2 %copy-start.2 = (bf16[384,3584]{1,0:T(8,128)(2,1)S(1)}, bf16[384,3584]{1,0:T(8,128)(2,1)}, u32[]{:S(2)}) copy-start(bf16[384,3584]{1,0:T(8,128)(2,1)} %refs_4_.1) | copy-start | bytes 8257540
  238.3 6.2 %copy-start.3 = (f32[384,1536]{1,0:T(8,128)S(1)}, f32[384,1536]{1,0:T(8,128)}, u32[]{:S(2)}) copy-start(f32[384,1536]{1,0:T(8,128)} %fusion.17.refs_0_) | copy-start | bytes 7077892
Sparse Core Ops, SparseCore 0:
  53.6 26.4 all-gather.2
  81.8 51.1 all-gather.4

commit v4 on v3

--- a/solution.py
+++ b/solution.py
@@ -87,19 +87,19 @@
         grad_hidden = grad_hidden + came_ref[...].astype(jnp.float32)
     gate_value = gate_ref[...].astype(jnp.float32)
     up_value = up_ref[...].astype(jnp.float32)
-    sigmoid_gate = 1.0 / (1.0 + jnp.exp(-gate_value))
+    sigmoid_gate = 0.5 + 0.5 * jnp.tanh(0.5 * gate_value)
     gate_out_ref[...] = (
         grad_hidden * up_value * sigmoid_gate * (1.0 + gate_value * (1.0 - sigmoid_gate))
     ).astype(jnp.bfloat16)
     up_out_ref[...] = (grad_hidden * (gate_value * sigmoid_gate)).astype(jnp.bfloat16)
 
 
-def finish(own, last, whole, gate_act, up_act, outs, start, block):
+def finish(own, came, gate_act, up_act, outs, start, block):
     tokens, width = own.shape
     inner = pl.BlockSpec((tokens, block), lambda i: (0, i))
     outer = pl.BlockSpec((tokens, block), lambda i: (0, start // block + i))
-    operands = [own, last, *whole, gate_act, up_act]
-    specs = [inner] * 2 + [outer] * (len(whole) + 2)
+    operands = [own, *came, gate_act, up_act]
+    specs = [inner] * (1 + len(came)) + [outer] * 2
     kernel, aliases = finish_kernel, {}
     if outs:
         aliases = {len(operands): 0, len(operands) + 1: 1}
@@ -142,9 +142,9 @@
     for step in range(1, steps - 1):
         gathered = gathered + [lax.ppermute(part, BOTH, pairs[step]) for part in gathered]
 
-    front, back = jnp.split(after(hidden, *pieces), [tokens * 3 // 4])
-    front_came = lax.ppermute(front, BOTH, pairs[-1])
-    back_came = lax.ppermute(back, BOTH, pairs[-1])
+    front, back = jnp.split(hidden, 2)
+    front_came = lax.ppermute(after(front, pieces[-1]), BOTH, pairs[-1])
+    back_came = lax.ppermute(after(back, *pieces), BOTH, pairs[-1])
     gathered.append(jnp.concatenate([front_came, back_came]))
 
     blocks = gather_tokens(pieces)
@@ -162,18 +162,12 @@
         return lax.ppermute(total, BOTH, pairs[step])
 
     unit = width // 7
-    total = [
-        product(blocks[-1], 0, 3 * unit, front_came).astype(jnp.bfloat16),
-        product(blocks[-1], 3 * unit, width, front_came).astype(jnp.bfloat16),
-    ]
-    tails = []
+    total = product(blocks[-1], 0, 3 * unit, front_came).astype(jnp.bfloat16)
+    rest = product(blocks[-1], 3 * unit, width, total).astype(jnp.bfloat16)
+    total = jnp.concatenate([total, rest], axis=1)
     for part in gathered[1 : rows // 2]:
-        fore, rear = jnp.split(part, 2)
-        fore = send(after(fore, total[0], back_came), steps - 1)
-        rear = send(after(rear, total[1], back_came), steps - 1)
-        gathered.append(jnp.concatenate([fore, rear]))
-        tails += [fore, rear]
-    total = after(jnp.concatenate(total, axis=1), *tails)
+        gathered.append(send(after(part, rest, back_came), steps - 1))
+    total = after(total, *gathered[rows // 2 + 1 :])
 
     blocks[:-1] = lax.optimization_barrier((*blocks[:-1], total))[:-1]
     turn = lax.axis_index("col") % steps
@@ -184,45 +178,58 @@
         for place in range(rows)
     ]
 
-    came = [[] for _ in range(rows)]
-    came[rows - 2].append(send(total, 0))
+    starts, stops = [0, 3 * unit, 6 * unit], [3 * unit, 6 * unit, width]
+    chunks = range(len(starts))
+    came = [[[] for _ in chunks] for _ in range(rows)]
+    whole = send(total, 0)
+    for chunk in chunks:
+        came[rows - 2][chunk].append(whole[:, starts[chunk] : stops[chunk]])
+
+    def message(place, chunk, *before):
+        total = product(grads[place], starts[chunk], stops[chunk], *before)
+        for block in came[place][chunk]:
+            total = total + block.astype(jnp.float32)
+        return total.astype(jnp.bfloat16)
+
+    def own_product(chunk, *before):
+        return product(grads[0], starts[chunk], stops[chunk], *before)
+
     for step in range(steps - 1):
         for place in reversed(range(rows - 1)):
             if place & ((1 << step) - 1) or not place >> step & 1:
                 continue
-            total = product(grads[place], 0, width, total)
-            for block in came[place]:
-                total = total + block.astype(jnp.float32)
-            total = total.astype(jnp.bfloat16)
-            came[place ^ (1 << step)].append(send(total, step))
-
-    starts, stops = [0, 3 * unit, 6 * unit], [3 * unit, 6 * unit, width]
-    last = []
-    for start, stop in zip(starts, stops):
-        total = product(grads[rows // 2], start, stop, total)
-        for block in came[rows // 2]:
-            total = total + block[:, start:stop].astype(jnp.float32)
-        total = total.astype(jnp.bfloat16)
-        last.append(send(total, steps - 1))
-    own = []
-    for start, stop in zip(starts, stops):
-        total = product(grads[0], start, stop, total)
-        own.append(total)
-
-    gathered, grads, own = lax.optimization_barrier((gathered, grads, own))
+            for chunk in chunks:
+                total = message(place, chunk, total)
+                came[place ^ (1 << step)][chunk].append(send(total, step))
+    own = [own_product(0, total)]
+    own.append(own_product(1, own[0]))
+    total = message(rows // 2, 0, own[1])
+    last = [send(total, steps - 1)]
+
+    gathered, grads, _ = lax.optimization_barrier((gathered, grads, total))
     grad_weight = lax.dot_general(
         jnp.concatenate(gathered, axis=0),
         jnp.concatenate(grads, axis=0),
         (((0,), (0,)), ((), ())),
         preferred_element_type=jnp.float32,
     )
-    own, grad_weight = lax.optimization_barrier((own, grad_weight))
+    total = after(message(rows // 2, 1, grad_weight), last[0], *sum(came[0], []))
+    last.append(send(total, steps - 1))
+    total = message(rows // 2, 2, total)
+    last.append(send(total, steps - 1))
+    own.append(own_product(2, total))
 
     gate_act, up_act = after(gate_act, hidden_came), after(up_act, hidden_came)
     outs = []
     for chunk, start in enumerate(starts):
         outs = finish(
-            own[chunk], last[chunk], came[0], gate_act, up_act, outs, start, math.gcd(unit, 256)
+            own[chunk],
+            [after(block, grad_weight) for block in (*came[0][chunk], last[chunk])],
+            gate_act,
+            up_act,
+            outs,
+            start,
+            math.gcd(unit, 256),
         )
     return (*outs, grad_weight)
 

time: 260 us -> 243 us (0.935)
  waiting for transfers between devices: 93.7 us -> 87.1 us
  local copies, waits for them, and re-layouts: 13.4 us -> 7.76 us
  matrix products: 85.8 us -> 82.9 us
    ppermute x7 -> x8, waiting for transfers between devices: 42.8 us -> 36.7 us  [send(): return lax.ppermute(total, BOTH, pairs[step])]
    unnamed x34 -> x32, local copies, waits for them, and re-layouts: 4.17 us -> 0.74 us
    ppermute x2, waiting for transfers between devices: 20.1 us -> 16.9 us  [the longest x1 16.3 us: on_device(): front_came = lax.ppermute(after(front, pieces[-1]), BOTH, pairs[-1])]
    all_gather x1, waiting for transfers between devices: 0.01 us -> 2.77 us  [gather_tokens(): rest = lax.all_gather(jnp.stack(blocks[:-1]), 'col', axis=1, tiled=True)]
    dot_general x9 -> x11, matrix products: 54.9 us -> 52.4 us  [product(): lax.dot_general(after(block, *before), down_weight[start:stop], (((1,), (...]
    ppermute x7 -> x8, starting transfers between devices: 7.73 us -> 8.79 us  [send(): return lax.ppermute(total, BOTH, pairs[step])]
  transfers between devices with their start and end apart: 19 -> 20, of which waited for: 11 -> 13; matrix products, arithmetic and copies ran while one was open for 40% -> 40% of each run, Pallas kernels for 5% -> 2%
where the time goes in v4:
time: 243 us; the launch traced here: 241 us
  waiting for transfers between devices  87.1 us (36%)
  matrix products  82.9 us (34%)
  starting transfers between devices  24.8 us (10%)
  between operations  14.3 us (6%)
  Pallas kernels  12.6 us (5%)
  other arithmetic  11.7 us (5%)
  local copies, waits for them, and re-layouts  7.76 us (3%)
    dot_general x11, matrix products, product(): lax.dot_general(after(block, *before), down_weight[start:stop], (((1,), (...  52.4 us
    ppermute x8, waiting for transfers between devices, send(): return lax.ppermute(total, BOTH, pairs[step])  36.7 us
    dot_general x1, matrix products, on_device(): lax.dot_general(jnp.concatenate(gathered, axis=0), jnp.concatenate(grads,...  30.5 us
    ppermute x4, waiting for transfers between devices, spread_tokens(): piece = lax.ppermute(piece, 'col', pairs)  18.5 us
    ppermute x1, waiting for transfers between devices, on_device(): front_came = lax.ppermute(after(front, pieces[-1]), BOTH, pairs[-1])  16.3 us
    pallas_call x3, Pallas kernels, finish(): pl.pallas_call(kernel, grid=(width // block,), in_specs=specs, out_specs=...  12.6 us
    ppermute x8, starting transfers between devices, send(): return lax.ppermute(total, BOTH, pairs[step])  8.79 us
    ppermute x3, waiting for transfers between devices, spread_tokens(): piece = lax.ppermute(piece, 'row', [(r, r ^ flip) for r in range(rows)])  8.2 us
  transfers between devices with their start and end apart: 20, of which 13 were waited for; matrix products, arithmetic and copies ran while one was open for 40% of the time, Pallas kernels for 2%

profile of v4, /device:TPU:0, one launch (start us, length us, event | category | flops | bytes accessed | tf_op | source)
XLA Modules:
  0.0 241.2 jit_solution(15145779115632111399)
XLA Ops:
  7.2 4.3 %fusion.21 = bf16[384,3584]{1,0:T(8,128)(2,1)S(1)} fusion(bf16[384,3584]{1,0:T(8,128)(2,1)} %refs_4_.1, bf16[384,3584]{1,0:T(8,128)(2,1)} %refs_3_.2), kind=kLoop, calls=%fused_computation.23 | loop fusion | flops 11010048 | bytes 8257536 | tf_op jit(solution)/shard_map/convert_element_type | solution.py:136
  11.5 3.0 %collective-permute-start = (bf16[384,3584]{1,0:T(8,128)(2,1)S(1)}, bf16[384,3584]{1,0:T(8,128)(2,1)}, u32[]{:S(2)}, u32[]{:S(2)}) collective-permute-start(bf16[384,3584]{1,0:T(8,128)(2,1)S(1)} %fusion.21), channel_id=1, source_target_pairs={{0,8},{1,17},{2,10},{3,19},{4,12},{5,21},{6,14},{7,23},{8,0},{9,25... | collective-permute-start | bytes 8257544 | tf_op jit(solution)/shard_map/ppermute | solution.py:139
  14.5 1.9 dynamic-slice_bitcast_fusion
  16.4 1.9 collective-permute-done.1
  18.7 0.8 constant_dynamic-slice_fusion
  19.5 3.6 %collective-permute-start.4 = (bf16[48,2048]{1,0:T(8,128)(2,1)}, bf16[48,2048]{1,0:T(8,128)(2,1)S(1)}, u32[]{:S(2)}, u32[]{:S(2)}) collective-permute-start(bf16[48,2048]{1,0:T(8,128)(2,1)} %get-tuple-element.107), channel_id=1, source_target_pairs={{0,6},{1,7},{2,4},{3,5},{4,2},{5,3},{6,0},{7,1},{8,14},{9,15},{10,... | collective-permute-start | bytes 589832 | tf_op jit(solution)/shard_map/ppermute | solution.py:61
  23.1 0.8 collective-permute-start.2
  23.9 5.5 %collective-permute-done.4 = bf16[48,2048]{1,0:T(8,128)(2,1)S(1)} collective-permute-done((bf16[48,2048]{1,0:T(8,128)(2,1)}, bf16[48,2048]{1,0:T(8,128)(2,1)S(1)}, u32[]{:S(2)}, u32[]{:S(2)}) %collective-permute-start.4) | collective-permute-done | bytes 196640 | tf_op jit(solution)/shard_map/ppermute | solution.py:61
  29.4 11.0 %collective-permute-done.3 = bf16[48,2048]{1,0:T(8,128)(2,1)} collective-permute-done((bf16[48,2048]{1,0:T(8,128)(2,1)S(1)}, bf16[48,2048]{1,0:T(8,128)(2,1)}, u32[]{:S(2)}, u32[]{:S(2)}) %collective-permute-start.3) | collective-permute-done | bytes 196640 | tf_op jit(solution)/shard_map/ppermute | solution.py:61
  40.4 1.1 pad_maximum_fusion.3
  41.5 4.1 %collective-permute-done = bf16[384,3584]{1,0:T(8,128)(2,1)} collective-permute-done((bf16[384,3584]{1,0:T(8,128)(2,1)S(1)}, bf16[384,3584]{1,0:T(8,128)(2,1)}, u32[]{:S(2)}, u32[]{:S(2)}) %collective-permute-start) | collective-permute-done | bytes 2752544 | tf_op jit(solution)/shard_map/ppermute | solution.py:139
  45.7 3.0 %collective-permute-start.5 = (bf16[48,2048]{1,0:T(8,128)(2,1)S(1)}, bf16[48,2048]{1,0:T(8,128)(2,1)S(1)}, u32[]{:S(2)}, u32[]{:S(2)}) collective-permute-start(bf16[48,2048]{1,0:T(8,128)(2,1)S(1)} %get-tuple-element.105), channel_id=1, source_target_pairs={{0,24},{8,16},{16,8},{24,0},{1,25},{9,17},{17,9},{25,1},{2,26},{10... | collective-permute-start | bytes 589832 | tf_op jit(solution)/shard_map/ppermute | solution.py:71
  48.7 4.0 %collective-permute-done.5 = bf16[48,2048]{1,0:T(8,128)(2,1)S(1)} collective-permute-done((bf16[48,2048]{1,0:T(8,128)(2,1)S(1)}, bf16[48,2048]{1,0:T(8,128)(2,1)S(1)}, u32[]{:S(2)}, u32[]{:S(2)}) %collective-permute-start.5) | collective-permute-done | bytes 196640 | tf_op jit(solution)/shard_map/ppermute | solution.py:71
  53.7 1.7 collective-permute-start.7
  55.5 1.5 collective-permute-start.8
  57.0 2.5 %collective-permute-done.7 = bf16[48,2048]{1,0:T(8,128)(2,1)S(1)} collective-permute-done((bf16[48,2048]{1,0:T(8,128)(2,1)S(1)}, bf16[48,2048]{1,0:T(8,128)(2,1)S(1)}, u32[]{:S(2)}, u32[]{:S(2)}) %collective-permute-start.7) | collective-permute-done | bytes 196640 | tf_op jit(solution)/shard_map/ppermute | solution.py:71
  59.5 1.7 collective-permute-done.8
  61.1 0.9 pad_maximum_fusion.4
  62.1 1.3 fusion.62
  63.3 1.5 collective-permute-start.6
  65.4 16.3 %collective-permute-done.6 = bf16[192,3584]{1,0:T(8,128)(2,1)S(1)} collective-permute-done((bf16[192,3584]{1,0:T(8,128)(2,1)S(1)}, bf16[192,3584]{1,0:T(8,128)(2,1)S(1)}, u32[]{:S(2)}, u32[]{:S(2)}) %collective-permute-start.6) | collective-permute-done | bytes 1376288 | tf_op jit(solution)/shard_map/ppermute | solution.py:146
  81.7 7.0 %fusion.39 = bf16[384,1536]{1,0:T(8,128)(2,1)} fusion(bf16[384,2048]{1,0:T(8,128)(2,1)} %all-gather.3.cloned.1.call-done, bf16[3584,2048]{1,0:T(8,128)(2,1)} %param.7), kind=kOutput, calls=%fused_computation.39 | convolution fusion | flops 2416508928 | bytes 9043968 | tf_op jit(solution)/shard_map/dot_general | solution.py:154
  88.7 7.2 %fusion.36 = bf16[384,2048]{1,0:T(8,128)(2,1)S(1)} fusion(bf16[384,2048]{1,0:T(8,128)(2,1)S(1)} %copy-done.11, bf16[3584,2048]{1,0:T(8,128)(2,1)} %param.7), kind=kOutput, calls=%fused_computation.38 | convolution fusion | flops 3222011904 | bytes 11534336 | tf_op jit(solution)/shard_map/dot_general | solution.py:154
  96.5 1.5 collective-permute-start.10
  98.0 3.2 %pad_maximum_fusion = bf16[384,3584]{1,0:T(8,128)(2,1)} fusion(bf16[192,3584]{1,0:T(8,128)(2,1)} %collective-permute-done.9, bf16[192,3584]{1,0:T(8,128)(2,1)S(1)} %collective-permute-done.6), kind=kLoop, calls=%fused_computation.42 | loop fusion | flops 5505024 | bytes 5505024 | tf_op jit(solution)/shard_map/concatenate | solution.py:148
  101.2 1.7 pad_maximum_fusion.1
  102.9 27.0 %collective-permute-done.10 = bf16[384,3584]{1,0:T(8,128)(2,1)} collective-permute-done((bf16[384,3584]{1,0:T(8,128)(2,1)}, bf16[384,3584]{1,0:T(8,128)(2,1)}, u32[]{:S(2)}, u32[]{:S(2)}) %collective-permute-start.10) | collective-permute-done | bytes 2752544 | tf_op jit(solution)/shard_map/ppermute | solution.py:162
  130.2 2.8 %all-gather.5.cloned.1.call-done = bf16[3,384,2048]{2,1,0:T(8,128)(2,1)} async-done(((bf16[3,48,2048]{2,1,0:T(8,128)(2,1)}), bf16[3,384,2048]{2,1,0:T(8,128)(2,1)}) %all-gather.5.cloned.1.call-update) | async-done | bytes 4718608 | tf_op jit(solution)/shard_map/all_gather | solution.py:78
  133.0 3.0 %slice_bitcast_fusion = (bf16[384,2048]{1,0:T(8,128)(2,1)S(1)}, bf16[384,2048]{1,0:T(8,128)(2,1)S(1)}, bf16[384,2048]{1,0:T(8,128)(2,1)S(1)}) fusion(bf16[3,384,2048]{2,1,0:T(8,128)(2,1)} %all-gather.5.cloned.1.call-done), kind=kLoop, calls=%fused_computation.52 | loop fusion | bytes 9437184 | tf_op jit(solution)/shard_map/squeeze | solution.py:79
  136.3 8.9 %fusion.42 = bf16[384,1536]{1,0:T(8,128)(2,1)} fusion(bf16[384,2048]{1,0:T(8,128)(2,1)S(1)} %get-tuple-element.75, bf16[3584,2048]{1,0:T(8,128)(2,1)} %param.7), kind=kOutput, calls=%fused_computation.40 | convolution fusion | flops 2416508928 | bytes 9043968 | tf_op jit(solution)/shard_map/dot_general | solution.py:154
  145.2 3.7 %fusion.45 = bf16[384,1536]{1,0:T(8,128)(2,1)} fusion(bf16[384,2048]{1,0:T(8,128)(2,1)S(1)} %get-tuple-element.75, bf16[3584,2048]{1,0:T(8,128)(2,1)S(1)} %bitcast.54), kind=kOutput, calls=%fused_computation.41 | convolution fusion | flops 2416508928 | bytes 9043968 | tf_op jit(solution)/shard_map/dot_general | solution.py:154
  148.8 1.5 collective-permute-start.14
  150.9 2.0 fusion.54
  152.9 1.5 collective-permute-start.15
  154.4 2.7 %fusion.30.own_ref = f32[384,1536]{1,0:T(8,128)S(1)} fusion(bf16[384,2048]{1,0:T(8,128)(2,1)S(1)} %get-tuple-element.80, bf16[3584,2048]{1,0:T(8,128)(2,1)S(1)} %bitcast.54), kind=kOutput, calls=%fused_computation.32 | convolution fusion | flops 2415919104 | bytes 10223616 | tf_op jit(solution)/shard_map/dot_general | solution.py:154
  157.1 4.1 %fusion.24.refs_0_ = f32[384,1536]{1,0:T(8,128)} fusion(bf16[384,2048]{1,0:T(8,128)(2,1)S(1)} %get-tuple-element.80, bf16[3584,2048]{1,0:T(8,128)(2,1)S(1)} %bitcast.54), kind=kOutput, calls=%fused_computation.26 | convolution fusion | flops 2415919104 | bytes 10223616 | tf_op jit(solution)/shard_map/dot_general | solution.py:154
  161.2 2.0 collective-permute-done.11
  163.2 4.8 %add_convert_fusion.1 = bf16[384,1536]{1,0:T(8,128)(2,1)} fusion(bf16[384,3584]{1,0:T(8,128)(2,1)} %collective-permute-done.11, bf16[384,2048]{1,0:T(8,128)(2,1)S(1)} %get-tuple-element.79, bf16[3584,2048]{1,0:T(8,128)(2,1)S(1)} %bitcast.54), kind=kOutput, calls=%fused_computation.45 | convolution fusion | flops 2417688576 | bytes 10223616 | tf_op jit(solution)/shard_map/dot_general | solution.py:154
  168.0 1.5 collective-permute-start.12
  169.6 30.5 %fusion = f32[3584,2048]{1,0:T(8,128)} fusion(bf16[384,3584]{1,0:T(8,128)(2,1)} %collective-permute-done.10, bf16[384,3584]{1,0:T(8,128)(2,1)} %pad_maximum_fusion, bf16[384,3584]{1,0:T(8,128)(2,1)} %collective-permute-done, bf16[384,3584]{1,0:T(8,128)(2,1)} %copy-done.3, bf16[384,2048]{1,0:T(8,128)(2,1)} %all-gather.3.cloned.1.call-done, ...), kind=kOutput, calls=%fused_computation | convolution fusion | flops 22617784320 | bytes 46661632 | tf_op jit(solution)/shard_map/dot_general | solution.py:210
  200.1 6.3 %add_convert_fusion = bf16[384,1536]{1,0:T(8,128)(2,1)S(1)} fusion(bf16[384,3584]{1,0:T(8,128)(2,1)} %collective-permute-done.11, bf16[384,2048]{1,0:T(8,128)(2,1)} %copy-done.6, bf16[3584,2048]{1,0:T(8,128)(2,1)} %param.7), kind=kOutput, calls=%fused_computation.44 | convolution fusion | flops 2417688576 | bytes 10223616 | tf_op jit(solution)/shard_map/dot_general | solution.py:154
  207.0 2.9 %add_convert_fusion.2 = bf16[384,512]{1,0:T(8,128)(2,1)S(1)} fusion(bf16[384,3584]{1,0:T(8,128)(2,1)} %collective-permute-done.11, bf16[384,2048]{1,0:T(8,128)(2,1)S(1)} %copy-done.7, bf16[3584,2048]{1,0:T(8,128)(2,1)} %param.7), kind=kOutput, calls=%fused_computation.64 | convolution fusion | flops 805896192 | bytes 4456448 | tf_op jit(solution)/shard_map/dot_general | solution.py:154
  210.0 1.3 collective-permute-start.16
  211.3 5.2 %shard_map.67 = (bf16[384,3584]{1,0:T(8,128)(2,1)}, bf16[384,3584]{1,0:T(8,128)(2,1)}) custom-call(f32[384,1536]{1,0:T(8,128)S(1)} %fusion.30.own_ref, bf16[384,1536]{1,0:T(8,128)(2,1)S(1)} %collective-permute-done.13.refs_0_, bf16[384,1536]{1,0:T(8,128)(2,1)} %collective-permute-done.12.refs_1_, bf16[384,3584]{1,0:T(8,128)(2,1)S(1)} %copy-done, ...), custom_call_target="tpu_custom_call" | custom-call | tf_op jit(solution)/shard_map/pallas_call | solution.py:114
  216.5 2.7 %fusion.48.refs_0_ = f32[384,512]{1,0:T(8,128)S(1)} fusion(bf16[384,2048]{1,0:T(8,128)(2,1)S(1)} %copy-done.5, bf16[3584,2048]{1,0:T(8,128)(2,1)} %param.7), kind=kOutput, calls=%fused_computation.46 | convolution fusion | flops 805306368 | bytes 4456448 | tf_op jit(solution)/shard_map/dot_general | solution.py:154
  219.2 7.7 %collective-permute-done.16.refs_2_ = bf16[384,512]{1,0:T(8,128)(2,1)S(1)} collective-permute-done((bf16[384,512]{1,0:T(8,128)(2,1)S(1)}, bf16[384,512]{1,0:T(8,128)(2,1)S(1)}, u32[]{:S(2)}, u32[]{:S(2)}) %collective-permute-start.16) | collective-permute-done | bytes 393248 | tf_op jit(solution)/shard_map/ppermute | solution.py:162
  226.9 5.2 %shard_map.68 = (bf16[384,3584]{1,0:T(8,128)(2,1)}, bf16[384,3584]{1,0:T(8,128)(2,1)}) custom-call(f32[384,1536]{1,0:T(8,128)S(1)} %copy-done.2, bf16[384,1536]{1,0:T(8,128)(2,1)} %collective-permute-done.14.refs_1_, bf16[384,1536]{1,0:T(8,128)(2,1)S(1)} %collective-permute-done.17.refs_2_, ...), custom_call_target="tpu_custom_call", output_to_operand_aliasing={{0}: (5, {}), {1}: (6, {})} | custom-call | tf_op jit(solution)/shard_map/pallas_call | solution.py:114
  232.1 2.2 shard_map.69
  (55 shorter events, 4.2 us)
Async XLA Ops:
  7.2 74.5 %all-gather.3.cloned.1.call-start = ((), (), s32[]{:S(2)}) async-start(), calls=%async_computation | async-start | bytes 1769472 | tf_op jit(solution)/shard_map/all_gather | solution.py:77
  11.5 50.6 %copy-start.3 = (bf16[384,3584]{1,0:T(8,128)(2,1)}, bf16[384,3584]{1,0:T(8,128)(2,1)S(1)}, u32[]{:S(2)}) copy-start(bf16[384,3584]{1,0:T(8,128)(2,1)S(1)} %fusion.21) | copy-start | bytes 8257540
  11.5 34.1 %collective-permute-start = (bf16[384,3584]{1,0:T(8,128)(2,1)S(1)}, bf16[384,3584]{1,0:T(8,128)(2,1)}, u32[]{:S(2)}, u32[]{:S(2)}) collective-permute-start(bf16[384,3584]{1,0:T(8,128)(2,1)S(1)} %fusion.21), channel_id=1, source_target_pairs={{0,8},{1,17},{2,10},{3,19},{4,12},{5,21},{6,14},{7,23},{8,0},{9,25... | collective-permute-start | bytes 8257544 | tf_op jit(solution)/shard_map/ppermute | solution.py:139
  16.4 1.9 collective-permute-start.1
  19.5 9.9 %collective-permute-start.4 = (bf16[48,2048]{1,0:T(8,128)(2,1)}, bf16[48,2048]{1,0:T(8,128)(2,1)S(1)}, u32[]{:S(2)}, u32[]{:S(2)}) collective-permute-start(bf16[48,2048]{1,0:T(8,128)(2,1)} %get-tuple-element.107), channel_id=1, source_target_pairs={{0,6},{1,7},{2,4},{3,5},{4,2},{5,3},{6,0},{7,1},{8,14},{9,15},{10,... | collective-permute-start | bytes 589832 | tf_op jit(solution)/shard_map/ppermute | solution.py:61
  23.1 17.3 %collective-permute-start.3 = (bf16[48,2048]{1,0:T(8,128)(2,1)S(1)}, bf16[48,2048]{1,0:T(8,128)(2,1)}, u32[]{:S(2)}, u32[]{:S(2)}) collective-permute-start(bf16[48,2048]{1,0:T(8,128)(2,1)S(1)} %get-tuple-element.108), channel_id=1, source_target_pairs={{0,4},{1,5},{2,6},{3,7},{4,0},{5,1},{6,2},{7,3},{8,12},{9,13},{10,... | collective-permute-start | bytes 589832 | tf_op jit(solution)/shard_map/ppermute | solution.py:61
  23.1 17.3 %collective-permute-start.2 = (bf16[48,2048]{1,0:T(8,128)(2,1)S(1)}, bf16[48,2048]{1,0:T(8,128)(2,1)}, u32[]{:S(2)}, u32[]{:S(2)}) collective-permute-start(bf16[48,2048]{1,0:T(8,128)(2,1)S(1)} %get-tuple-element.109), channel_id=1, source_target_pairs={{0,2},{1,3},{2,0},{3,1},{4,6},{5,7},{6,4},{7,5},{8,10},{9,11},{10,... | collective-permute-start | bytes 589832 | tf_op jit(solution)/shard_map/ppermute | solution.py:61
  45.7 7.1 %collective-permute-start.5 = (bf16[48,2048]{1,0:T(8,128)(2,1)S(1)}, bf16[48,2048]{1,0:T(8,128)(2,1)S(1)}, u32[]{:S(2)}, u32[]{:S(2)}) collective-permute-start(bf16[48,2048]{1,0:T(8,128)(2,1)S(1)} %get-tuple-element.105), channel_id=1, source_target_pairs={{0,24},{8,16},{16,8},{24,0},{1,25},{9,17},{17,9},{25,1},{2,26},{10... | collective-permute-start | bytes 589832 | tf_op jit(solution)/shard_map/ppermute | solution.py:71
  52.8 0.7 copy-start.10
  53.5 79.5 %all-gather.5.cloned.1.call-start = ((), (), s32[]{:S(2)}) async-start(), calls=%async_computation.1 | async-start | bytes 5308416 | tf_op jit(solution)/shard_map/all_gather | solution.py:78
  53.7 5.7 %collective-permute-start.7 = (bf16[48,2048]{1,0:T(8,128)(2,1)S(1)}, bf16[48,2048]{1,0:T(8,128)(2,1)S(1)}, u32[]{:S(2)}, u32[]{:S(2)}) collective-permute-start(bf16[48,2048]{1,0:T(8,128)(2,1)S(1)} %get-tuple-element.53), channel_id=1, source_target_pairs={{0,8},{8,0},{16,24},{24,16},{1,9},{9,1},{17,25},{25,17},{2,10},{10... | collective-permute-start | bytes 589832 | tf_op jit(solution)/shard_map/ppermute | solution.py:71
  55.5 5.7 %collective-permute-start.8 = (bf16[48,2048]{1,0:T(8,128)(2,1)S(1)}, bf16[48,2048]{1,0:T(8,128)(2,1)S(1)}, u32[]{:S(2)}, u32[]{:S(2)}) collective-permute-start(bf16[48,2048]{1,0:T(8,128)(2,1)S(1)} %get-tuple-element.54), channel_id=1, source_target_pairs={{0,16},{8,24},{16,0},{24,8},{1,17},{9,25},{17,1},{25,9},{2,18},{10... | collective-permute-start | bytes 589832 | tf_op jit(solution)/shard_map/ppermute | solution.py:71
  63.3 18.3 %collective-permute-start.6 = (bf16[192,3584]{1,0:T(8,128)(2,1)S(1)}, bf16[192,3584]{1,0:T(8,128)(2,1)S(1)}, u32[]{:S(2)}, u32[]{:S(2)}) collective-permute-start(bf16[192,3584]{1,0:T(8,128)(2,1)S(1)} %get-tuple-element.51), channel_id=1, source_target_pairs={{0,16},{1,9},{2,18},{3,11},{4,20},{5,13},{6,22},{7,15},{8,24},{9,1... | collective-permute-start | bytes 4128776 | tf_op jit(solution)/shard_map/ppermute | solution.py:146
  64.9 31.6 %collective-permute-start.9 = (bf16[192,3584]{1,0:T(8,128)(2,1)}, bf16[192,3584]{1,0:T(8,128)(2,1)}, u32[]{:S(2)}, u32[]{:S(2)}) collective-permute-start(bf16[192,3584]{1,0:T(8,128)(2,1)} %get-tuple-element.55), channel_id=1, source_target_pairs={{0,16},{1,9},{2,18},{3,11},{4,20},{5,13},{6,22},{7,15},{8,24},{9,1... | collective-permute-start | bytes 4128776 | tf_op jit(solution)/shard_map/ppermute | solution.py:147
  81.6 7.0 %copy-start.11 = (bf16[384,2048]{1,0:T(8,128)(2,1)S(1)}, bf16[384,2048]{1,0:T(8,128)(2,1)}, u32[]{:S(2)}) copy-start(bf16[384,2048]{1,0:T(8,128)(2,1)} %all-gather.3.cloned.1.call-done) | copy-start | bytes 4718596
  96.5 33.4 %collective-permute-start.10 = (bf16[384,3584]{1,0:T(8,128)(2,1)}, bf16[384,3584]{1,0:T(8,128)(2,1)}, u32[]{:S(2)}, u32[]{:S(2)}) collective-permute-start(bf16[384,3584]{1,0:T(8,128)(2,1)} %collective-permute-done), channel_id=1, source_target_pairs={{0,16},{1,9},{2,18},{3,11},{4,20},{5,13},{6,22},{7,15},{8,24},{9,1... | collective-permute-start | bytes 8257544 | tf_op jit(solution)/shard_map/ppermute | solution.py:162
  98.0 3.2 %copy-start.9 = (bf16[384,1536]{1,0:T(8,128)(2,1)S(1)}, bf16[384,1536]{1,0:T(8,128)(2,1)}, u32[]{:S(2)}) copy-start(bf16[384,1536]{1,0:T(8,128)(2,1)} %fusion.39) | copy-start | bytes 3538948
  129.9 33.4 %collective-permute-start.11 = (bf16[384,3584]{1,0:T(8,128)(2,1)}, bf16[384,3584]{1,0:T(8,128)(2,1)}, u32[]{:S(2)}, u32[]{:S(2)}) collective-permute-start(bf16[384,3584]{1,0:T(8,128)(2,1)} %pad_maximum_fusion.1), channel_id=1, source_target_pairs={{0,8},{1,17},{2,10},{3,19},{4,12},{5,21},{6,14},{7,23},{8,0},{9,25... | collective-permute-start | bytes 8257544 | tf_op jit(solution)/shard_map/ppermute | solution.py:162
  133.0 12.1 %slice-start = ((s8[14680064]{0:T(1024)(128)(4,1)}), s8[4194304]{0:T(1024)(128)(4,1)S(1)}, s32[]{:S(2)}) async-start(s8[14680064]{0:T(1024)(128)(4,1)} %bitcast.53), calls=%async_computation.2 | async-start | bytes 8388608
  133.0 12.2 %slice-start.1 = ((s8[14680064]{0:T(1024)(128)(4,1)}), s8[4194304]{0:T(1024)(128)(4,1)S(1)}, s32[]{:S(2)}) async-start(s8[14680064]{0:T(1024)(128)(4,1)} %bitcast.53), calls=%async_computation.3 | async-start | bytes 8388608
  136.0 21.1 %copy-start.4 = (bf16[384,2048]{1,0:T(8,128)(2,1)}, bf16[384,2048]{1,0:T(8,128)(2,1)S(1)}, u32[]{:S(2)}) copy-start(bf16[384,2048]{1,0:T(8,128)(2,1)S(1)} %get-tuple-element.80) | copy-start | bytes 4718596
  136.2 14.6 %copy-start.8 = (bf16[384,2048]{1,0:T(8,128)(2,1)}, bf16[384,2048]{1,0:T(8,128)(2,1)S(1)}, u32[]{:S(2)}) copy-start(bf16[384,2048]{1,0:T(8,128)(2,1)S(1)} %get-tuple-element.75) | copy-start | bytes 4718596
  136.2 27.0 %copy-start.6 = (bf16[384,2048]{1,0:T(8,128)(2,1)}, bf16[384,2048]{1,0:T(8,128)(2,1)S(1)}, u32[]{:S(2)}) copy-start(bf16[384,2048]{1,0:T(8,128)(2,1)S(1)} %get-tuple-element.79) | copy-start | bytes 4718596
  136.3 8.9 %slice-start.2 = ((s8[14680064]{0:T(1024)(128)(4,1)}), s8[4194304]{0:T(1024)(128)(4,1)S(1)}, s32[]{:S(2)}) async-start(s8[14680064]{0:T(1024)(128)(4,1)} %bitcast.53), calls=%async_computation.4 | async-start | bytes 8388608
  136.3 8.9 %slice-start.3 = ((s8[14680064]{0:T(1024)(128)(4,1)}), s8[2097152]{0:T(1024)(128)(4,1)S(1)}, s32[]{:S(2)}) async-start(s8[14680064]{0:T(1024)(128)(4,1)} %bitcast.53), calls=%async_computation.5 | async-start | bytes 4194304
  148.8 57.6 %collective-permute-start.14 = (bf16[384,1536]{1,0:T(8,128)(2,1)}, bf16[384,1536]{1,0:T(8,128)(2,1)}, u32[]{:S(2)}, u32[]{:S(2)}) collective-permute-start(bf16[384,1536]{1,0:T(8,128)(2,1)} %fusion.45), channel_id=1, source_target_pairs={{0,8},{1,17},{2,10},{3,19},{4,12},{5,21},{6,14},{7,23},{8,0},{9,25... | collective-permute-start | bytes 3538952 | tf_op jit(solution)/shard_map/ppermute | solution.py:162
  150.4 56.1 %collective-permute-start.13 = (bf16[384,1536]{1,0:T(8,128)(2,1)}, bf16[384,1536]{1,0:T(8,128)(2,1)S(1)}, u32[]{:S(2)}, u32[]{:S(2)}) collective-permute-start(bf16[384,1536]{1,0:T(8,128)(2,1)} %fusion.42), channel_id=1, source_target_pairs={{0,8},{1,17},{2,10},{3,19},{4,12},{5,21},{6,14},{7,23},{8,0},{9,25... | collective-permute-start | bytes 3538952 | tf_op jit(solution)/shard_map/ppermute | solution.py:162
  152.9 53.6 %collective-permute-start.15 = (bf16[384,512]{1,0:T(8,128)(2,1)}, bf16[384,512]{1,0:T(8,128)(2,1)}, u32[]{:S(2)}, u32[]{:S(2)}) collective-permute-start(bf16[384,512]{1,0:T(8,128)(2,1)} %fusion.54), channel_id=1, source_target_pairs={{0,8},{1,17},{2,10},{3,19},{4,12},{5,21},{6,14},{7,23},{8,0},{9,25... | collective-permute-start | bytes 1179656 | tf_op jit(solution)/shard_map/ppermute | solution.py:162
  168.0 38.4 %collective-permute-start.12 = (bf16[384,1536]{1,0:T(8,128)(2,1)}, bf16[384,1536]{1,0:T(8,128)(2,1)}, u32[]{:S(2)}, u32[]{:S(2)}) collective-permute-start(bf16[384,1536]{1,0:T(8,128)(2,1)} %add_convert_fusion.1), channel_id=1, source_target_pairs={{0,16},{1,9},{2,18},{3,11},{4,20},{5,13},{6,22},{7,15},{8,24},{9,1... | collective-permute-start | bytes 3538952 | tf_op jit(solution)/shard_map/ppermute | solution.py:162
  200.1 6.9 %copy-start.7 = (bf16[384,2048]{1,0:T(8,128)(2,1)S(1)}, bf16[384,2048]{1,0:T(8,128)(2,1)}, u32[]{:S(2)}) copy-start(bf16[384,2048]{1,0:T(8,128)(2,1)} %copy-done.6) | copy-start | bytes 4718596
  206.4 4.9 %copy-start = (bf16[384,3584]{1,0:T(8,128)(2,1)S(1)}, bf16[384,3584]{1,0:T(8,128)(2,1)}, u32[]{:S(2)}) copy-start(bf16[384,3584]{1,0:T(8,128)(2,1)} %refs_3_.2) | copy-start | bytes 8257540
  206.4 4.9 %copy-start.1 = (bf16[384,3584]{1,0:T(8,128)(2,1)S(1)}, bf16[384,3584]{1,0:T(8,128)(2,1)}, u32[]{:S(2)}) copy-start(bf16[384,3584]{1,0:T(8,128)(2,1)} %refs_4_.1) | copy-start | bytes 8257540
  206.4 20.5 %collective-permute-start.17 = (bf16[384,1536]{1,0:T(8,128)(2,1)S(1)}, bf16[384,1536]{1,0:T(8,128)(2,1)S(1)}, u32[]{:S(2)}, u32[]{:S(2)}) collective-permute-start(bf16[384,1536]{1,0:T(8,128)(2,1)S(1)} %add_convert_fusion), channel_id=1, source_target_pairs={{0,16},{1,9},{2,18},{3,11},{4,20},{5,13},{6,22},{7,15},{8,24},{9,1... | collective-permute-start | bytes 3538952 | tf_op jit(solution)/shard_map/ppermute | solution.py:162
  209.9 6.5 %copy-start.5 = (bf16[384,2048]{1,0:T(8,128)(2,1)S(1)}, bf16[384,2048]{1,0:T(8,128)(2,1)}, u32[]{:S(2)}) copy-start(bf16[384,2048]{1,0:T(8,128)(2,1)} %copy-done.4) | copy-start | bytes 4718596
  210.0 17.0 %collective-permute-start.16 = (bf16[384,512]{1,0:T(8,128)(2,1)S(1)}, bf16[384,512]{1,0:T(8,128)(2,1)S(1)}, u32[]{:S(2)}, u32[]{:S(2)}) collective-permute-start(bf16[384,512]{1,0:T(8,128)(2,1)S(1)} %add_convert_fusion.2), channel_id=1, source_target_pairs={{0,16},{1,9},{2,18},{3,11},{4,20},{5,13},{6,22},{7,15},{8,24},{9,1... | collective-permute-start | bytes 1179656 | tf_op jit(solution)/shard_map/ppermute | solution.py:162
  216.5 10.5 %copy-start.2 = (f32[384,1536]{1,0:T(8,128)S(1)}, f32[384,1536]{1,0:T(8,128)}, u32[]{:S(2)}) copy-start(f32[384,1536]{1,0:T(8,128)} %fusion.24.refs_0_) | copy-start | bytes 7077892
Sparse Core Ops, SparseCore 0:
  53.6 26.4 all-gather.2
  81.7 51.1 all-gather.4

commit v5 on v4

--- a/solution.py
+++ b/solution.py
@@ -65,17 +65,16 @@
     blocks = [None] * rows
     for flip in reversed(range(rows)):
         piece = lax.dynamic_index_in_dim(held, row ^ flip ^ plane, 0, keepdims=False)
-        if flip < rows - 1:
-            piece, _ = lax.optimization_barrier((piece, blocks[-1]))
         if flip:
             piece = lax.ppermute(piece, "row", [(r, r ^ flip) for r in range(rows)])
         blocks[flip] = piece
     return blocks
 
 
-def gather_tokens(blocks):
+def gather_tokens(blocks, before):
     first = lax.all_gather(blocks[-1], "col", axis=0, tiled=True)
-    rest = lax.all_gather(jnp.stack(blocks[:-1]), "col", axis=1, tiled=True)
+    rest, _ = lax.optimization_barrier((jnp.stack(blocks[:-1]), before))
+    rest = lax.all_gather(rest, "col", axis=1, tiled=True)
     return [rest[flip] for flip in range(len(blocks) - 1)] + [first]
 
 
@@ -147,7 +146,7 @@
     back_came = lax.ppermute(after(back, *pieces), BOTH, pairs[-1])
     gathered.append(jnp.concatenate([front_came, back_came]))
 
-    blocks = gather_tokens(pieces)
+    blocks = gather_tokens(pieces, front_came)
     width = down_weight.shape[0]
 
     def product(block, start, stop, *before):
@@ -163,10 +162,10 @@
 
     unit = width // 7
     total = product(blocks[-1], 0, 3 * unit, front_came).astype(jnp.bfloat16)
+    for part in gathered[1 : rows // 2]:
+        gathered.append(send(after(part, total, back_came), steps - 1))
     rest = product(blocks[-1], 3 * unit, width, total).astype(jnp.bfloat16)
     total = jnp.concatenate([total, rest], axis=1)
-    for part in gathered[1 : rows // 2]:
-        gathered.append(send(after(part, rest, back_came), steps - 1))
     total = after(total, *gathered[rows // 2 + 1 :])
 
     blocks[:-1] = lax.optimization_barrier((*blocks[:-1], total))[:-1]
@@ -224,7 +223,7 @@
     for chunk, start in enumerate(starts):
         outs = finish(
             own[chunk],
-            [after(block, grad_weight) for block in (*came[0][chunk], last[chunk])],
+            [after(block, grad_weight, *outs) for block in (*came[0][chunk], last[chunk])],
             gate_act,
             up_act,
             outs,

time: 243 us -> 237 us (0.975)
  waiting for transfers between devices: 87.1 us -> 82.2 us
    ppermute x1, waiting for transfers between devices: 16.3 us -> 0.01 us  [on_device(): front_came = lax.ppermute(after(front, pieces[-1]), BOTH, pairs[-1])]
    ppermute x3, waiting for transfers between devices: 8.2 us -> 21.4 us  [spread_tokens(): piece = lax.ppermute(piece, 'row', [(r, r ^ flip) for r in range(rows)])]
    ppermute x8, waiting for transfers between devices: 36.7 us -> 25.3 us  [send(): return lax.ppermute(total, BOTH, pairs[step])]
    ppermute x1, waiting for transfers between devices: 0.58 us -> 8.9 us  [on_device(): back_came = lax.ppermute(after(back, *pieces), BOTH, pairs[-1])]
  transfers between devices with their start and end apart: 20 -> 20, of which waited for: 13 -> 12; matrix products, arithmetic and copies ran while one was open for 40% -> 41% of each run, Pallas kernels for 2% -> 4%
where the time goes in v5:
time: 237 us; the launch traced here: 236 us
  matrix products  82.6 us (35%)
  waiting for transfers between devices  82.2 us (35%)
  starting transfers between devices  25.7 us (11%)
  between operations  14.3 us (6%)
  Pallas kernels  12.6 us (5%)
  other arithmetic  10.3 us (4%)
  local copies, waits for them, and re-layouts  8.72 us (4%)
    dot_general x11, matrix products, product(): lax.dot_general(after(block, *before), down_weight[start:stop], (((1,), (...  52.1 us
    dot_general x1, matrix products, on_device(): lax.dot_general(jnp.concatenate(gathered, axis=0), jnp.concatenate(grads,...  30.5 us
    ppermute x8, waiting for transfers between devices, send(): return lax.ppermute(total, BOTH, pairs[step])  25.3 us
    ppermute x3, waiting for transfers between devices, spread_tokens(): piece = lax.ppermute(piece, 'row', [(r, r ^ flip) for r in range(rows)])  21.4 us
    ppermute x4, waiting for transfers between devices, spread_tokens(): piece = lax.ppermute(piece, 'col', pairs)  18.5 us
    pallas_call x3, Pallas kernels, finish(): pl.pallas_call(kernel, grid=(width // block,), in_specs=specs, out_specs=...  12.6 us
    ppermute x8, starting transfers between devices, send(): return lax.ppermute(total, BOTH, pairs[step])  9.72 us
    ppermute x1, waiting for transfers between devices, on_device(): back_came = lax.ppermute(after(back, *pieces), BOTH, pairs[-1])  8.9 us
  transfers between devices with their start and end apart: 20, of which 12 were waited for; matrix products, arithmetic and copies ran while one was open for 41% of the time, Pallas kernels for 4%

profile of v5, /device:TPU:0, one launch (start us, length us, event | category | flops | bytes accessed | tf_op | source)
XLA Modules:
  0.0 236.4 jit_solution(11379080024489568306)
XLA Ops:
  7.2 4.3 %fusion.21 = bf16[384,3584]{1,0:T(8,128)(2,1)S(1)} fusion(bf16[384,3584]{1,0:T(8,128)(2,1)} %refs_4_.1, bf16[384,3584]{1,0:T(8,128)(2,1)} %refs_3_.2), kind=kLoop, calls=%fused_computation.23 | loop fusion | flops 11010048 | bytes 8257536 | tf_op jit(solution)/shard_map/convert_element_type | solution.py:135
  11.5 3.0 %collective-permute-start = (bf16[384,3584]{1,0:T(8,128)(2,1)S(1)}, bf16[384,3584]{1,0:T(8,128)(2,1)}, u32[]{:S(2)}, u32[]{:S(2)}) collective-permute-start(bf16[384,3584]{1,0:T(8,128)(2,1)S(1)} %fusion.21), channel_id=1, source_target_pairs={{0,8},{1,17},{2,10},{3,19},{4,12},{5,21},{6,14},{7,23},{8,0},{9,25... | collective-permute-start | bytes 8257544 | tf_op jit(solution)/shard_map/ppermute | solution.py:138
  14.5 1.9 dynamic-slice_bitcast_fusion
  16.4 1.9 collective-permute-done.1
  19.5 3.6 %collective-permute-start.4 = (bf16[48,2048]{1,0:T(8,128)(2,1)}, bf16[48,2048]{1,0:T(8,128)(2,1)S(1)}, u32[]{:S(2)}, u32[]{:S(2)}) collective-permute-start(bf16[48,2048]{1,0:T(8,128)(2,1)} %get-tuple-element.103), channel_id=1, source_target_pairs={{0,6},{1,7},{2,4},{3,5},{4,2},{5,3},{6,0},{7,1},{8,14},{9,15},{10,... | collective-permute-start | bytes 589832 | tf_op jit(solution)/shard_map/ppermute | solution.py:61
  23.1 0.8 collective-permute-start.2
  23.9 5.5 %collective-permute-done.4 = bf16[48,2048]{1,0:T(8,128)(2,1)S(1)} collective-permute-done((bf16[48,2048]{1,0:T(8,128)(2,1)}, bf16[48,2048]{1,0:T(8,128)(2,1)S(1)}, u32[]{:S(2)}, u32[]{:S(2)}) %collective-permute-start.4) | collective-permute-done | bytes 196640 | tf_op jit(solution)/shard_map/ppermute | solution.py:61
  29.4 11.0 %collective-permute-done.3 = bf16[48,2048]{1,0:T(8,128)(2,1)} collective-permute-done((bf16[48,2048]{1,0:T(8,128)(2,1)S(1)}, bf16[48,2048]{1,0:T(8,128)(2,1)}, u32[]{:S(2)}, u32[]{:S(2)}) %collective-permute-start.3) | collective-permute-done | bytes 196640 | tf_op jit(solution)/shard_map/ppermute | solution.py:61
  40.4 1.1 pad_maximum_fusion.3
  41.5 4.1 %collective-permute-done = bf16[384,3584]{1,0:T(8,128)(2,1)} collective-permute-done((bf16[384,3584]{1,0:T(8,128)(2,1)S(1)}, bf16[384,3584]{1,0:T(8,128)(2,1)}, u32[]{:S(2)}, u32[]{:S(2)}) %collective-permute-start) | collective-permute-done | bytes 2752544 | tf_op jit(solution)/shard_map/ppermute | solution.py:138
  45.7 3.0 %collective-permute-start.5 = (bf16[48,2048]{1,0:T(8,128)(2,1)S(1)}, bf16[48,2048]{1,0:T(8,128)(2,1)S(1)}, u32[]{:S(2)}, u32[]{:S(2)}) collective-permute-start(bf16[48,2048]{1,0:T(8,128)(2,1)S(1)} %get-tuple-element.101), channel_id=1, source_target_pairs={{0,24},{8,16},{16,8},{24,0},{1,25},{9,17},{17,9},{25,1},{2,26},{10... | collective-permute-start | bytes 589832 | tf_op jit(solution)/shard_map/ppermute | solution.py:69
  48.7 4.0 %collective-permute-done.5 = bf16[48,2048]{1,0:T(8,128)(2,1)S(1)} collective-permute-done((bf16[48,2048]{1,0:T(8,128)(2,1)S(1)}, bf16[48,2048]{1,0:T(8,128)(2,1)S(1)}, u32[]{:S(2)}, u32[]{:S(2)}) %collective-permute-start.5) | collective-permute-done | bytes 196640 | tf_op jit(solution)/shard_map/ppermute | solution.py:69
  53.7 1.7 fusion.62
  55.5 1.7 collective-permute-start.6
  57.5 1.7 collective-permute-start.7
  59.2 17.3 %collective-permute-done.8 = bf16[48,2048]{1,0:T(8,128)(2,1)S(1)} collective-permute-done((bf16[48,2048]{1,0:T(8,128)(2,1)S(1)}, bf16[48,2048]{1,0:T(8,128)(2,1)S(1)}, u32[]{:S(2)}, u32[]{:S(2)}) %collective-permute-start.8) | collective-permute-done | bytes 196640 | tf_op jit(solution)/shard_map/ppermute | solution.py:69
  76.5 0.9 pad_maximum_fusion.4
  77.4 1.6 collective-permute-start.9
  79.0 1.2 all-gather.3.cloned.1.call-done
  80.2 6.9 %fusion.39 = bf16[384,1536]{1,0:T(8,128)(2,1)} fusion(bf16[384,2048]{1,0:T(8,128)(2,1)} %all-gather.3.cloned.1.call-done, bf16[3584,2048]{1,0:T(8,128)(2,1)} %param.7), kind=kOutput, calls=%fused_computation.39 | convolution fusion | flops 2416508928 | bytes 9043968 | tf_op jit(solution)/shard_map/dot_general | solution.py:153
  87.1 8.9 %collective-permute-done.9 = bf16[192,3584]{1,0:T(8,128)(2,1)S(1)} collective-permute-done((bf16[192,3584]{1,0:T(8,128)(2,1)}, bf16[192,3584]{1,0:T(8,128)(2,1)S(1)}, u32[]{:S(2)}, u32[]{:S(2)}) %collective-permute-start.9) | collective-permute-done | bytes 1376288 | tf_op jit(solution)/shard_map/ppermute | solution.py:146
  96.0 1.5 collective-permute-start.10
  97.5 1.7 pad_maximum_fusion
  99.7 7.0 %fusion.36 = bf16[384,2048]{1,0:T(8,128)(2,1)S(1)} fusion(bf16[384,2048]{1,0:T(8,128)(2,1)S(1)} %copy-done.11, bf16[3584,2048]{1,0:T(8,128)(2,1)} %param.7), kind=kOutput, calls=%fused_computation.38 | convolution fusion | flops 3222011904 | bytes 11534336 | tf_op jit(solution)/shard_map/dot_general | solution.py:153
  106.7 1.7 pad_maximum_fusion.1
  108.5 20.9 %collective-permute-done.10 = bf16[384,3584]{1,0:T(8,128)(2,1)} collective-permute-done((bf16[384,3584]{1,0:T(8,128)(2,1)}, bf16[384,3584]{1,0:T(8,128)(2,1)}, u32[]{:S(2)}, u32[]{:S(2)}) %collective-permute-start.10) | collective-permute-done | bytes 2752544 | tf_op jit(solution)/shard_map/ppermute | solution.py:161
  129.3 1.3 collective-permute-start.11
  130.6 2.9 %all-gather.5.cloned.1.call-done = bf16[3,384,2048]{2,1,0:T(8,128)(2,1)} async-done(((bf16[3,48,2048]{2,1,0:T(8,128)(2,1)}), bf16[3,384,2048]{2,1,0:T(8,128)(2,1)}) %all-gather.5.cloned.1.call-update) | async-done | bytes 4718608 | tf_op jit(solution)/shard_map/all_gather | solution.py:77
  133.6 3.0 %slice_bitcast_fusion = (bf16[384,2048]{1,0:T(8,128)(2,1)S(1)}, bf16[384,2048]{1,0:T(8,128)(2,1)S(1)}, bf16[384,2048]{1,0:T(8,128)(2,1)S(1)}) fusion(bf16[3,384,2048]{2,1,0:T(8,128)(2,1)} %all-gather.5.cloned.1.call-done), kind=kLoop, calls=%fused_computation.52 | loop fusion | bytes 9437184 | tf_op jit(solution)/shard_map/squeeze | solution.py:78
  136.9 8.9 %fusion.42 = bf16[384,1536]{1,0:T(8,128)(2,1)} fusion(bf16[384,2048]{1,0:T(8,128)(2,1)S(1)} %get-tuple-element.71, bf16[3584,2048]{1,0:T(8,128)(2,1)} %param.7), kind=kOutput, calls=%fused_computation.40 | convolution fusion | flops 2416508928 | bytes 9043968 | tf_op jit(solution)/shard_map/dot_general | solution.py:153
  145.7 3.7 %fusion.45 = bf16[384,1536]{1,0:T(8,128)(2,1)} fusion(bf16[384,2048]{1,0:T(8,128)(2,1)S(1)} %get-tuple-element.71, bf16[3584,2048]{1,0:T(8,128)(2,1)S(1)} %bitcast.50), kind=kOutput, calls=%fused_computation.41 | convolution fusion | flops 2416508928 | bytes 9043968 | tf_op jit(solution)/shard_map/dot_general | solution.py:153
  149.4 1.5 collective-permute-start.14
  151.5 2.0 fusion.54
  153.4 1.5 collective-permute-start.15
  155.0 2.7 %fusion.30.own_ref = f32[384,1536]{1,0:T(8,128)S(1)} fusion(bf16[384,2048]{1,0:T(8,128)(2,1)S(1)} %get-tuple-element.76, bf16[3584,2048]{1,0:T(8,128)(2,1)S(1)} %bitcast.50), kind=kOutput, calls=%fused_computation.32 | convolution fusion | flops 2415919104 | bytes 10223616 | tf_op jit(solution)/shard_map/dot_general | solution.py:153
  157.7 4.1 %fusion.24.refs_0_ = f32[384,1536]{1,0:T(8,128)} fusion(bf16[384,2048]{1,0:T(8,128)(2,1)S(1)} %get-tuple-element.76, bf16[3584,2048]{1,0:T(8,128)(2,1)S(1)} %bitcast.50), kind=kOutput, calls=%fused_computation.26 | convolution fusion | flops 2415919104 | bytes 10223616 | tf_op jit(solution)/shard_map/dot_general | solution.py:153
  161.8 0.9 collective-permute-done.11
  162.7 4.8 %add_convert_fusion.1 = bf16[384,1536]{1,0:T(8,128)(2,1)} fusion(bf16[384,3584]{1,0:T(8,128)(2,1)} %collective-permute-done.11, bf16[384,2048]{1,0:T(8,128)(2,1)S(1)} %get-tuple-element.75, bf16[3584,2048]{1,0:T(8,128)(2,1)S(1)} %bitcast.50), kind=kOutput, calls=%fused_computation.45 | convolution fusion | flops 2417688576 | bytes 10223616 | tf_op jit(solution)/shard_map/dot_general | solution.py:153
  167.5 1.5 collective-permute-start.12
  169.0 30.5 %fusion = f32[3584,2048]{1,0:T(8,128)} fusion(bf16[384,3584]{1,0:T(8,128)(2,1)} %collective-permute-done.10, bf16[384,3584]{1,0:T(8,128)(2,1)} %pad_maximum_fusion, bf16[384,3584]{1,0:T(8,128)(2,1)} %collective-permute-done, bf16[384,3584]{1,0:T(8,128)(2,1)} %copy-done.3, bf16[384,2048]{1,0:T(8,128)(2,1)} %all-gather.3.cloned.1.call-done, ...), kind=kOutput, calls=%fused_computation | convolution fusion | flops 22617784320 | bytes 46661632 | tf_op jit(solution)/shard_map/dot_general | solution.py:209
  199.6 6.3 %add_convert_fusion = bf16[384,1536]{1,0:T(8,128)(2,1)S(1)} fusion(bf16[384,3584]{1,0:T(8,128)(2,1)} %collective-permute-done.11, bf16[384,2048]{1,0:T(8,128)(2,1)} %copy-done.6, bf16[3584,2048]{1,0:T(8,128)(2,1)} %param.7), kind=kOutput, calls=%fused_computation.44 | convolution fusion | flops 2417688576 | bytes 10223616 | tf_op jit(solution)/shard_map/dot_general | solution.py:153
  206.5 2.9 %add_convert_fusion.2 = bf16[384,512]{1,0:T(8,128)(2,1)S(1)} fusion(bf16[384,3584]{1,0:T(8,128)(2,1)} %collective-permute-done.11, bf16[384,2048]{1,0:T(8,128)(2,1)S(1)} %copy-done.7, bf16[3584,2048]{1,0:T(8,128)(2,1)} %param.7), kind=kOutput, calls=%fused_computation.64 | convolution fusion | flops 805896192 | bytes 4456448 | tf_op jit(solution)/shard_map/dot_general | solution.py:153
  209.4 1.3 collective-permute-start.17
  210.7 5.2 %shard_map.67 = (bf16[384,3584]{1,0:T(8,128)(2,1)}, bf16[384,3584]{1,0:T(8,128)(2,1)}) custom-call(f32[384,1536]{1,0:T(8,128)S(1)} %fusion.30.own_ref, bf16[384,1536]{1,0:T(8,128)(2,1)S(1)} %collective-permute-done.13.refs_0_, bf16[384,1536]{1,0:T(8,128)(2,1)} %collective-permute-done.12.refs_1_, bf16[384,3584]{1,0:T(8,128)(2,1)S(1)} %copy-done, ...), custom_call_target="tpu_custom_call" | custom-call | tf_op jit(solution)/shard_map/pallas_call | solution.py:113
  215.9 2.7 %fusion.48.refs_0_ = f32[384,512]{1,0:T(8,128)S(1)} fusion(bf16[384,2048]{1,0:T(8,128)(2,1)S(1)} %copy-done.5, bf16[3584,2048]{1,0:T(8,128)(2,1)} %param.7), kind=kOutput, calls=%fused_computation.46 | convolution fusion | flops 805306368 | bytes 4456448 | tf_op jit(solution)/shard_map/dot_general | solution.py:153
  218.7 3.5 %collective-permute-done.16.refs_2_ = bf16[384,1536]{1,0:T(8,128)(2,1)S(1)} collective-permute-done((bf16[384,1536]{1,0:T(8,128)(2,1)S(1)}, bf16[384,1536]{1,0:T(8,128)(2,1)S(1)}, u32[]{:S(2)}, u32[]{:S(2)}) %collective-permute-start.16) | collective-permute-done | bytes 1179680 | tf_op jit(solution)/shard_map/ppermute | solution.py:161
  222.2 5.2 %shard_map.68 = (bf16[384,3584]{1,0:T(8,128)(2,1)}, bf16[384,3584]{1,0:T(8,128)(2,1)}) custom-call(f32[384,1536]{1,0:T(8,128)S(1)} %copy-done.2, bf16[384,1536]{1,0:T(8,128)(2,1)} %collective-permute-done.14.refs_1_, bf16[384,1536]{1,0:T(8,128)(2,1)S(1)} %collective-permute-done.16.refs_2_, ...), custom_call_target="tpu_custom_call", output_to_operand_aliasing={{0}: (5, {}), {1}: (6, {})} | custom-call | tf_op jit(solution)/shard_map/pallas_call | solution.py:113
  227.4 2.2 shard_map.69
  (55 shorter events, 4.3 us)
Async XLA Ops:
  7.2 73.0 %all-gather.3.cloned.1.call-start = ((), (), s32[]{:S(2)}) async-start(), calls=%async_computation | async-start | bytes 1769472 | tf_op jit(solution)/shard_map/all_gather | solution.py:75
  11.5 42.2 %copy-start.3 = (bf16[384,3584]{1,0:T(8,128)(2,1)}, bf16[384,3584]{1,0:T(8,128)(2,1)S(1)}, u32[]{:S(2)}) copy-start(bf16[384,3584]{1,0:T(8,128)(2,1)S(1)} %fusion.21) | copy-start | bytes 8257540
  11.5 34.1 %collective-permute-start = (bf16[384,3584]{1,0:T(8,128)(2,1)S(1)}, bf16[384,3584]{1,0:T(8,128)(2,1)}, u32[]{:S(2)}, u32[]{:S(2)}) collective-permute-start(bf16[384,3584]{1,0:T(8,128)(2,1)S(1)} %fusion.21), channel_id=1, source_target_pairs={{0,8},{1,17},{2,10},{3,19},{4,12},{5,21},{6,14},{7,23},{8,0},{9,25... | collective-permute-start | bytes 8257544 | tf_op jit(solution)/shard_map/ppermute | solution.py:138
  16.4 1.9 collective-permute-start.1
  19.5 9.9 %collective-permute-start.4 = (bf16[48,2048]{1,0:T(8,128)(2,1)}, bf16[48,2048]{1,0:T(8,128)(2,1)S(1)}, u32[]{:S(2)}, u32[]{:S(2)}) collective-permute-start(bf16[48,2048]{1,0:T(8,128)(2,1)} %get-tuple-element.103), channel_id=1, source_target_pairs={{0,6},{1,7},{2,4},{3,5},{4,2},{5,3},{6,0},{7,1},{8,14},{9,15},{10,... | collective-permute-start | bytes 589832 | tf_op jit(solution)/shard_map/ppermute | solution.py:61
  23.1 17.3 %collective-permute-start.3 = (bf16[48,2048]{1,0:T(8,128)(2,1)S(1)}, bf16[48,2048]{1,0:T(8,128)(2,1)}, u32[]{:S(2)}, u32[]{:S(2)}) collective-permute-start(bf16[48,2048]{1,0:T(8,128)(2,1)S(1)} %get-tuple-element.104), channel_id=1, source_target_pairs={{0,4},{1,5},{2,6},{3,7},{4,0},{5,1},{6,2},{7,3},{8,12},{9,13},{10,... | collective-permute-start | bytes 589832 | tf_op jit(solution)/shard_map/ppermute | solution.py:61
  23.1 17.3 %collective-permute-start.2 = (bf16[48,2048]{1,0:T(8,128)(2,1)S(1)}, bf16[48,2048]{1,0:T(8,128)(2,1)}, u32[]{:S(2)}, u32[]{:S(2)}) collective-permute-start(bf16[48,2048]{1,0:T(8,128)(2,1)S(1)} %get-tuple-element.105), channel_id=1, source_target_pairs={{0,2},{1,3},{2,0},{3,1},{4,6},{5,7},{6,4},{7,5},{8,10},{9,11},{10,... | collective-permute-start | bytes 589832 | tf_op jit(solution)/shard_map/ppermute | solution.py:61
  45.7 7.1 %collective-permute-start.5 = (bf16[48,2048]{1,0:T(8,128)(2,1)S(1)}, bf16[48,2048]{1,0:T(8,128)(2,1)S(1)}, u32[]{:S(2)}, u32[]{:S(2)}) collective-permute-start(bf16[48,2048]{1,0:T(8,128)(2,1)S(1)} %get-tuple-element.101), channel_id=1, source_target_pairs={{0,24},{8,16},{16,8},{24,0},{1,25},{9,17},{17,9},{25,1},{2,26},{10... | collective-permute-start | bytes 589832 | tf_op jit(solution)/shard_map/ppermute | solution.py:69
  52.8 0.7 copy-start.10
  53.5 80.1 %all-gather.5.cloned.1.call-start = ((), (), s32[]{:S(2)}) async-start(), calls=%async_computation.1 | async-start | bytes 5308416 | tf_op jit(solution)/shard_map/all_gather | solution.py:77
  55.5 21.9 %collective-permute-start.6 = (bf16[192,3584]{1,0:T(8,128)(2,1)}, bf16[192,3584]{1,0:T(8,128)(2,1)S(1)}, u32[]{:S(2)}, u32[]{:S(2)}) collective-permute-start(bf16[192,3584]{1,0:T(8,128)(2,1)} %get-tuple-element.49), channel_id=1, source_target_pairs={{0,16},{1,9},{2,18},{3,11},{4,20},{5,13},{6,22},{7,15},{8,24},{9,1... | collective-permute-start | bytes 4128776 | tf_op jit(solution)/shard_map/ppermute | solution.py:145
  57.2 19.3 %collective-permute-start.8 = (bf16[48,2048]{1,0:T(8,128)(2,1)S(1)}, bf16[48,2048]{1,0:T(8,128)(2,1)S(1)}, u32[]{:S(2)}, u32[]{:S(2)}) collective-permute-start(bf16[48,2048]{1,0:T(8,128)(2,1)S(1)} %get-tuple-element.99), channel_id=1, source_target_pairs={{0,16},{8,24},{16,0},{24,8},{1,17},{9,25},{17,1},{25,9},{2,18},{10... | collective-permute-start | bytes 589832 | tf_op jit(solution)/shard_map/ppermute | solution.py:69
  57.5 19.0 %collective-permute-start.7 = (bf16[48,2048]{1,0:T(8,128)(2,1)S(1)}, bf16[48,2048]{1,0:T(8,128)(2,1)S(1)}, u32[]{:S(2)}, u32[]{:S(2)}) collective-permute-start(bf16[48,2048]{1,0:T(8,128)(2,1)S(1)} %get-tuple-element.100), channel_id=1, source_target_pairs={{0,8},{8,0},{16,24},{24,16},{1,9},{9,1},{17,25},{25,17},{2,10},{10... | collective-permute-start | bytes 589832 | tf_op jit(solution)/shard_map/ppermute | solution.py:69
  77.4 18.6 %collective-permute-start.9 = (bf16[192,3584]{1,0:T(8,128)(2,1)}, bf16[192,3584]{1,0:T(8,128)(2,1)S(1)}, u32[]{:S(2)}, u32[]{:S(2)}) collective-permute-start(bf16[192,3584]{1,0:T(8,128)(2,1)} %get-tuple-element.50), channel_id=1, source_target_pairs={{0,16},{1,9},{2,18},{3,11},{4,20},{5,13},{6,22},{7,15},{8,24},{9,1... | collective-permute-start | bytes 4128776 | tf_op jit(solution)/shard_map/ppermute | solution.py:146
  96.0 33.4 %collective-permute-start.10 = (bf16[384,3584]{1,0:T(8,128)(2,1)}, bf16[384,3584]{1,0:T(8,128)(2,1)}, u32[]{:S(2)}, u32[]{:S(2)}) collective-permute-start(bf16[384,3584]{1,0:T(8,128)(2,1)} %collective-permute-done), channel_id=1, source_target_pairs={{0,16},{1,9},{2,18},{3,11},{4,20},{5,13},{6,22},{7,15},{8,24},{9,1... | collective-permute-start | bytes 8257544 | tf_op jit(solution)/shard_map/ppermute | solution.py:161
  97.5 2.2 copy-start.11
  99.7 7.0 %copy-start.9 = (bf16[384,1536]{1,0:T(8,128)(2,1)S(1)}, bf16[384,1536]{1,0:T(8,128)(2,1)}, u32[]{:S(2)}) copy-start(bf16[384,1536]{1,0:T(8,128)(2,1)} %fusion.39) | copy-start | bytes 3538948
  129.3 33.4 %collective-permute-start.11 = (bf16[384,3584]{1,0:T(8,128)(2,1)}, bf16[384,3584]{1,0:T(8,128)(2,1)}, u32[]{:S(2)}, u32[]{:S(2)}) collective-permute-start(bf16[384,3584]{1,0:T(8,128)(2,1)} %pad_maximum_fusion.1), channel_id=1, source_target_pairs={{0,8},{1,17},{2,10},{3,19},{4,12},{5,21},{6,14},{7,23},{8,0},{9,25... | collective-permute-start | bytes 8257544 | tf_op jit(solution)/shard_map/ppermute | solution.py:161
  133.6 12.1 %slice-start = ((s8[14680064]{0:T(1024)(128)(4,1)}), s8[4194304]{0:T(1024)(128)(4,1)S(1)}, s32[]{:S(2)}) async-start(s8[14680064]{0:T(1024)(128)(4,1)} %bitcast.49), calls=%async_computation.2 | async-start | bytes 8388608
  133.6 12.1 %slice-start.1 = ((s8[14680064]{0:T(1024)(128)(4,1)}), s8[4194304]{0:T(1024)(128)(4,1)S(1)}, s32[]{:S(2)}) async-start(s8[14680064]{0:T(1024)(128)(4,1)} %bitcast.49), calls=%async_computation.3 | async-start | bytes 8388608
  136.6 21.1 %copy-start.4 = (bf16[384,2048]{1,0:T(8,128)(2,1)}, bf16[384,2048]{1,0:T(8,128)(2,1)S(1)}, u32[]{:S(2)}) copy-start(bf16[384,2048]{1,0:T(8,128)(2,1)S(1)} %get-tuple-element.76) | copy-start | bytes 4718596
  136.8 14.6 %copy-start.8 = (bf16[384,2048]{1,0:T(8,128)(2,1)}, bf16[384,2048]{1,0:T(8,128)(2,1)S(1)}, u32[]{:S(2)}) copy-start(bf16[384,2048]{1,0:T(8,128)(2,1)S(1)} %get-tuple-element.71) | copy-start | bytes 4718596
  136.8 25.9 %copy-start.6 = (bf16[384,2048]{1,0:T(8,128)(2,1)}, bf16[384,2048]{1,0:T(8,128)(2,1)S(1)}, u32[]{:S(2)}) copy-start(bf16[384,2048]{1,0:T(8,128)(2,1)S(1)} %get-tuple-element.75) | copy-start | bytes 4718596
  136.8 8.9 %slice-start.2 = ((s8[14680064]{0:T(1024)(128)(4,1)}), s8[4194304]{0:T(1024)(128)(4,1)S(1)}, s32[]{:S(2)}) async-start(s8[14680064]{0:T(1024)(128)(4,1)} %bitcast.49), calls=%async_computation.4 | async-start | bytes 8388608
  136.9 8.9 %slice-start.3 = ((s8[14680064]{0:T(1024)(128)(4,1)}), s8[2097152]{0:T(1024)(128)(4,1)S(1)}, s32[]{:S(2)}) async-start(s8[14680064]{0:T(1024)(128)(4,1)} %bitcast.49), calls=%async_computation.5 | async-start | bytes 4194304
  149.4 56.4 %collective-permute-start.14 = (bf16[384,1536]{1,0:T(8,128)(2,1)}, bf16[384,1536]{1,0:T(8,128)(2,1)}, u32[]{:S(2)}, u32[]{:S(2)}) collective-permute-start(bf16[384,1536]{1,0:T(8,128)(2,1)} %fusion.45), channel_id=1, source_target_pairs={{0,8},{1,17},{2,10},{3,19},{4,12},{5,21},{6,14},{7,23},{8,0},{9,25... | collective-permute-start | bytes 3538952 | tf_op jit(solution)/shard_map/ppermute | solution.py:161
  150.9 54.9 %collective-permute-start.13 = (bf16[384,1536]{1,0:T(8,128)(2,1)}, bf16[384,1536]{1,0:T(8,128)(2,1)S(1)}, u32[]{:S(2)}, u32[]{:S(2)}) collective-permute-start(bf16[384,1536]{1,0:T(8,128)(2,1)} %fusion.42), channel_id=1, source_target_pairs={{0,8},{1,17},{2,10},{3,19},{4,12},{5,21},{6,14},{7,23},{8,0},{9,25... | collective-permute-start | bytes 3538952 | tf_op jit(solution)/shard_map/ppermute | solution.py:161
  153.4 52.4 %collective-permute-start.15 = (bf16[384,512]{1,0:T(8,128)(2,1)}, bf16[384,512]{1,0:T(8,128)(2,1)}, u32[]{:S(2)}, u32[]{:S(2)}) collective-permute-start(bf16[384,512]{1,0:T(8,128)(2,1)} %fusion.54), channel_id=1, source_target_pairs={{0,8},{1,17},{2,10},{3,19},{4,12},{5,21},{6,14},{7,23},{8,0},{9,25... | collective-permute-start | bytes 1179656 | tf_op jit(solution)/shard_map/ppermute | solution.py:161
  167.5 38.4 %collective-permute-start.12 = (bf16[384,1536]{1,0:T(8,128)(2,1)}, bf16[384,1536]{1,0:T(8,128)(2,1)}, u32[]{:S(2)}, u32[]{:S(2)}) collective-permute-start(bf16[384,1536]{1,0:T(8,128)(2,1)} %add_convert_fusion.1), channel_id=1, source_target_pairs={{0,16},{1,9},{2,18},{3,11},{4,20},{5,13},{6,22},{7,15},{8,24},{9,1... | collective-permute-start | bytes 3538952 | tf_op jit(solution)/shard_map/ppermute | solution.py:161
  199.6 6.9 %copy-start.7 = (bf16[384,2048]{1,0:T(8,128)(2,1)S(1)}, bf16[384,2048]{1,0:T(8,128)(2,1)}, u32[]{:S(2)}) copy-start(bf16[384,2048]{1,0:T(8,128)(2,1)} %copy-done.6) | copy-start | bytes 4718596
  205.8 4.9 %copy-start = (bf16[384,3584]{1,0:T(8,128)(2,1)S(1)}, bf16[384,3584]{1,0:T(8,128)(2,1)}, u32[]{:S(2)}) copy-start(bf16[384,3584]{1,0:T(8,128)(2,1)} %refs_3_.2) | copy-start | bytes 8257540
  205.9 4.9 %copy-start.1 = (bf16[384,3584]{1,0:T(8,128)(2,1)S(1)}, bf16[384,3584]{1,0:T(8,128)(2,1)}, u32[]{:S(2)}) copy-start(bf16[384,3584]{1,0:T(8,128)(2,1)} %refs_4_.1) | copy-start | bytes 8257540
  205.9 16.3 %collective-permute-start.16 = (bf16[384,1536]{1,0:T(8,128)(2,1)S(1)}, bf16[384,1536]{1,0:T(8,128)(2,1)S(1)}, u32[]{:S(2)}, u32[]{:S(2)}) collective-permute-start(bf16[384,1536]{1,0:T(8,128)(2,1)S(1)} %add_convert_fusion), channel_id=1, source_target_pairs={{0,16},{1,9},{2,18},{3,11},{4,20},{5,13},{6,22},{7,15},{8,24},{9,1... | collective-permute-start | bytes 3538952 | tf_op jit(solution)/shard_map/ppermute | solution.py:161
  209.4 6.5 %copy-start.5 = (bf16[384,2048]{1,0:T(8,128)(2,1)S(1)}, bf16[384,2048]{1,0:T(8,128)(2,1)}, u32[]{:S(2)}) copy-start(bf16[384,2048]{1,0:T(8,128)(2,1)} %copy-done.4) | copy-start | bytes 4718596
  209.4 17.9 %collective-permute-start.17 = (bf16[384,512]{1,0:T(8,128)(2,1)S(1)}, bf16[384,512]{1,0:T(8,128)(2,1)S(1)}, u32[]{:S(2)}, u32[]{:S(2)}) collective-permute-start(bf16[384,512]{1,0:T(8,128)(2,1)S(1)} %add_convert_fusion.2), channel_id=1, source_target_pairs={{0,16},{1,9},{2,18},{3,11},{4,20},{5,13},{6,22},{7,15},{8,24},{9,1... | collective-permute-start | bytes 1179656 | tf_op jit(solution)/shard_map/ppermute | solution.py:161
  215.9 6.2 %copy-start.2 = (f32[384,1536]{1,0:T(8,128)S(1)}, f32[384,1536]{1,0:T(8,128)}, u32[]{:S(2)}) copy-start(f32[384,1536]{1,0:T(8,128)} %fusion.24.refs_0_) | copy-start | bytes 7077892
Sparse Core Ops, SparseCore 0:
  53.6 26.4 all-gather.2
  82.3 51.1 all-gather.4

commit v6 on v4

--- a/solution.py
+++ b/solution.py
@@ -60,15 +60,17 @@
             pairs = [(c, (c // share ^ flip) * share + c % share) for c in range(cols)]
             piece = lax.ppermute(piece, "col", pairs)
         held.append(piece)
-    held, _ = lax.optimization_barrier((jnp.stack(held), hidden_came))
+    held = jnp.stack(held)
 
     blocks = [None] * rows
     for flip in reversed(range(rows)):
         piece = lax.dynamic_index_in_dim(held, row ^ flip ^ plane, 0, keepdims=False)
         if flip < rows - 1:
-            piece, _ = lax.optimization_barrier((piece, blocks[-1]))
+            piece = lax.optimization_barrier((piece, blocks[-1]))[0]
         if flip:
             piece = lax.ppermute(piece, "row", [(r, r ^ flip) for r in range(rows)])
+        if flip == rows - 1:
+            piece = lax.optimization_barrier((piece, hidden_came))[0]
         blocks[flip] = piece
     return blocks
 
@@ -142,10 +144,7 @@
     for step in range(1, steps - 1):
         gathered = gathered + [lax.ppermute(part, BOTH, pairs[step]) for part in gathered]
 
-    front, back = jnp.split(hidden, 2)
-    front_came = lax.ppermute(after(front, pieces[-1]), BOTH, pairs[-1])
-    back_came = lax.ppermute(after(back, *pieces), BOTH, pairs[-1])
-    gathered.append(jnp.concatenate([front_came, back_came]))
+    gathered.append(lax.ppermute(after(hidden, *pieces), BOTH, pairs[-1]))
 
     blocks = gather_tokens(pieces)
     width = down_weight.shape[0]
@@ -162,11 +161,11 @@
         return lax.ppermute(total, BOTH, pairs[step])
 
     unit = width // 7
-    total = product(blocks[-1], 0, 3 * unit, front_came).astype(jnp.bfloat16)
-    rest = product(blocks[-1], 3 * unit, width, total).astype(jnp.bfloat16)
+    total = product(blocks[-1], 0, 3 * unit).astype(jnp.bfloat16)
+    for part in gathered[1 : rows // 2]:
+        gathered.append(send(after(part, total), steps - 1))
+    rest = product(blocks[-1], 3 * unit, width, total, gathered[rows // 2]).astype(jnp.bfloat16)
     total = jnp.concatenate([total, rest], axis=1)
-    for part in gathered[1 : rows // 2]:
-        gathered.append(send(after(part, rest, back_came), steps - 1))
     total = after(total, *gathered[rows // 2 + 1 :])
 
     blocks[:-1] = lax.optimization_barrier((*blocks[:-1], total))[:-1]
@@ -213,9 +212,10 @@
         (((0,), (0,)), ((), ())),
         preferred_element_type=jnp.float32,
     )
-    total = after(message(rows // 2, 1, grad_weight), last[0], *sum(came[0], []))
+
+    total = after(message(rows // 2, 1, grad_weight), *sum(came[0], []))
     last.append(send(total, steps - 1))
-    total = message(rows // 2, 2, total)
+    total = after(message(rows // 2, 2, total), last[0])
     last.append(send(total, steps - 1))
     own.append(own_product(2, total))
 
@@ -224,7 +224,7 @@
     for chunk, start in enumerate(starts):
         outs = finish(
             own[chunk],
-            [after(block, grad_weight) for block in (*came[0][chunk], last[chunk])],
+            [after(block, grad_weight, *outs) for block in (*came[0][chunk], last[chunk])],
             gate_act,
             up_act,
             outs,

time: 243 us -> 233 us (0.959)
  starting transfers between devices: 24.8 us -> 20.6 us
  other arithmetic: 11.7 us -> 8.57 us
    all_gather x1, waiting for transfers between devices: 0.01 us -> 16.6 us  [gather_tokens(): first = lax.all_gather(blocks[-1], 'col', axis=0, tiled=True)]
    ppermute x8, waiting for transfers between devices: 36.7 us -> 26 us  [send(): return lax.ppermute(total, BOTH, pairs[step])]
    ppermute x2 -> x1, waiting for transfers between devices: 16.9 us -> 7.7 us  [on_device(): gathered.append(lax.ppermute(after(hidden, *pieces), BOTH, pairs[-1]))]
    ppermute x3, waiting for transfers between devices: 8.2 us -> 12.9 us  [spread_tokens(): piece = lax.ppermute(piece, 'row', [(r, r ^ flip) for r in range(rows)])]
    ppermute x1, waiting for transfers between devices: 4.11 us -> 0.01 us  [on_device(): hidden_came = lax.ppermute(hidden, BOTH, pairs[0])]
    concatenate x1 -> x0, other arithmetic: 3.16 us -> none  [on_device(): gathered.append(jnp.concatenate([front_came, back_came]))]
    all_gather x1, waiting for transfers between devices: 2.77 us -> 5.61 us  [gather_tokens(): rest = lax.all_gather(jnp.stack(blocks[:-1]), 'col', axis=1, tiled=True)]
  transfers between devices with their start and end apart: 20 -> 19, of which waited for: 13 -> 11; matrix products, arithmetic and copies ran while one was open for 40% -> 40% of each run, Pallas kernels for 2% -> 4%
where the time goes in v6:
time: 233 us
  waiting for transfers between devices  87.2 us (37%)
  matrix products  83 us (36%)
  starting transfers between devices  20.6 us (9%)
  between operations  14.3 us (6%)
  Pallas kernels  12.6 us (5%)
  other arithmetic  8.57 us (4%)
  local copies, waits for them, and re-layouts  6.51 us (3%)
    dot_general x11, matrix products, product(): lax.dot_general(after(block, *before), down_weight[start:stop], (((1,), (...  52.5 us
    dot_general x1, matrix products, on_device(): lax.dot_general(jnp.concatenate(gathered, axis=0), jnp.concatenate(grads,...  30.5 us
    ppermute x8, waiting for transfers between devices, send(): return lax.ppermute(total, BOTH, pairs[step])  26 us
    ppermute x4, waiting for transfers between devices, spread_tokens(): piece = lax.ppermute(piece, 'col', pairs)  18.5 us
    all_gather x1, waiting for transfers between devices, gather_tokens(): first = lax.all_gather(blocks[-1], 'col', axis=0, tiled=True)  16.6 us
    ppermute x3, waiting for transfers between devices, spread_tokens(): piece = lax.ppermute(piece, 'row', [(r, r ^ flip) for r in range(rows)])  12.9 us
    pallas_call x3, Pallas kernels, finish(): pl.pallas_call(kernel, grid=(width // block,), in_specs=specs, out_specs=...  12.6 us
    ppermute x8, starting transfers between devices, send(): return lax.ppermute(total, BOTH, pairs[step])  8.36 us
  transfers between devices with their start and end apart: 19, of which 11 were waited for; matrix products, arithmetic and copies ran while one was open for 40% of the time, Pallas kernels for 4%

profile of v6, /device:TPU:0, one launch (start us, length us, event | category | flops | bytes accessed | tf_op | source)
XLA Modules:
  0.0 232.7 jit_solution(13191230509896237442)
XLA Ops:
  7.2 4.3 %fusion.21 = bf16[384,3584]{1,0:T(8,128)(2,1)S(1)} fusion(bf16[384,3584]{1,0:T(8,128)(2,1)} %refs_4_.1, bf16[384,3584]{1,0:T(8,128)(2,1)} %refs_3_.2), kind=kLoop, calls=%fused_computation.23 | loop fusion | flops 11010048 | bytes 8257536 | tf_op jit(solution)/shard_map/convert_element_type | solution.py:138
  11.5 3.0 %collective-permute-start = (bf16[384,3584]{1,0:T(8,128)(2,1)S(1)}, bf16[384,3584]{1,0:T(8,128)(2,1)}, u32[]{:S(2)}, u32[]{:S(2)}) collective-permute-start(bf16[384,3584]{1,0:T(8,128)(2,1)S(1)} %fusion.21), channel_id=1, source_target_pairs={{0,8},{1,17},{2,10},{3,19},{4,12},{5,21},{6,14},{7,23},{8,0},{9,25... | collective-permute-start | bytes 8257544 | tf_op jit(solution)/shard_map/ppermute | solution.py:141
  14.5 1.9 dynamic-slice_bitcast_fusion
  16.4 1.9 collective-permute-done.1
  18.7 0.8 constant_dynamic-slice_fusion
  19.5 3.6 %collective-permute-start.4 = (bf16[48,2048]{1,0:T(8,128)(2,1)}, bf16[48,2048]{1,0:T(8,128)(2,1)S(1)}, u32[]{:S(2)}, u32[]{:S(2)}) collective-permute-start(bf16[48,2048]{1,0:T(8,128)(2,1)} %get-tuple-element.103), channel_id=1, source_target_pairs={{0,6},{1,7},{2,4},{3,5},{4,2},{5,3},{6,0},{7,1},{8,14},{9,15},{10,... | collective-permute-start | bytes 589832 | tf_op jit(solution)/shard_map/ppermute | solution.py:61
  23.1 0.8 collective-permute-start.2
  23.9 5.5 %collective-permute-done.4 = bf16[48,2048]{1,0:T(8,128)(2,1)S(1)} collective-permute-done((bf16[48,2048]{1,0:T(8,128)(2,1)}, bf16[48,2048]{1,0:T(8,128)(2,1)S(1)}, u32[]{:S(2)}, u32[]{:S(2)}) %collective-permute-start.4) | collective-permute-done | bytes 196640 | tf_op jit(solution)/shard_map/ppermute | solution.py:61
  29.4 11.0 %collective-permute-done.3 = bf16[48,2048]{1,0:T(8,128)(2,1)} collective-permute-done((bf16[48,2048]{1,0:T(8,128)(2,1)S(1)}, bf16[48,2048]{1,0:T(8,128)(2,1)}, u32[]{:S(2)}, u32[]{:S(2)}) %collective-permute-start.3) | collective-permute-done | bytes 196640 | tf_op jit(solution)/shard_map/ppermute | solution.py:61
  40.4 1.1 pad_maximum_fusion.2
  41.6 1.9 collective-permute-start.5
  43.5 7.7 %collective-permute-done.5 = bf16[48,2048]{1,0:T(8,128)(2,1)S(1)} collective-permute-done((bf16[48,2048]{1,0:T(8,128)(2,1)S(1)}, bf16[48,2048]{1,0:T(8,128)(2,1)S(1)}, u32[]{:S(2)}, u32[]{:S(2)}) %collective-permute-start.5) | collective-permute-done | bytes 196640 | tf_op jit(solution)/shard_map/ppermute | solution.py:71
  51.2 0.7 copy-done.10
  52.2 1.6 collective-permute-start.6
  53.7 0.5 collective-permute-start.7
  54.2 3.7 %collective-permute-done.6 = bf16[48,2048]{1,0:T(8,128)(2,1)S(1)} collective-permute-done((bf16[48,2048]{1,0:T(8,128)(2,1)S(1)}, bf16[48,2048]{1,0:T(8,128)(2,1)S(1)}, u32[]{:S(2)}, u32[]{:S(2)}) %collective-permute-start.6) | collective-permute-done | bytes 196640 | tf_op jit(solution)/shard_map/ppermute | solution.py:71
  57.9 1.5 collective-permute-done.7
  59.4 0.9 pad_maximum_fusion.3
  60.3 0.6 collective-permute-start.8
  60.9 16.6 %all-gather.3.cloned.1.call-done = bf16[384,2048]{1,0:T(8,128)(2,1)} async-done(((bf16[48,2048]{1,0:T(8,128)(2,1)}), bf16[384,2048]{1,0:T(8,128)(2,1)}) %all-gather.3.cloned.1.call-update) | async-done | bytes 1572880 | tf_op jit(solution)/shard_map/all_gather | solution.py:79
  77.4 6.9 %fusion.39 = bf16[384,1536]{1,0:T(8,128)(2,1)} fusion(bf16[384,2048]{1,0:T(8,128)(2,1)} %all-gather.3.cloned.1.call-done, bf16[3584,2048]{1,0:T(8,128)(2,1)} %param.7), kind=kOutput, calls=%fused_computation.39 | convolution fusion | flops 2416508928 | bytes 9043968 | tf_op jit(solution)/shard_map/dot_general | solution.py:153
  84.4 1.5 collective-permute-start.9
  85.8 7.7 %collective-permute-done.8 = bf16[384,3584]{1,0:T(8,128)(2,1)} collective-permute-done((bf16[384,3584]{1,0:T(8,128)(2,1)S(1)}, bf16[384,3584]{1,0:T(8,128)(2,1)}, u32[]{:S(2)}, u32[]{:S(2)}) %collective-permute-start.8) | collective-permute-done | bytes 2752544 | tf_op jit(solution)/shard_map/ppermute | solution.py:147
  93.5 7.4 %fusion.36 = bf16[384,2048]{1,0:T(8,128)(2,1)S(1)} fusion(bf16[384,2048]{1,0:T(8,128)(2,1)} %all-gather.3.cloned.1.call-done, bf16[3584,2048]{1,0:T(8,128)(2,1)} %param.7), kind=kOutput, calls=%fused_computation.38 | convolution fusion | flops 3222011904 | bytes 11534336 | tf_op jit(solution)/shard_map/dot_general | solution.py:153
  101.0 1.7 pad_maximum_fusion
  102.7 22.5 %collective-permute-done.9 = bf16[384,3584]{1,0:T(8,128)(2,1)} collective-permute-done((bf16[384,3584]{1,0:T(8,128)(2,1)}, bf16[384,3584]{1,0:T(8,128)(2,1)}, u32[]{:S(2)}, u32[]{:S(2)}) %collective-permute-start.9) | collective-permute-done | bytes 2752544 | tf_op jit(solution)/shard_map/ppermute | solution.py:161
  125.2 5.6 %all-gather.5.cloned.1.call-done = bf16[3,384,2048]{2,1,0:T(8,128)(2,1)} async-done(((bf16[3,48,2048]{2,1,0:T(8,128)(2,1)}), bf16[3,384,2048]{2,1,0:T(8,128)(2,1)}) %all-gather.5.cloned.1.call-update) | async-done | bytes 4718608 | tf_op jit(solution)/shard_map/all_gather | solution.py:80
  130.9 3.0 %slice_bitcast_fusion = (bf16[384,2048]{1,0:T(8,128)(2,1)S(1)}, bf16[384,2048]{1,0:T(8,128)(2,1)S(1)}, bf16[384,2048]{1,0:T(8,128)(2,1)S(1)}) fusion(bf16[3,384,2048]{2,1,0:T(8,128)(2,1)} %all-gather.5.cloned.1.call-done), kind=kLoop, calls=%fused_computation.51 | loop fusion | bytes 9437184 | tf_op jit(solution)/shard_map/squeeze | solution.py:81
  134.1 8.9 %fusion.42 = bf16[384,1536]{1,0:T(8,128)(2,1)} fusion(bf16[384,2048]{1,0:T(8,128)(2,1)S(1)} %get-tuple-element.72, bf16[3584,2048]{1,0:T(8,128)(2,1)} %param.7), kind=kOutput, calls=%fused_computation.40 | convolution fusion | flops 2416508928 | bytes 9043968 | tf_op jit(solution)/shard_map/dot_general | solution.py:153
  143.0 3.7 %fusion.45 = bf16[384,1536]{1,0:T(8,128)(2,1)} fusion(bf16[384,2048]{1,0:T(8,128)(2,1)S(1)} %get-tuple-element.72, bf16[3584,2048]{1,0:T(8,128)(2,1)S(1)} %bitcast.54), kind=kOutput, calls=%fused_computation.41 | convolution fusion | flops 2416508928 | bytes 9043968 | tf_op jit(solution)/shard_map/dot_general | solution.py:153
  146.7 1.5 collective-permute-start.12
  148.2 0.5 collective-permute-start.11
  148.7 2.0 fusion.54
  150.7 1.5 collective-permute-start.13
  152.3 2.7 %fusion.30.own_ref = f32[384,1536]{1,0:T(8,128)S(1)} fusion(bf16[384,2048]{1,0:T(8,128)(2,1)S(1)} %get-tuple-element.78, bf16[3584,2048]{1,0:T(8,128)(2,1)S(1)} %bitcast.54), kind=kOutput, calls=%fused_computation.32 | convolution fusion | flops 2415919104 | bytes 10223616 | tf_op jit(solution)/shard_map/dot_general | solution.py:153
  155.0 4.1 %fusion.24.refs_0_ = f32[384,1536]{1,0:T(8,128)} fusion(bf16[384,2048]{1,0:T(8,128)(2,1)S(1)} %get-tuple-element.78, bf16[3584,2048]{1,0:T(8,128)(2,1)S(1)} %bitcast.54), kind=kOutput, calls=%fused_computation.26 | convolution fusion | flops 2415919104 | bytes 10223616 | tf_op jit(solution)/shard_map/dot_general | solution.py:153
  159.1 4.8 %add_convert_fusion.1 = bf16[384,1536]{1,0:T(8,128)(2,1)} fusion(bf16[384,3584]{1,0:T(8,128)(2,1)} %collective-permute-done.10, bf16[384,2048]{1,0:T(8,128)(2,1)S(1)} %get-tuple-element.76, bf16[3584,2048]{1,0:T(8,128)(2,1)S(1)} %bitcast.54), kind=kOutput, calls=%fused_computation.44 | convolution fusion | flops 2417688576 | bytes 10223616 | tf_op jit(solution)/shard_map/dot_general | solution.py:153
  163.9 1.5 collective-permute-start.14
  165.4 30.5 %fusion = f32[3584,2048]{1,0:T(8,128)} fusion(bf16[384,3584]{1,0:T(8,128)(2,1)} %collective-permute-done.9, bf16[384,3584]{1,0:T(8,128)(2,1)} %collective-permute-done.8, bf16[384,3584]{1,0:T(8,128)(2,1)} %collective-permute-done, bf16[384,3584]{1,0:T(8,128)(2,1)} %copy-done.3, bf16[384,2048]{1,0:T(8,128)(2,1)} %all-gather.3.cloned.1.call-done, ...), kind=kOutput, calls=%fused_computation | convolution fusion | flops 22617784320 | bytes 46661632 | tf_op jit(solution)/shard_map/dot_general | solution.py:209
  195.9 6.3 %add_convert_fusion = bf16[384,1536]{1,0:T(8,128)(2,1)S(1)} fusion(bf16[384,3584]{1,0:T(8,128)(2,1)} %collective-permute-done.10, bf16[384,2048]{1,0:T(8,128)(2,1)} %copy-done.6, bf16[3584,2048]{1,0:T(8,128)(2,1)} %param.7), kind=kOutput, calls=%fused_computation.43 | convolution fusion | flops 2417688576 | bytes 10223616 | tf_op jit(solution)/shard_map/dot_general | solution.py:153
  202.3 0.6 collective-permute-start.15
  202.9 3.0 %add_convert_fusion.2 = bf16[384,512]{1,0:T(8,128)(2,1)S(1)} fusion(bf16[384,3584]{1,0:T(8,128)(2,1)} %collective-permute-done.10, bf16[384,2048]{1,0:T(8,128)(2,1)S(1)} %copy-done.7, bf16[3584,2048]{1,0:T(8,128)(2,1)} %param.7), kind=kOutput, calls=%fused_computation.63 | convolution fusion | flops 805896192 | bytes 4456448 | tf_op jit(solution)/shard_map/dot_general | solution.py:153
  205.9 1.3 collective-permute-start.16
  207.1 5.2 %shard_map.67 = (bf16[384,3584]{1,0:T(8,128)(2,1)}, bf16[384,3584]{1,0:T(8,128)(2,1)}) custom-call(f32[384,1536]{1,0:T(8,128)S(1)} %fusion.30.own_ref, bf16[384,1536]{1,0:T(8,128)(2,1)S(1)} %collective-permute-done.11.refs_0_, bf16[384,1536]{1,0:T(8,128)(2,1)} %collective-permute-done.14.refs_1_, bf16[384,3584]{1,0:T(8,128)(2,1)S(1)} %copy-done, ...), custom_call_target="tpu_custom_call" | custom-call | tf_op jit(solution)/shard_map/pallas_call | solution.py:116
  212.3 2.8 %fusion.48.refs_0_ = f32[384,512]{1,0:T(8,128)S(1)} fusion(bf16[384,2048]{1,0:T(8,128)(2,1)S(1)} %copy-done.5, bf16[3584,2048]{1,0:T(8,128)(2,1)} %param.7), kind=kOutput, calls=%fused_computation.45 | convolution fusion | flops 805306368 | bytes 4456448 | tf_op jit(solution)/shard_map/dot_general | solution.py:153
  215.1 3.4 %collective-permute-done.15.refs_2_ = bf16[384,1536]{1,0:T(8,128)(2,1)S(1)} collective-permute-done((bf16[384,1536]{1,0:T(8,128)(2,1)S(1)}, bf16[384,1536]{1,0:T(8,128)(2,1)S(1)}, u32[]{:S(2)}, u32[]{:S(2)}) %collective-permute-start.15) | collective-permute-done | bytes 1179680 | tf_op jit(solution)/shard_map/ppermute | solution.py:161
  218.5 5.2 %shard_map.68 = (bf16[384,3584]{1,0:T(8,128)(2,1)}, bf16[384,3584]{1,0:T(8,128)(2,1)}) custom-call(f32[384,1536]{1,0:T(8,128)S(1)} %copy-done.2, bf16[384,1536]{1,0:T(8,128)(2,1)} %collective-permute-done.12.refs_1_, bf16[384,1536]{1,0:T(8,128)(2,1)S(1)} %collective-permute-done.15.refs_2_, ...), custom_call_target="tpu_custom_call", output_to_operand_aliasing={{0}: (5, {}), {1}: (6, {})} | custom-call | tf_op jit(solution)/shard_map/pallas_call | solution.py:116
  223.7 2.2 shard_map.69
  (49 shorter events, 1.0 us)
Async XLA Ops:
  7.2 70.3 %all-gather.3.cloned.1.call-start = ((), (), s32[]{:S(2)}) async-start(), calls=%async_computation | async-start | bytes 1769472 | tf_op jit(solution)/shard_map/all_gather | solution.py:79
  11.5 48.8 %copy-start.3 = (bf16[384,3584]{1,0:T(8,128)(2,1)}, bf16[384,3584]{1,0:T(8,128)(2,1)S(1)}, u32[]{:S(2)}) copy-start(bf16[384,3584]{1,0:T(8,128)(2,1)S(1)} %fusion.21) | copy-start | bytes 8257540
  11.5 39.7 %collective-permute-start = (bf16[384,3584]{1,0:T(8,128)(2,1)S(1)}, bf16[384,3584]{1,0:T(8,128)(2,1)}, u32[]{:S(2)}, u32[]{:S(2)}) collective-permute-start(bf16[384,3584]{1,0:T(8,128)(2,1)S(1)} %fusion.21), channel_id=1, source_target_pairs={{0,8},{1,17},{2,10},{3,19},{4,12},{5,21},{6,14},{7,23},{8,0},{9,25... | collective-permute-start | bytes 8257544 | tf_op jit(solution)/shard_map/ppermute | solution.py:141
  16.4 1.9 collective-permute-start.1
  19.5 9.9 %collective-permute-start.4 = (bf16[48,2048]{1,0:T(8,128)(2,1)}, bf16[48,2048]{1,0:T(8,128)(2,1)S(1)}, u32[]{:S(2)}, u32[]{:S(2)}) collective-permute-start(bf16[48,2048]{1,0:T(8,128)(2,1)} %get-tuple-element.103), channel_id=1, source_target_pairs={{0,6},{1,7},{2,4},{3,5},{4,2},{5,3},{6,0},{7,1},{8,14},{9,15},{10,... | collective-permute-start | bytes 589832 | tf_op jit(solution)/shard_map/ppermute | solution.py:61
  23.1 17.3 %collective-permute-start.3 = (bf16[48,2048]{1,0:T(8,128)(2,1)S(1)}, bf16[48,2048]{1,0:T(8,128)(2,1)}, u32[]{:S(2)}, u32[]{:S(2)}) collective-permute-start(bf16[48,2048]{1,0:T(8,128)(2,1)S(1)} %get-tuple-element.104), channel_id=1, source_target_pairs={{0,4},{1,5},{2,6},{3,7},{4,0},{5,1},{6,2},{7,3},{8,12},{9,13},{10,... | collective-permute-start | bytes 589832 | tf_op jit(solution)/shard_map/ppermute | solution.py:61
  23.1 17.3 %collective-permute-start.2 = (bf16[48,2048]{1,0:T(8,128)(2,1)S(1)}, bf16[48,2048]{1,0:T(8,128)(2,1)}, u32[]{:S(2)}, u32[]{:S(2)}) collective-permute-start(bf16[48,2048]{1,0:T(8,128)(2,1)S(1)} %get-tuple-element.105), channel_id=1, source_target_pairs={{0,2},{1,3},{2,0},{3,1},{4,6},{5,7},{6,4},{7,5},{8,10},{9,11},{10,... | collective-permute-start | bytes 589832 | tf_op jit(solution)/shard_map/ppermute | solution.py:61
  41.6 9.6 %collective-permute-start.5 = (bf16[48,2048]{1,0:T(8,128)(2,1)S(1)}, bf16[48,2048]{1,0:T(8,128)(2,1)S(1)}, u32[]{:S(2)}, u32[]{:S(2)}) collective-permute-start(bf16[48,2048]{1,0:T(8,128)(2,1)S(1)} %get-tuple-element.100), channel_id=1, source_target_pairs={{0,24},{8,16},{16,8},{24,0},{1,25},{9,17},{17,9},{25,1},{2,26},{10... | collective-permute-start | bytes 589832 | tf_op jit(solution)/shard_map/ppermute | solution.py:71
  51.2 0.7 copy-start.10
  51.9 78.9 %all-gather.5.cloned.1.call-start = ((), (), s32[]{:S(2)}) async-start(), calls=%async_computation.1 | async-start | bytes 5308416 | tf_op jit(solution)/shard_map/all_gather | solution.py:80
  52.2 5.7 %collective-permute-start.6 = (bf16[48,2048]{1,0:T(8,128)(2,1)S(1)}, bf16[48,2048]{1,0:T(8,128)(2,1)S(1)}, u32[]{:S(2)}, u32[]{:S(2)}) collective-permute-start(bf16[48,2048]{1,0:T(8,128)(2,1)S(1)} %get-tuple-element.51), channel_id=1, source_target_pairs={{0,8},{8,0},{16,24},{24,16},{1,9},{9,1},{17,25},{25,17},{2,10},{10... | collective-permute-start | bytes 589832 | tf_op jit(solution)/shard_map/ppermute | solution.py:71
  53.7 5.7 %collective-permute-start.7 = (bf16[48,2048]{1,0:T(8,128)(2,1)S(1)}, bf16[48,2048]{1,0:T(8,128)(2,1)S(1)}, u32[]{:S(2)}, u32[]{:S(2)}) collective-permute-start(bf16[48,2048]{1,0:T(8,128)(2,1)S(1)} %get-tuple-element.52), channel_id=1, source_target_pairs={{0,16},{8,24},{16,0},{24,8},{1,17},{9,25},{17,1},{25,9},{2,18},{10... | collective-permute-start | bytes 589832 | tf_op jit(solution)/shard_map/ppermute | solution.py:71
  60.3 33.2 %collective-permute-start.8 = (bf16[384,3584]{1,0:T(8,128)(2,1)S(1)}, bf16[384,3584]{1,0:T(8,128)(2,1)}, u32[]{:S(2)}, u32[]{:S(2)}) collective-permute-start(bf16[384,3584]{1,0:T(8,128)(2,1)S(1)} %fusion.21), channel_id=1, source_target_pairs={{0,16},{1,9},{2,18},{3,11},{4,20},{5,13},{6,22},{7,15},{8,24},{9,1... | collective-permute-start | bytes 8257544 | tf_op jit(solution)/shard_map/ppermute | solution.py:147
  84.4 40.9 %collective-permute-start.9 = (bf16[384,3584]{1,0:T(8,128)(2,1)}, bf16[384,3584]{1,0:T(8,128)(2,1)}, u32[]{:S(2)}, u32[]{:S(2)}) collective-permute-start(bf16[384,3584]{1,0:T(8,128)(2,1)} %collective-permute-done), channel_id=1, source_target_pairs={{0,16},{1,9},{2,18},{3,11},{4,20},{5,13},{6,22},{7,15},{8,24},{9,1... | collective-permute-start | bytes 8257544 | tf_op jit(solution)/shard_map/ppermute | solution.py:161
  85.8 15.1 %copy-start.9 = (bf16[384,1536]{1,0:T(8,128)(2,1)S(1)}, bf16[384,1536]{1,0:T(8,128)(2,1)}, u32[]{:S(2)}) copy-start(bf16[384,1536]{1,0:T(8,128)(2,1)} %fusion.39) | copy-start | bytes 3538948
  125.2 33.9 %collective-permute-start.10 = (bf16[384,3584]{1,0:T(8,128)(2,1)}, bf16[384,3584]{1,0:T(8,128)(2,1)}, u32[]{:S(2)}, u32[]{:S(2)}) collective-permute-start(bf16[384,3584]{1,0:T(8,128)(2,1)} %pad_maximum_fusion), channel_id=1, source_target_pairs={{0,8},{1,17},{2,10},{3,19},{4,12},{5,21},{6,14},{7,23},{8,0},{9,25... | collective-permute-start | bytes 8257544 | tf_op jit(solution)/shard_map/ppermute | solution.py:161
  130.9 12.1 %slice-start = ((s8[14680064]{0:T(1024)(128)(4,1)}), s8[4194304]{0:T(1024)(128)(4,1)S(1)}, s32[]{:S(2)}) async-start(s8[14680064]{0:T(1024)(128)(4,1)} %bitcast.53), calls=%async_computation.2 | async-start | bytes 8388608
  130.9 12.1 %slice-start.1 = ((s8[14680064]{0:T(1024)(128)(4,1)}), s8[4194304]{0:T(1024)(128)(4,1)S(1)}, s32[]{:S(2)}) async-start(s8[14680064]{0:T(1024)(128)(4,1)} %bitcast.53), calls=%async_computation.3 | async-start | bytes 8388608
  133.9 21.1 %copy-start.4 = (bf16[384,2048]{1,0:T(8,128)(2,1)}, bf16[384,2048]{1,0:T(8,128)(2,1)S(1)}, u32[]{:S(2)}) copy-start(bf16[384,2048]{1,0:T(8,128)(2,1)S(1)} %get-tuple-element.78) | copy-start | bytes 4718596
  134.1 14.6 %copy-start.8 = (bf16[384,2048]{1,0:T(8,128)(2,1)}, bf16[384,2048]{1,0:T(8,128)(2,1)S(1)}, u32[]{:S(2)}) copy-start(bf16[384,2048]{1,0:T(8,128)(2,1)S(1)} %get-tuple-element.72) | copy-start | bytes 4718596
  134.1 25.0 %copy-start.6 = (bf16[384,2048]{1,0:T(8,128)(2,1)}, bf16[384,2048]{1,0:T(8,128)(2,1)S(1)}, u32[]{:S(2)}) copy-start(bf16[384,2048]{1,0:T(8,128)(2,1)S(1)} %get-tuple-element.76) | copy-start | bytes 4718596
  134.1 8.9 %slice-start.2 = ((s8[14680064]{0:T(1024)(128)(4,1)}), s8[4194304]{0:T(1024)(128)(4,1)S(1)}, s32[]{:S(2)}) async-start(s8[14680064]{0:T(1024)(128)(4,1)} %bitcast.53), calls=%async_computation.4 | async-start | bytes 8388608
  134.1 8.9 %slice-start.3 = ((s8[14680064]{0:T(1024)(128)(4,1)}), s8[2097152]{0:T(1024)(128)(4,1)S(1)}, s32[]{:S(2)}) async-start(s8[14680064]{0:T(1024)(128)(4,1)} %bitcast.53), calls=%async_computation.5 | async-start | bytes 4194304
  146.7 55.5 %collective-permute-start.12 = (bf16[384,1536]{1,0:T(8,128)(2,1)}, bf16[384,1536]{1,0:T(8,128)(2,1)}, u32[]{:S(2)}, u32[]{:S(2)}) collective-permute-start(bf16[384,1536]{1,0:T(8,128)(2,1)} %fusion.45), channel_id=1, source_target_pairs={{0,8},{1,17},{2,10},{3,19},{4,12},{5,21},{6,14},{7,23},{8,0},{9,25... | collective-permute-start | bytes 3538952 | tf_op jit(solution)/shard_map/ppermute | solution.py:161
  148.2 54.0 %collective-permute-start.11 = (bf16[384,1536]{1,0:T(8,128)(2,1)}, bf16[384,1536]{1,0:T(8,128)(2,1)S(1)}, u32[]{:S(2)}, u32[]{:S(2)}) collective-permute-start(bf16[384,1536]{1,0:T(8,128)(2,1)} %fusion.42), channel_id=1, source_target_pairs={{0,8},{1,17},{2,10},{3,19},{4,12},{5,21},{6,14},{7,23},{8,0},{9,25... | collective-permute-start | bytes 3538952 | tf_op jit(solution)/shard_map/ppermute | solution.py:161
  150.7 51.5 %collective-permute-start.13 = (bf16[384,512]{1,0:T(8,128)(2,1)}, bf16[384,512]{1,0:T(8,128)(2,1)}, u32[]{:S(2)}, u32[]{:S(2)}) collective-permute-start(bf16[384,512]{1,0:T(8,128)(2,1)} %fusion.54), channel_id=1, source_target_pairs={{0,8},{1,17},{2,10},{3,19},{4,12},{5,21},{6,14},{7,23},{8,0},{9,25... | collective-permute-start | bytes 1179656 | tf_op jit(solution)/shard_map/ppermute | solution.py:161
  163.9 41.9 %collective-permute-start.14 = (bf16[384,1536]{1,0:T(8,128)(2,1)}, bf16[384,1536]{1,0:T(8,128)(2,1)}, u32[]{:S(2)}, u32[]{:S(2)}) collective-permute-start(bf16[384,1536]{1,0:T(8,128)(2,1)} %add_convert_fusion.1), channel_id=1, source_target_pairs={{0,16},{1,9},{2,18},{3,11},{4,20},{5,13},{6,22},{7,15},{8,24},{9,1... | collective-permute-start | bytes 3538952 | tf_op jit(solution)/shard_map/ppermute | solution.py:161
  195.9 7.0 %copy-start.7 = (bf16[384,2048]{1,0:T(8,128)(2,1)S(1)}, bf16[384,2048]{1,0:T(8,128)(2,1)}, u32[]{:S(2)}) copy-start(bf16[384,2048]{1,0:T(8,128)(2,1)} %copy-done.6) | copy-start | bytes 4718596
  202.2 4.9 %copy-start = (bf16[384,3584]{1,0:T(8,128)(2,1)S(1)}, bf16[384,3584]{1,0:T(8,128)(2,1)}, u32[]{:S(2)}) copy-start(bf16[384,3584]{1,0:T(8,128)(2,1)} %refs_3_.2) | copy-start | bytes 8257540
  202.2 4.9 %copy-start.1 = (bf16[384,3584]{1,0:T(8,128)(2,1)S(1)}, bf16[384,3584]{1,0:T(8,128)(2,1)}, u32[]{:S(2)}) copy-start(bf16[384,3584]{1,0:T(8,128)(2,1)} %refs_4_.1) | copy-start | bytes 8257540
  202.3 16.3 %collective-permute-start.15 = (bf16[384,1536]{1,0:T(8,128)(2,1)S(1)}, bf16[384,1536]{1,0:T(8,128)(2,1)S(1)}, u32[]{:S(2)}, u32[]{:S(2)}) collective-permute-start(bf16[384,1536]{1,0:T(8,128)(2,1)S(1)} %add_convert_fusion), channel_id=1, source_target_pairs={{0,16},{1,9},{2,18},{3,11},{4,20},{5,13},{6,22},{7,15},{8,24},{9,1... | collective-permute-start | bytes 3538952 | tf_op jit(solution)/shard_map/ppermute | solution.py:161
  205.8 6.5 %copy-start.5 = (bf16[384,2048]{1,0:T(8,128)(2,1)S(1)}, bf16[384,2048]{1,0:T(8,128)(2,1)}, u32[]{:S(2)}) copy-start(bf16[384,2048]{1,0:T(8,128)(2,1)} %copy-done.4) | copy-start | bytes 4718596
  205.9 17.8 %collective-permute-start.16 = (bf16[384,512]{1,0:T(8,128)(2,1)S(1)}, bf16[384,512]{1,0:T(8,128)(2,1)S(1)}, u32[]{:S(2)}, u32[]{:S(2)}) collective-permute-start(bf16[384,512]{1,0:T(8,128)(2,1)S(1)} %add_convert_fusion.2), channel_id=1, source_target_pairs={{0,16},{1,9},{2,18},{3,11},{4,20},{5,13},{6,22},{7,15},{8,24},{9,1... | collective-permute-start | bytes 1179656 | tf_op jit(solution)/shard_map/ppermute | solution.py:161
  212.3 6.2 %copy-start.2 = (f32[384,1536]{1,0:T(8,128)S(1)}, f32[384,1536]{1,0:T(8,128)}, u32[]{:S(2)}) copy-start(f32[384,1536]{1,0:T(8,128)} %fusion.24.refs_0_) | copy-start | bytes 7077892
Sparse Core Ops, SparseCore 0:
  52.1 25.3 all-gather.2
  79.6 51.1 all-gather.4

commit v7 on v6

--- a/solution.py
+++ b/solution.py
@@ -65,20 +65,11 @@
     blocks = [None] * rows
     for flip in reversed(range(rows)):
         piece = lax.dynamic_index_in_dim(held, row ^ flip ^ plane, 0, keepdims=False)
-        if flip < rows - 1:
-            piece = lax.optimization_barrier((piece, blocks[-1]))[0]
         if flip:
             piece = lax.ppermute(piece, "row", [(r, r ^ flip) for r in range(rows)])
-        if flip == rows - 1:
-            piece = lax.optimization_barrier((piece, hidden_came))[0]
         blocks[flip] = piece
+    blocks[-1] = lax.optimization_barrier((blocks[-1], *blocks[1:-1], *hidden_came))[0]
     return blocks
-
-
-def gather_tokens(blocks):
-    first = lax.all_gather(blocks[-1], "col", axis=0, tiled=True)
-    rest = lax.all_gather(jnp.stack(blocks[:-1]), "col", axis=1, tiled=True)
-    return [rest[flip] for flip in range(len(blocks) - 1)] + [first]
 
 
 def finish_kernel(own_ref, *refs):
@@ -137,16 +128,20 @@
         gate = gate.astype(jnp.float32)
         return (gate * jax.nn.sigmoid(gate) * up.astype(jnp.float32)).astype(jnp.bfloat16)
 
-    hidden = activation(gate_act, up_act)
-    hidden_came = lax.ppermute(hidden, BOTH, pairs[0])
-    pieces = spread_tokens(grad_out, hidden, hidden_came, rows, cols)
-    gathered = [hidden, hidden_came]
+    gate_halves, up_halves = jnp.split(gate_act, 2), jnp.split(up_act, 2)
+    front = activation(gate_halves[0], up_halves[0])
+    back = activation(after(gate_halves[1], front), after(up_halves[1], front))
+    hidden_came = [lax.ppermute(half, BOTH, pairs[0]) for half in (front, back)]
+    pieces = spread_tokens(grad_out, back, hidden_came, rows, cols)
+    hidden = jnp.concatenate([front, back])
+    gathered = [hidden, jnp.concatenate(hidden_came)]
     for step in range(1, steps - 1):
         gathered = gathered + [lax.ppermute(part, BOTH, pairs[step]) for part in gathered]
 
     gathered.append(lax.ppermute(after(hidden, *pieces), BOTH, pairs[-1]))
 
-    blocks = gather_tokens(pieces)
+    first = lax.all_gather(pieces[-1], "col", axis=0, tiled=True)
+    others = lax.all_gather(after(jnp.stack(pieces[:-1]), first), "col", axis=1, tiled=True)
     width = down_weight.shape[0]
 
     def product(block, start, stop, *before):
@@ -161,14 +156,15 @@
         return lax.ppermute(total, BOTH, pairs[step])
 
     unit = width // 7
-    total = product(blocks[-1], 0, 3 * unit).astype(jnp.bfloat16)
+    total = product(first, 0, 3 * unit).astype(jnp.bfloat16)
     for part in gathered[1 : rows // 2]:
         gathered.append(send(after(part, total), steps - 1))
-    rest = product(blocks[-1], 3 * unit, width, total, gathered[rows // 2]).astype(jnp.bfloat16)
+    rest = product(first, 3 * unit, width, total, gathered[rows // 2]).astype(jnp.bfloat16)
     total = jnp.concatenate([total, rest], axis=1)
     total = after(total, *gathered[rows // 2 + 1 :])
 
-    blocks[:-1] = lax.optimization_barrier((*blocks[:-1], total))[:-1]
+    others = after(others, total)
+    blocks = [*(others[flip] for flip in range(rows - 1)), first]
     turn = lax.axis_index("col") % steps
     grads = [
         lax.select_n(turn, *(blocks[row_offset(rows, place, t)] for t in range(steps)))
@@ -200,12 +196,16 @@
             for chunk in chunks:
                 total = message(place, chunk, total)
                 came[place ^ (1 << step)][chunk].append(send(total, step))
-    own = [own_product(0, total)]
-    own.append(own_product(1, own[0]))
-    total = message(rows // 2, 0, own[1])
-    last = [send(total, steps - 1)]
-
-    gathered, grads, _ = lax.optimization_barrier((gathered, grads, total))
+    last = []
+    for chunk in chunks[:-1]:
+        total = message(rows // 2, chunk, total)
+        last.append(send(total, steps - 1))
+    own = []
+    for chunk in chunks:
+        total = own_product(chunk, total)
+        own.append(total)
+
+    gathered, grads, own = lax.optimization_barrier((gathered, grads, own))
     grad_weight = lax.dot_general(
         jnp.concatenate(gathered, axis=0),
         jnp.concatenate(grads, axis=0),
@@ -213,13 +213,10 @@
         preferred_element_type=jnp.float32,
     )
 
-    total = after(message(rows // 2, 1, grad_weight), *sum(came[0], []))
-    last.append(send(total, steps - 1))
-    total = after(message(rows // 2, 2, total), last[0])
-    last.append(send(total, steps - 1))
-    own.append(own_product(2, total))
-
-    gate_act, up_act = after(gate_act, hidden_came), after(up_act, hidden_came)
+    total = message(rows // 2, len(last), grad_weight)
+    last.append(send(after(total, last[0], *sum(came[0], [])), steps - 1))
+
+    gate_act, up_act = after(gate_act, front), after(up_act, front)
     outs = []
     for chunk, start in enumerate(starts):
         outs = finish(

time: 233 us -> 258 us (1.11)
  waiting for transfers between devices: 87.2 us -> 106 us
  other arithmetic: 8.57 us -> 13.2 us
  starting transfers between devices: 20.6 us -> 23.5 us
    ppermute x1, waiting for transfers between devices: 7.7 us -> 22.2 us  [on_device(): gathered.append(lax.ppermute(after(hidden, *pieces), BOTH, pairs[-1]))]
    ppermute x8, waiting for transfers between devices: 26 us -> 30.5 us  [send(): return lax.ppermute(total, BOTH, pairs[step])]
    all_gather x2, waiting for transfers between devices: 22.2 us -> 25.8 us  [the longest x1 25.8 us: on_device(): first = lax.all_gather(pieces[-1], 'col', axis=0, tiled=True)]
    squeeze x2 -> x0, local copies, waits for them, and re-layouts: 3.08 us -> none  [the longest x1 3.01 us: gather_tokens(): return [rest[flip] for flip in range(len(blocks) - 1)] + [first]]
    convert_element_type x1 -> x2, other arithmetic: 4.27 us -> 5.57 us  [activation(): (gate * jax.nn.sigmoid(gate) * up.astype(jnp.float32)).astype(jnp.bfloat16)]
  transfers between devices with their start and end apart: 19 -> 20, of which waited for: 11 -> 8; matrix products, arithmetic and copies ran while one was open for 40% -> 38% of each run, Pallas kernels for 4% -> 4%
where the time goes in v7:
time: 258 us
  waiting for transfers between devices  106 us (41%)
  matrix products  82.4 us (32%)
  starting transfers between devices  23.5 us (9%)
  between operations  14.4 us (6%)
  other arithmetic  13.2 us (5%)
  Pallas kernels  13 us (5%)
  local copies, waits for them, and re-layouts  5.33 us (2%)
    dot_general x11, matrix products, product(): lax.dot_general(after(block, *before), down_weight[start:stop], (((1,), (...  51.8 us
    dot_general x1, matrix products, on_device(): lax.dot_general(jnp.concatenate(gathered, axis=0), jnp.concatenate(grads,...  30.5 us
    ppermute x8, waiting for transfers between devices, send(): return lax.ppermute(total, BOTH, pairs[step])  30.5 us
    all_gather x1, waiting for transfers between devices, on_device(): first = lax.all_gather(pieces[-1], 'col', axis=0, tiled=True)  25.8 us
    ppermute x1, waiting for transfers between devices, on_device(): gathered.append(lax.ppermute(after(hidden, *pieces), BOTH, pairs[-1]))  22.2 us
    ppermute x4, waiting for transfers between devices, spread_tokens(): piece = lax.ppermute(piece, 'col', pairs)  16.3 us
    pallas_call x3, Pallas kernels, finish(): pl.pallas_call(kernel, grid=(width // block,), in_specs=specs, out_specs=...  13 us
    ppermute x3, waiting for transfers between devices, spread_tokens(): piece = lax.ppermute(piece, 'row', [(r, r ^ flip) for r in range(rows)])  11.1 us
  transfers between devices with their start and end apart: 20, of which 8 were waited for; matrix products, arithmetic and copies ran while one was open for 38% of the time, Pallas kernels for 4%

profile of v7, /device:TPU:0, one launch (start us, length us, event | category | flops | bytes accessed | tf_op | source)
XLA Modules:
  0.0 257.6 jit_solution(12022961036835480961)
XLA Ops:
  7.3 1.9 dynamic-slice_bitcast_fusion
  9.7 3.7 %fusion.52 = bf16[192,3584]{1,0:T(8,128)(2,1)} fusion(bf16[384,3584]{1,0:T(8,128)(2,1)} %refs_4_.1, bf16[384,3584]{1,0:T(8,128)(2,1)} %refs_3_.2), kind=kLoop, calls=%fused_computation.50 | loop fusion | flops 5505024 | bytes 4128768 | tf_op jit(solution)/shard_map/convert_element_type | solution.py:129
  13.3 2.5 collective-permute-start
  15.8 1.9 fusion.51
  17.7 1.7 collective-permute-start.1
  19.9 3.7 %collective-permute-start.5 = (bf16[48,2048]{1,0:T(8,128)(2,1)S(1)}, bf16[48,2048]{1,0:T(8,128)(2,1)S(1)}, u32[]{:S(2)}, u32[]{:S(2)}) collective-permute-start(bf16[48,2048]{1,0:T(8,128)(2,1)S(1)} %get-tuple-element.101), channel_id=1, source_target_pairs={{0,6},{1,7},{2,4},{3,5},{4,2},{5,3},{6,0},{7,1},{8,14},{9,15},{10,... | collective-permute-start | bytes 589832 | tf_op jit(solution)/shard_map/ppermute | solution.py:61
  23.6 0.8 collective-permute-start.3
  24.4 5.3 %collective-permute-done.5 = bf16[48,2048]{1,0:T(8,128)(2,1)S(1)} collective-permute-done((bf16[48,2048]{1,0:T(8,128)(2,1)S(1)}, bf16[48,2048]{1,0:T(8,128)(2,1)S(1)}, u32[]{:S(2)}, u32[]{:S(2)}) %collective-permute-start.5) | collective-permute-done | bytes 196640 | tf_op jit(solution)/shard_map/ppermute | solution.py:61
  29.6 11.0 %collective-permute-done.4 = bf16[48,2048]{1,0:T(8,128)(2,1)S(1)} collective-permute-done((bf16[48,2048]{1,0:T(8,128)(2,1)S(1)}, bf16[48,2048]{1,0:T(8,128)(2,1)S(1)}, u32[]{:S(2)}, u32[]{:S(2)}) %collective-permute-start.4) | collective-permute-done | bytes 196640 | tf_op jit(solution)/shard_map/ppermute | solution.py:61
  40.9 1.5 collective-permute-start.8
  42.4 1.0 collective-permute-start.7
  43.4 1.0 collective-permute-start.6
  44.4 10.5 %collective-permute-done.8 = bf16[48,2048]{1,0:T(8,128)(2,1)S(1)} collective-permute-done((bf16[48,2048]{1,0:T(8,128)(2,1)S(1)}, bf16[48,2048]{1,0:T(8,128)(2,1)S(1)}, u32[]{:S(2)}, u32[]{:S(2)}) %collective-permute-start.8) | collective-permute-done | bytes 196640 | tf_op jit(solution)/shard_map/ppermute | solution.py:69
  55.0 0.5 collective-permute-done.6
  55.9 0.9 pad_maximum_fusion.4
  56.8 25.8 %all-gather.3.cloned.1.call-done = bf16[384,2048]{1,0:T(8,128)(2,1)} async-done(((bf16[48,2048]{1,0:T(8,128)(2,1)}), bf16[384,2048]{1,0:T(8,128)(2,1)}) %all-gather.3.cloned.1.call-update) | async-done | bytes 1572880 | tf_op jit(solution)/shard_map/all_gather | solution.py:143
  82.6 1.9 pad_maximum_fusion
  84.5 1.5 collective-permute-start.9
  86.1 1.4 constant_dynamic-update-slice_fusion.1
  87.6 6.6 %fusion.34 = bf16[384,1536]{1,0:T(8,128)(2,1)S(1)} fusion(bf16[384,2048]{1,0:T(8,128)(2,1)S(1)} %copy-done.11, bf16[3584,2048]{1,0:T(8,128)(2,1)} %param.7), kind=kOutput, calls=%fused_computation.36 | convolution fusion | flops 2416508928 | bytes 9043968 | tf_op jit(solution)/shard_map/dot_general | solution.py:148
  94.2 1.4 collective-permute-start.10
  95.6 22.2 %collective-permute-done.9 = bf16[384,3584]{1,0:T(8,128)(2,1)} collective-permute-done((bf16[384,3584]{1,0:T(8,128)(2,1)S(1)}, bf16[384,3584]{1,0:T(8,128)(2,1)}, u32[]{:S(2)}, u32[]{:S(2)}) %collective-permute-start.9) | collective-permute-done | bytes 2752544 | tf_op jit(solution)/shard_map/ppermute | solution.py:141
  117.8 6.9 %fusion.31 = bf16[384,2048]{1,0:T(8,128)(2,1)S(1)} fusion(bf16[384,2048]{1,0:T(8,128)(2,1)S(1)} %copy-done.11, bf16[3584,2048]{1,0:T(8,128)(2,1)} %param.7), kind=kOutput, calls=%fused_computation.35 | convolution fusion | flops 3222011904 | bytes 11534336 | tf_op jit(solution)/shard_map/dot_general | solution.py:148
  124.7 1.7 pad_maximum_fusion.1
  126.4 20.7 %collective-permute-done.10 = bf16[384,3584]{1,0:T(8,128)(2,1)S(1)} collective-permute-done((bf16[384,3584]{1,0:T(8,128)(2,1)S(1)}, bf16[384,3584]{1,0:T(8,128)(2,1)S(1)}, u32[]{:S(2)}, u32[]{:S(2)}) %collective-permute-start.10) | collective-permute-done | bytes 2752544 | tf_op jit(solution)/shard_map/ppermute | solution.py:156
  147.2 1.5 copy-done.10
  148.7 1.5 collective-permute-start.11
  150.2 2.7 %select_bitcast_fusion = (bf16[384,2048]{1,0:T(8,128)(2,1)S(1)}, bf16[384,2048]{1,0:T(8,128)(2,1)S(1)}, bf16[384,2048]{1,0:T(8,128)(2,1)S(1)}) fusion(pred[]{:T(512)S(6)} %select_n.100, bf16[3,384,2048]{2,1,0:T(8,128)(2,1)} %all-gather.5.cloned.1.call-done), kind=kLoop, calls=%fused_computation.59 | loop fusion | flops 1572864 | bytes 9437185 | tf_op jit(solution)/shard_map/select_n | solution.py:170
  152.9 8.2 %fusion.37 = bf16[384,1536]{1,0:T(8,128)(2,1)} fusion(bf16[384,2048]{1,0:T(8,128)(2,1)S(1)} %get-tuple-element.72, bf16[3584,2048]{1,0:T(8,128)(2,1)} %param.7), kind=kOutput, calls=%fused_computation.37 | convolution fusion | flops 2416508928 | bytes 9043968 | tf_op jit(solution)/shard_map/dot_general | solution.py:148
  161.1 6.6 %fusion.40 = bf16[384,1536]{1,0:T(8,128)(2,1)} fusion(bf16[384,2048]{1,0:T(8,128)(2,1)S(1)} %get-tuple-element.72, bf16[3584,2048]{1,0:T(8,128)(2,1)} %param.7), kind=kOutput, calls=%fused_computation.38 | convolution fusion | flops 2416508928 | bytes 9043968 | tf_op jit(solution)/shard_map/dot_general | solution.py:148
  167.7 0.6 collective-permute-start.13
  168.2 1.5 collective-permute-start.14
  169.7 2.1 fusion.59
  171.8 0.6 collective-permute-start.12
  172.3 9.7 %collective-permute-done.11 = bf16[384,3584]{1,0:T(8,128)(2,1)} collective-permute-done((bf16[384,3584]{1,0:T(8,128)(2,1)}, bf16[384,3584]{1,0:T(8,128)(2,1)}, u32[]{:S(2)}, u32[]{:S(2)}) %collective-permute-start.11) | collective-permute-done | bytes 2752544 | tf_op jit(solution)/shard_map/ppermute | solution.py:156
  182.1 4.8 %add_convert_fusion.1 = bf16[384,1536]{1,0:T(8,128)(2,1)} fusion(bf16[384,3584]{1,0:T(8,128)(2,1)} %collective-permute-done.11, bf16[384,2048]{1,0:T(8,128)(2,1)S(1)} %get-tuple-element.88, bf16[3584,2048]{1,0:T(8,128)(2,1)S(1)} %bitcast.52), kind=kOutput, calls=%fused_computation.52 | convolution fusion | flops 2417688576 | bytes 10223616 | tf_op jit(solution)/shard_map/dot_general | solution.py:148
  186.9 1.5 collective-permute-start.15
  188.3 4.8 %add_convert_fusion = bf16[384,1536]{1,0:T(8,128)(2,1)} fusion(bf16[384,3584]{1,0:T(8,128)(2,1)} %collective-permute-done.11, bf16[384,2048]{1,0:T(8,128)(2,1)S(1)} %get-tuple-element.88, bf16[3584,2048]{1,0:T(8,128)(2,1)S(1)} %bitcast.52), kind=kOutput, calls=%fused_computation.51 | convolution fusion | flops 2417688576 | bytes 10223616 | tf_op jit(solution)/shard_map/dot_general | solution.py:148
  193.1 0.6 collective-permute-start.16
  193.7 2.6 %fusion.23.own_ref = f32[384,1536]{1,0:T(8,128)S(1)} fusion(bf16[384,2048]{1,0:T(8,128)(2,1)S(1)} %get-tuple-element.71, bf16[3584,2048]{1,0:T(8,128)(2,1)S(1)} %bitcast.52), kind=kOutput, calls=%fused_computation.23 | convolution fusion | flops 2415919104 | bytes 10223616 | tf_op jit(solution)/shard_map/dot_general | solution.py:148
  196.4 4.1 %fusion.17.refs_0_ = f32[384,1536]{1,0:T(8,128)} fusion(bf16[384,2048]{1,0:T(8,128)(2,1)S(1)} %get-tuple-element.71, bf16[3584,2048]{1,0:T(8,128)(2,1)S(1)} %bitcast.52), kind=kOutput, calls=%fused_computation.17 | convolution fusion | flops 2415919104 | bytes 10223616 | tf_op jit(solution)/shard_map/dot_general | solution.py:148
  200.4 1.9 fusion.55.refs_0_
  202.3 30.5 %fusion = f32[3584,2048]{1,0:T(8,128)} fusion(bf16[384,3584]{1,0:T(8,128)(2,1)} %copy-done.10, bf16[384,3584]{1,0:T(8,128)(2,1)} %collective-permute-done.9, bf16[384,3584]{1,0:T(8,128)(2,1)} %copy-done.8, bf16[384,3584]{1,0:T(8,128)(2,1)} %copy-done.4, bf16[384,2048]{1,0:T(8,128)(2,1)} %all-gather.3.cloned.1.call-done, bf16[384,2048]{1,0:T(8,128)(2,1)} %copy-done.5, ...), kind=kOutput, calls=%fused_computation | convolution fusion | flops 22617784320 | bytes 46661632 | tf_op jit(solution)/shard_map/dot_general | solution.py:209
  232.9 3.3 %add_convert_fusion.2 = bf16[384,512]{1,0:T(8,128)(2,1)S(1)} fusion(bf16[384,3584]{1,0:T(8,128)(2,1)} %collective-permute-done.11, bf16[384,2048]{1,0:T(8,128)(2,1)} %copy-done.5, bf16[3584,2048]{1,0:T(8,128)(2,1)} %param.7), kind=kOutput, calls=%fused_computation.69 | convolution fusion | flops 805896192 | bytes 4456448 | tf_op jit(solution)/shard_map/dot_general | solution.py:148
  236.2 1.5 collective-permute-start.17
  237.7 5.2 %shard_map.67 = (bf16[384,3584]{1,0:T(8,128)(2,1)}, bf16[384,3584]{1,0:T(8,128)(2,1)}) custom-call(f32[384,1536]{1,0:T(8,128)S(1)} %fusion.23.own_ref, bf16[384,1536]{1,0:T(8,128)(2,1)S(1)} %collective-permute-done.14.refs_0_, bf16[384,1536]{1,0:T(8,128)(2,1)} %collective-permute-done.15.refs_1_, bf16[384,3584]{1,0:T(8,128)(2,1)S(1)} %copy-done, ...), custom_call_target="tpu_custom_call" | custom-call | tf_op jit(solution)/shard_map/pallas_call | solution.py:107
  243.0 5.6 %shard_map.68 = (bf16[384,3584]{1,0:T(8,128)(2,1)}, bf16[384,3584]{1,0:T(8,128)(2,1)}) custom-call(f32[384,1536]{1,0:T(8,128)S(1)} %copy-done.2, bf16[384,1536]{1,0:T(8,128)(2,1)} %collective-permute-done.13.refs_1_, bf16[384,1536]{1,0:T(8,128)(2,1)} %collective-permute-done.16.refs_2_, ...), custom_call_target="tpu_custom_call", output_to_operand_aliasing={{0}: (5, {}), {1}: (6, {})} | custom-call | tf_op jit(solution)/shard_map/pallas_call | solution.py:107
  248.6 2.2 shard_map.69
  (60 shorter events, 1.6 us)
Async XLA Ops:
  7.2 75.4 %all-gather.3.cloned.1.call-start = ((), (), s32[]{:S(2)}) async-start(), calls=%async_computation | async-start | bytes 1769472 | tf_op jit(solution)/shard_map/all_gather | solution.py:143
  9.2 10.3 %collective-permute-start.2 = (bf16[4,48,1024]{2,1,0:T(8,128)(2,1)}, bf16[4,48,1024]{2,1,0:T(8,128)(2,1)S(1)}, u32[]{:S(2)}, u32[]{:S(2)}) collective-permute-start(bf16[4,48,1024]{2,1,0:T(8,128)(2,1)} %get-tuple-element.106), channel_id=1, source_target_pairs={{0,1},{1,0},{2,3},{3,2},{4,5},{5,4},{6,7},{7,6},{8,9},{9,8},{10,11... | collective-permute-start | bytes 1179656 | tf_op jit(solution)/shard_map/ppermute | solution.py:43
  13.3 2.5 slice-start
  13.3 2.5 slice-start.1
  13.3 42.2 %collective-permute-start = (bf16[192,3584]{1,0:T(8,128)(2,1)}, bf16[192,3584]{1,0:T(8,128)(2,1)}, u32[]{:S(2)}, u32[]{:S(2)}) collective-permute-start(bf16[192,3584]{1,0:T(8,128)(2,1)} %fusion.52), channel_id=1, source_target_pairs={{0,8},{1,17},{2,10},{3,19},{4,12},{5,21},{6,14},{7,23},{8,0},{9,25... | collective-permute-start | bytes 4128776 | tf_op jit(solution)/shard_map/ppermute | solution.py:134
  17.7 37.8 %collective-permute-start.1 = (bf16[192,3584]{1,0:T(8,128)(2,1)}, bf16[192,3584]{1,0:T(8,128)(2,1)S(1)}, u32[]{:S(2)}, u32[]{:S(2)}) collective-permute-start(bf16[192,3584]{1,0:T(8,128)(2,1)} %fusion.51), channel_id=1, source_target_pairs={{0,8},{1,17},{2,10},{3,19},{4,12},{5,21},{6,14},{7,23},{8,0},{9,25... | collective-permute-start | bytes 4128776 | tf_op jit(solution)/shard_map/ppermute | solution.py:134
  19.9 9.7 %collective-permute-start.5 = (bf16[48,2048]{1,0:T(8,128)(2,1)S(1)}, bf16[48,2048]{1,0:T(8,128)(2,1)S(1)}, u32[]{:S(2)}, u32[]{:S(2)}) collective-permute-start(bf16[48,2048]{1,0:T(8,128)(2,1)S(1)} %get-tuple-element.101), channel_id=1, source_target_pairs={{0,6},{1,7},{2,4},{3,5},{4,2},{5,3},{6,0},{7,1},{8,14},{9,15},{10,... | collective-permute-start | bytes 589832 | tf_op jit(solution)/shard_map/ppermute | solution.py:61
  23.6 17.1 %collective-permute-start.4 = (bf16[48,2048]{1,0:T(8,128)(2,1)S(1)}, bf16[48,2048]{1,0:T(8,128)(2,1)S(1)}, u32[]{:S(2)}, u32[]{:S(2)}) collective-permute-start(bf16[48,2048]{1,0:T(8,128)(2,1)S(1)} %get-tuple-element.102), channel_id=1, source_target_pairs={{0,4},{1,5},{2,6},{3,7},{4,0},{5,1},{6,2},{7,3},{8,12},{9,13},{10,... | collective-permute-start | bytes 589832 | tf_op jit(solution)/shard_map/ppermute | solution.py:61
  23.6 17.1 %collective-permute-start.3 = (bf16[48,2048]{1,0:T(8,128)(2,1)S(1)}, bf16[48,2048]{1,0:T(8,128)(2,1)S(1)}, u32[]{:S(2)}, u32[]{:S(2)}) collective-permute-start(bf16[48,2048]{1,0:T(8,128)(2,1)S(1)} %get-tuple-element.103), channel_id=1, source_target_pairs={{0,2},{1,3},{2,0},{3,1},{4,6},{5,7},{6,4},{7,5},{8,10},{9,11},{10,... | collective-permute-start | bytes 589832 | tf_op jit(solution)/shard_map/ppermute | solution.py:61
  40.9 14.1 %collective-permute-start.8 = (bf16[48,2048]{1,0:T(8,128)(2,1)S(1)}, bf16[48,2048]{1,0:T(8,128)(2,1)S(1)}, u32[]{:S(2)}, u32[]{:S(2)}) collective-permute-start(bf16[48,2048]{1,0:T(8,128)(2,1)S(1)} %get-tuple-element.97), channel_id=1, source_target_pairs={{0,24},{8,16},{16,8},{24,0},{1,25},{9,17},{17,9},{25,1},{2,26},{10... | collective-permute-start | bytes 589832 | tf_op jit(solution)/shard_map/ppermute | solution.py:69
  42.4 12.6 %collective-permute-start.7 = (bf16[48,2048]{1,0:T(8,128)(2,1)S(1)}, bf16[48,2048]{1,0:T(8,128)(2,1)S(1)}, u32[]{:S(2)}, u32[]{:S(2)}) collective-permute-start(bf16[48,2048]{1,0:T(8,128)(2,1)S(1)} %get-tuple-element.98), channel_id=1, source_target_pairs={{0,16},{8,24},{16,0},{24,8},{1,17},{9,25},{17,1},{25,9},{2,18},{10... | collective-permute-start | bytes 589832 | tf_op jit(solution)/shard_map/ppermute | solution.py:69
  43.4 12.1 %collective-permute-start.6 = (bf16[48,2048]{1,0:T(8,128)(2,1)S(1)}, bf16[48,2048]{1,0:T(8,128)(2,1)S(1)}, u32[]{:S(2)}, u32[]{:S(2)}) collective-permute-start(bf16[48,2048]{1,0:T(8,128)(2,1)S(1)} %get-tuple-element.99), channel_id=1, source_target_pairs={{0,8},{8,0},{16,24},{24,16},{1,9},{9,1},{17,25},{25,17},{2,10},{10... | collective-permute-start | bytes 589832 | tf_op jit(solution)/shard_map/ppermute | solution.py:69
  55.0 0.7 copy-start.9
  55.7 94.5 %all-gather.5.cloned.1.call-start = ((), (), s32[]{:S(2)}) async-start(), calls=%async_computation.1 | async-start | bytes 5308416 | tf_op jit(solution)/shard_map/all_gather | solution.py:144
  84.5 3.1 %copy-start.4 = (bf16[384,3584]{1,0:T(8,128)(2,1)}, bf16[384,3584]{1,0:T(8,128)(2,1)S(1)}, u32[]{:S(2)}) copy-start(bf16[384,3584]{1,0:T(8,128)(2,1)S(1)} %pad_maximum_fusion) | copy-start | bytes 8257540
  84.5 3.1 %copy-start.11 = (bf16[384,2048]{1,0:T(8,128)(2,1)S(1)}, bf16[384,2048]{1,0:T(8,128)(2,1)}, u32[]{:S(2)}) copy-start(bf16[384,2048]{1,0:T(8,128)(2,1)} %all-gather.3.cloned.1.call-done) | copy-start | bytes 4718596
  84.5 33.2 %collective-permute-start.9 = (bf16[384,3584]{1,0:T(8,128)(2,1)S(1)}, bf16[384,3584]{1,0:T(8,128)(2,1)}, u32[]{:S(2)}, u32[]{:S(2)}) collective-permute-start(bf16[384,3584]{1,0:T(8,128)(2,1)S(1)} %pad_maximum_fusion), channel_id=1, source_target_pairs={{0,16},{1,9},{2,18},{3,11},{4,20},{5,13},{6,22},{7,15},{8,24},{9,1... | collective-permute-start | bytes 8257544 | tf_op jit(solution)/shard_map/ppermute | solution.py:141
  87.6 6.6 %copy-start.8 = (bf16[384,3584]{1,0:T(8,128)(2,1)}, bf16[384,3584]{1,0:T(8,128)(2,1)S(1)}, u32[]{:S(2)}) copy-start(bf16[384,3584]{1,0:T(8,128)(2,1)S(1)} %constant_dynamic-update-slice_fusion) | copy-start | bytes 8257540
  94.2 52.9 %collective-permute-start.10 = (bf16[384,3584]{1,0:T(8,128)(2,1)S(1)}, bf16[384,3584]{1,0:T(8,128)(2,1)S(1)}, u32[]{:S(2)}, u32[]{:S(2)}) collective-permute-start(bf16[384,3584]{1,0:T(8,128)(2,1)S(1)} %constant_dynamic-update-slice_fusion), channel_id=1, source_target_pairs={{0,16},{1,9},{2,18},{3,11},{4,20},{5,13},{6,22},{7,15},{8,24},{9,1... | collective-permute-start | bytes 8257544 | tf_op jit(solution)/shard_map/ppermute | solution.py:156
  147.1 1.5 copy-start.10
  148.7 33.4 %collective-permute-start.11 = (bf16[384,3584]{1,0:T(8,128)(2,1)}, bf16[384,3584]{1,0:T(8,128)(2,1)}, u32[]{:S(2)}, u32[]{:S(2)}) collective-permute-start(bf16[384,3584]{1,0:T(8,128)(2,1)} %pad_maximum_fusion.1), channel_id=1, source_target_pairs={{0,8},{1,17},{2,10},{3,19},{4,12},{5,21},{6,14},{7,23},{8,0},{9,25... | collective-permute-start | bytes 8257544 | tf_op jit(solution)/shard_map/ppermute | solution.py:156
  152.8 16.9 %copy-start.7 = (bf16[384,2048]{1,0:T(8,128)(2,1)}, bf16[384,2048]{1,0:T(8,128)(2,1)S(1)}, u32[]{:S(2)}) copy-start(bf16[384,2048]{1,0:T(8,128)(2,1)S(1)} %get-tuple-element.72) | copy-start | bytes 4718596
  152.8 35.5 %copy-start.5 = (bf16[384,2048]{1,0:T(8,128)(2,1)}, bf16[384,2048]{1,0:T(8,128)(2,1)S(1)}, u32[]{:S(2)}) copy-start(bf16[384,2048]{1,0:T(8,128)(2,1)S(1)} %get-tuple-element.88) | copy-start | bytes 4718596
  152.8 47.6 %copy-start.6 = (bf16[384,2048]{1,0:T(8,128)(2,1)}, bf16[384,2048]{1,0:T(8,128)(2,1)S(1)}, u32[]{:S(2)}) copy-start(bf16[384,2048]{1,0:T(8,128)(2,1)S(1)} %get-tuple-element.71) | copy-start | bytes 4718596
  152.8 16.8 %slice-start.2 = ((s8[14680064]{0:T(1024)(128)(4,1)}), s8[4194304]{0:T(1024)(128)(4,1)S(1)}, s32[]{:S(2)}) async-start(s8[14680064]{0:T(1024)(128)(4,1)} %bitcast.51), calls=%async_computation.4 | async-start | bytes 8388608
  152.9 16.8 %slice-start.3 = ((s8[14680064]{0:T(1024)(128)(4,1)}), s8[4194304]{0:T(1024)(128)(4,1)S(1)}, s32[]{:S(2)}) async-start(s8[14680064]{0:T(1024)(128)(4,1)} %bitcast.51), calls=%async_computation.5 | async-start | bytes 8388608
  161.1 8.6 %slice-start.4 = ((s8[14680064]{0:T(1024)(128)(4,1)}), s8[4194304]{0:T(1024)(128)(4,1)S(1)}, s32[]{:S(2)}) async-start(s8[14680064]{0:T(1024)(128)(4,1)} %bitcast.51), calls=%async_computation.6 | async-start | bytes 8388608
  161.1 8.6 %slice-start.5 = ((s8[14680064]{0:T(1024)(128)(4,1)}), s8[2097152]{0:T(1024)(128)(4,1)S(1)}, s32[]{:S(2)}) async-start(s8[14680064]{0:T(1024)(128)(4,1)} %bitcast.51), calls=%async_computation.7 | async-start | bytes 4194304
  167.7 68.5 %collective-permute-start.13 = (bf16[384,1536]{1,0:T(8,128)(2,1)}, bf16[384,1536]{1,0:T(8,128)(2,1)}, u32[]{:S(2)}, u32[]{:S(2)}) collective-permute-start(bf16[384,1536]{1,0:T(8,128)(2,1)} %fusion.40), channel_id=1, source_target_pairs={{0,8},{1,17},{2,10},{3,19},{4,12},{5,21},{6,14},{7,23},{8,0},{9,25... | collective-permute-start | bytes 3538952 | tf_op jit(solution)/shard_map/ppermute | solution.py:156
  168.2 68.0 %collective-permute-start.14 = (bf16[384,1536]{1,0:T(8,128)(2,1)}, bf16[384,1536]{1,0:T(8,128)(2,1)S(1)}, u32[]{:S(2)}, u32[]{:S(2)}) collective-permute-start(bf16[384,1536]{1,0:T(8,128)(2,1)} %fusion.37), channel_id=1, source_target_pairs={{0,8},{1,17},{2,10},{3,19},{4,12},{5,21},{6,14},{7,23},{8,0},{9,25... | collective-permute-start | bytes 3538952 | tf_op jit(solution)/shard_map/ppermute | solution.py:156
  171.8 64.4 %collective-permute-start.12 = (bf16[384,512]{1,0:T(8,128)(2,1)}, bf16[384,512]{1,0:T(8,128)(2,1)}, u32[]{:S(2)}, u32[]{:S(2)}) collective-permute-start(bf16[384,512]{1,0:T(8,128)(2,1)} %fusion.59), channel_id=1, source_target_pairs={{0,8},{1,17},{2,10},{3,19},{4,12},{5,21},{6,14},{7,23},{8,0},{9,25... | collective-permute-start | bytes 1179656 | tf_op jit(solution)/shard_map/ppermute | solution.py:156
  186.9 49.3 %collective-permute-start.15 = (bf16[384,1536]{1,0:T(8,128)(2,1)}, bf16[384,1536]{1,0:T(8,128)(2,1)}, u32[]{:S(2)}, u32[]{:S(2)}) collective-permute-start(bf16[384,1536]{1,0:T(8,128)(2,1)} %add_convert_fusion.1), channel_id=1, source_target_pairs={{0,16},{1,9},{2,18},{3,11},{4,20},{5,13},{6,22},{7,15},{8,24},{9,1... | collective-permute-start | bytes 3538952 | tf_op jit(solution)/shard_map/ppermute | solution.py:156
  193.1 49.8 %collective-permute-start.16 = (bf16[384,1536]{1,0:T(8,128)(2,1)}, bf16[384,1536]{1,0:T(8,128)(2,1)}, u32[]{:S(2)}, u32[]{:S(2)}) collective-permute-start(bf16[384,1536]{1,0:T(8,128)(2,1)} %add_convert_fusion), channel_id=1, source_target_pairs={{0,16},{1,9},{2,18},{3,11},{4,20},{5,13},{6,22},{7,15},{8,24},{9,1... | collective-permute-start | bytes 3538952 | tf_op jit(solution)/shard_map/ppermute | solution.py:156
  232.9 4.9 %copy-start = (bf16[384,3584]{1,0:T(8,128)(2,1)S(1)}, bf16[384,3584]{1,0:T(8,128)(2,1)}, u32[]{:S(2)}) copy-start(bf16[384,3584]{1,0:T(8,128)(2,1)} %refs_3_.2) | copy-start | bytes 8257540
  232.9 4.9 %copy-start.1 = (bf16[384,3584]{1,0:T(8,128)(2,1)S(1)}, bf16[384,3584]{1,0:T(8,128)(2,1)}, u32[]{:S(2)}) copy-start(bf16[384,3584]{1,0:T(8,128)(2,1)} %refs_4_.1) | copy-start | bytes 8257540
  236.1 6.8 %copy-start.2 = (f32[384,1536]{1,0:T(8,128)S(1)}, f32[384,1536]{1,0:T(8,128)}, u32[]{:S(2)}) copy-start(f32[384,1536]{1,0:T(8,128)} %fusion.17.refs_0_) | copy-start | bytes 7077892
  236.2 12.4 %collective-permute-start.17 = (bf16[384,512]{1,0:T(8,128)(2,1)S(1)}, bf16[384,512]{1,0:T(8,128)(2,1)S(1)}, u32[]{:S(2)}, u32[]{:S(2)}) collective-permute-start(bf16[384,512]{1,0:T(8,128)(2,1)S(1)} %add_convert_fusion.2), channel_id=1, source_target_pairs={{0,16},{1,9},{2,18},{3,11},{4,20},{5,13},{6,22},{7,15},{8,24},{9,1... | collective-permute-start | bytes 1179656 | tf_op jit(solution)/shard_map/ppermute | solution.py:156
  242.9 5.6 %copy-start.3 = (f32[384,512]{1,0:T(8,128)S(1)}, f32[384,512]{1,0:T(8,128)}, u32[]{:S(2)}) copy-start(f32[384,512]{1,0:T(8,128)} %fusion.55.refs_0_) | copy-start | bytes 2359300
Sparse Core Ops, SparseCore 0:
  55.8 26.7 all-gather.2
  84.7 51.1 all-gather.4

commit v8 on v6

--- a/solution.py
+++ b/solution.py
@@ -75,9 +75,10 @@
     return blocks
 
 
-def gather_tokens(blocks):
+def gather_tokens(blocks, before):
     first = lax.all_gather(blocks[-1], "col", axis=0, tiled=True)
-    rest = lax.all_gather(jnp.stack(blocks[:-1]), "col", axis=1, tiled=True)
+    rest, _ = lax.optimization_barrier((jnp.stack(blocks[:-1]), before))
+    rest = lax.all_gather(rest, "col", axis=1, tiled=True)
     return [rest[flip] for flip in range(len(blocks) - 1)] + [first]
 
 
@@ -144,9 +145,12 @@
     for step in range(1, steps - 1):
         gathered = gathered + [lax.ppermute(part, BOTH, pairs[step]) for part in gathered]
 
-    gathered.append(lax.ppermute(after(hidden, *pieces), BOTH, pairs[-1]))
-
-    blocks = gather_tokens(pieces)
+    little, large = jnp.split(hidden, [tokens // 8])
+    little_came = lax.ppermute(after(little, pieces[-1]), BOTH, pairs[-1])
+    large_came = lax.ppermute(after(large, *pieces, little_came), BOTH, pairs[-1])
+    gathered.append(jnp.concatenate([little_came, large_came]))
+
+    blocks = gather_tokens(pieces, little_came)
     width = down_weight.shape[0]
 
     def product(block, start, stop, *before):
@@ -164,7 +168,7 @@
     total = product(blocks[-1], 0, 3 * unit).astype(jnp.bfloat16)
     for part in gathered[1 : rows // 2]:
         gathered.append(send(after(part, total), steps - 1))
-    rest = product(blocks[-1], 3 * unit, width, total, gathered[rows // 2]).astype(jnp.bfloat16)
+    rest = product(blocks[-1], 3 * unit, width, total, large_came).astype(jnp.bfloat16)
     total = jnp.concatenate([total, rest], axis=1)
     total = after(total, *gathered[rows // 2 + 1 :])
 
@@ -177,7 +181,7 @@
         for place in range(rows)
     ]
 
-    starts, stops = [0, 3 * unit, 6 * unit], [3 * unit, 6 * unit, width]
+    starts, stops = [0, 4 * unit, 6 * unit], [4 * unit, 6 * unit, width]
     chunks = range(len(starts))
     came = [[[] for _ in chunks] for _ in range(rows)]
     whole = send(total, 0)
@@ -200,9 +204,11 @@
             for chunk in chunks:
                 total = message(place, chunk, total)
                 came[place ^ (1 << step)][chunk].append(send(total, step))
-    own = [own_product(0, total)]
-    own.append(own_product(1, own[0]))
-    total = message(rows // 2, 0, own[1])
+    own = []
+    for chunk in chunks:
+        total = own_product(chunk, total)
+        own.append(total)
+    total = message(rows // 2, 0, total)
     last = [send(total, steps - 1)]
 
     gathered, grads, _ = lax.optimization_barrier((gathered, grads, total))
@@ -217,7 +223,6 @@
     last.append(send(total, steps - 1))
     total = after(message(rows // 2, 2, total), last[0])
     last.append(send(total, steps - 1))
-    own.append(own_product(2, total))
 
     gate_act, up_act = after(gate_act, hidden_came), after(up_act, hidden_came)
     outs = []

time: 233 us -> 232 us (level); the launches traced: 233 us -> 228 us
  waiting for transfers between devices: 87.2 us -> 77.9 us
  other arithmetic: 8.57 us -> 11.3 us
    ppermute x8, waiting for transfers between devices: 26 us -> 18.7 us  [send(): return lax.ppermute(total, BOTH, pairs[step])]
    all_gather x1, waiting for transfers between devices: 16.6 us -> 12.1 us  [gather_tokens(): first = lax.all_gather(blocks[-1], 'col', axis=0, tiled=True)]
    ppermute x1 -> x2, waiting for transfers between devices: 7.7 us -> 10.6 us  [the longest x1 8.54 us: on_device(): lax.ppermute(after(large, *pieces, little_came), BOTH, pairs[-1])]
    concatenate x0 -> x1, other arithmetic: none -> 2.69 us  [on_device(): gathered.append(jnp.concatenate([little_came, large_came]))]
  transfers between devices with their start and end apart: 19 -> 20, of which waited for: 11 -> 13; matrix products, arithmetic and copies ran while one was open for 40% -> 42% of each run, Pallas kernels for 4% -> 5%
where the time goes in v8:
time: 232 us; the launch traced here: 228 us
  matrix products  81.3 us (35%)
  waiting for transfers between devices  77.9 us (34%)
  starting transfers between devices  22.3 us (10%)
  between operations  14.3 us (6%)
  Pallas kernels  12.2 us (5%)
  other arithmetic  11.3 us (5%)
  local copies, waits for them, and re-layouts  8.2 us (4%)
    dot_general x11, matrix products, product(): lax.dot_general(after(block, *before), down_weight[start:stop], (((1,), (...  50.8 us
    dot_general x1, matrix products, on_device(): lax.dot_general(jnp.concatenate(gathered, axis=0), jnp.concatenate(grads,...  30.5 us
    ppermute x8, waiting for transfers between devices, send(): return lax.ppermute(total, BOTH, pairs[step])  18.7 us
    ppermute x4, waiting for transfers between devices, spread_tokens(): piece = lax.ppermute(piece, 'col', pairs)  18.5 us
    pallas_call x3, Pallas kernels, finish(): pl.pallas_call(kernel, grid=(width // block,), in_specs=specs, out_specs=...  12.2 us
    all_gather x1, waiting for transfers between devices, gather_tokens(): first = lax.all_gather(blocks[-1], 'col', axis=0, tiled=True)  12.1 us
    ppermute x3, waiting for transfers between devices, spread_tokens(): piece = lax.ppermute(piece, 'row', [(r, r ^ flip) for r in range(rows)])  11.7 us
    ppermute x8, starting transfers between devices, send(): return lax.ppermute(total, BOTH, pairs[step])  8.68 us
  transfers between devices with their start and end apart: 20, of which 13 were waited for; matrix products, arithmetic and copies ran while one was open for 42% of the time, Pallas kernels for 5%

profile of v8, /device:TPU:0, one launch (start us, length us, event | category | flops | bytes accessed | tf_op | source)
XLA Modules:
  0.0 227.5 jit_solution(5598892032549095)
XLA Ops:
  7.2 4.3 %fusion.29 = bf16[384,3584]{1,0:T(8,128)(2,1)S(1)} fusion(bf16[384,3584]{1,0:T(8,128)(2,1)} %refs_4_.1, bf16[384,3584]{1,0:T(8,128)(2,1)} %refs_3_.2), kind=kLoop, calls=%fused_computation.31 | loop fusion | flops 11010048 | bytes 8257536 | tf_op jit(solution)/shard_map/convert_element_type | solution.py:139
  11.5 3.0 %collective-permute-start.5 = (bf16[384,3584]{1,0:T(8,128)(2,1)S(1)}, bf16[384,3584]{1,0:T(8,128)(2,1)}, u32[]{:S(2)}, u32[]{:S(2)}) collective-permute-start(bf16[384,3584]{1,0:T(8,128)(2,1)S(1)} %fusion.29), channel_id=1, source_target_pairs={{0,8},{1,17},{2,10},{3,19},{4,12},{5,21},{6,14},{7,23},{8,0},{9,25... | collective-permute-start | bytes 8257544 | tf_op jit(solution)/shard_map/ppermute | solution.py:142
  14.5 1.9 dynamic-slice_bitcast_fusion
  16.4 1.9 collective-permute-done
  18.7 0.8 constant_dynamic-slice_fusion
  19.5 3.6 %collective-permute-start.3 = (bf16[48,2048]{1,0:T(8,128)(2,1)}, bf16[48,2048]{1,0:T(8,128)(2,1)S(1)}, u32[]{:S(2)}, u32[]{:S(2)}) collective-permute-start(bf16[48,2048]{1,0:T(8,128)(2,1)} %get-tuple-element.107), channel_id=1, source_target_pairs={{0,6},{1,7},{2,4},{3,5},{4,2},{5,3},{6,0},{7,1},{8,14},{9,15},{10,... | collective-permute-start | bytes 589832 | tf_op jit(solution)/shard_map/ppermute | solution.py:61
  23.1 0.8 collective-permute-start.1
  23.9 5.5 %collective-permute-done.3 = bf16[48,2048]{1,0:T(8,128)(2,1)S(1)} collective-permute-done((bf16[48,2048]{1,0:T(8,128)(2,1)}, bf16[48,2048]{1,0:T(8,128)(2,1)S(1)}, u32[]{:S(2)}, u32[]{:S(2)}) %collective-permute-start.3) | collective-permute-done | bytes 196640 | tf_op jit(solution)/shard_map/ppermute | solution.py:61
  29.4 11.0 %collective-permute-done.2 = bf16[48,2048]{1,0:T(8,128)(2,1)} collective-permute-done((bf16[48,2048]{1,0:T(8,128)(2,1)S(1)}, bf16[48,2048]{1,0:T(8,128)(2,1)}, u32[]{:S(2)}, u32[]{:S(2)}) %collective-permute-start.2) | collective-permute-done | bytes 196640 | tf_op jit(solution)/shard_map/ppermute | solution.py:61
  40.4 1.1 pad_maximum_fusion.3
  41.5 0.8 dynamic-slice_bitcast_fusion.5
  42.3 1.8 collective-permute-start.4
  44.1 7.2 %collective-permute-done.4 = bf16[48,2048]{1,0:T(8,128)(2,1)} collective-permute-done((bf16[48,2048]{1,0:T(8,128)(2,1)S(1)}, bf16[48,2048]{1,0:T(8,128)(2,1)}, u32[]{:S(2)}, u32[]{:S(2)}) %collective-permute-start.4) | collective-permute-done | bytes 196640 | tf_op jit(solution)/shard_map/ppermute | solution.py:71
  51.6 1.6 collective-permute-start.6
  53.7 1.6 collective-permute-start.8
  55.3 4.4 %collective-permute-done.6 = bf16[48,2048]{1,0:T(8,128)(2,1)S(1)} collective-permute-done((bf16[48,2048]{1,0:T(8,128)(2,1)}, bf16[48,2048]{1,0:T(8,128)(2,1)S(1)}, u32[]{:S(2)}, u32[]{:S(2)}) %collective-permute-start.6) | collective-permute-done | bytes 196640 | tf_op jit(solution)/shard_map/ppermute | solution.py:71
  59.7 0.9 pad_maximum_fusion.4
  60.6 2.0 collective-permute-done.8
  62.7 1.6 split.9
  64.7 12.1 %all-gather.5.cloned.1.call-done = bf16[384,2048]{1,0:T(8,128)(2,1)} async-done(((bf16[48,2048]{1,0:T(8,128)(2,1)}), bf16[384,2048]{1,0:T(8,128)(2,1)}) %all-gather.5.cloned.1.call-update) | async-done | bytes 1572880 | tf_op jit(solution)/shard_map/all_gather | solution.py:79
  76.9 6.9 %fusion.42 = bf16[384,1536]{1,0:T(8,128)(2,1)} fusion(bf16[384,2048]{1,0:T(8,128)(2,1)} %all-gather.5.cloned.1.call-done, bf16[3584,2048]{1,0:T(8,128)(2,1)} %param.7), kind=kOutput, calls=%fused_computation.41 | convolution fusion | flops 2416508928 | bytes 9043968 | tf_op jit(solution)/shard_map/dot_general | solution.py:157
  83.8 1.5 collective-permute-start.10
  85.3 8.5 %collective-permute-done.9 = bf16[336,3584]{1,0:T(8,128)(2,1)S(1)} collective-permute-done((bf16[336,3584]{1,0:T(8,128)(2,1)}, bf16[336,3584]{1,0:T(8,128)(2,1)S(1)}, u32[]{:S(2)}, u32[]{:S(2)}) %collective-permute-start.9) | collective-permute-done | bytes 2408480 | tf_op jit(solution)/shard_map/ppermute | solution.py:150
  93.8 7.4 %fusion.39 = bf16[384,2048]{1,0:T(8,128)(2,1)S(1)} fusion(bf16[384,2048]{1,0:T(8,128)(2,1)} %all-gather.5.cloned.1.call-done, bf16[3584,2048]{1,0:T(8,128)(2,1)} %param.7), kind=kOutput, calls=%fused_computation.40 | convolution fusion | flops 3222011904 | bytes 11534336 | tf_op jit(solution)/shard_map/dot_general | solution.py:157
  101.2 1.7 pad_maximum_fusion
  103.0 2.7 %pad_maximum_fusion.1 = bf16[384,3584]{1,0:T(8,128)(2,1)} fusion(bf16[336,3584]{1,0:T(8,128)(2,1)S(1)} %collective-permute-done.9, bf16[48,3584]{1,0:T(8,128)(2,1)} %collective-permute-done.8), kind=kLoop, calls=%fused_computation.43 | loop fusion | flops 5505024 | bytes 5505024 | tf_op jit(solution)/shard_map/concatenate | solution.py:151
  105.7 17.7 %collective-permute-done.10 = bf16[384,3584]{1,0:T(8,128)(2,1)} collective-permute-done((bf16[384,3584]{1,0:T(8,128)(2,1)}, bf16[384,3584]{1,0:T(8,128)(2,1)}, u32[]{:S(2)}, u32[]{:S(2)}) %collective-permute-start.10) | collective-permute-done | bytes 2752544 | tf_op jit(solution)/shard_map/ppermute | solution.py:165
  123.4 0.5 collective-permute-start.12
  123.9 6.3 %all-gather.3.cloned.1.call-done = bf16[3,384,2048]{2,1,0:T(8,128)(2,1)} async-done(((bf16[3,48,2048]{2,1,0:T(8,128)(2,1)}), bf16[3,384,2048]{2,1,0:T(8,128)(2,1)}) %all-gather.3.cloned.1.call-update) | async-done | bytes 4718608 | tf_op jit(solution)/shard_map/all_gather | solution.py:81
  130.3 3.1 %slice_bitcast_fusion = (bf16[384,2048]{1,0:T(8,128)(2,1)S(1)}, bf16[384,2048]{1,0:T(8,128)(2,1)S(1)}, bf16[384,2048]{1,0:T(8,128)(2,1)S(1)}) fusion(bf16[3,384,2048]{2,1,0:T(8,128)(2,1)} %all-gather.3.cloned.1.call-done), kind=kLoop, calls=%fused_computation.50 | loop fusion | bytes 9437184 | tf_op jit(solution)/shard_map/squeeze | solution.py:82
  133.7 9.8 %fusion.36 = bf16[384,2048]{1,0:T(8,128)(2,1)} fusion(bf16[384,2048]{1,0:T(8,128)(2,1)S(1)} %get-tuple-element.76, bf16[3584,2048]{1,0:T(8,128)(2,1)} %param.7), kind=kOutput, calls=%fused_computation.39 | convolution fusion | flops 3222011904 | bytes 11534336 | tf_op jit(solution)/shard_map/dot_general | solution.py:157
  143.5 2.7 %fusion.51 = bf16[384,1024]{1,0:T(8,128)(2,1)} fusion(bf16[384,2048]{1,0:T(8,128)(2,1)S(1)} %get-tuple-element.76, bf16[3584,2048]{1,0:T(8,128)(2,1)S(1)} %bitcast.54), kind=kOutput, calls=%fused_computation.56 | convolution fusion | flops 1611005952 | bytes 6553600 | tf_op jit(solution)/shard_map/dot_general | solution.py:157
  146.2 1.5 collective-permute-start.13
  147.7 0.5 collective-permute-start.14
  148.3 2.0 fusion.54
  150.2 1.5 collective-permute-start.11
  151.7 3.5 %fusion.12.own_ref = f32[384,2048]{1,0:T(8,128)S(1)} fusion(bf16[384,2048]{1,0:T(8,128)(2,1)S(1)} %get-tuple-element.75, bf16[3584,2048]{1,0:T(8,128)(2,1)S(1)} %bitcast.54), kind=kOutput, calls=%fused_computation.14 | convolution fusion | flops 3221225472 | bytes 13107200 | tf_op jit(solution)/shard_map/dot_general | solution.py:157
  155.2 3.0 %fusion.32.refs_0_ = f32[384,1024]{1,0:T(8,128)} fusion(bf16[384,2048]{1,0:T(8,128)(2,1)S(1)} %get-tuple-element.75, bf16[3584,2048]{1,0:T(8,128)(2,1)S(1)} %bitcast.54), kind=kOutput, calls=%fused_computation.34 | convolution fusion | flops 1610612736 | bytes 7340032 | tf_op jit(solution)/shard_map/dot_general | solution.py:157
  158.2 1.9 fusion.47.refs_0_
  160.1 5.7 %add_convert_fusion = bf16[384,2048]{1,0:T(8,128)(2,1)} fusion(bf16[384,3584]{1,0:T(8,128)(2,1)} %collective-permute-done.12, bf16[384,2048]{1,0:T(8,128)(2,1)S(1)} %get-tuple-element.92, bf16[3584,2048]{1,0:T(8,128)(2,1)S(1)} %bitcast.54), kind=kOutput, calls=%fused_computation.38 | convolution fusion | flops 3223584768 | bytes 13107200 | tf_op jit(solution)/shard_map/dot_general | solution.py:157
  165.9 1.5 collective-permute-start.15
  167.3 30.5 %fusion = f32[3584,2048]{1,0:T(8,128)} fusion(bf16[384,3584]{1,0:T(8,128)(2,1)} %collective-permute-done.10, bf16[384,3584]{1,0:T(8,128)(2,1)} %pad_maximum_fusion.1, bf16[384,3584]{1,0:T(8,128)(2,1)} %collective-permute-done.5, bf16[384,3584]{1,0:T(8,128)(2,1)} %copy-done.4, bf16[384,2048]{1,0:T(8,128)(2,1)} %all-gather.5.cloned.1.call-done, ...), kind=kOutput, calls=%fused_computation | convolution fusion | flops 22617784320 | bytes 46661632 | tf_op jit(solution)/shard_map/dot_general | solution.py:215
  197.9 4.8 %add_convert_fusion.1 = bf16[384,1024]{1,0:T(8,128)(2,1)S(1)} fusion(bf16[384,3584]{1,0:T(8,128)(2,1)} %collective-permute-done.12, bf16[384,2048]{1,0:T(8,128)(2,1)} %copy-done.6, bf16[3584,2048]{1,0:T(8,128)(2,1)} %param.7), kind=kOutput, calls=%fused_computation.53 | convolution fusion | flops 1611792384 | bytes 7340032 | tf_op jit(solution)/shard_map/dot_general | solution.py:157
  203.5 3.1 %add_convert_fusion.2 = bf16[384,512]{1,0:T(8,128)(2,1)S(1)} fusion(bf16[384,3584]{1,0:T(8,128)(2,1)} %collective-permute-done.12, bf16[384,2048]{1,0:T(8,128)(2,1)S(1)} %copy-done.7, bf16[3584,2048]{1,0:T(8,128)(2,1)} %param.7), kind=kOutput, calls=%fused_computation.64 | convolution fusion | flops 805896192 | bytes 4456448 | tf_op jit(solution)/shard_map/dot_general | solution.py:157
  206.6 1.2 collective-permute-start.17
  207.8 6.9 %shard_map.67 = (bf16[384,3584]{1,0:T(8,128)(2,1)}, bf16[384,3584]{1,0:T(8,128)(2,1)}) custom-call(f32[384,2048]{1,0:T(8,128)S(1)} %fusion.12.own_ref, bf16[384,2048]{1,0:T(8,128)(2,1)} %collective-permute-done.14.refs_0_, bf16[384,2048]{1,0:T(8,128)(2,1)} %collective-permute-done.15.refs_1_, bf16[384,3584]{1,0:T(8,128)(2,1)S(1)} %copy-done, ...), custom_call_target="tpu_custom_call" | custom-call | tf_op jit(solution)/shard_map/pallas_call | solution.py:117
  215.0 3.9 %shard_map.68 = (bf16[384,3584]{1,0:T(8,128)(2,1)}, bf16[384,3584]{1,0:T(8,128)(2,1)}) custom-call(f32[384,1024]{1,0:T(8,128)S(1)} %copy-done.2, bf16[384,1024]{1,0:T(8,128)(2,1)} %collective-permute-done.13.refs_1_, bf16[384,1024]{1,0:T(8,128)(2,1)S(1)} %collective-permute-done.16.refs_2_, ...), custom_call_target="tpu_custom_call", output_to_operand_aliasing={{0}: (5, {}), {1}: (6, {})} | custom-call | tf_op jit(solution)/shard_map/pallas_call | solution.py:117
  219.2 1.4 shard_map.69
  (52 shorter events, 3.5 us)
Async XLA Ops:
  7.2 69.7 %all-gather.5.cloned.1.call-start = ((), (), s32[]{:S(2)}) async-start(), calls=%async_computation.1 | async-start | bytes 1769472 | tf_op jit(solution)/shard_map/all_gather | solution.py:79
  11.5 51.2 %copy-start.4 = (bf16[384,3584]{1,0:T(8,128)(2,1)}, bf16[384,3584]{1,0:T(8,128)(2,1)S(1)}, u32[]{:S(2)}) copy-start(bf16[384,3584]{1,0:T(8,128)(2,1)S(1)} %fusion.29) | copy-start | bytes 8257540
  11.5 39.8 %collective-permute-start.5 = (bf16[384,3584]{1,0:T(8,128)(2,1)S(1)}, bf16[384,3584]{1,0:T(8,128)(2,1)}, u32[]{:S(2)}, u32[]{:S(2)}) collective-permute-start(bf16[384,3584]{1,0:T(8,128)(2,1)S(1)} %fusion.29), channel_id=1, source_target_pairs={{0,8},{1,17},{2,10},{3,19},{4,12},{5,21},{6,14},{7,23},{8,0},{9,25... | collective-permute-start | bytes 8257544 | tf_op jit(solution)/shard_map/ppermute | solution.py:142
  16.4 1.9 collective-permute-start
  19.5 9.9 %collective-permute-start.3 = (bf16[48,2048]{1,0:T(8,128)(2,1)}, bf16[48,2048]{1,0:T(8,128)(2,1)S(1)}, u32[]{:S(2)}, u32[]{:S(2)}) collective-permute-start(bf16[48,2048]{1,0:T(8,128)(2,1)} %get-tuple-element.107), channel_id=1, source_target_pairs={{0,6},{1,7},{2,4},{3,5},{4,2},{5,3},{6,0},{7,1},{8,14},{9,15},{10,... | collective-permute-start | bytes 589832 | tf_op jit(solution)/shard_map/ppermute | solution.py:61
  23.1 17.3 %collective-permute-start.2 = (bf16[48,2048]{1,0:T(8,128)(2,1)S(1)}, bf16[48,2048]{1,0:T(8,128)(2,1)}, u32[]{:S(2)}, u32[]{:S(2)}) collective-permute-start(bf16[48,2048]{1,0:T(8,128)(2,1)S(1)} %get-tuple-element.108), channel_id=1, source_target_pairs={{0,4},{1,5},{2,6},{3,7},{4,0},{5,1},{6,2},{7,3},{8,12},{9,13},{10,... | collective-permute-start | bytes 589832 | tf_op jit(solution)/shard_map/ppermute | solution.py:61
  23.1 17.3 %collective-permute-start.1 = (bf16[48,2048]{1,0:T(8,128)(2,1)S(1)}, bf16[48,2048]{1,0:T(8,128)(2,1)}, u32[]{:S(2)}, u32[]{:S(2)}) collective-permute-start(bf16[48,2048]{1,0:T(8,128)(2,1)S(1)} %get-tuple-element.109), channel_id=1, source_target_pairs={{0,2},{1,3},{2,0},{3,1},{4,6},{5,7},{6,4},{7,5},{8,10},{9,11},{10,... | collective-permute-start | bytes 589832 | tf_op jit(solution)/shard_map/ppermute | solution.py:61
  42.3 9.1 %collective-permute-start.4 = (bf16[48,2048]{1,0:T(8,128)(2,1)S(1)}, bf16[48,2048]{1,0:T(8,128)(2,1)}, u32[]{:S(2)}, u32[]{:S(2)}) collective-permute-start(bf16[48,2048]{1,0:T(8,128)(2,1)S(1)} %get-tuple-element.105), channel_id=1, source_target_pairs={{0,24},{8,16},{16,8},{24,0},{1,25},{9,17},{17,9},{25,1},{2,26},{10... | collective-permute-start | bytes 589832 | tf_op jit(solution)/shard_map/ppermute | solution.py:71
  51.4 78.9 %all-gather.3.cloned.1.call-start = ((), (), s32[]{:S(2)}) async-start(), calls=%async_computation | async-start | bytes 5308416 | tf_op jit(solution)/shard_map/all_gather | solution.py:81
  51.6 8.1 %collective-permute-start.6 = (bf16[48,2048]{1,0:T(8,128)(2,1)}, bf16[48,2048]{1,0:T(8,128)(2,1)S(1)}, u32[]{:S(2)}, u32[]{:S(2)}) collective-permute-start(bf16[48,2048]{1,0:T(8,128)(2,1)} %get-tuple-element.53), channel_id=1, source_target_pairs={{0,8},{8,0},{16,24},{24,16},{1,9},{9,1},{17,25},{25,17},{2,10},{10... | collective-permute-start | bytes 589832 | tf_op jit(solution)/shard_map/ppermute | solution.py:71
  53.2 6.6 %collective-permute-start.7 = (bf16[48,2048]{1,0:T(8,128)(2,1)S(1)}, bf16[48,2048]{1,0:T(8,128)(2,1)S(1)}, u32[]{:S(2)}, u32[]{:S(2)}) collective-permute-start(bf16[48,2048]{1,0:T(8,128)(2,1)S(1)} %get-tuple-element.54), channel_id=1, source_target_pairs={{0,16},{8,24},{16,0},{24,8},{1,17},{9,25},{17,1},{25,9},{2,18},{10... | collective-permute-start | bytes 589832 | tf_op jit(solution)/shard_map/ppermute | solution.py:71
  53.7 8.9 %collective-permute-start.8 = (bf16[48,3584]{1,0:T(8,128)(2,1)S(1)}, bf16[48,3584]{1,0:T(8,128)(2,1)}, u32[]{:S(2)}, u32[]{:S(2)}) collective-permute-start(bf16[48,3584]{1,0:T(8,128)(2,1)S(1)} %split.8), channel_id=1, source_target_pairs={{0,16},{1,9},{2,18},{3,11},{4,20},{5,13},{6,22},{7,15},{8,24},{9,1... | collective-permute-start | bytes 1032200 | tf_op jit(solution)/shard_map/ppermute | solution.py:149
  64.2 29.6 %collective-permute-start.9 = (bf16[336,3584]{1,0:T(8,128)(2,1)}, bf16[336,3584]{1,0:T(8,128)(2,1)S(1)}, u32[]{:S(2)}, u32[]{:S(2)}) collective-permute-start(bf16[336,3584]{1,0:T(8,128)(2,1)} %split.9), channel_id=1, source_target_pairs={{0,16},{1,9},{2,18},{3,11},{4,20},{5,13},{6,22},{7,15},{8,24},{9,1... | collective-permute-start | bytes 7225352 | tf_op jit(solution)/shard_map/ppermute | solution.py:150
  83.8 39.6 %collective-permute-start.10 = (bf16[384,3584]{1,0:T(8,128)(2,1)}, bf16[384,3584]{1,0:T(8,128)(2,1)}, u32[]{:S(2)}, u32[]{:S(2)}) collective-permute-start(bf16[384,3584]{1,0:T(8,128)(2,1)} %collective-permute-done.5), channel_id=1, source_target_pairs={{0,16},{1,9},{2,18},{3,11},{4,20},{5,13},{6,22},{7,15},{8,24},{9,1... | collective-permute-start | bytes 8257544 | tf_op jit(solution)/shard_map/ppermute | solution.py:165
  85.3 16.0 %copy-start.9 = (bf16[384,1536]{1,0:T(8,128)(2,1)S(1)}, bf16[384,1536]{1,0:T(8,128)(2,1)}, u32[]{:S(2)}) copy-start(bf16[384,1536]{1,0:T(8,128)(2,1)} %fusion.42) | copy-start | bytes 3538948
  123.4 36.7 %collective-permute-start.12 = (bf16[384,3584]{1,0:T(8,128)(2,1)}, bf16[384,3584]{1,0:T(8,128)(2,1)}, u32[]{:S(2)}, u32[]{:S(2)}) collective-permute-start(bf16[384,3584]{1,0:T(8,128)(2,1)} %pad_maximum_fusion), channel_id=1, source_target_pairs={{0,8},{1,17},{2,10},{3,19},{4,12},{5,21},{6,14},{7,23},{8,0},{9,25... | collective-permute-start | bytes 8257544 | tf_op jit(solution)/shard_map/ppermute | solution.py:165
  130.3 13.2 %slice-start = ((s8[14680064]{0:T(1024)(128)(4,1)}), s8[4194304]{0:T(1024)(128)(4,1)S(1)}, s32[]{:S(2)}) async-start(s8[14680064]{0:T(1024)(128)(4,1)} %bitcast.53), calls=%async_computation.2 | async-start | bytes 8388608
  133.4 24.8 %copy-start.5 = (bf16[384,2048]{1,0:T(8,128)(2,1)}, bf16[384,2048]{1,0:T(8,128)(2,1)S(1)}, u32[]{:S(2)}) copy-start(bf16[384,2048]{1,0:T(8,128)(2,1)S(1)} %get-tuple-element.75) | copy-start | bytes 4718596
  133.4 10.1 %slice-start.1 = ((s8[14680064]{0:T(1024)(128)(4,1)}), s8[4194304]{0:T(1024)(128)(4,1)S(1)}, s32[]{:S(2)}) async-start(s8[14680064]{0:T(1024)(128)(4,1)} %bitcast.53), calls=%async_computation.3 | async-start | bytes 8388608
  133.6 14.6 %copy-start.8 = (bf16[384,2048]{1,0:T(8,128)(2,1)}, bf16[384,2048]{1,0:T(8,128)(2,1)S(1)}, u32[]{:S(2)}) copy-start(bf16[384,2048]{1,0:T(8,128)(2,1)S(1)} %get-tuple-element.76) | copy-start | bytes 4718596
  133.6 26.5 %copy-start.6 = (bf16[384,2048]{1,0:T(8,128)(2,1)}, bf16[384,2048]{1,0:T(8,128)(2,1)S(1)}, u32[]{:S(2)}) copy-start(bf16[384,2048]{1,0:T(8,128)(2,1)S(1)} %get-tuple-element.92) | copy-start | bytes 4718596
  133.6 9.8 %slice-start.2 = ((s8[14680064]{0:T(1024)(128)(4,1)}), s8[4194304]{0:T(1024)(128)(4,1)S(1)}, s32[]{:S(2)}) async-start(s8[14680064]{0:T(1024)(128)(4,1)} %bitcast.53), calls=%async_computation.4 | async-start | bytes 8388608
  133.7 9.8 %slice-start.3 = ((s8[14680064]{0:T(1024)(128)(4,1)}), s8[2097152]{0:T(1024)(128)(4,1)S(1)}, s32[]{:S(2)}) async-start(s8[14680064]{0:T(1024)(128)(4,1)} %bitcast.53), calls=%async_computation.5 | async-start | bytes 4194304
  146.2 56.8 %collective-permute-start.13 = (bf16[384,1024]{1,0:T(8,128)(2,1)}, bf16[384,1024]{1,0:T(8,128)(2,1)}, u32[]{:S(2)}, u32[]{:S(2)}) collective-permute-start(bf16[384,1024]{1,0:T(8,128)(2,1)} %fusion.51), channel_id=1, source_target_pairs={{0,8},{1,17},{2,10},{3,19},{4,12},{5,21},{6,14},{7,23},{8,0},{9,25... | collective-permute-start | bytes 2359304 | tf_op jit(solution)/shard_map/ppermute | solution.py:165
  147.7 55.3 %collective-permute-start.14 = (bf16[384,2048]{1,0:T(8,128)(2,1)}, bf16[384,2048]{1,0:T(8,128)(2,1)}, u32[]{:S(2)}, u32[]{:S(2)}) collective-permute-start(bf16[384,2048]{1,0:T(8,128)(2,1)} %fusion.36), channel_id=1, source_target_pairs={{0,8},{1,17},{2,10},{3,19},{4,12},{5,21},{6,14},{7,23},{8,0},{9,25... | collective-permute-start | bytes 4718600 | tf_op jit(solution)/shard_map/ppermute | solution.py:165
  150.2 52.8 %collective-permute-start.11 = (bf16[384,512]{1,0:T(8,128)(2,1)}, bf16[384,512]{1,0:T(8,128)(2,1)S(1)}, u32[]{:S(2)}, u32[]{:S(2)}) collective-permute-start(bf16[384,512]{1,0:T(8,128)(2,1)} %fusion.54), channel_id=1, source_target_pairs={{0,8},{1,17},{2,10},{3,19},{4,12},{5,21},{6,14},{7,23},{8,0},{9,25... | collective-permute-start | bytes 1179656 | tf_op jit(solution)/shard_map/ppermute | solution.py:165
  165.9 40.8 %collective-permute-start.15 = (bf16[384,2048]{1,0:T(8,128)(2,1)}, bf16[384,2048]{1,0:T(8,128)(2,1)}, u32[]{:S(2)}, u32[]{:S(2)}) collective-permute-start(bf16[384,2048]{1,0:T(8,128)(2,1)} %add_convert_fusion), channel_id=1, source_target_pairs={{0,16},{1,9},{2,18},{3,11},{4,20},{5,13},{6,22},{7,15},{8,24},{9,1... | collective-permute-start | bytes 4718600 | tf_op jit(solution)/shard_map/ppermute | solution.py:165
  197.9 5.7 %copy-start.7 = (bf16[384,2048]{1,0:T(8,128)(2,1)S(1)}, bf16[384,2048]{1,0:T(8,128)(2,1)}, u32[]{:S(2)}) copy-start(bf16[384,2048]{1,0:T(8,128)(2,1)} %copy-done.6) | copy-start | bytes 4718596
  202.7 5.1 %copy-start = (bf16[384,3584]{1,0:T(8,128)(2,1)S(1)}, bf16[384,3584]{1,0:T(8,128)(2,1)}, u32[]{:S(2)}) copy-start(bf16[384,3584]{1,0:T(8,128)(2,1)} %refs_3_.2) | copy-start | bytes 8257540
  202.7 5.1 %copy-start.1 = (bf16[384,3584]{1,0:T(8,128)(2,1)S(1)}, bf16[384,3584]{1,0:T(8,128)(2,1)}, u32[]{:S(2)}) copy-start(bf16[384,3584]{1,0:T(8,128)(2,1)} %refs_4_.1) | copy-start | bytes 8257540
  203.0 12.0 %collective-permute-start.16 = (bf16[384,1024]{1,0:T(8,128)(2,1)S(1)}, bf16[384,1024]{1,0:T(8,128)(2,1)S(1)}, u32[]{:S(2)}, u32[]{:S(2)}) collective-permute-start(bf16[384,1024]{1,0:T(8,128)(2,1)S(1)} %add_convert_fusion.1), channel_id=1, source_target_pairs={{0,16},{1,9},{2,18},{3,11},{4,20},{5,13},{6,22},{7,15},{8,24},{9,1... | collective-permute-start | bytes 2359304 | tf_op jit(solution)/shard_map/ppermute | solution.py:165
  206.6 8.4 %copy-start.2 = (f32[384,1024]{1,0:T(8,128)S(1)}, f32[384,1024]{1,0:T(8,128)}, u32[]{:S(2)}) copy-start(f32[384,1024]{1,0:T(8,128)} %fusion.32.refs_0_) | copy-start | bytes 4718596
  206.6 12.6 %collective-permute-start.17 = (bf16[384,512]{1,0:T(8,128)(2,1)S(1)}, bf16[384,512]{1,0:T(8,128)(2,1)S(1)}, u32[]{:S(2)}, u32[]{:S(2)}) collective-permute-start(bf16[384,512]{1,0:T(8,128)(2,1)S(1)} %add_convert_fusion.2), channel_id=1, source_target_pairs={{0,16},{1,9},{2,18},{3,11},{4,20},{5,13},{6,22},{7,15},{8,24},{9,1... | collective-permute-start | bytes 1179656 | tf_op jit(solution)/shard_map/ppermute | solution.py:165
  214.7 4.5 %copy-start.3 = (f32[384,512]{1,0:T(8,128)S(1)}, f32[384,512]{1,0:T(8,128)}, u32[]{:S(2)}) copy-start(f32[384,512]{1,0:T(8,128)} %fusion.47.refs_0_) | copy-start | bytes 2359300
Sparse Core Ops, SparseCore 0:
  51.5 25.3 all-gather.4
  79.0 51.1 all-gather.2

commit v9 on v8

--- a/solution.py
+++ b/solution.py
@@ -184,9 +184,9 @@
     starts, stops = [0, 4 * unit, 6 * unit], [4 * unit, 6 * unit, width]
     chunks = range(len(starts))
     came = [[[] for _ in chunks] for _ in range(rows)]
-    whole = send(total, 0)
+    whole = send(total, steps - 1)
     for chunk in chunks:
-        came[rows - 2][chunk].append(whole[:, starts[chunk] : stops[chunk]])
+        came[rows // 2 - 1][chunk].append(whole[:, starts[chunk] : stops[chunk]])
 
     def message(place, chunk, *before):
         total = product(grads[place], starts[chunk], stops[chunk], *before)
@@ -197,9 +197,9 @@
     def own_product(chunk, *before):
         return product(grads[0], starts[chunk], stops[chunk], *before)
 
-    for step in range(steps - 1):
-        for place in reversed(range(rows - 1)):
-            if place & ((1 << step) - 1) or not place >> step & 1:
+    for step in reversed(range(1, steps)):
+        for place in reversed(range(1 << step, 2 << step)):
+            if place == rows - 1:
                 continue
             for chunk in chunks:
                 total = message(place, chunk, total)
@@ -208,8 +208,8 @@
     for chunk in chunks:
         total = own_product(chunk, total)
         own.append(total)
-    total = message(rows // 2, 0, total)
-    last = [send(total, steps - 1)]
+    total = message(1, 0, total)
+    last = [send(total, 0)]
 
     gathered, grads, _ = lax.optimization_barrier((gathered, grads, total))
     grad_weight = lax.dot_general(
@@ -219,10 +219,10 @@
         preferred_element_type=jnp.float32,
     )
 
-    total = after(message(rows // 2, 1, grad_weight), *sum(came[0], []))
-    last.append(send(total, steps - 1))
-    total = after(message(rows // 2, 2, total), last[0])
-    last.append(send(total, steps - 1))
+    total = after(message(1, 1, grad_weight), *sum(came[0], []))
+    last.append(send(total, 0))
+    total = after(message(1, 2, total), last[0])
+    last.append(send(total, 0))
 
     gate_act, up_act = after(gate_act, hidden_came), after(up_act, hidden_came)
     outs = []

time: 232 us -> 228 us (0.983); the launches traced: 228 us -> 228 us
  no operation moved by 1% of the time
where the time goes in v9:
time: 228 us
  matrix products  81.3 us (36%)
  waiting for transfers between devices  77.9 us (34%)
  starting transfers between devices  22.3 us (10%)
  between operations  14.3 us (6%)
  Pallas kernels  12.2 us (5%)
  other arithmetic  11.3 us (5%)
  local copies, waits for them, and re-layouts  8.2 us (4%)
    dot_general x11, matrix products, product(): lax.dot_general(after(block, *before), down_weight[start:stop], (((1,), (...  50.8 us
    dot_general x1, matrix products, on_device(): lax.dot_general(jnp.concatenate(gathered, axis=0), jnp.concatenate(grads,...  30.5 us
    ppermute x8, waiting for transfers between devices, send(): return lax.ppermute(total, BOTH, pairs[step])  18.7 us
    ppermute x4, waiting for transfers between devices, spread_tokens(): piece = lax.ppermute(piece, 'col', pairs)  18.5 us
    pallas_call x3, Pallas kernels, finish(): pl.pallas_call(kernel, grid=(width // block,), in_specs=specs, out_specs=...  12.2 us
    all_gather x1, waiting for transfers between devices, gather_tokens(): first = lax.all_gather(blocks[-1], 'col', axis=0, tiled=True)  12.1 us
    ppermute x3, waiting for transfers between devices, spread_tokens(): piece = lax.ppermute(piece, 'row', [(r, r ^ flip) for r in range(rows)])  11.7 us
    ppermute x8, starting transfers between devices, send(): return lax.ppermute(total, BOTH, pairs[step])  8.64 us
  transfers between devices with their start and end apart: 20, of which 13 were waited for; matrix products, arithmetic and copies ran while one was open for 42% of the time, Pallas kernels for 5%

profile of v9, /device:TPU:0, one launch (start us, length us, event | category | flops | bytes accessed | tf_op | source)
XLA Modules:
  0.0 227.5 jit_solution(3212549675024823025)
XLA Ops:
  7.2 4.3 %fusion.29 = bf16[384,3584]{1,0:T(8,128)(2,1)S(1)} fusion(bf16[384,3584]{1,0:T(8,128)(2,1)} %refs_4_.1, bf16[384,3584]{1,0:T(8,128)(2,1)} %refs_3_.2), kind=kLoop, calls=%fused_computation.31 | loop fusion | flops 11010048 | bytes 8257536 | tf_op jit(solution)/shard_map/convert_element_type | solution.py:139
  11.5 3.0 %collective-permute-start.5 = (bf16[384,3584]{1,0:T(8,128)(2,1)S(1)}, bf16[384,3584]{1,0:T(8,128)(2,1)}, u32[]{:S(2)}, u32[]{:S(2)}) collective-permute-start(bf16[384,3584]{1,0:T(8,128)(2,1)S(1)} %fusion.29), channel_id=1, source_target_pairs={{0,8},{1,17},{2,10},{3,19},{4,12},{5,21},{6,14},{7,23},{8,0},{9,25... | collective-permute-start | bytes 8257544 | tf_op jit(solution)/shard_map/ppermute | solution.py:142
  14.5 1.9 dynamic-slice_bitcast_fusion
  16.4 1.9 collective-permute-done
  18.7 0.8 constant_dynamic-slice_fusion
  19.5 3.6 %collective-permute-start.3 = (bf16[48,2048]{1,0:T(8,128)(2,1)}, bf16[48,2048]{1,0:T(8,128)(2,1)S(1)}, u32[]{:S(2)}, u32[]{:S(2)}) collective-permute-start(bf16[48,2048]{1,0:T(8,128)(2,1)} %get-tuple-element.107), channel_id=1, source_target_pairs={{0,6},{1,7},{2,4},{3,5},{4,2},{5,3},{6,0},{7,1},{8,14},{9,15},{10,... | collective-permute-start | bytes 589832 | tf_op jit(solution)/shard_map/ppermute | solution.py:61
  23.1 0.8 collective-permute-start.1
  23.9 5.5 %collective-permute-done.3 = bf16[48,2048]{1,0:T(8,128)(2,1)S(1)} collective-permute-done((bf16[48,2048]{1,0:T(8,128)(2,1)}, bf16[48,2048]{1,0:T(8,128)(2,1)S(1)}, u32[]{:S(2)}, u32[]{:S(2)}) %collective-permute-start.3) | collective-permute-done | bytes 196640 | tf_op jit(solution)/shard_map/ppermute | solution.py:61
  29.4 11.0 %collective-permute-done.2 = bf16[48,2048]{1,0:T(8,128)(2,1)} collective-permute-done((bf16[48,2048]{1,0:T(8,128)(2,1)S(1)}, bf16[48,2048]{1,0:T(8,128)(2,1)}, u32[]{:S(2)}, u32[]{:S(2)}) %collective-permute-start.2) | collective-permute-done | bytes 196640 | tf_op jit(solution)/shard_map/ppermute | solution.py:61
  40.4 1.1 pad_maximum_fusion.3
  41.5 0.8 dynamic-slice_bitcast_fusion.5
  42.3 1.8 collective-permute-start.4
  44.1 7.2 %collective-permute-done.4 = bf16[48,2048]{1,0:T(8,128)(2,1)} collective-permute-done((bf16[48,2048]{1,0:T(8,128)(2,1)S(1)}, bf16[48,2048]{1,0:T(8,128)(2,1)}, u32[]{:S(2)}, u32[]{:S(2)}) %collective-permute-start.4) | collective-permute-done | bytes 196640 | tf_op jit(solution)/shard_map/ppermute | solution.py:71
  51.6 1.6 collective-permute-start.6
  53.7 1.6 collective-permute-start.8
  55.3 4.4 %collective-permute-done.6 = bf16[48,2048]{1,0:T(8,128)(2,1)S(1)} collective-permute-done((bf16[48,2048]{1,0:T(8,128)(2,1)}, bf16[48,2048]{1,0:T(8,128)(2,1)S(1)}, u32[]{:S(2)}, u32[]{:S(2)}) %collective-permute-start.6) | collective-permute-done | bytes 196640 | tf_op jit(solution)/shard_map/ppermute | solution.py:71
  59.7 0.9 pad_maximum_fusion.4
  60.6 2.0 collective-permute-done.8
  62.7 1.6 split.9
  64.7 12.1 %all-gather.5.cloned.1.call-done = bf16[384,2048]{1,0:T(8,128)(2,1)} async-done(((bf16[48,2048]{1,0:T(8,128)(2,1)}), bf16[384,2048]{1,0:T(8,128)(2,1)}) %all-gather.5.cloned.1.call-update) | async-done | bytes 1572880 | tf_op jit(solution)/shard_map/all_gather | solution.py:79
  76.9 6.9 %fusion.42 = bf16[384,1536]{1,0:T(8,128)(2,1)} fusion(bf16[384,2048]{1,0:T(8,128)(2,1)} %all-gather.5.cloned.1.call-done, bf16[3584,2048]{1,0:T(8,128)(2,1)} %param.7), kind=kOutput, calls=%fused_computation.41 | convolution fusion | flops 2416508928 | bytes 9043968 | tf_op jit(solution)/shard_map/dot_general | solution.py:157
  83.8 1.5 collective-permute-start.10
  85.3 8.5 %collective-permute-done.9 = bf16[336,3584]{1,0:T(8,128)(2,1)S(1)} collective-permute-done((bf16[336,3584]{1,0:T(8,128)(2,1)}, bf16[336,3584]{1,0:T(8,128)(2,1)S(1)}, u32[]{:S(2)}, u32[]{:S(2)}) %collective-permute-start.9) | collective-permute-done | bytes 2408480 | tf_op jit(solution)/shard_map/ppermute | solution.py:150
  93.8 7.4 %fusion.39 = bf16[384,2048]{1,0:T(8,128)(2,1)S(1)} fusion(bf16[384,2048]{1,0:T(8,128)(2,1)} %all-gather.5.cloned.1.call-done, bf16[3584,2048]{1,0:T(8,128)(2,1)} %param.7), kind=kOutput, calls=%fused_computation.40 | convolution fusion | flops 3222011904 | bytes 11534336 | tf_op jit(solution)/shard_map/dot_general | solution.py:157
  101.2 1.7 pad_maximum_fusion
  103.0 2.7 %pad_maximum_fusion.1 = bf16[384,3584]{1,0:T(8,128)(2,1)} fusion(bf16[336,3584]{1,0:T(8,128)(2,1)S(1)} %collective-permute-done.9, bf16[48,3584]{1,0:T(8,128)(2,1)} %collective-permute-done.8), kind=kLoop, calls=%fused_computation.43 | loop fusion | flops 5505024 | bytes 5505024 | tf_op jit(solution)/shard_map/concatenate | solution.py:151
  105.7 17.7 %collective-permute-done.10 = bf16[384,3584]{1,0:T(8,128)(2,1)} collective-permute-done((bf16[384,3584]{1,0:T(8,128)(2,1)}, bf16[384,3584]{1,0:T(8,128)(2,1)}, u32[]{:S(2)}, u32[]{:S(2)}) %collective-permute-start.10) | collective-permute-done | bytes 2752544 | tf_op jit(solution)/shard_map/ppermute | solution.py:165
  123.9 6.4 %all-gather.3.cloned.1.call-done = bf16[3,384,2048]{2,1,0:T(8,128)(2,1)} async-done(((bf16[3,48,2048]{2,1,0:T(8,128)(2,1)}), bf16[3,384,2048]{2,1,0:T(8,128)(2,1)}) %all-gather.3.cloned.1.call-update) | async-done | bytes 4718608 | tf_op jit(solution)/shard_map/all_gather | solution.py:81
  130.3 3.1 %slice_bitcast_fusion = (bf16[384,2048]{1,0:T(8,128)(2,1)S(1)}, bf16[384,2048]{1,0:T(8,128)(2,1)S(1)}, bf16[384,2048]{1,0:T(8,128)(2,1)S(1)}) fusion(bf16[3,384,2048]{2,1,0:T(8,128)(2,1)} %all-gather.3.cloned.1.call-done), kind=kLoop, calls=%fused_computation.50 | loop fusion | bytes 9437184 | tf_op jit(solution)/shard_map/squeeze | solution.py:82
  133.7 9.8 %fusion.36 = bf16[384,2048]{1,0:T(8,128)(2,1)} fusion(bf16[384,2048]{1,0:T(8,128)(2,1)S(1)} %get-tuple-element.77, bf16[3584,2048]{1,0:T(8,128)(2,1)} %param.7), kind=kOutput, calls=%fused_computation.39 | convolution fusion | flops 3222011904 | bytes 11534336 | tf_op jit(solution)/shard_map/dot_general | solution.py:157
  143.5 2.7 %fusion.51 = bf16[384,1024]{1,0:T(8,128)(2,1)} fusion(bf16[384,2048]{1,0:T(8,128)(2,1)S(1)} %get-tuple-element.77, bf16[3584,2048]{1,0:T(8,128)(2,1)S(1)} %bitcast.54), kind=kOutput, calls=%fused_computation.56 | convolution fusion | flops 1611005952 | bytes 6553600 | tf_op jit(solution)/shard_map/dot_general | solution.py:157
  146.2 1.5 collective-permute-start.13
  147.7 0.5 collective-permute-start.14
  148.3 2.0 fusion.54
  150.2 1.5 collective-permute-start.11
  151.7 3.5 %fusion.12.own_ref = f32[384,2048]{1,0:T(8,128)S(1)} fusion(bf16[384,2048]{1,0:T(8,128)(2,1)S(1)} %get-tuple-element.75, bf16[3584,2048]{1,0:T(8,128)(2,1)S(1)} %bitcast.54), kind=kOutput, calls=%fused_computation.14 | convolution fusion | flops 3221225472 | bytes 13107200 | tf_op jit(solution)/shard_map/dot_general | solution.py:157
  155.2 3.0 %fusion.32.refs_0_ = f32[384,1024]{1,0:T(8,128)} fusion(bf16[384,2048]{1,0:T(8,128)(2,1)S(1)} %get-tuple-element.75, bf16[3584,2048]{1,0:T(8,128)(2,1)S(1)} %bitcast.54), kind=kOutput, calls=%fused_computation.34 | convolution fusion | flops 1610612736 | bytes 7340032 | tf_op jit(solution)/shard_map/dot_general | solution.py:157
  158.2 1.9 fusion.47.refs_0_
  160.1 5.7 %add_convert_fusion = bf16[384,2048]{1,0:T(8,128)(2,1)} fusion(bf16[384,3584]{1,0:T(8,128)(2,1)} %collective-permute-done.12, bf16[384,2048]{1,0:T(8,128)(2,1)S(1)} %get-tuple-element.92, bf16[3584,2048]{1,0:T(8,128)(2,1)S(1)} %bitcast.54), kind=kOutput, calls=%fused_computation.38 | convolution fusion | flops 3223584768 | bytes 13107200 | tf_op jit(solution)/shard_map/dot_general | solution.py:157
  165.9 1.5 collective-permute-start.15
  167.3 30.5 %fusion = f32[3584,2048]{1,0:T(8,128)} fusion(bf16[384,3584]{1,0:T(8,128)(2,1)} %collective-permute-done.10, bf16[384,3584]{1,0:T(8,128)(2,1)} %pad_maximum_fusion.1, bf16[384,3584]{1,0:T(8,128)(2,1)} %collective-permute-done.5, bf16[384,3584]{1,0:T(8,128)(2,1)} %copy-done.4, bf16[384,2048]{1,0:T(8,128)(2,1)} %all-gather.5.cloned.1.call-done, ...), kind=kOutput, calls=%fused_computation | convolution fusion | flops 22617784320 | bytes 46661632 | tf_op jit(solution)/shard_map/dot_general | solution.py:215
  197.9 4.8 %add_convert_fusion.1 = bf16[384,1024]{1,0:T(8,128)(2,1)S(1)} fusion(bf16[384,3584]{1,0:T(8,128)(2,1)} %collective-permute-done.12, bf16[384,2048]{1,0:T(8,128)(2,1)} %copy-done.6, bf16[3584,2048]{1,0:T(8,128)(2,1)} %param.7), kind=kOutput, calls=%fused_computation.53 | convolution fusion | flops 1611792384 | bytes 7340032 | tf_op jit(solution)/shard_map/dot_general | solution.py:157
  203.0 0.5 collective-permute-start.16
  203.6 3.1 %add_convert_fusion.2 = bf16[384,512]{1,0:T(8,128)(2,1)S(1)} fusion(bf16[384,3584]{1,0:T(8,128)(2,1)} %collective-permute-done.12, bf16[384,2048]{1,0:T(8,128)(2,1)S(1)} %copy-done.7, bf16[3584,2048]{1,0:T(8,128)(2,1)} %param.7), kind=kOutput, calls=%fused_computation.64 | convolution fusion | flops 805896192 | bytes 4456448 | tf_op jit(solution)/shard_map/dot_general | solution.py:157
  206.7 1.1 collective-permute-start.17
  207.8 6.9 %shard_map.67 = (bf16[384,3584]{1,0:T(8,128)(2,1)}, bf16[384,3584]{1,0:T(8,128)(2,1)}) custom-call(f32[384,2048]{1,0:T(8,128)S(1)} %fusion.12.own_ref, bf16[384,2048]{1,0:T(8,128)(2,1)} %collective-permute-done.14.refs_0_, bf16[384,2048]{1,0:T(8,128)(2,1)} %collective-permute-done.15.refs_1_, bf16[384,3584]{1,0:T(8,128)(2,1)S(1)} %copy-done, ...), custom_call_target="tpu_custom_call" | custom-call | tf_op jit(solution)/shard_map/pallas_call | solution.py:117
  215.0 3.9 %shard_map.68 = (bf16[384,3584]{1,0:T(8,128)(2,1)}, bf16[384,3584]{1,0:T(8,128)(2,1)}) custom-call(f32[384,1024]{1,0:T(8,128)S(1)} %copy-done.2, bf16[384,1024]{1,0:T(8,128)(2,1)} %collective-permute-done.13.refs_1_, bf16[384,1024]{1,0:T(8,128)(2,1)S(1)} %collective-permute-done.16.refs_2_, ...), custom_call_target="tpu_custom_call", output_to_operand_aliasing={{0}: (5, {}), {1}: (6, {})} | custom-call | tf_op jit(solution)/shard_map/pallas_call | solution.py:117
  219.2 1.4 shard_map.69
  (52 shorter events, 3.5 us)
Async XLA Ops:
  7.2 69.7 %all-gather.5.cloned.1.call-start = ((), (), s32[]{:S(2)}) async-start(), calls=%async_computation.1 | async-start | bytes 1769472 | tf_op jit(solution)/shard_map/all_gather | solution.py:79
  11.5 51.2 %copy-start.4 = (bf16[384,3584]{1,0:T(8,128)(2,1)}, bf16[384,3584]{1,0:T(8,128)(2,1)S(1)}, u32[]{:S(2)}) copy-start(bf16[384,3584]{1,0:T(8,128)(2,1)S(1)} %fusion.29) | copy-start | bytes 8257540
  11.5 39.8 %collective-permute-start.5 = (bf16[384,3584]{1,0:T(8,128)(2,1)S(1)}, bf16[384,3584]{1,0:T(8,128)(2,1)}, u32[]{:S(2)}, u32[]{:S(2)}) collective-permute-start(bf16[384,3584]{1,0:T(8,128)(2,1)S(1)} %fusion.29), channel_id=1, source_target_pairs={{0,8},{1,17},{2,10},{3,19},{4,12},{5,21},{6,14},{7,23},{8,0},{9,25... | collective-permute-start | bytes 8257544 | tf_op jit(solution)/shard_map/ppermute | solution.py:142
  16.4 1.9 collective-permute-start
  19.5 9.9 %collective-permute-start.3 = (bf16[48,2048]{1,0:T(8,128)(2,1)}, bf16[48,2048]{1,0:T(8,128)(2,1)S(1)}, u32[]{:S(2)}, u32[]{:S(2)}) collective-permute-start(bf16[48,2048]{1,0:T(8,128)(2,1)} %get-tuple-element.107), channel_id=1, source_target_pairs={{0,6},{1,7},{2,4},{3,5},{4,2},{5,3},{6,0},{7,1},{8,14},{9,15},{10,... | collective-permute-start | bytes 589832 | tf_op jit(solution)/shard_map/ppermute | solution.py:61
  23.1 17.3 %collective-permute-start.2 = (bf16[48,2048]{1,0:T(8,128)(2,1)S(1)}, bf16[48,2048]{1,0:T(8,128)(2,1)}, u32[]{:S(2)}, u32[]{:S(2)}) collective-permute-start(bf16[48,2048]{1,0:T(8,128)(2,1)S(1)} %get-tuple-element.108), channel_id=1, source_target_pairs={{0,4},{1,5},{2,6},{3,7},{4,0},{5,1},{6,2},{7,3},{8,12},{9,13},{10,... | collective-permute-start | bytes 589832 | tf_op jit(solution)/shard_map/ppermute | solution.py:61
  23.1 17.3 %collective-permute-start.1 = (bf16[48,2048]{1,0:T(8,128)(2,1)S(1)}, bf16[48,2048]{1,0:T(8,128)(2,1)}, u32[]{:S(2)}, u32[]{:S(2)}) collective-permute-start(bf16[48,2048]{1,0:T(8,128)(2,1)S(1)} %get-tuple-element.109), channel_id=1, source_target_pairs={{0,2},{1,3},{2,0},{3,1},{4,6},{5,7},{6,4},{7,5},{8,10},{9,11},{10,... | collective-permute-start | bytes 589832 | tf_op jit(solution)/shard_map/ppermute | solution.py:61
  42.3 9.1 %collective-permute-start.4 = (bf16[48,2048]{1,0:T(8,128)(2,1)S(1)}, bf16[48,2048]{1,0:T(8,128)(2,1)}, u32[]{:S(2)}, u32[]{:S(2)}) collective-permute-start(bf16[48,2048]{1,0:T(8,128)(2,1)S(1)} %get-tuple-element.105), channel_id=1, source_target_pairs={{0,24},{8,16},{16,8},{24,0},{1,25},{9,17},{17,9},{25,1},{2,26},{10... | collective-permute-start | bytes 589832 | tf_op jit(solution)/shard_map/ppermute | solution.py:71
  51.4 78.9 %all-gather.3.cloned.1.call-start = ((), (), s32[]{:S(2)}) async-start(), calls=%async_computation | async-start | bytes 5308416 | tf_op jit(solution)/shard_map/all_gather | solution.py:81
  51.6 8.1 %collective-permute-start.6 = (bf16[48,2048]{1,0:T(8,128)(2,1)}, bf16[48,2048]{1,0:T(8,128)(2,1)S(1)}, u32[]{:S(2)}, u32[]{:S(2)}) collective-permute-start(bf16[48,2048]{1,0:T(8,128)(2,1)} %get-tuple-element.53), channel_id=1, source_target_pairs={{0,8},{8,0},{16,24},{24,16},{1,9},{9,1},{17,25},{25,17},{2,10},{10... | collective-permute-start | bytes 589832 | tf_op jit(solution)/shard_map/ppermute | solution.py:71
  53.2 6.6 %collective-permute-start.7 = (bf16[48,2048]{1,0:T(8,128)(2,1)S(1)}, bf16[48,2048]{1,0:T(8,128)(2,1)S(1)}, u32[]{:S(2)}, u32[]{:S(2)}) collective-permute-start(bf16[48,2048]{1,0:T(8,128)(2,1)S(1)} %get-tuple-element.54), channel_id=1, source_target_pairs={{0,16},{8,24},{16,0},{24,8},{1,17},{9,25},{17,1},{25,9},{2,18},{10... | collective-permute-start | bytes 589832 | tf_op jit(solution)/shard_map/ppermute | solution.py:71
  53.7 8.9 %collective-permute-start.8 = (bf16[48,3584]{1,0:T(8,128)(2,1)S(1)}, bf16[48,3584]{1,0:T(8,128)(2,1)}, u32[]{:S(2)}, u32[]{:S(2)}) collective-permute-start(bf16[48,3584]{1,0:T(8,128)(2,1)S(1)} %split.8), channel_id=1, source_target_pairs={{0,16},{1,9},{2,18},{3,11},{4,20},{5,13},{6,22},{7,15},{8,24},{9,1... | collective-permute-start | bytes 1032200 | tf_op jit(solution)/shard_map/ppermute | solution.py:149
  64.2 29.6 %collective-permute-start.9 = (bf16[336,3584]{1,0:T(8,128)(2,1)}, bf16[336,3584]{1,0:T(8,128)(2,1)S(1)}, u32[]{:S(2)}, u32[]{:S(2)}) collective-permute-start(bf16[336,3584]{1,0:T(8,128)(2,1)} %split.9), channel_id=1, source_target_pairs={{0,16},{1,9},{2,18},{3,11},{4,20},{5,13},{6,22},{7,15},{8,24},{9,1... | collective-permute-start | bytes 7225352 | tf_op jit(solution)/shard_map/ppermute | solution.py:150
  83.8 39.6 %collective-permute-start.10 = (bf16[384,3584]{1,0:T(8,128)(2,1)}, bf16[384,3584]{1,0:T(8,128)(2,1)}, u32[]{:S(2)}, u32[]{:S(2)}) collective-permute-start(bf16[384,3584]{1,0:T(8,128)(2,1)} %collective-permute-done.5), channel_id=1, source_target_pairs={{0,16},{1,9},{2,18},{3,11},{4,20},{5,13},{6,22},{7,15},{8,24},{9,1... | collective-permute-start | bytes 8257544 | tf_op jit(solution)/shard_map/ppermute | solution.py:165
  85.3 16.0 %copy-start.9 = (bf16[384,1536]{1,0:T(8,128)(2,1)S(1)}, bf16[384,1536]{1,0:T(8,128)(2,1)}, u32[]{:S(2)}) copy-start(bf16[384,1536]{1,0:T(8,128)(2,1)} %fusion.42) | copy-start | bytes 3538948
  123.4 36.7 %collective-permute-start.12 = (bf16[384,3584]{1,0:T(8,128)(2,1)}, bf16[384,3584]{1,0:T(8,128)(2,1)}, u32[]{:S(2)}, u32[]{:S(2)}) collective-permute-start(bf16[384,3584]{1,0:T(8,128)(2,1)} %pad_maximum_fusion), channel_id=1, source_target_pairs={{0,16},{1,9},{2,18},{3,11},{4,20},{5,13},{6,22},{7,15},{8,24},{9,1... | collective-permute-start | bytes 8257544 | tf_op jit(solution)/shard_map/ppermute | solution.py:165
  130.3 13.2 %slice-start = ((s8[14680064]{0:T(1024)(128)(4,1)}), s8[4194304]{0:T(1024)(128)(4,1)S(1)}, s32[]{:S(2)}) async-start(s8[14680064]{0:T(1024)(128)(4,1)} %bitcast.53), calls=%async_computation.2 | async-start | bytes 8388608
  133.4 24.8 %copy-start.5 = (bf16[384,2048]{1,0:T(8,128)(2,1)}, bf16[384,2048]{1,0:T(8,128)(2,1)S(1)}, u32[]{:S(2)}) copy-start(bf16[384,2048]{1,0:T(8,128)(2,1)S(1)} %get-tuple-element.75) | copy-start | bytes 4718596
  133.4 10.1 %slice-start.1 = ((s8[14680064]{0:T(1024)(128)(4,1)}), s8[4194304]{0:T(1024)(128)(4,1)S(1)}, s32[]{:S(2)}) async-start(s8[14680064]{0:T(1024)(128)(4,1)} %bitcast.53), calls=%async_computation.3 | async-start | bytes 8388608
  133.6 14.6 %copy-start.8 = (bf16[384,2048]{1,0:T(8,128)(2,1)}, bf16[384,2048]{1,0:T(8,128)(2,1)S(1)}, u32[]{:S(2)}) copy-start(bf16[384,2048]{1,0:T(8,128)(2,1)S(1)} %get-tuple-element.77) | copy-start | bytes 4718596
  133.6 26.5 %copy-start.6 = (bf16[384,2048]{1,0:T(8,128)(2,1)}, bf16[384,2048]{1,0:T(8,128)(2,1)S(1)}, u32[]{:S(2)}) copy-start(bf16[384,2048]{1,0:T(8,128)(2,1)S(1)} %get-tuple-element.92) | copy-start | bytes 4718596
  133.6 9.8 %slice-start.2 = ((s8[14680064]{0:T(1024)(128)(4,1)}), s8[4194304]{0:T(1024)(128)(4,1)S(1)}, s32[]{:S(2)}) async-start(s8[14680064]{0:T(1024)(128)(4,1)} %bitcast.53), calls=%async_computation.4 | async-start | bytes 8388608
  133.7 9.8 %slice-start.3 = ((s8[14680064]{0:T(1024)(128)(4,1)}), s8[2097152]{0:T(1024)(128)(4,1)S(1)}, s32[]{:S(2)}) async-start(s8[14680064]{0:T(1024)(128)(4,1)} %bitcast.53), calls=%async_computation.5 | async-start | bytes 4194304
  146.2 56.8 %collective-permute-start.13 = (bf16[384,1024]{1,0:T(8,128)(2,1)}, bf16[384,1024]{1,0:T(8,128)(2,1)}, u32[]{:S(2)}, u32[]{:S(2)}) collective-permute-start(bf16[384,1024]{1,0:T(8,128)(2,1)} %fusion.51), channel_id=1, source_target_pairs={{0,16},{1,9},{2,18},{3,11},{4,20},{5,13},{6,22},{7,15},{8,24},{9,1... | collective-permute-start | bytes 2359304 | tf_op jit(solution)/shard_map/ppermute | solution.py:165
  147.7 55.3 %collective-permute-start.14 = (bf16[384,2048]{1,0:T(8,128)(2,1)}, bf16[384,2048]{1,0:T(8,128)(2,1)}, u32[]{:S(2)}, u32[]{:S(2)}) collective-permute-start(bf16[384,2048]{1,0:T(8,128)(2,1)} %fusion.36), channel_id=1, source_target_pairs={{0,16},{1,9},{2,18},{3,11},{4,20},{5,13},{6,22},{7,15},{8,24},{9,1... | collective-permute-start | bytes 4718600 | tf_op jit(solution)/shard_map/ppermute | solution.py:165
  150.2 52.8 %collective-permute-start.11 = (bf16[384,512]{1,0:T(8,128)(2,1)}, bf16[384,512]{1,0:T(8,128)(2,1)S(1)}, u32[]{:S(2)}, u32[]{:S(2)}) collective-permute-start(bf16[384,512]{1,0:T(8,128)(2,1)} %fusion.54), channel_id=1, source_target_pairs={{0,16},{1,9},{2,18},{3,11},{4,20},{5,13},{6,22},{7,15},{8,24},{9,1... | collective-permute-start | bytes 1179656 | tf_op jit(solution)/shard_map/ppermute | solution.py:165
  165.9 40.8 %collective-permute-start.15 = (bf16[384,2048]{1,0:T(8,128)(2,1)}, bf16[384,2048]{1,0:T(8,128)(2,1)}, u32[]{:S(2)}, u32[]{:S(2)}) collective-permute-start(bf16[384,2048]{1,0:T(8,128)(2,1)} %add_convert_fusion), channel_id=1, source_target_pairs={{0,8},{1,17},{2,10},{3,19},{4,12},{5,21},{6,14},{7,23},{8,0},{9,25... | collective-permute-start | bytes 4718600 | tf_op jit(solution)/shard_map/ppermute | solution.py:165
  197.9 5.7 %copy-start.7 = (bf16[384,2048]{1,0:T(8,128)(2,1)S(1)}, bf16[384,2048]{1,0:T(8,128)(2,1)}, u32[]{:S(2)}) copy-start(bf16[384,2048]{1,0:T(8,128)(2,1)} %copy-done.6) | copy-start | bytes 4718596
  202.7 5.1 %copy-start = (bf16[384,3584]{1,0:T(8,128)(2,1)S(1)}, bf16[384,3584]{1,0:T(8,128)(2,1)}, u32[]{:S(2)}) copy-start(bf16[384,3584]{1,0:T(8,128)(2,1)} %refs_3_.2) | copy-start | bytes 8257540
  202.7 5.1 %copy-start.1 = (bf16[384,3584]{1,0:T(8,128)(2,1)S(1)}, bf16[384,3584]{1,0:T(8,128)(2,1)}, u32[]{:S(2)}) copy-start(bf16[384,3584]{1,0:T(8,128)(2,1)} %refs_4_.1) | copy-start | bytes 8257540
  203.0 12.0 %collective-permute-start.16 = (bf16[384,1024]{1,0:T(8,128)(2,1)S(1)}, bf16[384,1024]{1,0:T(8,128)(2,1)S(1)}, u32[]{:S(2)}, u32[]{:S(2)}) collective-permute-start(bf16[384,1024]{1,0:T(8,128)(2,1)S(1)} %add_convert_fusion.1), channel_id=1, source_target_pairs={{0,8},{1,17},{2,10},{3,19},{4,12},{5,21},{6,14},{7,23},{8,0},{9,25... | collective-permute-start | bytes 2359304 | tf_op jit(solution)/shard_map/ppermute | solution.py:165
  206.6 8.4 %copy-start.2 = (f32[384,1024]{1,0:T(8,128)S(1)}, f32[384,1024]{1,0:T(8,128)}, u32[]{:S(2)}) copy-start(f32[384,1024]{1,0:T(8,128)} %fusion.32.refs_0_) | copy-start | bytes 4718596
  206.7 12.6 %collective-permute-start.17 = (bf16[384,512]{1,0:T(8,128)(2,1)S(1)}, bf16[384,512]{1,0:T(8,128)(2,1)S(1)}, u32[]{:S(2)}, u32[]{:S(2)}) collective-permute-start(bf16[384,512]{1,0:T(8,128)(2,1)S(1)} %add_convert_fusion.2), channel_id=1, source_target_pairs={{0,8},{1,17},{2,10},{3,19},{4,12},{5,21},{6,14},{7,23},{8,0},{9,25... | collective-permute-start | bytes 1179656 | tf_op jit(solution)/shard_map/ppermute | solution.py:165
  214.7 4.5 %copy-start.3 = (f32[384,512]{1,0:T(8,128)S(1)}, f32[384,512]{1,0:T(8,128)}, u32[]{:S(2)}) copy-start(f32[384,512]{1,0:T(8,128)} %fusion.47.refs_0_) | copy-start | bytes 2359300
Sparse Core Ops, SparseCore 0:
  51.5 25.3 all-gather.4
  79.0 51.1 all-gather.2

commit v10 on v9

--- a/solution.py
+++ b/solution.py
@@ -51,7 +51,7 @@
         axis=2,
     )
 
-    mine, _ = lax.optimization_barrier((mine, hidden))
+    mine = lax.optimization_barrier((mine, *hidden))[0]
 
     held = []
     for flip in range(rows):
@@ -140,12 +140,12 @@
 
     hidden = activation(gate_act, up_act)
     hidden_came = lax.ppermute(hidden, BOTH, pairs[0])
-    pieces = spread_tokens(grad_out, hidden, hidden_came, rows, cols)
+    little, large = jnp.split(hidden, [tokens // 8])
+    pieces = spread_tokens(grad_out, [hidden, little, large], hidden_came, rows, cols)
     gathered = [hidden, hidden_came]
     for step in range(1, steps - 1):
         gathered = gathered + [lax.ppermute(part, BOTH, pairs[step]) for part in gathered]
 
-    little, large = jnp.split(hidden, [tokens // 8])
     little_came = lax.ppermute(after(little, pieces[-1]), BOTH, pairs[-1])
     large_came = lax.ppermute(after(large, *pieces, little_came), BOTH, pairs[-1])
     gathered.append(jnp.concatenate([little_came, large_came]))

time: 228 us -> 228 us (level)
  transfers between devices with their start and end apart: 20 -> 20, of which waited for: 13 -> 11; matrix products, arithmetic and copies ran while one was open for 42% -> 42% of each run, Pallas kernels for 5% -> 5%
where the time goes in v10:
time: 228 us; the launch traced here: 227 us
  matrix products  81.2 us (36%)
  waiting for transfers between devices  77.7 us (34%)
  starting transfers between devices  22.5 us (10%)
  between operations  14.3 us (6%)
  Pallas kernels  12.2 us (5%)
  other arithmetic  10.4 us (5%)
  local copies, waits for them, and re-layouts  9 us (4%)
    dot_general x11, matrix products, product(): lax.dot_general(after(block, *before), down_weight[start:stop], (((1,), (...  50.7 us
    dot_general x1, matrix products, on_device(): lax.dot_general(jnp.concatenate(gathered, axis=0), jnp.concatenate(grads,...  30.5 us
    ppermute x8, waiting for transfers between devices, send(): return lax.ppermute(total, BOTH, pairs[step])  19.4 us
    ppermute x4, waiting for transfers between devices, spread_tokens(): piece = lax.ppermute(piece, 'col', pairs)  16.9 us
    all_gather x1, waiting for transfers between devices, gather_tokens(): first = lax.all_gather(blocks[-1], 'col', axis=0, tiled=True)  13.8 us
    pallas_call x3, Pallas kernels, finish(): pl.pallas_call(kernel, grid=(width // block,), in_specs=specs, out_specs=...  12.2 us
    ppermute x3, waiting for transfers between devices, spread_tokens(): piece = lax.ppermute(piece, 'row', [(r, r ^ flip) for r in range(rows)])  10.8 us
    ppermute x8, starting transfers between devices, send(): return lax.ppermute(total, BOTH, pairs[step])  8.86 us
  transfers between devices with their start and end apart: 20, of which 11 were waited for; matrix products, arithmetic and copies ran while one was open for 42% of the time, Pallas kernels for 5%

profile of v10, /device:TPU:0, one launch (start us, length us, event | category | flops | bytes accessed | tf_op | source)
XLA Modules:
  0.0 227.3 jit_solution(5421252605790862454)
XLA Ops:
  7.2 4.3 %fusion.29 = bf16[384,3584]{1,0:T(8,128)(2,1)S(1)} fusion(bf16[384,3584]{1,0:T(8,128)(2,1)} %refs_4_.1, bf16[384,3584]{1,0:T(8,128)(2,1)} %refs_3_.2), kind=kLoop, calls=%fused_computation.31 | loop fusion | flops 11010048 | bytes 8257536 | tf_op jit(solution)/shard_map/convert_element_type | solution.py:139
  11.5 3.0 %collective-permute-start.5 = (bf16[384,3584]{1,0:T(8,128)(2,1)S(1)}, bf16[384,3584]{1,0:T(8,128)(2,1)}, u32[]{:S(2)}, u32[]{:S(2)}) collective-permute-start(bf16[384,3584]{1,0:T(8,128)(2,1)S(1)} %fusion.29), channel_id=1, source_target_pairs={{0,8},{1,17},{2,10},{3,19},{4,12},{5,21},{6,14},{7,23},{8,0},{9,25... | collective-permute-start | bytes 8257544 | tf_op jit(solution)/shard_map/ppermute | solution.py:142
  14.5 1.9 dynamic-slice_bitcast_fusion
  16.4 0.8 split.8
  17.2 1.6 split.9
  19.1 0.8 constant_dynamic-slice_fusion
  20.0 3.6 %collective-permute-start.3 = (bf16[48,2048]{1,0:T(8,128)(2,1)}, bf16[48,2048]{1,0:T(8,128)(2,1)}, u32[]{:S(2)}, u32[]{:S(2)}) collective-permute-start(bf16[48,2048]{1,0:T(8,128)(2,1)} %get-tuple-element.107), channel_id=1, source_target_pairs={{0,6},{1,7},{2,4},{3,5},{4,2},{5,3},{6,0},{7,1},{8,14},{9,15},{10,... | collective-permute-start | bytes 589832 | tf_op jit(solution)/shard_map/ppermute | solution.py:61
  23.6 0.8 collective-permute-start.1
  24.4 5.6 %collective-permute-done.3 = bf16[48,2048]{1,0:T(8,128)(2,1)} collective-permute-done((bf16[48,2048]{1,0:T(8,128)(2,1)}, bf16[48,2048]{1,0:T(8,128)(2,1)}, u32[]{:S(2)}, u32[]{:S(2)}) %collective-permute-start.3) | collective-permute-done | bytes 196640 | tf_op jit(solution)/shard_map/ppermute | solution.py:61
  29.9 11.3 %collective-permute-done.2 = bf16[48,2048]{1,0:T(8,128)(2,1)} collective-permute-done((bf16[48,2048]{1,0:T(8,128)(2,1)}, bf16[48,2048]{1,0:T(8,128)(2,1)}, u32[]{:S(2)}, u32[]{:S(2)}) %collective-permute-start.2) | collective-permute-done | bytes 196640 | tf_op jit(solution)/shard_map/ppermute | solution.py:61
  41.3 1.2 pad_maximum_fusion.3
  42.5 0.8 dynamic-slice_bitcast_fusion.5
  43.2 1.8 collective-permute-start.4
  45.1 6.3 %collective-permute-done.4 = bf16[48,2048]{1,0:T(8,128)(2,1)} collective-permute-done((bf16[48,2048]{1,0:T(8,128)(2,1)S(1)}, bf16[48,2048]{1,0:T(8,128)(2,1)}, u32[]{:S(2)}, u32[]{:S(2)}) %collective-permute-start.4) | collective-permute-done | bytes 196640 | tf_op jit(solution)/shard_map/ppermute | solution.py:71
  51.6 1.6 collective-permute-start.6
  53.7 1.5 collective-permute-start.8
  55.2 4.5 %collective-permute-done.6 = bf16[48,2048]{1,0:T(8,128)(2,1)S(1)} collective-permute-done((bf16[48,2048]{1,0:T(8,128)(2,1)}, bf16[48,2048]{1,0:T(8,128)(2,1)S(1)}, u32[]{:S(2)}, u32[]{:S(2)}) %collective-permute-start.6) | collective-permute-done | bytes 196640 | tf_op jit(solution)/shard_map/ppermute | solution.py:71
  59.7 0.9 pad_maximum_fusion.4
  60.6 1.9 collective-permute-done.8
  62.5 0.6 collective-permute-start.9
  63.1 13.8 %all-gather.5.cloned.1.call-done = bf16[384,2048]{1,0:T(8,128)(2,1)} async-done(((bf16[48,2048]{1,0:T(8,128)(2,1)}), bf16[384,2048]{1,0:T(8,128)(2,1)}) %all-gather.5.cloned.1.call-update) | async-done | bytes 1572880 | tf_op jit(solution)/shard_map/all_gather | solution.py:79
  76.9 6.9 %fusion.42 = bf16[384,1536]{1,0:T(8,128)(2,1)} fusion(bf16[384,2048]{1,0:T(8,128)(2,1)} %all-gather.5.cloned.1.call-done, bf16[3584,2048]{1,0:T(8,128)(2,1)} %param.7), kind=kOutput, calls=%fused_computation.41 | convolution fusion | flops 2416508928 | bytes 9043968 | tf_op jit(solution)/shard_map/dot_general | solution.py:157
  83.8 1.5 collective-permute-start.10
  85.3 6.9 %collective-permute-done.9 = bf16[336,3584]{1,0:T(8,128)(2,1)S(1)} collective-permute-done((bf16[336,3584]{1,0:T(8,128)(2,1)}, bf16[336,3584]{1,0:T(8,128)(2,1)S(1)}, u32[]{:S(2)}, u32[]{:S(2)}) %collective-permute-start.9) | collective-permute-done | bytes 2408480 | tf_op jit(solution)/shard_map/ppermute | solution.py:150
  92.2 7.4 %fusion.39 = bf16[384,2048]{1,0:T(8,128)(2,1)S(1)} fusion(bf16[384,2048]{1,0:T(8,128)(2,1)} %all-gather.5.cloned.1.call-done, bf16[3584,2048]{1,0:T(8,128)(2,1)} %param.7), kind=kOutput, calls=%fused_computation.40 | convolution fusion | flops 3222011904 | bytes 11534336 | tf_op jit(solution)/shard_map/dot_general | solution.py:157
  99.6 1.7 pad_maximum_fusion
  101.3 1.7 pad_maximum_fusion.1
  103.0 18.8 %collective-permute-done.10 = bf16[384,3584]{1,0:T(8,128)(2,1)} collective-permute-done((bf16[384,3584]{1,0:T(8,128)(2,1)}, bf16[384,3584]{1,0:T(8,128)(2,1)}, u32[]{:S(2)}, u32[]{:S(2)}) %collective-permute-start.10) | collective-permute-done | bytes 2752544 | tf_op jit(solution)/shard_map/ppermute | solution.py:165
  122.3 8.0 %all-gather.3.cloned.1.call-done = bf16[3,384,2048]{2,1,0:T(8,128)(2,1)} async-done(((bf16[3,48,2048]{2,1,0:T(8,128)(2,1)}), bf16[3,384,2048]{2,1,0:T(8,128)(2,1)}) %all-gather.3.cloned.1.call-update) | async-done | bytes 4718608 | tf_op jit(solution)/shard_map/all_gather | solution.py:81
  130.3 3.1 %slice_bitcast_fusion = (bf16[384,2048]{1,0:T(8,128)(2,1)S(1)}, bf16[384,2048]{1,0:T(8,128)(2,1)S(1)}, bf16[384,2048]{1,0:T(8,128)(2,1)S(1)}) fusion(bf16[3,384,2048]{2,1,0:T(8,128)(2,1)} %all-gather.3.cloned.1.call-done), kind=kLoop, calls=%fused_computation.50 | loop fusion | bytes 9437184 | tf_op jit(solution)/shard_map/squeeze | solution.py:82
  133.7 9.8 %fusion.36 = bf16[384,2048]{1,0:T(8,128)(2,1)} fusion(bf16[384,2048]{1,0:T(8,128)(2,1)S(1)} %get-tuple-element.77, bf16[3584,2048]{1,0:T(8,128)(2,1)} %param.7), kind=kOutput, calls=%fused_computation.39 | convolution fusion | flops 3222011904 | bytes 11534336 | tf_op jit(solution)/shard_map/dot_general | solution.py:157
  143.5 2.7 %fusion.51 = bf16[384,1024]{1,0:T(8,128)(2,1)} fusion(bf16[384,2048]{1,0:T(8,128)(2,1)S(1)} %get-tuple-element.77, bf16[3584,2048]{1,0:T(8,128)(2,1)S(1)} %bitcast.53), kind=kOutput, calls=%fused_computation.56 | convolution fusion | flops 1611005952 | bytes 6553600 | tf_op jit(solution)/shard_map/dot_general | solution.py:157
  146.2 1.5 collective-permute-start.13
  148.2 2.0 fusion.54
  150.2 1.5 collective-permute-start.11
  151.7 3.5 %fusion.12.own_ref = f32[384,2048]{1,0:T(8,128)S(1)} fusion(bf16[384,2048]{1,0:T(8,128)(2,1)S(1)} %get-tuple-element.75, bf16[3584,2048]{1,0:T(8,128)(2,1)S(1)} %bitcast.53), kind=kOutput, calls=%fused_computation.14 | convolution fusion | flops 3221225472 | bytes 13107200 | tf_op jit(solution)/shard_map/dot_general | solution.py:157
  155.2 3.0 %fusion.32.refs_0_ = f32[384,1024]{1,0:T(8,128)} fusion(bf16[384,2048]{1,0:T(8,128)(2,1)S(1)} %get-tuple-element.75, bf16[3584,2048]{1,0:T(8,128)(2,1)S(1)} %bitcast.53), kind=kOutput, calls=%fused_computation.34 | convolution fusion | flops 1610612736 | bytes 7340032 | tf_op jit(solution)/shard_map/dot_general | solution.py:157
  158.2 1.9 fusion.47.refs_0_
  160.1 5.7 %add_convert_fusion = bf16[384,2048]{1,0:T(8,128)(2,1)} fusion(bf16[384,3584]{1,0:T(8,128)(2,1)} %collective-permute-done.12, bf16[384,2048]{1,0:T(8,128)(2,1)S(1)} %get-tuple-element.92, bf16[3584,2048]{1,0:T(8,128)(2,1)S(1)} %bitcast.53), kind=kOutput, calls=%fused_computation.38 | convolution fusion | flops 3223584768 | bytes 13107200 | tf_op jit(solution)/shard_map/dot_general | solution.py:157
  165.9 1.5 collective-permute-start.15
  167.3 30.5 %fusion = f32[3584,2048]{1,0:T(8,128)} fusion(bf16[384,3584]{1,0:T(8,128)(2,1)} %collective-permute-done.10, bf16[384,3584]{1,0:T(8,128)(2,1)} %pad_maximum_fusion.1, bf16[384,3584]{1,0:T(8,128)(2,1)} %collective-permute-done.5, bf16[384,3584]{1,0:T(8,128)(2,1)} %copy-done.4, bf16[384,2048]{1,0:T(8,128)(2,1)} %all-gather.5.cloned.1.call-done, ...), kind=kOutput, calls=%fused_computation | convolution fusion | flops 22617784320 | bytes 46661632 | tf_op jit(solution)/shard_map/dot_general | solution.py:215
  197.9 4.8 %add_convert_fusion.1 = bf16[384,1024]{1,0:T(8,128)(2,1)S(1)} fusion(bf16[384,3584]{1,0:T(8,128)(2,1)} %collective-permute-done.12, bf16[384,2048]{1,0:T(8,128)(2,1)} %copy-done.6, bf16[3584,2048]{1,0:T(8,128)(2,1)} %param.7), kind=kOutput, calls=%fused_computation.53 | convolution fusion | flops 1611792384 | bytes 7340032 | tf_op jit(solution)/shard_map/dot_general | solution.py:157
  202.7 0.6 collective-permute-start.16
  203.3 3.0 %add_convert_fusion.2 = bf16[384,512]{1,0:T(8,128)(2,1)S(1)} fusion(bf16[384,3584]{1,0:T(8,128)(2,1)} %collective-permute-done.12, bf16[384,2048]{1,0:T(8,128)(2,1)S(1)} %copy-done.7, bf16[3584,2048]{1,0:T(8,128)(2,1)} %param.7), kind=kOutput, calls=%fused_computation.64 | convolution fusion | flops 805896192 | bytes 4456448 | tf_op jit(solution)/shard_map/dot_general | solution.py:157
  206.3 1.3 collective-permute-start.17
  207.6 6.9 %shard_map.67 = (bf16[384,3584]{1,0:T(8,128)(2,1)}, bf16[384,3584]{1,0:T(8,128)(2,1)}) custom-call(f32[384,2048]{1,0:T(8,128)S(1)} %fusion.12.own_ref, bf16[384,2048]{1,0:T(8,128)(2,1)} %collective-permute-done.14.refs_0_, bf16[384,2048]{1,0:T(8,128)(2,1)} %collective-permute-done.15.refs_1_, bf16[384,3584]{1,0:T(8,128)(2,1)S(1)} %copy-done, ...), custom_call_target="tpu_custom_call" | custom-call | tf_op jit(solution)/shard_map/pallas_call | solution.py:117
  214.8 3.9 %shard_map.68 = (bf16[384,3584]{1,0:T(8,128)(2,1)}, bf16[384,3584]{1,0:T(8,128)(2,1)}) custom-call(f32[384,1024]{1,0:T(8,128)S(1)} %copy-done.2, bf16[384,1024]{1,0:T(8,128)(2,1)} %collective-permute-done.13.refs_1_, bf16[384,1024]{1,0:T(8,128)(2,1)S(1)} %collective-permute-done.16.refs_2_, ...), custom_call_target="tpu_custom_call", output_to_operand_aliasing={{0}: (5, {}), {1}: (6, {})} | custom-call | tf_op jit(solution)/shard_map/pallas_call | solution.py:117
  219.0 1.4 shard_map.69
  (54 shorter events, 3.1 us)
Async XLA Ops:
  7.2 69.7 %all-gather.5.cloned.1.call-start = ((), (), s32[]{:S(2)}) async-start(), calls=%async_computation.1 | async-start | bytes 1769472 | tf_op jit(solution)/shard_map/all_gather | solution.py:79
  11.5 7.3 %copy-start.4 = (bf16[384,3584]{1,0:T(8,128)(2,1)}, bf16[384,3584]{1,0:T(8,128)(2,1)S(1)}, u32[]{:S(2)}) copy-start(bf16[384,3584]{1,0:T(8,128)(2,1)S(1)} %fusion.29) | copy-start | bytes 8257540
  11.5 39.8 %collective-permute-start.5 = (bf16[384,3584]{1,0:T(8,128)(2,1)S(1)}, bf16[384,3584]{1,0:T(8,128)(2,1)}, u32[]{:S(2)}, u32[]{:S(2)}) collective-permute-start(bf16[384,3584]{1,0:T(8,128)(2,1)S(1)} %fusion.29), channel_id=1, source_target_pairs={{0,8},{1,17},{2,10},{3,19},{4,12},{5,21},{6,14},{7,23},{8,0},{9,25... | collective-permute-start | bytes 8257544 | tf_op jit(solution)/shard_map/ppermute | solution.py:142
  16.4 2.3 %collective-permute-start = (bf16[4,48,1024]{2,1,0:T(8,128)(2,1)}, bf16[4,48,1024]{2,1,0:T(8,128)(2,1)S(1)}, u32[]{:S(2)}, u32[]{:S(2)}) collective-permute-start(bf16[4,48,1024]{2,1,0:T(8,128)(2,1)} %get-tuple-element.112), channel_id=1, source_target_pairs={{0,1},{1,0},{2,3},{3,2},{4,5},{5,4},{6,7},{7,6},{8,9},{9,8},{10,11... | collective-permute-start | bytes 1179656 | tf_op jit(solution)/shard_map/ppermute | solution.py:43
  19.1 34.5 %copy-start.10 = (bf16[48,3584]{1,0:T(8,128)(2,1)S(1)}, bf16[48,3584]{1,0:T(8,128)(2,1)}, u32[]{:S(2)}) copy-start(bf16[48,3584]{1,0:T(8,128)(2,1)} %split.8) | copy-start | bytes 1032196
  20.0 9.9 %collective-permute-start.3 = (bf16[48,2048]{1,0:T(8,128)(2,1)}, bf16[48,2048]{1,0:T(8,128)(2,1)}, u32[]{:S(2)}, u32[]{:S(2)}) collective-permute-start(bf16[48,2048]{1,0:T(8,128)(2,1)} %get-tuple-element.107), channel_id=1, source_target_pairs={{0,6},{1,7},{2,4},{3,5},{4,2},{5,3},{6,0},{7,1},{8,14},{9,15},{10,... | collective-permute-start | bytes 589832 | tf_op jit(solution)/shard_map/ppermute | solution.py:61
  23.6 17.7 %collective-permute-start.2 = (bf16[48,2048]{1,0:T(8,128)(2,1)}, bf16[48,2048]{1,0:T(8,128)(2,1)}, u32[]{:S(2)}, u32[]{:S(2)}) collective-permute-start(bf16[48,2048]{1,0:T(8,128)(2,1)} %get-tuple-element.108), channel_id=1, source_target_pairs={{0,4},{1,5},{2,6},{3,7},{4,0},{5,1},{6,2},{7,3},{8,12},{9,13},{10,... | collective-permute-start | bytes 589832 | tf_op jit(solution)/shard_map/ppermute | solution.py:61
  23.6 17.7 %collective-permute-start.1 = (bf16[48,2048]{1,0:T(8,128)(2,1)S(1)}, bf16[48,2048]{1,0:T(8,128)(2,1)}, u32[]{:S(2)}, u32[]{:S(2)}) collective-permute-start(bf16[48,2048]{1,0:T(8,128)(2,1)S(1)} %get-tuple-element.109), channel_id=1, source_target_pairs={{0,2},{1,3},{2,0},{3,1},{4,6},{5,7},{6,4},{7,5},{8,10},{9,11},{10,... | collective-permute-start | bytes 589832 | tf_op jit(solution)/shard_map/ppermute | solution.py:61
  43.2 8.1 %collective-permute-start.4 = (bf16[48,2048]{1,0:T(8,128)(2,1)S(1)}, bf16[48,2048]{1,0:T(8,128)(2,1)}, u32[]{:S(2)}, u32[]{:S(2)}) collective-permute-start(bf16[48,2048]{1,0:T(8,128)(2,1)S(1)} %get-tuple-element.105), channel_id=1, source_target_pairs={{0,24},{8,16},{16,8},{24,0},{1,25},{9,17},{17,9},{25,1},{2,26},{10... | collective-permute-start | bytes 589832 | tf_op jit(solution)/shard_map/ppermute | solution.py:71
  51.4 78.9 %all-gather.3.cloned.1.call-start = ((), (), s32[]{:S(2)}) async-start(), calls=%async_computation | async-start | bytes 5308416 | tf_op jit(solution)/shard_map/all_gather | solution.py:81
  51.6 8.1 %collective-permute-start.6 = (bf16[48,2048]{1,0:T(8,128)(2,1)}, bf16[48,2048]{1,0:T(8,128)(2,1)S(1)}, u32[]{:S(2)}, u32[]{:S(2)}) collective-permute-start(bf16[48,2048]{1,0:T(8,128)(2,1)} %get-tuple-element.53), channel_id=1, source_target_pairs={{0,8},{8,0},{16,24},{24,16},{1,9},{9,1},{17,25},{25,17},{2,10},{10... | collective-permute-start | bytes 589832 | tf_op jit(solution)/shard_map/ppermute | solution.py:71
  53.2 6.6 %collective-permute-start.7 = (bf16[48,2048]{1,0:T(8,128)(2,1)S(1)}, bf16[48,2048]{1,0:T(8,128)(2,1)S(1)}, u32[]{:S(2)}, u32[]{:S(2)}) collective-permute-start(bf16[48,2048]{1,0:T(8,128)(2,1)S(1)} %get-tuple-element.54), channel_id=1, source_target_pairs={{0,16},{8,24},{16,0},{24,8},{1,17},{9,25},{17,1},{25,9},{2,18},{10... | collective-permute-start | bytes 589832 | tf_op jit(solution)/shard_map/ppermute | solution.py:71
  53.7 8.8 %collective-permute-start.8 = (bf16[48,3584]{1,0:T(8,128)(2,1)S(1)}, bf16[48,3584]{1,0:T(8,128)(2,1)S(1)}, u32[]{:S(2)}, u32[]{:S(2)}) collective-permute-start(bf16[48,3584]{1,0:T(8,128)(2,1)S(1)} %copy-done.10), channel_id=1, source_target_pairs={{0,16},{1,9},{2,18},{3,11},{4,20},{5,13},{6,22},{7,15},{8,24},{9,1... | collective-permute-start | bytes 1032200 | tf_op jit(solution)/shard_map/ppermute | solution.py:149
  62.5 29.6 %collective-permute-start.9 = (bf16[336,3584]{1,0:T(8,128)(2,1)}, bf16[336,3584]{1,0:T(8,128)(2,1)S(1)}, u32[]{:S(2)}, u32[]{:S(2)}) collective-permute-start(bf16[336,3584]{1,0:T(8,128)(2,1)} %split.9), channel_id=1, source_target_pairs={{0,16},{1,9},{2,18},{3,11},{4,20},{5,13},{6,22},{7,15},{8,24},{9,1... | collective-permute-start | bytes 7225352 | tf_op jit(solution)/shard_map/ppermute | solution.py:150
  83.8 38.0 %collective-permute-start.10 = (bf16[384,3584]{1,0:T(8,128)(2,1)}, bf16[384,3584]{1,0:T(8,128)(2,1)}, u32[]{:S(2)}, u32[]{:S(2)}) collective-permute-start(bf16[384,3584]{1,0:T(8,128)(2,1)} %collective-permute-done.5), channel_id=1, source_target_pairs={{0,16},{1,9},{2,18},{3,11},{4,20},{5,13},{6,22},{7,15},{8,24},{9,1... | collective-permute-start | bytes 8257544 | tf_op jit(solution)/shard_map/ppermute | solution.py:165
  85.3 14.3 %copy-start.9 = (bf16[384,1536]{1,0:T(8,128)(2,1)S(1)}, bf16[384,1536]{1,0:T(8,128)(2,1)}, u32[]{:S(2)}) copy-start(bf16[384,1536]{1,0:T(8,128)(2,1)} %fusion.42) | copy-start | bytes 3538948
  121.8 38.3 %collective-permute-start.12 = (bf16[384,3584]{1,0:T(8,128)(2,1)}, bf16[384,3584]{1,0:T(8,128)(2,1)}, u32[]{:S(2)}, u32[]{:S(2)}) collective-permute-start(bf16[384,3584]{1,0:T(8,128)(2,1)} %pad_maximum_fusion), channel_id=1, source_target_pairs={{0,16},{1,9},{2,18},{3,11},{4,20},{5,13},{6,22},{7,15},{8,24},{9,1... | collective-permute-start | bytes 8257544 | tf_op jit(solution)/shard_map/ppermute | solution.py:165
  130.3 13.2 %slice-start = ((s8[14680064]{0:T(1024)(128)(4,1)}), s8[4194304]{0:T(1024)(128)(4,1)S(1)}, s32[]{:S(2)}) async-start(s8[14680064]{0:T(1024)(128)(4,1)} %bitcast.52), calls=%async_computation.2 | async-start | bytes 8388608
  133.4 24.8 %copy-start.5 = (bf16[384,2048]{1,0:T(8,128)(2,1)}, bf16[384,2048]{1,0:T(8,128)(2,1)S(1)}, u32[]{:S(2)}) copy-start(bf16[384,2048]{1,0:T(8,128)(2,1)S(1)} %get-tuple-element.75) | copy-start | bytes 4718596
  133.4 10.1 %slice-start.1 = ((s8[14680064]{0:T(1024)(128)(4,1)}), s8[4194304]{0:T(1024)(128)(4,1)S(1)}, s32[]{:S(2)}) async-start(s8[14680064]{0:T(1024)(128)(4,1)} %bitcast.52), calls=%async_computation.3 | async-start | bytes 8388608
  133.6 14.6 %copy-start.8 = (bf16[384,2048]{1,0:T(8,128)(2,1)}, bf16[384,2048]{1,0:T(8,128)(2,1)S(1)}, u32[]{:S(2)}) copy-start(bf16[384,2048]{1,0:T(8,128)(2,1)S(1)} %get-tuple-element.77) | copy-start | bytes 4718596
  133.6 26.5 %copy-start.6 = (bf16[384,2048]{1,0:T(8,128)(2,1)}, bf16[384,2048]{1,0:T(8,128)(2,1)S(1)}, u32[]{:S(2)}) copy-start(bf16[384,2048]{1,0:T(8,128)(2,1)S(1)} %get-tuple-element.92) | copy-start | bytes 4718596
  133.6 9.8 %slice-start.2 = ((s8[14680064]{0:T(1024)(128)(4,1)}), s8[4194304]{0:T(1024)(128)(4,1)S(1)}, s32[]{:S(2)}) async-start(s8[14680064]{0:T(1024)(128)(4,1)} %bitcast.52), calls=%async_computation.4 | async-start | bytes 8388608
  133.7 9.8 %slice-start.3 = ((s8[14680064]{0:T(1024)(128)(4,1)}), s8[2097152]{0:T(1024)(128)(4,1)S(1)}, s32[]{:S(2)}) async-start(s8[14680064]{0:T(1024)(128)(4,1)} %bitcast.52), calls=%async_computation.5 | async-start | bytes 4194304
  146.2 56.5 %collective-permute-start.13 = (bf16[384,1024]{1,0:T(8,128)(2,1)}, bf16[384,1024]{1,0:T(8,128)(2,1)}, u32[]{:S(2)}, u32[]{:S(2)}) collective-permute-start(bf16[384,1024]{1,0:T(8,128)(2,1)} %fusion.51), channel_id=1, source_target_pairs={{0,16},{1,9},{2,18},{3,11},{4,20},{5,13},{6,22},{7,15},{8,24},{9,1... | collective-permute-start | bytes 2359304 | tf_op jit(solution)/shard_map/ppermute | solution.py:165
  147.7 55.0 %collective-permute-start.14 = (bf16[384,2048]{1,0:T(8,128)(2,1)}, bf16[384,2048]{1,0:T(8,128)(2,1)}, u32[]{:S(2)}, u32[]{:S(2)}) collective-permute-start(bf16[384,2048]{1,0:T(8,128)(2,1)} %fusion.36), channel_id=1, source_target_pairs={{0,16},{1,9},{2,18},{3,11},{4,20},{5,13},{6,22},{7,15},{8,24},{9,1... | collective-permute-start | bytes 4718600 | tf_op jit(solution)/shard_map/ppermute | solution.py:165
  150.2 52.5 %collective-permute-start.11 = (bf16[384,512]{1,0:T(8,128)(2,1)}, bf16[384,512]{1,0:T(8,128)(2,1)S(1)}, u32[]{:S(2)}, u32[]{:S(2)}) collective-permute-start(bf16[384,512]{1,0:T(8,128)(2,1)} %fusion.54), channel_id=1, source_target_pairs={{0,16},{1,9},{2,18},{3,11},{4,20},{5,13},{6,22},{7,15},{8,24},{9,1... | collective-permute-start | bytes 1179656 | tf_op jit(solution)/shard_map/ppermute | solution.py:165
  165.9 40.5 %collective-permute-start.15 = (bf16[384,2048]{1,0:T(8,128)(2,1)}, bf16[384,2048]{1,0:T(8,128)(2,1)}, u32[]{:S(2)}, u32[]{:S(2)}) collective-permute-start(bf16[384,2048]{1,0:T(8,128)(2,1)} %add_convert_fusion), channel_id=1, source_target_pairs={{0,8},{1,17},{2,10},{3,19},{4,12},{5,21},{6,14},{7,23},{8,0},{9,25... | collective-permute-start | bytes 4718600 | tf_op jit(solution)/shard_map/ppermute | solution.py:165
  197.9 5.5 %copy-start.7 = (bf16[384,2048]{1,0:T(8,128)(2,1)S(1)}, bf16[384,2048]{1,0:T(8,128)(2,1)}, u32[]{:S(2)}) copy-start(bf16[384,2048]{1,0:T(8,128)(2,1)} %copy-done.6) | copy-start | bytes 4718596
  202.7 4.9 %copy-start = (bf16[384,3584]{1,0:T(8,128)(2,1)S(1)}, bf16[384,3584]{1,0:T(8,128)(2,1)}, u32[]{:S(2)}) copy-start(bf16[384,3584]{1,0:T(8,128)(2,1)} %refs_3_.2) | copy-start | bytes 8257540
  202.7 4.9 %copy-start.1 = (bf16[384,3584]{1,0:T(8,128)(2,1)S(1)}, bf16[384,3584]{1,0:T(8,128)(2,1)}, u32[]{:S(2)}) copy-start(bf16[384,3584]{1,0:T(8,128)(2,1)} %refs_4_.1) | copy-start | bytes 8257540
  202.7 12.1 %collective-permute-start.16 = (bf16[384,1024]{1,0:T(8,128)(2,1)S(1)}, bf16[384,1024]{1,0:T(8,128)(2,1)S(1)}, u32[]{:S(2)}, u32[]{:S(2)}) collective-permute-start(bf16[384,1024]{1,0:T(8,128)(2,1)S(1)} %add_convert_fusion.1), channel_id=1, source_target_pairs={{0,8},{1,17},{2,10},{3,19},{4,12},{5,21},{6,14},{7,23},{8,0},{9,25... | collective-permute-start | bytes 2359304 | tf_op jit(solution)/shard_map/ppermute | solution.py:165
  206.3 8.5 %copy-start.2 = (f32[384,1024]{1,0:T(8,128)S(1)}, f32[384,1024]{1,0:T(8,128)}, u32[]{:S(2)}) copy-start(f32[384,1024]{1,0:T(8,128)} %fusion.32.refs_0_) | copy-start | bytes 4718596
  206.3 12.7 %collective-permute-start.17 = (bf16[384,512]{1,0:T(8,128)(2,1)S(1)}, bf16[384,512]{1,0:T(8,128)(2,1)S(1)}, u32[]{:S(2)}, u32[]{:S(2)}) collective-permute-start(bf16[384,512]{1,0:T(8,128)(2,1)S(1)} %add_convert_fusion.2), channel_id=1, source_target_pairs={{0,8},{1,17},{2,10},{3,19},{4,12},{5,21},{6,14},{7,23},{8,0},{9,25... | collective-permute-start | bytes 1179656 | tf_op jit(solution)/shard_map/ppermute | solution.py:165
  214.5 4.4 %copy-start.3 = (f32[384,512]{1,0:T(8,128)S(1)}, f32[384,512]{1,0:T(8,128)}, u32[]{:S(2)}) copy-start(f32[384,512]{1,0:T(8,128)} %fusion.47.refs_0_) | copy-start | bytes 2359300
Sparse Core Ops, SparseCore 0:
  51.5 25.3 all-gather.4
  79.0 51.1 all-gather.2

commit v11 on v10

--- a/solution.py
+++ b/solution.py
@@ -188,11 +188,11 @@
     for chunk in chunks:
         came[rows // 2 - 1][chunk].append(whole[:, starts[chunk] : stops[chunk]])
 
-    def message(place, chunk, *before):
+    def message(place, chunk, step, *before):
         total = product(grads[place], starts[chunk], stops[chunk], *before)
         for block in came[place][chunk]:
             total = total + block.astype(jnp.float32)
-        return total.astype(jnp.bfloat16)
+        return total.astype(jnp.bfloat16 if step >= steps - 2 else jnp.float32)
 
     def own_product(chunk, *before):
         return product(grads[0], starts[chunk], stops[chunk], *before)
@@ -202,13 +202,13 @@
             if place == rows - 1:
                 continue
             for chunk in chunks:
-                total = message(place, chunk, total)
+                total = message(place, chunk, step, total)
                 came[place ^ (1 << step)][chunk].append(send(total, step))
     own = []
     for chunk in chunks:
         total = own_product(chunk, total)
         own.append(total)
-    total = message(1, 0, total)
+    total = message(1, 0, 0, total)
     last = [send(total, 0)]
 
     gathered, grads, _ = lax.optimization_barrier((gathered, grads, total))
@@ -219,9 +219,9 @@
         preferred_element_type=jnp.float32,
     )
 
-    total = after(message(1, 1, grad_weight), *sum(came[0], []))
+    total = after(message(1, 1, 0, grad_weight), *sum(came[0], []))
     last.append(send(total, 0))
-    total = after(message(1, 2, total), last[0])
+    total = after(message(1, 2, 0, total), last[0])
     last.append(send(total, 0))
 
     gate_act, up_act = after(gate_act, hidden_came), after(up_act, hidden_came)

time: 228 us -> 228 us (level)
  no operation moved by 1% of the time
where the time goes in v11:
time: 228 us; the launch traced here: 227 us
  matrix products  81.2 us (36%)
  waiting for transfers between devices  77.7 us (34%)
  starting transfers between devices  22.5 us (10%)
  between operations  14.3 us (6%)
  Pallas kernels  12.2 us (5%)
  other arithmetic  10.4 us (5%)
  local copies, waits for them, and re-layouts  9 us (4%)
    dot_general x11, matrix products, product(): lax.dot_general(after(block, *before), down_weight[start:stop], (((1,), (...  50.7 us
    dot_general x1, matrix products, on_device(): lax.dot_general(jnp.concatenate(gathered, axis=0), jnp.concatenate(grads,...  30.5 us
    ppermute x8, waiting for transfers between devices, send(): return lax.ppermute(total, BOTH, pairs[step])  19.4 us
    ppermute x4, waiting for transfers between devices, spread_tokens(): piece = lax.ppermute(piece, 'col', pairs)  16.9 us
    all_gather x1, waiting for transfers between devices, gather_tokens(): first = lax.all_gather(blocks[-1], 'col', axis=0, tiled=True)  13.8 us
    pallas_call x3, Pallas kernels, finish(): pl.pallas_call(kernel, grid=(width // block,), in_specs=specs, out_specs=...  12.2 us
    ppermute x3, waiting for transfers between devices, spread_tokens(): piece = lax.ppermute(piece, 'row', [(r, r ^ flip) for r in range(rows)])  10.8 us
    ppermute x8, starting transfers between devices, send(): return lax.ppermute(total, BOTH, pairs[step])  8.86 us
  transfers between devices with their start and end apart: 20, of which 11 were waited for; matrix products, arithmetic and copies ran while one was open for 42% of the time, Pallas kernels for 5%

profile of v11, /device:TPU:0, one launch (start us, length us, event | category | flops | bytes accessed | tf_op | source)
XLA Modules:
  0.0 227.3 jit_solution(5421252605790862454)
XLA Ops:
  7.2 4.3 %fusion.29 = bf16[384,3584]{1,0:T(8,128)(2,1)S(1)} fusion(bf16[384,3584]{1,0:T(8,128)(2,1)} %refs_4_.1, bf16[384,3584]{1,0:T(8,128)(2,1)} %refs_3_.2), kind=kLoop, calls=%fused_computation.31 | loop fusion | flops 11010048 | bytes 8257536 | tf_op jit(solution)/shard_map/convert_element_type | solution.py:139
  11.5 3.0 %collective-permute-start.5 = (bf16[384,3584]{1,0:T(8,128)(2,1)S(1)}, bf16[384,3584]{1,0:T(8,128)(2,1)}, u32[]{:S(2)}, u32[]{:S(2)}) collective-permute-start(bf16[384,3584]{1,0:T(8,128)(2,1)S(1)} %fusion.29), channel_id=1, source_target_pairs={{0,8},{1,17},{2,10},{3,19},{4,12},{5,21},{6,14},{7,23},{8,0},{9,25... | collective-permute-start | bytes 8257544 | tf_op jit(solution)/shard_map/ppermute | solution.py:142
  14.5 1.9 dynamic-slice_bitcast_fusion
  16.4 0.8 split.8
  17.2 1.6 split.9
  19.1 0.8 constant_dynamic-slice_fusion
  20.0 3.6 %collective-permute-start.3 = (bf16[48,2048]{1,0:T(8,128)(2,1)}, bf16[48,2048]{1,0:T(8,128)(2,1)}, u32[]{:S(2)}, u32[]{:S(2)}) collective-permute-start(bf16[48,2048]{1,0:T(8,128)(2,1)} %get-tuple-element.107), channel_id=1, source_target_pairs={{0,6},{1,7},{2,4},{3,5},{4,2},{5,3},{6,0},{7,1},{8,14},{9,15},{10,... | collective-permute-start | bytes 589832 | tf_op jit(solution)/shard_map/ppermute | solution.py:61
  23.6 0.8 collective-permute-start.1
  24.4 5.6 %collective-permute-done.3 = bf16[48,2048]{1,0:T(8,128)(2,1)} collective-permute-done((bf16[48,2048]{1,0:T(8,128)(2,1)}, bf16[48,2048]{1,0:T(8,128)(2,1)}, u32[]{:S(2)}, u32[]{:S(2)}) %collective-permute-start.3) | collective-permute-done | bytes 196640 | tf_op jit(solution)/shard_map/ppermute | solution.py:61
  29.9 11.3 %collective-permute-done.2 = bf16[48,2048]{1,0:T(8,128)(2,1)} collective-permute-done((bf16[48,2048]{1,0:T(8,128)(2,1)}, bf16[48,2048]{1,0:T(8,128)(2,1)}, u32[]{:S(2)}, u32[]{:S(2)}) %collective-permute-start.2) | collective-permute-done | bytes 196640 | tf_op jit(solution)/shard_map/ppermute | solution.py:61
  41.3 1.2 pad_maximum_fusion.3
  42.5 0.8 dynamic-slice_bitcast_fusion.5
  43.2 1.8 collective-permute-start.4
  45.1 6.3 %collective-permute-done.4 = bf16[48,2048]{1,0:T(8,128)(2,1)} collective-permute-done((bf16[48,2048]{1,0:T(8,128)(2,1)S(1)}, bf16[48,2048]{1,0:T(8,128)(2,1)}, u32[]{:S(2)}, u32[]{:S(2)}) %collective-permute-start.4) | collective-permute-done | bytes 196640 | tf_op jit(solution)/shard_map/ppermute | solution.py:71
  51.6 1.6 collective-permute-start.6
  53.7 1.5 collective-permute-start.8
  55.2 4.5 %collective-permute-done.6 = bf16[48,2048]{1,0:T(8,128)(2,1)S(1)} collective-permute-done((bf16[48,2048]{1,0:T(8,128)(2,1)}, bf16[48,2048]{1,0:T(8,128)(2,1)S(1)}, u32[]{:S(2)}, u32[]{:S(2)}) %collective-permute-start.6) | collective-permute-done | bytes 196640 | tf_op jit(solution)/shard_map/ppermute | solution.py:71
  59.7 0.9 pad_maximum_fusion.4
  60.6 1.9 collective-permute-done.8
  62.5 0.6 collective-permute-start.9
  63.1 13.8 %all-gather.5.cloned.1.call-done = bf16[384,2048]{1,0:T(8,128)(2,1)} async-done(((bf16[48,2048]{1,0:T(8,128)(2,1)}), bf16[384,2048]{1,0:T(8,128)(2,1)}) %all-gather.5.cloned.1.call-update) | async-done | bytes 1572880 | tf_op jit(solution)/shard_map/all_gather | solution.py:79
  76.9 6.9 %fusion.42 = bf16[384,1536]{1,0:T(8,128)(2,1)} fusion(bf16[384,2048]{1,0:T(8,128)(2,1)} %all-gather.5.cloned.1.call-done, bf16[3584,2048]{1,0:T(8,128)(2,1)} %param.7), kind=kOutput, calls=%fused_computation.41 | convolution fusion | flops 2416508928 | bytes 9043968 | tf_op jit(solution)/shard_map/dot_general | solution.py:157
  83.8 1.5 collective-permute-start.10
  85.3 6.9 %collective-permute-done.9 = bf16[336,3584]{1,0:T(8,128)(2,1)S(1)} collective-permute-done((bf16[336,3584]{1,0:T(8,128)(2,1)}, bf16[336,3584]{1,0:T(8,128)(2,1)S(1)}, u32[]{:S(2)}, u32[]{:S(2)}) %collective-permute-start.9) | collective-permute-done | bytes 2408480 | tf_op jit(solution)/shard_map/ppermute | solution.py:150
  92.2 7.4 %fusion.39 = bf16[384,2048]{1,0:T(8,128)(2,1)S(1)} fusion(bf16[384,2048]{1,0:T(8,128)(2,1)} %all-gather.5.cloned.1.call-done, bf16[3584,2048]{1,0:T(8,128)(2,1)} %param.7), kind=kOutput, calls=%fused_computation.40 | convolution fusion | flops 3222011904 | bytes 11534336 | tf_op jit(solution)/shard_map/dot_general | solution.py:157
  99.6 1.7 pad_maximum_fusion
  101.3 1.7 pad_maximum_fusion.1
  103.0 18.8 %collective-permute-done.10 = bf16[384,3584]{1,0:T(8,128)(2,1)} collective-permute-done((bf16[384,3584]{1,0:T(8,128)(2,1)}, bf16[384,3584]{1,0:T(8,128)(2,1)}, u32[]{:S(2)}, u32[]{:S(2)}) %collective-permute-start.10) | collective-permute-done | bytes 2752544 | tf_op jit(solution)/shard_map/ppermute | solution.py:165
  122.3 8.0 %all-gather.3.cloned.1.call-done = bf16[3,384,2048]{2,1,0:T(8,128)(2,1)} async-done(((bf16[3,48,2048]{2,1,0:T(8,128)(2,1)}), bf16[3,384,2048]{2,1,0:T(8,128)(2,1)}) %all-gather.3.cloned.1.call-update) | async-done | bytes 4718608 | tf_op jit(solution)/shard_map/all_gather | solution.py:81
  130.3 3.1 %slice_bitcast_fusion = (bf16[384,2048]{1,0:T(8,128)(2,1)S(1)}, bf16[384,2048]{1,0:T(8,128)(2,1)S(1)}, bf16[384,2048]{1,0:T(8,128)(2,1)S(1)}) fusion(bf16[3,384,2048]{2,1,0:T(8,128)(2,1)} %all-gather.3.cloned.1.call-done), kind=kLoop, calls=%fused_computation.50 | loop fusion | bytes 9437184 | tf_op jit(solution)/shard_map/squeeze | solution.py:82
  133.7 9.8 %fusion.36 = bf16[384,2048]{1,0:T(8,128)(2,1)} fusion(bf16[384,2048]{1,0:T(8,128)(2,1)S(1)} %get-tuple-element.77, bf16[3584,2048]{1,0:T(8,128)(2,1)} %param.7), kind=kOutput, calls=%fused_computation.39 | convolution fusion | flops 3222011904 | bytes 11534336 | tf_op jit(solution)/shard_map/dot_general | solution.py:157
  143.5 2.7 %fusion.51 = bf16[384,1024]{1,0:T(8,128)(2,1)} fusion(bf16[384,2048]{1,0:T(8,128)(2,1)S(1)} %get-tuple-element.77, bf16[3584,2048]{1,0:T(8,128)(2,1)S(1)} %bitcast.53), kind=kOutput, calls=%fused_computation.56 | convolution fusion | flops 1611005952 | bytes 6553600 | tf_op jit(solution)/shard_map/dot_general | solution.py:157
  146.2 1.5 collective-permute-start.13
  148.2 2.0 fusion.54
  150.2 1.5 collective-permute-start.11
  151.7 3.5 %fusion.12.own_ref = f32[384,2048]{1,0:T(8,128)S(1)} fusion(bf16[384,2048]{1,0:T(8,128)(2,1)S(1)} %get-tuple-element.75, bf16[3584,2048]{1,0:T(8,128)(2,1)S(1)} %bitcast.53), kind=kOutput, calls=%fused_computation.14 | convolution fusion | flops 3221225472 | bytes 13107200 | tf_op jit(solution)/shard_map/dot_general | solution.py:157
  155.2 3.0 %fusion.32.refs_0_ = f32[384,1024]{1,0:T(8,128)} fusion(bf16[384,2048]{1,0:T(8,128)(2,1)S(1)} %get-tuple-element.75, bf16[3584,2048]{1,0:T(8,128)(2,1)S(1)} %bitcast.53), kind=kOutput, calls=%fused_computation.34 | convolution fusion | flops 1610612736 | bytes 7340032 | tf_op jit(solution)/shard_map/dot_general | solution.py:157
  158.2 1.9 fusion.47.refs_0_
  160.1 5.7 %add_convert_fusion = bf16[384,2048]{1,0:T(8,128)(2,1)} fusion(bf16[384,3584]{1,0:T(8,128)(2,1)} %collective-permute-done.12, bf16[384,2048]{1,0:T(8,128)(2,1)S(1)} %get-tuple-element.92, bf16[3584,2048]{1,0:T(8,128)(2,1)S(1)} %bitcast.53), kind=kOutput, calls=%fused_computation.38 | convolution fusion | flops 3223584768 | bytes 13107200 | tf_op jit(solution)/shard_map/dot_general | solution.py:157
  165.9 1.5 collective-permute-start.15
  167.3 30.5 %fusion = f32[3584,2048]{1,0:T(8,128)} fusion(bf16[384,3584]{1,0:T(8,128)(2,1)} %collective-permute-done.10, bf16[384,3584]{1,0:T(8,128)(2,1)} %pad_maximum_fusion.1, bf16[384,3584]{1,0:T(8,128)(2,1)} %collective-permute-done.5, bf16[384,3584]{1,0:T(8,128)(2,1)} %copy-done.4, bf16[384,2048]{1,0:T(8,128)(2,1)} %all-gather.5.cloned.1.call-done, ...), kind=kOutput, calls=%fused_computation | convolution fusion | flops 22617784320 | bytes 46661632 | tf_op jit(solution)/shard_map/dot_general | solution.py:215
  197.9 4.8 %add_convert_fusion.1 = bf16[384,1024]{1,0:T(8,128)(2,1)S(1)} fusion(bf16[384,3584]{1,0:T(8,128)(2,1)} %collective-permute-done.12, bf16[384,2048]{1,0:T(8,128)(2,1)} %copy-done.6, bf16[3584,2048]{1,0:T(8,128)(2,1)} %param.7), kind=kOutput, calls=%fused_computation.53 | convolution fusion | flops 1611792384 | bytes 7340032 | tf_op jit(solution)/shard_map/dot_general | solution.py:157
  202.7 0.6 collective-permute-start.16
  203.3 3.0 %add_convert_fusion.2 = bf16[384,512]{1,0:T(8,128)(2,1)S(1)} fusion(bf16[384,3584]{1,0:T(8,128)(2,1)} %collective-permute-done.12, bf16[384,2048]{1,0:T(8,128)(2,1)S(1)} %copy-done.7, bf16[3584,2048]{1,0:T(8,128)(2,1)} %param.7), kind=kOutput, calls=%fused_computation.64 | convolution fusion | flops 805896192 | bytes 4456448 | tf_op jit(solution)/shard_map/dot_general | solution.py:157
  206.3 1.3 collective-permute-start.17
  207.6 6.9 %shard_map.67 = (bf16[384,3584]{1,0:T(8,128)(2,1)}, bf16[384,3584]{1,0:T(8,128)(2,1)}) custom-call(f32[384,2048]{1,0:T(8,128)S(1)} %fusion.12.own_ref, bf16[384,2048]{1,0:T(8,128)(2,1)} %collective-permute-done.14.refs_0_, bf16[384,2048]{1,0:T(8,128)(2,1)} %collective-permute-done.15.refs_1_, bf16[384,3584]{1,0:T(8,128)(2,1)S(1)} %copy-done, ...), custom_call_target="tpu_custom_call" | custom-call | tf_op jit(solution)/shard_map/pallas_call | solution.py:117
  214.8 3.9 %shard_map.68 = (bf16[384,3584]{1,0:T(8,128)(2,1)}, bf16[384,3584]{1,0:T(8,128)(2,1)}) custom-call(f32[384,1024]{1,0:T(8,128)S(1)} %copy-done.2, bf16[384,1024]{1,0:T(8,128)(2,1)} %collective-permute-done.13.refs_1_, bf16[384,1024]{1,0:T(8,128)(2,1)S(1)} %collective-permute-done.16.refs_2_, ...), custom_call_target="tpu_custom_call", output_to_operand_aliasing={{0}: (5, {}), {1}: (6, {})} | custom-call | tf_op jit(solution)/shard_map/pallas_call | solution.py:117
  219.0 1.4 shard_map.69
  (54 shorter events, 3.1 us)
Async XLA Ops:
  7.2 69.7 %all-gather.5.cloned.1.call-start = ((), (), s32[]{:S(2)}) async-start(), calls=%async_computation.1 | async-start | bytes 1769472 | tf_op jit(solution)/shard_map/all_gather | solution.py:79
  11.5 7.3 %copy-start.4 = (bf16[384,3584]{1,0:T(8,128)(2,1)}, bf16[384,3584]{1,0:T(8,128)(2,1)S(1)}, u32[]{:S(2)}) copy-start(bf16[384,3584]{1,0:T(8,128)(2,1)S(1)} %fusion.29) | copy-start | bytes 8257540
  11.5 39.8 %collective-permute-start.5 = (bf16[384,3584]{1,0:T(8,128)(2,1)S(1)}, bf16[384,3584]{1,0:T(8,128)(2,1)}, u32[]{:S(2)}, u32[]{:S(2)}) collective-permute-start(bf16[384,3584]{1,0:T(8,128)(2,1)S(1)} %fusion.29), channel_id=1, source_target_pairs={{0,8},{1,17},{2,10},{3,19},{4,12},{5,21},{6,14},{7,23},{8,0},{9,25... | collective-permute-start | bytes 8257544 | tf_op jit(solution)/shard_map/ppermute | solution.py:142
  16.4 2.3 %collective-permute-start = (bf16[4,48,1024]{2,1,0:T(8,128)(2,1)}, bf16[4,48,1024]{2,1,0:T(8,128)(2,1)S(1)}, u32[]{:S(2)}, u32[]{:S(2)}) collective-permute-start(bf16[4,48,1024]{2,1,0:T(8,128)(2,1)} %get-tuple-element.112), channel_id=1, source_target_pairs={{0,1},{1,0},{2,3},{3,2},{4,5},{5,4},{6,7},{7,6},{8,9},{9,8},{10,11... | collective-permute-start | bytes 1179656 | tf_op jit(solution)/shard_map/ppermute | solution.py:43
  19.1 34.5 %copy-start.10 = (bf16[48,3584]{1,0:T(8,128)(2,1)S(1)}, bf16[48,3584]{1,0:T(8,128)(2,1)}, u32[]{:S(2)}) copy-start(bf16[48,3584]{1,0:T(8,128)(2,1)} %split.8) | copy-start | bytes 1032196
  20.0 9.9 %collective-permute-start.3 = (bf16[48,2048]{1,0:T(8,128)(2,1)}, bf16[48,2048]{1,0:T(8,128)(2,1)}, u32[]{:S(2)}, u32[]{:S(2)}) collective-permute-start(bf16[48,2048]{1,0:T(8,128)(2,1)} %get-tuple-element.107), channel_id=1, source_target_pairs={{0,6},{1,7},{2,4},{3,5},{4,2},{5,3},{6,0},{7,1},{8,14},{9,15},{10,... | collective-permute-start | bytes 589832 | tf_op jit(solution)/shard_map/ppermute | solution.py:61
  23.6 17.7 %collective-permute-start.2 = (bf16[48,2048]{1,0:T(8,128)(2,1)}, bf16[48,2048]{1,0:T(8,128)(2,1)}, u32[]{:S(2)}, u32[]{:S(2)}) collective-permute-start(bf16[48,2048]{1,0:T(8,128)(2,1)} %get-tuple-element.108), channel_id=1, source_target_pairs={{0,4},{1,5},{2,6},{3,7},{4,0},{5,1},{6,2},{7,3},{8,12},{9,13},{10,... | collective-permute-start | bytes 589832 | tf_op jit(solution)/shard_map/ppermute | solution.py:61
  23.6 17.7 %collective-permute-start.1 = (bf16[48,2048]{1,0:T(8,128)(2,1)S(1)}, bf16[48,2048]{1,0:T(8,128)(2,1)}, u32[]{:S(2)}, u32[]{:S(2)}) collective-permute-start(bf16[48,2048]{1,0:T(8,128)(2,1)S(1)} %get-tuple-element.109), channel_id=1, source_target_pairs={{0,2},{1,3},{2,0},{3,1},{4,6},{5,7},{6,4},{7,5},{8,10},{9,11},{10,... | collective-permute-start | bytes 589832 | tf_op jit(solution)/shard_map/ppermute | solution.py:61
  43.2 8.1 %collective-permute-start.4 = (bf16[48,2048]{1,0:T(8,128)(2,1)S(1)}, bf16[48,2048]{1,0:T(8,128)(2,1)}, u32[]{:S(2)}, u32[]{:S(2)}) collective-permute-start(bf16[48,2048]{1,0:T(8,128)(2,1)S(1)} %get-tuple-element.105), channel_id=1, source_target_pairs={{0,24},{8,16},{16,8},{24,0},{1,25},{9,17},{17,9},{25,1},{2,26},{10... | collective-permute-start | bytes 589832 | tf_op jit(solution)/shard_map/ppermute | solution.py:71
  51.4 78.9 %all-gather.3.cloned.1.call-start = ((), (), s32[]{:S(2)}) async-start(), calls=%async_computation | async-start | bytes 5308416 | tf_op jit(solution)/shard_map/all_gather | solution.py:81
  51.6 8.1 %collective-permute-start.6 = (bf16[48,2048]{1,0:T(8,128)(2,1)}, bf16[48,2048]{1,0:T(8,128)(2,1)S(1)}, u32[]{:S(2)}, u32[]{:S(2)}) collective-permute-start(bf16[48,2048]{1,0:T(8,128)(2,1)} %get-tuple-element.53), channel_id=1, source_target_pairs={{0,8},{8,0},{16,24},{24,16},{1,9},{9,1},{17,25},{25,17},{2,10},{10... | collective-permute-start | bytes 589832 | tf_op jit(solution)/shard_map/ppermute | solution.py:71
  53.2 6.6 %collective-permute-start.7 = (bf16[48,2048]{1,0:T(8,128)(2,1)S(1)}, bf16[48,2048]{1,0:T(8,128)(2,1)S(1)}, u32[]{:S(2)}, u32[]{:S(2)}) collective-permute-start(bf16[48,2048]{1,0:T(8,128)(2,1)S(1)} %get-tuple-element.54), channel_id=1, source_target_pairs={{0,16},{8,24},{16,0},{24,8},{1,17},{9,25},{17,1},{25,9},{2,18},{10... | collective-permute-start | bytes 589832 | tf_op jit(solution)/shard_map/ppermute | solution.py:71
  53.7 8.8 %collective-permute-start.8 = (bf16[48,3584]{1,0:T(8,128)(2,1)S(1)}, bf16[48,3584]{1,0:T(8,128)(2,1)S(1)}, u32[]{:S(2)}, u32[]{:S(2)}) collective-permute-start(bf16[48,3584]{1,0:T(8,128)(2,1)S(1)} %copy-done.10), channel_id=1, source_target_pairs={{0,16},{1,9},{2,18},{3,11},{4,20},{5,13},{6,22},{7,15},{8,24},{9,1... | collective-permute-start | bytes 1032200 | tf_op jit(solution)/shard_map/ppermute | solution.py:149
  62.5 29.6 %collective-permute-start.9 = (bf16[336,3584]{1,0:T(8,128)(2,1)}, bf16[336,3584]{1,0:T(8,128)(2,1)S(1)}, u32[]{:S(2)}, u32[]{:S(2)}) collective-permute-start(bf16[336,3584]{1,0:T(8,128)(2,1)} %split.9), channel_id=1, source_target_pairs={{0,16},{1,9},{2,18},{3,11},{4,20},{5,13},{6,22},{7,15},{8,24},{9,1... | collective-permute-start | bytes 7225352 | tf_op jit(solution)/shard_map/ppermute | solution.py:150
  83.8 38.0 %collective-permute-start.10 = (bf16[384,3584]{1,0:T(8,128)(2,1)}, bf16[384,3584]{1,0:T(8,128)(2,1)}, u32[]{:S(2)}, u32[]{:S(2)}) collective-permute-start(bf16[384,3584]{1,0:T(8,128)(2,1)} %collective-permute-done.5), channel_id=1, source_target_pairs={{0,16},{1,9},{2,18},{3,11},{4,20},{5,13},{6,22},{7,15},{8,24},{9,1... | collective-permute-start | bytes 8257544 | tf_op jit(solution)/shard_map/ppermute | solution.py:165
  85.3 14.3 %copy-start.9 = (bf16[384,1536]{1,0:T(8,128)(2,1)S(1)}, bf16[384,1536]{1,0:T(8,128)(2,1)}, u32[]{:S(2)}) copy-start(bf16[384,1536]{1,0:T(8,128)(2,1)} %fusion.42) | copy-start | bytes 3538948
  121.8 38.3 %collective-permute-start.12 = (bf16[384,3584]{1,0:T(8,128)(2,1)}, bf16[384,3584]{1,0:T(8,128)(2,1)}, u32[]{:S(2)}, u32[]{:S(2)}) collective-permute-start(bf16[384,3584]{1,0:T(8,128)(2,1)} %pad_maximum_fusion), channel_id=1, source_target_pairs={{0,16},{1,9},{2,18},{3,11},{4,20},{5,13},{6,22},{7,15},{8,24},{9,1... | collective-permute-start | bytes 8257544 | tf_op jit(solution)/shard_map/ppermute | solution.py:165
  130.3 13.2 %slice-start = ((s8[14680064]{0:T(1024)(128)(4,1)}), s8[4194304]{0:T(1024)(128)(4,1)S(1)}, s32[]{:S(2)}) async-start(s8[14680064]{0:T(1024)(128)(4,1)} %bitcast.52), calls=%async_computation.2 | async-start | bytes 8388608
  133.4 24.8 %copy-start.5 = (bf16[384,2048]{1,0:T(8,128)(2,1)}, bf16[384,2048]{1,0:T(8,128)(2,1)S(1)}, u32[]{:S(2)}) copy-start(bf16[384,2048]{1,0:T(8,128)(2,1)S(1)} %get-tuple-element.75) | copy-start | bytes 4718596
  133.4 10.1 %slice-start.1 = ((s8[14680064]{0:T(1024)(128)(4,1)}), s8[4194304]{0:T(1024)(128)(4,1)S(1)}, s32[]{:S(2)}) async-start(s8[14680064]{0:T(1024)(128)(4,1)} %bitcast.52), calls=%async_computation.3 | async-start | bytes 8388608
  133.6 14.6 %copy-start.8 = (bf16[384,2048]{1,0:T(8,128)(2,1)}, bf16[384,2048]{1,0:T(8,128)(2,1)S(1)}, u32[]{:S(2)}) copy-start(bf16[384,2048]{1,0:T(8,128)(2,1)S(1)} %get-tuple-element.77) | copy-start | bytes 4718596
  133.6 26.5 %copy-start.6 = (bf16[384,2048]{1,0:T(8,128)(2,1)}, bf16[384,2048]{1,0:T(8,128)(2,1)S(1)}, u32[]{:S(2)}) copy-start(bf16[384,2048]{1,0:T(8,128)(2,1)S(1)} %get-tuple-element.92) | copy-start | bytes 4718596
  133.6 9.8 %slice-start.2 = ((s8[14680064]{0:T(1024)(128)(4,1)}), s8[4194304]{0:T(1024)(128)(4,1)S(1)}, s32[]{:S(2)}) async-start(s8[14680064]{0:T(1024)(128)(4,1)} %bitcast.52), calls=%async_computation.4 | async-start | bytes 8388608
  133.7 9.8 %slice-start.3 = ((s8[14680064]{0:T(1024)(128)(4,1)}), s8[2097152]{0:T(1024)(128)(4,1)S(1)}, s32[]{:S(2)}) async-start(s8[14680064]{0:T(1024)(128)(4,1)} %bitcast.52), calls=%async_computation.5 | async-start | bytes 4194304
  146.2 56.5 %collective-permute-start.13 = (bf16[384,1024]{1,0:T(8,128)(2,1)}, bf16[384,1024]{1,0:T(8,128)(2,1)}, u32[]{:S(2)}, u32[]{:S(2)}) collective-permute-start(bf16[384,1024]{1,0:T(8,128)(2,1)} %fusion.51), channel_id=1, source_target_pairs={{0,16},{1,9},{2,18},{3,11},{4,20},{5,13},{6,22},{7,15},{8,24},{9,1... | collective-permute-start | bytes 2359304 | tf_op jit(solution)/shard_map/ppermute | solution.py:165
  147.7 55.0 %collective-permute-start.14 = (bf16[384,2048]{1,0:T(8,128)(2,1)}, bf16[384,2048]{1,0:T(8,128)(2,1)}, u32[]{:S(2)}, u32[]{:S(2)}) collective-permute-start(bf16[384,2048]{1,0:T(8,128)(2,1)} %fusion.36), channel_id=1, source_target_pairs={{0,16},{1,9},{2,18},{3,11},{4,20},{5,13},{6,22},{7,15},{8,24},{9,1... | collective-permute-start | bytes 4718600 | tf_op jit(solution)/shard_map/ppermute | solution.py:165
  150.2 52.5 %collective-permute-start.11 = (bf16[384,512]{1,0:T(8,128)(2,1)}, bf16[384,512]{1,0:T(8,128)(2,1)S(1)}, u32[]{:S(2)}, u32[]{:S(2)}) collective-permute-start(bf16[384,512]{1,0:T(8,128)(2,1)} %fusion.54), channel_id=1, source_target_pairs={{0,16},{1,9},{2,18},{3,11},{4,20},{5,13},{6,22},{7,15},{8,24},{9,1... | collective-permute-start | bytes 1179656 | tf_op jit(solution)/shard_map/ppermute | solution.py:165
  165.9 40.5 %collective-permute-start.15 = (bf16[384,2048]{1,0:T(8,128)(2,1)}, bf16[384,2048]{1,0:T(8,128)(2,1)}, u32[]{:S(2)}, u32[]{:S(2)}) collective-permute-start(bf16[384,2048]{1,0:T(8,128)(2,1)} %add_convert_fusion), channel_id=1, source_target_pairs={{0,8},{1,17},{2,10},{3,19},{4,12},{5,21},{6,14},{7,23},{8,0},{9,25... | collective-permute-start | bytes 4718600 | tf_op jit(solution)/shard_map/ppermute | solution.py:165
  197.9 5.5 %copy-start.7 = (bf16[384,2048]{1,0:T(8,128)(2,1)S(1)}, bf16[384,2048]{1,0:T(8,128)(2,1)}, u32[]{:S(2)}) copy-start(bf16[384,2048]{1,0:T(8,128)(2,1)} %copy-done.6) | copy-start | bytes 4718596
  202.7 4.9 %copy-start = (bf16[384,3584]{1,0:T(8,128)(2,1)S(1)}, bf16[384,3584]{1,0:T(8,128)(2,1)}, u32[]{:S(2)}) copy-start(bf16[384,3584]{1,0:T(8,128)(2,1)} %refs_3_.2) | copy-start | bytes 8257540
  202.7 4.9 %copy-start.1 = (bf16[384,3584]{1,0:T(8,128)(2,1)S(1)}, bf16[384,3584]{1,0:T(8,128)(2,1)}, u32[]{:S(2)}) copy-start(bf16[384,3584]{1,0:T(8,128)(2,1)} %refs_4_.1) | copy-start | bytes 8257540
  202.7 12.1 %collective-permute-start.16 = (bf16[384,1024]{1,0:T(8,128)(2,1)S(1)}, bf16[384,1024]{1,0:T(8,128)(2,1)S(1)}, u32[]{:S(2)}, u32[]{:S(2)}) collective-permute-start(bf16[384,1024]{1,0:T(8,128)(2,1)S(1)} %add_convert_fusion.1), channel_id=1, source_target_pairs={{0,8},{1,17},{2,10},{3,19},{4,12},{5,21},{6,14},{7,23},{8,0},{9,25... | collective-permute-start | bytes 2359304 | tf_op jit(solution)/shard_map/ppermute | solution.py:165
  206.3 8.5 %copy-start.2 = (f32[384,1024]{1,0:T(8,128)S(1)}, f32[384,1024]{1,0:T(8,128)}, u32[]{:S(2)}) copy-start(f32[384,1024]{1,0:T(8,128)} %fusion.32.refs_0_) | copy-start | bytes 4718596
  206.3 12.7 %collective-permute-start.17 = (bf16[384,512]{1,0:T(8,128)(2,1)S(1)}, bf16[384,512]{1,0:T(8,128)(2,1)S(1)}, u32[]{:S(2)}, u32[]{:S(2)}) collective-permute-start(bf16[384,512]{1,0:T(8,128)(2,1)S(1)} %add_convert_fusion.2), channel_id=1, source_target_pairs={{0,8},{1,17},{2,10},{3,19},{4,12},{5,21},{6,14},{7,23},{8,0},{9,25... | collective-permute-start | bytes 1179656 | tf_op jit(solution)/shard_map/ppermute | solution.py:165
  214.5 4.4 %copy-start.3 = (f32[384,512]{1,0:T(8,128)S(1)}, f32[384,512]{1,0:T(8,128)}, u32[]{:S(2)}) copy-start(f32[384,512]{1,0:T(8,128)} %fusion.47.refs_0_) | copy-start | bytes 2359300
Sparse Core Ops, SparseCore 0:
  51.5 25.3 all-gather.4
  79.0 51.1 all-gather.2

commit v12 on v11

--- a/solution.py
+++ b/solution.py
@@ -234,7 +234,7 @@
             up_act,
             outs,
             start,
-            math.gcd(unit, 256),
+            math.gcd(unit, 512),
         )
     return (*outs, grad_weight)
 

time: 228 us -> 227 us (level)
  Pallas kernels: 12.2 us -> 9.22 us
  waiting for transfers between devices: 77.7 us -> 80.6 us
    pallas_call x3, Pallas kernels: 12.2 us -> 9.22 us  [finish(): pl.pallas_call(kernel, grid=(width // block,), in_specs=specs, out_specs=...]
    ppermute x8, waiting for transfers between devices: 19.4 us -> 22.2 us  [send(): return lax.ppermute(total, BOTH, pairs[step])]
  transfers between devices with their start and end apart: 20 -> 20, of which waited for: 11 -> 11; matrix products, arithmetic and copies ran while one was open for 42% -> 42% of each run, Pallas kernels for 5% -> 3%
where the time goes in v12:
time: 227 us
  matrix products  81.2 us (36%)
  waiting for transfers between devices  80.6 us (36%)
  starting transfers between devices  22.5 us (10%)
  between operations  14.3 us (6%)
  other arithmetic  10.4 us (5%)
  Pallas kernels  9.22 us (4%)
  local copies, waits for them, and re-layouts  9 us (4%)
    dot_general x11, matrix products, product(): lax.dot_general(after(block, *before), down_weight[start:stop], (((1,), (...  50.7 us
    dot_general x1, matrix products, on_device(): lax.dot_general(jnp.concatenate(gathered, axis=0), jnp.concatenate(grads,...  30.5 us
    ppermute x8, waiting for transfers between devices, send(): return lax.ppermute(total, BOTH, pairs[step])  22.2 us
    ppermute x4, waiting for transfers between devices, spread_tokens(): piece = lax.ppermute(piece, 'col', pairs)  16.9 us
    all_gather x1, waiting for transfers between devices, gather_tokens(): first = lax.all_gather(blocks[-1], 'col', axis=0, tiled=True)  13.8 us
    ppermute x3, waiting for transfers between devices, spread_tokens(): piece = lax.ppermute(piece, 'row', [(r, r ^ flip) for r in range(rows)])  10.8 us
    pallas_call x3, Pallas kernels, finish(): pl.pallas_call(kernel, grid=(width // block,), in_specs=specs, out_specs=...  9.22 us
    ppermute x8, starting transfers between devices, send(): return lax.ppermute(total, BOTH, pairs[step])  8.86 us
  transfers between devices with their start and end apart: 20, of which 11 were waited for; matrix products, arithmetic and copies ran while one was open for 42% of the time, Pallas kernels for 3%

profile of v12, /device:TPU:0, one launch (start us, length us, event | category | flops | bytes accessed | tf_op | source)
XLA Modules:
  0.0 227.1 jit_solution(7376120500658797343)
XLA Ops:
  7.2 4.3 %fusion.29 = bf16[384,3584]{1,0:T(8,128)(2,1)S(1)} fusion(bf16[384,3584]{1,0:T(8,128)(2,1)} %refs_4_.1, bf16[384,3584]{1,0:T(8,128)(2,1)} %refs_3_.2), kind=kLoop, calls=%fused_computation.31 | loop fusion | flops 11010048 | bytes 8257536 | tf_op jit(solution)/shard_map/convert_element_type | solution.py:139
  11.5 3.0 %collective-permute-start.5 = (bf16[384,3584]{1,0:T(8,128)(2,1)S(1)}, bf16[384,3584]{1,0:T(8,128)(2,1)}, u32[]{:S(2)}, u32[]{:S(2)}) collective-permute-start(bf16[384,3584]{1,0:T(8,128)(2,1)S(1)} %fusion.29), channel_id=1, source_target_pairs={{0,8},{1,17},{2,10},{3,19},{4,12},{5,21},{6,14},{7,23},{8,0},{9,25... | collective-permute-start | bytes 8257544 | tf_op jit(solution)/shard_map/ppermute | solution.py:142
  14.5 1.9 dynamic-slice_bitcast_fusion
  16.4 0.8 split.8
  17.2 1.6 split.9
  19.1 0.8 constant_dynamic-slice_fusion
  20.0 3.6 %collective-permute-start.3 = (bf16[48,2048]{1,0:T(8,128)(2,1)}, bf16[48,2048]{1,0:T(8,128)(2,1)}, u32[]{:S(2)}, u32[]{:S(2)}) collective-permute-start(bf16[48,2048]{1,0:T(8,128)(2,1)} %get-tuple-element.107), channel_id=1, source_target_pairs={{0,6},{1,7},{2,4},{3,5},{4,2},{5,3},{6,0},{7,1},{8,14},{9,15},{10,... | collective-permute-start | bytes 589832 | tf_op jit(solution)/shard_map/ppermute | solution.py:61
  23.6 0.8 collective-permute-start.1
  24.4 5.6 %collective-permute-done.3 = bf16[48,2048]{1,0:T(8,128)(2,1)} collective-permute-done((bf16[48,2048]{1,0:T(8,128)(2,1)}, bf16[48,2048]{1,0:T(8,128)(2,1)}, u32[]{:S(2)}, u32[]{:S(2)}) %collective-permute-start.3) | collective-permute-done | bytes 196640 | tf_op jit(solution)/shard_map/ppermute | solution.py:61
  29.9 11.3 %collective-permute-done.2 = bf16[48,2048]{1,0:T(8,128)(2,1)} collective-permute-done((bf16[48,2048]{1,0:T(8,128)(2,1)}, bf16[48,2048]{1,0:T(8,128)(2,1)}, u32[]{:S(2)}, u32[]{:S(2)}) %collective-permute-start.2) | collective-permute-done | bytes 196640 | tf_op jit(solution)/shard_map/ppermute | solution.py:61
  41.3 1.2 pad_maximum_fusion.3
  42.5 0.8 dynamic-slice_bitcast_fusion.5
  43.2 1.8 collective-permute-start.4
  45.1 6.3 %collective-permute-done.4 = bf16[48,2048]{1,0:T(8,128)(2,1)} collective-permute-done((bf16[48,2048]{1,0:T(8,128)(2,1)S(1)}, bf16[48,2048]{1,0:T(8,128)(2,1)}, u32[]{:S(2)}, u32[]{:S(2)}) %collective-permute-start.4) | collective-permute-done | bytes 196640 | tf_op jit(solution)/shard_map/ppermute | solution.py:71
  51.6 1.6 collective-permute-start.6
  53.7 1.5 collective-permute-start.8
  55.2 4.5 %collective-permute-done.6 = bf16[48,2048]{1,0:T(8,128)(2,1)S(1)} collective-permute-done((bf16[48,2048]{1,0:T(8,128)(2,1)}, bf16[48,2048]{1,0:T(8,128)(2,1)S(1)}, u32[]{:S(2)}, u32[]{:S(2)}) %collective-permute-start.6) | collective-permute-done | bytes 196640 | tf_op jit(solution)/shard_map/ppermute | solution.py:71
  59.7 0.9 pad_maximum_fusion.4
  60.6 1.9 collective-permute-done.8
  63.1 13.8 %all-gather.5.cloned.1.call-done = bf16[384,2048]{1,0:T(8,128)(2,1)} async-done(((bf16[48,2048]{1,0:T(8,128)(2,1)}), bf16[384,2048]{1,0:T(8,128)(2,1)}) %all-gather.5.cloned.1.call-update) | async-done | bytes 1572880 | tf_op jit(solution)/shard_map/all_gather | solution.py:79
  76.9 6.9 %fusion.42 = bf16[384,1536]{1,0:T(8,128)(2,1)} fusion(bf16[384,2048]{1,0:T(8,128)(2,1)} %all-gather.5.cloned.1.call-done, bf16[3584,2048]{1,0:T(8,128)(2,1)} %param.7), kind=kOutput, calls=%fused_computation.41 | convolution fusion | flops 2416508928 | bytes 9043968 | tf_op jit(solution)/shard_map/dot_general | solution.py:157
  83.8 1.5 collective-permute-start.10
  85.3 6.9 %collective-permute-done.9 = bf16[336,3584]{1,0:T(8,128)(2,1)S(1)} collective-permute-done((bf16[336,3584]{1,0:T(8,128)(2,1)}, bf16[336,3584]{1,0:T(8,128)(2,1)S(1)}, u32[]{:S(2)}, u32[]{:S(2)}) %collective-permute-start.9) | collective-permute-done | bytes 2408480 | tf_op jit(solution)/shard_map/ppermute | solution.py:150
  92.2 7.4 %fusion.39 = bf16[384,2048]{1,0:T(8,128)(2,1)S(1)} fusion(bf16[384,2048]{1,0:T(8,128)(2,1)} %all-gather.5.cloned.1.call-done, bf16[3584,2048]{1,0:T(8,128)(2,1)} %param.7), kind=kOutput, calls=%fused_computation.40 | convolution fusion | flops 3222011904 | bytes 11534336 | tf_op jit(solution)/shard_map/dot_general | solution.py:157
  99.6 1.7 pad_maximum_fusion
  101.3 1.7 pad_maximum_fusion.1
  103.0 18.8 %collective-permute-done.10 = bf16[384,3584]{1,0:T(8,128)(2,1)} collective-permute-done((bf16[384,3584]{1,0:T(8,128)(2,1)}, bf16[384,3584]{1,0:T(8,128)(2,1)}, u32[]{:S(2)}, u32[]{:S(2)}) %collective-permute-start.10) | collective-permute-done | bytes 2752544 | tf_op jit(solution)/shard_map/ppermute | solution.py:165
  122.3 8.0 %all-gather.3.cloned.1.call-done = bf16[3,384,2048]{2,1,0:T(8,128)(2,1)} async-done(((bf16[3,48,2048]{2,1,0:T(8,128)(2,1)}), bf16[3,384,2048]{2,1,0:T(8,128)(2,1)}) %all-gather.3.cloned.1.call-update) | async-done | bytes 4718608 | tf_op jit(solution)/shard_map/all_gather | solution.py:81
  130.3 3.1 %slice_bitcast_fusion = (bf16[384,2048]{1,0:T(8,128)(2,1)S(1)}, bf16[384,2048]{1,0:T(8,128)(2,1)S(1)}, bf16[384,2048]{1,0:T(8,128)(2,1)S(1)}) fusion(bf16[3,384,2048]{2,1,0:T(8,128)(2,1)} %all-gather.3.cloned.1.call-done), kind=kLoop, calls=%fused_computation.50 | loop fusion | bytes 9437184 | tf_op jit(solution)/shard_map/squeeze | solution.py:82
  133.7 9.8 %fusion.36 = bf16[384,2048]{1,0:T(8,128)(2,1)} fusion(bf16[384,2048]{1,0:T(8,128)(2,1)S(1)} %get-tuple-element.77, bf16[3584,2048]{1,0:T(8,128)(2,1)} %param.7), kind=kOutput, calls=%fused_computation.39 | convolution fusion | flops 3222011904 | bytes 11534336 | tf_op jit(solution)/shard_map/dot_general | solution.py:157
  143.5 2.7 %fusion.51 = bf16[384,1024]{1,0:T(8,128)(2,1)} fusion(bf16[384,2048]{1,0:T(8,128)(2,1)S(1)} %get-tuple-element.77, bf16[3584,2048]{1,0:T(8,128)(2,1)S(1)} %bitcast.53), kind=kOutput, calls=%fused_computation.56 | convolution fusion | flops 1611005952 | bytes 6553600 | tf_op jit(solution)/shard_map/dot_general | solution.py:157
  146.2 1.5 collective-permute-start.13
  148.2 2.0 fusion.54
  150.2 1.5 collective-permute-start.11
  151.7 3.5 %fusion.12.own_ref = f32[384,2048]{1,0:T(8,128)S(1)} fusion(bf16[384,2048]{1,0:T(8,128)(2,1)S(1)} %get-tuple-element.75, bf16[3584,2048]{1,0:T(8,128)(2,1)S(1)} %bitcast.53), kind=kOutput, calls=%fused_computation.14 | convolution fusion | flops 3221225472 | bytes 13107200 | tf_op jit(solution)/shard_map/dot_general | solution.py:157
  155.2 3.0 %fusion.32.refs_0_ = f32[384,1024]{1,0:T(8,128)} fusion(bf16[384,2048]{1,0:T(8,128)(2,1)S(1)} %get-tuple-element.75, bf16[3584,2048]{1,0:T(8,128)(2,1)S(1)} %bitcast.53), kind=kOutput, calls=%fused_computation.34 | convolution fusion | flops 1610612736 | bytes 7340032 | tf_op jit(solution)/shard_map/dot_general | solution.py:157
  158.2 1.9 fusion.47.refs_0_
  160.1 5.7 %add_convert_fusion = bf16[384,2048]{1,0:T(8,128)(2,1)} fusion(bf16[384,3584]{1,0:T(8,128)(2,1)} %collective-permute-done.12, bf16[384,2048]{1,0:T(8,128)(2,1)S(1)} %get-tuple-element.92, bf16[3584,2048]{1,0:T(8,128)(2,1)S(1)} %bitcast.53), kind=kOutput, calls=%fused_computation.38 | convolution fusion | flops 3223584768 | bytes 13107200 | tf_op jit(solution)/shard_map/dot_general | solution.py:157
  165.9 1.5 collective-permute-start.15
  167.3 30.5 %fusion = f32[3584,2048]{1,0:T(8,128)} fusion(bf16[384,3584]{1,0:T(8,128)(2,1)} %collective-permute-done.10, bf16[384,3584]{1,0:T(8,128)(2,1)} %pad_maximum_fusion.1, bf16[384,3584]{1,0:T(8,128)(2,1)} %collective-permute-done.5, bf16[384,3584]{1,0:T(8,128)(2,1)} %copy-done.4, bf16[384,2048]{1,0:T(8,128)(2,1)} %all-gather.5.cloned.1.call-done, ...), kind=kOutput, calls=%fused_computation | convolution fusion | flops 22617784320 | bytes 46661632 | tf_op jit(solution)/shard_map/dot_general | solution.py:215
  197.9 4.8 %add_convert_fusion.1 = bf16[384,1024]{1,0:T(8,128)(2,1)S(1)} fusion(bf16[384,3584]{1,0:T(8,128)(2,1)} %collective-permute-done.12, bf16[384,2048]{1,0:T(8,128)(2,1)} %copy-done.6, bf16[3584,2048]{1,0:T(8,128)(2,1)} %param.7), kind=kOutput, calls=%fused_computation.53 | convolution fusion | flops 1611792384 | bytes 7340032 | tf_op jit(solution)/shard_map/dot_general | solution.py:157
  203.3 3.0 %add_convert_fusion.2 = bf16[384,512]{1,0:T(8,128)(2,1)S(1)} fusion(bf16[384,3584]{1,0:T(8,128)(2,1)} %collective-permute-done.12, bf16[384,2048]{1,0:T(8,128)(2,1)S(1)} %copy-done.7, bf16[3584,2048]{1,0:T(8,128)(2,1)} %param.7), kind=kOutput, calls=%fused_computation.64 | convolution fusion | flops 805896192 | bytes 4456448 | tf_op jit(solution)/shard_map/dot_general | solution.py:157
  206.3 1.3 collective-permute-start.17
  207.6 5.0 %shard_map.67 = (bf16[384,3584]{1,0:T(8,128)(2,1)}, bf16[384,3584]{1,0:T(8,128)(2,1)}) custom-call(f32[384,2048]{1,0:T(8,128)S(1)} %fusion.12.own_ref, bf16[384,2048]{1,0:T(8,128)(2,1)} %collective-permute-done.14.refs_0_, bf16[384,2048]{1,0:T(8,128)(2,1)} %collective-permute-done.15.refs_1_, bf16[384,3584]{1,0:T(8,128)(2,1)S(1)} %copy-done, ...), custom_call_target="tpu_custom_call" | custom-call | tf_op jit(solution)/shard_map/pallas_call | solution.py:117
  212.6 2.2 collective-permute-done.16.refs_2_
  214.8 2.9 %shard_map.68 = (bf16[384,3584]{1,0:T(8,128)(2,1)}, bf16[384,3584]{1,0:T(8,128)(2,1)}) custom-call(f32[384,1024]{1,0:T(8,128)S(1)} %copy-done.2, bf16[384,1024]{1,0:T(8,128)(2,1)} %collective-permute-done.13.refs_1_, bf16[384,1024]{1,0:T(8,128)(2,1)S(1)} %collective-permute-done.16.refs_2_, ...), custom_call_target="tpu_custom_call", output_to_operand_aliasing={{0}: (5, {}), {1}: (6, {})} | custom-call | tf_op jit(solution)/shard_map/pallas_call | solution.py:117
  217.7 1.3 collective-permute-done.17.refs_2_
  219.0 1.3 shard_map.69
  (54 shorter events, 3.7 us)
Async XLA Ops:
  7.2 69.7 %all-gather.5.cloned.1.call-start = ((), (), s32[]{:S(2)}) async-start(), calls=%async_computation.1 | async-start | bytes 1769472 | tf_op jit(solution)/shard_map/all_gather | solution.py:79
  11.5 7.3 %copy-start.4 = (bf16[384,3584]{1,0:T(8,128)(2,1)}, bf16[384,3584]{1,0:T(8,128)(2,1)S(1)}, u32[]{:S(2)}) copy-start(bf16[384,3584]{1,0:T(8,128)(2,1)S(1)} %fusion.29) | copy-start | bytes 8257540
  11.5 39.8 %collective-permute-start.5 = (bf16[384,3584]{1,0:T(8,128)(2,1)S(1)}, bf16[384,3584]{1,0:T(8,128)(2,1)}, u32[]{:S(2)}, u32[]{:S(2)}) collective-permute-start(bf16[384,3584]{1,0:T(8,128)(2,1)S(1)} %fusion.29), channel_id=1, source_target_pairs={{0,8},{1,17},{2,10},{3,19},{4,12},{5,21},{6,14},{7,23},{8,0},{9,25... | collective-permute-start | bytes 8257544 | tf_op jit(solution)/shard_map/ppermute | solution.py:142
  16.4 2.3 %collective-permute-start = (bf16[4,48,1024]{2,1,0:T(8,128)(2,1)}, bf16[4,48,1024]{2,1,0:T(8,128)(2,1)S(1)}, u32[]{:S(2)}, u32[]{:S(2)}) collective-permute-start(bf16[4,48,1024]{2,1,0:T(8,128)(2,1)} %get-tuple-element.112), channel_id=1, source_target_pairs={{0,1},{1,0},{2,3},{3,2},{4,5},{5,4},{6,7},{7,6},{8,9},{9,8},{10,11... | collective-permute-start | bytes 1179656 | tf_op jit(solution)/shard_map/ppermute | solution.py:43
  19.1 34.5 %copy-start.10 = (bf16[48,3584]{1,0:T(8,128)(2,1)S(1)}, bf16[48,3584]{1,0:T(8,128)(2,1)}, u32[]{:S(2)}) copy-start(bf16[48,3584]{1,0:T(8,128)(2,1)} %split.8) | copy-start | bytes 1032196
  20.0 9.9 %collective-permute-start.3 = (bf16[48,2048]{1,0:T(8,128)(2,1)}, bf16[48,2048]{1,0:T(8,128)(2,1)}, u32[]{:S(2)}, u32[]{:S(2)}) collective-permute-start(bf16[48,2048]{1,0:T(8,128)(2,1)} %get-tuple-element.107), channel_id=1, source_target_pairs={{0,6},{1,7},{2,4},{3,5},{4,2},{5,3},{6,0},{7,1},{8,14},{9,15},{10,... | collective-permute-start | bytes 589832 | tf_op jit(solution)/shard_map/ppermute | solution.py:61
  23.6 17.7 %collective-permute-start.2 = (bf16[48,2048]{1,0:T(8,128)(2,1)}, bf16[48,2048]{1,0:T(8,128)(2,1)}, u32[]{:S(2)}, u32[]{:S(2)}) collective-permute-start(bf16[48,2048]{1,0:T(8,128)(2,1)} %get-tuple-element.108), channel_id=1, source_target_pairs={{0,4},{1,5},{2,6},{3,7},{4,0},{5,1},{6,2},{7,3},{8,12},{9,13},{10,... | collective-permute-start | bytes 589832 | tf_op jit(solution)/shard_map/ppermute | solution.py:61
  23.6 17.7 %collective-permute-start.1 = (bf16[48,2048]{1,0:T(8,128)(2,1)S(1)}, bf16[48,2048]{1,0:T(8,128)(2,1)}, u32[]{:S(2)}, u32[]{:S(2)}) collective-permute-start(bf16[48,2048]{1,0:T(8,128)(2,1)S(1)} %get-tuple-element.109), channel_id=1, source_target_pairs={{0,2},{1,3},{2,0},{3,1},{4,6},{5,7},{6,4},{7,5},{8,10},{9,11},{10,... | collective-permute-start | bytes 589832 | tf_op jit(solution)/shard_map/ppermute | solution.py:61
  43.2 8.1 %collective-permute-start.4 = (bf16[48,2048]{1,0:T(8,128)(2,1)S(1)}, bf16[48,2048]{1,0:T(8,128)(2,1)}, u32[]{:S(2)}, u32[]{:S(2)}) collective-permute-start(bf16[48,2048]{1,0:T(8,128)(2,1)S(1)} %get-tuple-element.105), channel_id=1, source_target_pairs={{0,24},{8,16},{16,8},{24,0},{1,25},{9,17},{17,9},{25,1},{2,26},{10... | collective-permute-start | bytes 589832 | tf_op jit(solution)/shard_map/ppermute | solution.py:71
  51.4 78.9 %all-gather.3.cloned.1.call-start = ((), (), s32[]{:S(2)}) async-start(), calls=%async_computation | async-start | bytes 5308416 | tf_op jit(solution)/shard_map/all_gather | solution.py:81
  51.6 8.1 %collective-permute-start.6 = (bf16[48,2048]{1,0:T(8,128)(2,1)}, bf16[48,2048]{1,0:T(8,128)(2,1)S(1)}, u32[]{:S(2)}, u32[]{:S(2)}) collective-permute-start(bf16[48,2048]{1,0:T(8,128)(2,1)} %get-tuple-element.53), channel_id=1, source_target_pairs={{0,8},{8,0},{16,24},{24,16},{1,9},{9,1},{17,25},{25,17},{2,10},{10... | collective-permute-start | bytes 589832 | tf_op jit(solution)/shard_map/ppermute | solution.py:71
  53.2 6.6 %collective-permute-start.7 = (bf16[48,2048]{1,0:T(8,128)(2,1)S(1)}, bf16[48,2048]{1,0:T(8,128)(2,1)S(1)}, u32[]{:S(2)}, u32[]{:S(2)}) collective-permute-start(bf16[48,2048]{1,0:T(8,128)(2,1)S(1)} %get-tuple-element.54), channel_id=1, source_target_pairs={{0,16},{8,24},{16,0},{24,8},{1,17},{9,25},{17,1},{25,9},{2,18},{10... | collective-permute-start | bytes 589832 | tf_op jit(solution)/shard_map/ppermute | solution.py:71
  53.7 8.8 %collective-permute-start.8 = (bf16[48,3584]{1,0:T(8,128)(2,1)S(1)}, bf16[48,3584]{1,0:T(8,128)(2,1)S(1)}, u32[]{:S(2)}, u32[]{:S(2)}) collective-permute-start(bf16[48,3584]{1,0:T(8,128)(2,1)S(1)} %copy-done.10), channel_id=1, source_target_pairs={{0,16},{1,9},{2,18},{3,11},{4,20},{5,13},{6,22},{7,15},{8,24},{9,1... | collective-permute-start | bytes 1032200 | tf_op jit(solution)/shard_map/ppermute | solution.py:149
  62.5 29.6 %collective-permute-start.9 = (bf16[336,3584]{1,0:T(8,128)(2,1)}, bf16[336,3584]{1,0:T(8,128)(2,1)S(1)}, u32[]{:S(2)}, u32[]{:S(2)}) collective-permute-start(bf16[336,3584]{1,0:T(8,128)(2,1)} %split.9), channel_id=1, source_target_pairs={{0,16},{1,9},{2,18},{3,11},{4,20},{5,13},{6,22},{7,15},{8,24},{9,1... | collective-permute-start | bytes 7225352 | tf_op jit(solution)/shard_map/ppermute | solution.py:150
  83.8 38.0 %collective-permute-start.10 = (bf16[384,3584]{1,0:T(8,128)(2,1)}, bf16[384,3584]{1,0:T(8,128)(2,1)}, u32[]{:S(2)}, u32[]{:S(2)}) collective-permute-start(bf16[384,3584]{1,0:T(8,128)(2,1)} %collective-permute-done.5), channel_id=1, source_target_pairs={{0,16},{1,9},{2,18},{3,11},{4,20},{5,13},{6,22},{7,15},{8,24},{9,1... | collective-permute-start | bytes 8257544 | tf_op jit(solution)/shard_map/ppermute | solution.py:165
  85.3 14.3 %copy-start.9 = (bf16[384,1536]{1,0:T(8,128)(2,1)S(1)}, bf16[384,1536]{1,0:T(8,128)(2,1)}, u32[]{:S(2)}) copy-start(bf16[384,1536]{1,0:T(8,128)(2,1)} %fusion.42) | copy-start | bytes 3538948
  121.8 38.3 %collective-permute-start.12 = (bf16[384,3584]{1,0:T(8,128)(2,1)}, bf16[384,3584]{1,0:T(8,128)(2,1)}, u32[]{:S(2)}, u32[]{:S(2)}) collective-permute-start(bf16[384,3584]{1,0:T(8,128)(2,1)} %pad_maximum_fusion), channel_id=1, source_target_pairs={{0,16},{1,9},{2,18},{3,11},{4,20},{5,13},{6,22},{7,15},{8,24},{9,1... | collective-permute-start | bytes 8257544 | tf_op jit(solution)/shard_map/ppermute | solution.py:165
  130.3 13.2 %slice-start = ((s8[14680064]{0:T(1024)(128)(4,1)}), s8[4194304]{0:T(1024)(128)(4,1)S(1)}, s32[]{:S(2)}) async-start(s8[14680064]{0:T(1024)(128)(4,1)} %bitcast.52), calls=%async_computation.2 | async-start | bytes 8388608
  133.4 24.8 %copy-start.5 = (bf16[384,2048]{1,0:T(8,128)(2,1)}, bf16[384,2048]{1,0:T(8,128)(2,1)S(1)}, u32[]{:S(2)}) copy-start(bf16[384,2048]{1,0:T(8,128)(2,1)S(1)} %get-tuple-element.75) | copy-start | bytes 4718596
  133.4 10.1 %slice-start.1 = ((s8[14680064]{0:T(1024)(128)(4,1)}), s8[4194304]{0:T(1024)(128)(4,1)S(1)}, s32[]{:S(2)}) async-start(s8[14680064]{0:T(1024)(128)(4,1)} %bitcast.52), calls=%async_computation.3 | async-start | bytes 8388608
  133.6 14.6 %copy-start.8 = (bf16[384,2048]{1,0:T(8,128)(2,1)}, bf16[384,2048]{1,0:T(8,128)(2,1)S(1)}, u32[]{:S(2)}) copy-start(bf16[384,2048]{1,0:T(8,128)(2,1)S(1)} %get-tuple-element.77) | copy-start | bytes 4718596
  133.6 26.5 %copy-start.6 = (bf16[384,2048]{1,0:T(8,128)(2,1)}, bf16[384,2048]{1,0:T(8,128)(2,1)S(1)}, u32[]{:S(2)}) copy-start(bf16[384,2048]{1,0:T(8,128)(2,1)S(1)} %get-tuple-element.92) | copy-start | bytes 4718596
  133.6 9.8 %slice-start.2 = ((s8[14680064]{0:T(1024)(128)(4,1)}), s8[4194304]{0:T(1024)(128)(4,1)S(1)}, s32[]{:S(2)}) async-start(s8[14680064]{0:T(1024)(128)(4,1)} %bitcast.52), calls=%async_computation.4 | async-start | bytes 8388608
  133.7 9.8 %slice-start.3 = ((s8[14680064]{0:T(1024)(128)(4,1)}), s8[2097152]{0:T(1024)(128)(4,1)S(1)}, s32[]{:S(2)}) async-start(s8[14680064]{0:T(1024)(128)(4,1)} %bitcast.52), calls=%async_computation.5 | async-start | bytes 4194304
  146.2 56.5 %collective-permute-start.13 = (bf16[384,1024]{1,0:T(8,128)(2,1)}, bf16[384,1024]{1,0:T(8,128)(2,1)}, u32[]{:S(2)}, u32[]{:S(2)}) collective-permute-start(bf16[384,1024]{1,0:T(8,128)(2,1)} %fusion.51), channel_id=1, source_target_pairs={{0,16},{1,9},{2,18},{3,11},{4,20},{5,13},{6,22},{7,15},{8,24},{9,1... | collective-permute-start | bytes 2359304 | tf_op jit(solution)/shard_map/ppermute | solution.py:165
  147.7 55.0 %collective-permute-start.14 = (bf16[384,2048]{1,0:T(8,128)(2,1)}, bf16[384,2048]{1,0:T(8,128)(2,1)}, u32[]{:S(2)}, u32[]{:S(2)}) collective-permute-start(bf16[384,2048]{1,0:T(8,128)(2,1)} %fusion.36), channel_id=1, source_target_pairs={{0,16},{1,9},{2,18},{3,11},{4,20},{5,13},{6,22},{7,15},{8,24},{9,1... | collective-permute-start | bytes 4718600 | tf_op jit(solution)/shard_map/ppermute | solution.py:165
  150.2 52.5 %collective-permute-start.11 = (bf16[384,512]{1,0:T(8,128)(2,1)}, bf16[384,512]{1,0:T(8,128)(2,1)S(1)}, u32[]{:S(2)}, u32[]{:S(2)}) collective-permute-start(bf16[384,512]{1,0:T(8,128)(2,1)} %fusion.54), channel_id=1, source_target_pairs={{0,16},{1,9},{2,18},{3,11},{4,20},{5,13},{6,22},{7,15},{8,24},{9,1... | collective-permute-start | bytes 1179656 | tf_op jit(solution)/shard_map/ppermute | solution.py:165
  165.9 40.5 %collective-permute-start.15 = (bf16[384,2048]{1,0:T(8,128)(2,1)}, bf16[384,2048]{1,0:T(8,128)(2,1)}, u32[]{:S(2)}, u32[]{:S(2)}) collective-permute-start(bf16[384,2048]{1,0:T(8,128)(2,1)} %add_convert_fusion), channel_id=1, source_target_pairs={{0,8},{1,17},{2,10},{3,19},{4,12},{5,21},{6,14},{7,23},{8,0},{9,25... | collective-permute-start | bytes 4718600 | tf_op jit(solution)/shard_map/ppermute | solution.py:165
  197.9 5.5 %copy-start.7 = (bf16[384,2048]{1,0:T(8,128)(2,1)S(1)}, bf16[384,2048]{1,0:T(8,128)(2,1)}, u32[]{:S(2)}) copy-start(bf16[384,2048]{1,0:T(8,128)(2,1)} %copy-done.6) | copy-start | bytes 4718596
  202.7 4.9 %copy-start = (bf16[384,3584]{1,0:T(8,128)(2,1)S(1)}, bf16[384,3584]{1,0:T(8,128)(2,1)}, u32[]{:S(2)}) copy-start(bf16[384,3584]{1,0:T(8,128)(2,1)} %refs_3_.2) | copy-start | bytes 8257540
  202.7 4.9 %copy-start.1 = (bf16[384,3584]{1,0:T(8,128)(2,1)S(1)}, bf16[384,3584]{1,0:T(8,128)(2,1)}, u32[]{:S(2)}) copy-start(bf16[384,3584]{1,0:T(8,128)(2,1)} %refs_4_.1) | copy-start | bytes 8257540
  202.7 12.1 %collective-permute-start.16 = (bf16[384,1024]{1,0:T(8,128)(2,1)S(1)}, bf16[384,1024]{1,0:T(8,128)(2,1)S(1)}, u32[]{:S(2)}, u32[]{:S(2)}) collective-permute-start(bf16[384,1024]{1,0:T(8,128)(2,1)S(1)} %add_convert_fusion.1), channel_id=1, source_target_pairs={{0,8},{1,17},{2,10},{3,19},{4,12},{5,21},{6,14},{7,23},{8,0},{9,25... | collective-permute-start | bytes 2359304 | tf_op jit(solution)/shard_map/ppermute | solution.py:165
  206.3 8.5 %copy-start.2 = (f32[384,1024]{1,0:T(8,128)S(1)}, f32[384,1024]{1,0:T(8,128)}, u32[]{:S(2)}) copy-start(f32[384,1024]{1,0:T(8,128)} %fusion.32.refs_0_) | copy-start | bytes 4718596
  206.3 12.7 %collective-permute-start.17 = (bf16[384,512]{1,0:T(8,128)(2,1)S(1)}, bf16[384,512]{1,0:T(8,128)(2,1)S(1)}, u32[]{:S(2)}, u32[]{:S(2)}) collective-permute-start(bf16[384,512]{1,0:T(8,128)(2,1)S(1)} %add_convert_fusion.2), channel_id=1, source_target_pairs={{0,8},{1,17},{2,10},{3,19},{4,12},{5,21},{6,14},{7,23},{8,0},{9,25... | collective-permute-start | bytes 1179656 | tf_op jit(solution)/shard_map/ppermute | solution.py:165
  212.6 6.4 %copy-start.3 = (f32[384,512]{1,0:T(8,128)S(1)}, f32[384,512]{1,0:T(8,128)}, u32[]{:S(2)}) copy-start(f32[384,512]{1,0:T(8,128)} %fusion.47.refs_0_) | copy-start | bytes 2359300
Sparse Core Ops, SparseCore 0:
  51.5 25.3 all-gather.4
  79.0 51.1 all-gather.2
